TPU v7x, 32 devices: a whole 2x2x4 slice. The times are simulated.
32 devices in a mesh: groups: 2 (over x), blocks: 16 (over z, y, core).
Axes of the slice: x: 2, y: 2, z: 4, core: 2. Of those that a mesh axis runs over, the one named last changes fastest.
Arguments:
- sketches: bfloat16 [24576, 8192], P(('groups', 'blocks')), parts along dimension 0, may hold values from -60 to 60
- test_sketches: bfloat16 [128, 8192], replicated, may hold values from -60 to 60
- domain_map: int32 [24576], P(('groups', 'blocks')), parts along dimension 0, may hold values from 0 to 63
Outputs:
- gram_tiles: float32 [2, 24576, 768], P(None, ('groups', 'blocks')), parts along dimension 1
- redundancy: float32 [24576], P(('groups', 'blocks')), parts along dimension 0
- domain_scores: float32 [128, 128], P(('groups', 'blocks')), parts along dimension 0
There are 2 independent parts, one for each index of `groups`. A program takes and returns all parts, laid end to end along the dimension named above; an argument that names none is the same for every part. Nothing has to cross between parts.
All inputs are finite; a program needn't handle non-finite values.
Results may differ from a plain program's by a relative error of at most 0.0029.
Values may be sent and summed in bfloat16 or wider, within the bound.
No kernel may reach another device: no remote copies, remote signals or barrier semaphores. Data moves between devices by JAX's collectives and lax.ppermute only.
A program may use at most 128 MiB of HBM per device.

v0:
```python
import math

import jax
import jax.numpy as jnp
from jax import lax
from jax.sharding import PartitionSpec as P

ROUNDS = 2
DOM_DEV = 4


def from_behind(value, axis, by):
    size = lax.axis_size(axis)
    return lax.ppermute(value, axis, [(i, (i + by) % size) for i in range(size)])


def inverse_norm(matrix):
    values = matrix.astype(jnp.float32)
    return lax.rsqrt(jnp.mean(values * values, axis=1) + 1e-06)


def cross_tile(left, right, left_inverse, right_inverse):
    product = lax.dot_general(
        left, right, (((1,), (1,)), ((), ())), preferred_element_type=jnp.float32
    )
    return (
        product * left_inverse[:, None] * right_inverse[None, :] * (1.0 / math.sqrt(left.shape[1]))
    )


def local(sketches, test_sketches, domain_map):
    rows_here = sketches.shape[0]
    own_inverse = inverse_norm(sketches)
    visiting = sketches
    all_tiles = []
    mass = jnp.zeros((rows_here,), jnp.float32)
    for offset in range(1, ROUNDS + 1):
        visiting = from_behind(sketches, "blocks", offset)
        tiles_now = cross_tile(sketches, visiting, own_inverse, inverse_norm(visiting))
        all_tiles.append(tiles_now)
        squared = tiles_now * tiles_now
        mass = mass + jnp.sum(squared, axis=1)
        column_mass = jnp.sum(squared, axis=0)
        mass = mass + from_behind(column_mass, "blocks", -offset)
    gram_tiles = jnp.stack(all_tiles)
    redundancy = mass / float(2 * ROUNDS * rows_here)
    test_inverse = inverse_norm(test_sketches)
    similarity = cross_tile(sketches, test_sketches, own_inverse, test_inverse).astype(jnp.bfloat16)
    members = (
        domain_map[:, None] == lax.iota(jnp.int32, DOM_DEV * lax.axis_size("blocks"))[None, :]
    ).astype(jnp.bfloat16)
    domain_total = lax.psum_scatter(
        lax.dot_general(
            members, similarity, (((0,), (0,)), ((), ())), preferred_element_type=jnp.float32
        ),
        "blocks",
        scatter_dimension=0,
        tiled=True,
    )
    domain_scores = domain_total * (1.0 / math.sqrt(rows_here / DOM_DEV))
    return (gram_tiles, redundancy, domain_scores)


def solution(mesh):
    in_specs = (P(("groups", "blocks"), None), P(), P(("groups", "blocks")))
    out_specs = (
        P(None, ("groups", "blocks"), None),
        P(("groups", "blocks")),
        P(("groups", "blocks"), None),
    )
    return jax.shard_map(local, mesh=mesh, in_specs=in_specs, out_specs=out_specs, check_vma=False)
```

profile of v0, /device:TPU:0, one launch (start us, length us, event | category | flops | bytes accessed | tf_op | source)
XLA Modules:
  0.0 517.0 jit_solution(9303120125206283812)
XLA Ops:
  0.6 3.0 collective-permute-start.1
  3.6 0.0 collective-permute-start
  3.7 1.2 dynamic-slice
  5.5 2.1 multiply_reduce_fusion.3
  7.6 0.0 copy-start
  7.6 0.0 copy-start.1
  7.7 7.2 %multiply_reduce_fusion.2 = f32[768]{0:T(1024)S(1)} fusion(bf16[768,8192]{1,0:T(8,128)(2,1)} %param.3), kind=kLoop, calls=%fused_computation.2 | loop fusion | flops 18873600 | bytes 12585984 | tf_op jit(solution)/shard_map/reduce_sum | solution.py:19
  14.9 0.0 copy-done
  14.9 0.0 copy-done.1
  14.9 7.1 %fusion.5 = f32[64,128]{1,0:T(8,128)S(1)} fusion(bf16[768,8192]{1,0:T(8,128)(2,1)} %param.3, bf16[128,8192]{1,0:T(8,128)(2,1)S(1)} %copy-done, f32[128]{0:T(128)S(1)} %add_rsqrt_fusion.3, f32[768]{0:T(1024)S(1)} %add_rsqrt_fusion.2, s32[768]{0:T(1024)S(1)} %copy-done.1), kind=kOutput, calls=%fused_computation.17 | convolution fusion | flops 1623638016 | bytes 14719488 | tf_op jit(solution)/shard_map/dot_general | solution.py:53
  22.0 440.8 %all-reduce = f32[64,128]{1,0:T(8,128)S(1)} all-reduce(f32[64,128]{1,0:T(8,128)S(1)} %fusion.5), channel_id=2, replica_groups=mesh['groups'=2,'blocks'=16] {'blocks'}, use_global_device_ids=true, to_apply=%region_8.0.clone | all-reduce | flops 8192 | bytes 65536
  462.8 0.6 dynamic-slice_multiply_fusion
  463.4 0.0 collective-permute-done.1
  463.4 7.1 %multiply_reduce_fusion = f32[768]{0:T(1024)S(1)} fusion(bf16[768,8192]{1,0:T(8,128)(2,1)} %collective-permute-done.1), kind=kLoop, calls=%fused_computation | loop fusion | flops 18873600 | bytes 12585984 | tf_op jit(solution)/shard_map/reduce_sum | solution.py:19
  470.5 0.0 collective-permute-done
  470.5 7.1 %multiply_reduce_fusion.1 = f32[768]{0:T(1024)S(1)} fusion(bf16[768,8192]{1,0:T(8,128)(2,1)} %collective-permute-done), kind=kLoop, calls=%fused_computation.1 | loop fusion | flops 18873600 | bytes 12585984 | tf_op jit(solution)/shard_map/reduce_sum | solution.py:19
  477.6 16.2 %fusion.11 = f32[768,768]{1,0:T(8,128)} fusion(bf16[768,8192]{1,0:T(8,128)(2,1)} %param.3, bf16[768,8192]{1,0:T(8,128)(2,1)} %collective-permute-done.1), kind=kOutput, calls=%fused_computation.30 | convolution fusion | flops 9663676416 | bytes 27525120 | tf_op jit(solution)/shard_map/dot_general | solution.py:23
  493.8 18.5 %multiply_reduce_fusion.6 = (f32[768]{0:T(1024)S(1)}, f32[768]{0:T(1024)S(1)}, f32[768]{0:T(1024)S(1)}, f32[768]{0:T(1024)S(1)}, f32[1,768,768]{2,1,0:T(8,128)S(1)}, /*index=5*/f32[1,768,768]{2,1,0:T(8,128)}) fusion(f32[768]{0:T(1024)S(1)} %add_rsqrt_fusion.1, f32[768]{0:T(1024)S(1)} %add_rsqrt_fusion.2, f32[768]{0:T(1024)S(1)} %add_rsqrt_fusion, ...), kind=kOutput, calls=%fused_computation.9 | convolution fusion | flops 9670750208 | bytes 32265216 | tf_op jit(solution)/shard_map/dot_general | solution.py:23
  512.3 0.0 collective-permute-start.2
  512.3 0.0 collective-permute-start.3
  512.3 4.2 pad_maximum_fusion
  516.4 0.0 collective-permute-done.2
  516.4 0.0 collective-permute-done.3
  516.4 0.6 add_multiply_fusion
  (4 shorter events, 0.0 us)
Async XLA Ops:
  0.6 462.8 %collective-permute-start.1 = (bf16[768,8192]{1,0:T(8,128)(2,1)}, bf16[768,8192]{1,0:T(8,128)(2,1)}, u32[]{:S(2)}, u32[]{:S(2)}) collective-permute-start(bf16[768,8192]{1,0:T(8,128)(2,1)} %param.3), channel_id=1, source_target_pairs={{0,2},{1,3},{2,4},{3,5},{4,6},{5,7},{6,8},{7,9},{8,10},{9,11},{10,... | collective-permute-start | bytes 37748744 | tf_op jit(solution)/shard_map/ppermute | solution.py:14
  3.6 466.9 %collective-permute-start = (bf16[768,8192]{1,0:T(8,128)(2,1)}, bf16[768,8192]{1,0:T(8,128)(2,1)}, u32[]{:S(2)}, u32[]{:S(2)}) collective-permute-start(bf16[768,8192]{1,0:T(8,128)(2,1)} %param.3), channel_id=1, source_target_pairs={{0,1},{1,2},{2,3},{3,4},{4,5},{5,6},{6,7},{7,8},{8,9},{9,10},{10,1... | collective-permute-start | bytes 37748744 | tf_op jit(solution)/shard_map/ppermute | solution.py:14
  7.6 7.3 %copy-start = (bf16[128,8192]{1,0:T(8,128)(2,1)S(1)}, bf16[128,8192]{1,0:T(8,128)(2,1)}, u32[]{:S(2)}) copy-start(bf16[128,8192]{1,0:T(8,128)(2,1)} %param.4) | copy-start | bytes 6291460
  7.6 7.3 %copy-start.1 = (s32[768]{0:T(1024)S(1)}, s32[768]{0:T(1024)}, u32[]{:S(2)}) copy-start(s32[768]{0:T(1024)} %param.5) | copy-start | bytes 9220
  512.3 4.2 collective-permute-start.2
  512.3 4.2 collective-permute-start.3
where the time goes:
time: 517 us
  blocking collectives  441 us (85%)
  matrix products  41.8 us (8%)
  other arithmetic  28.9 us (6%)
    unnamed x1, blocking collectives  441 us
    dot_general x2, matrix products, cross_tile(): lax.dot_general(left, right, (((1,), (1,)), ((), ())), preferred_element_...  34.7 us
    reduce_sum x4, other arithmetic, inverse_norm(): return lax.rsqrt(jnp.mean(values * values, axis=1) + 1e-06)  23.5 us
  transfers between devices with their start and end apart: 4, of which 0 were waited for; matrix products, arithmetic and copies ran while one was open for 6% of the time, Pallas kernels for 0%

commit v1 on v0

v1 whole, which is shorter than its diff:
```python
import functools
import math

import jax
import jax.numpy as jnp
from jax import lax
from jax.experimental import pallas as pl
from jax.experimental.pallas import tpu as pltpu
from jax.sharding import PartitionSpec as P

ROUNDS = 2
DOM_DEV = 4
LATE = 128
DEPTH = 512
NT = (((1,), (1,)), ((), ()))


def send(value, pairs):
    return lax.ppermute(value, "blocks", pairs)


def inverse_norm(matrix):
    values = matrix.astype(jnp.float32)
    return lax.rsqrt(jnp.mean(values * values, axis=1) + 1e-06)


def nt(left, right):
    return lax.dot_general(left, right, NT, preferred_element_type=jnp.float32)


def early_kernel(place, own, partner, near, other, u_out, v_out, x_out, s, w, u, v, x):
    step = pl.program_id(0)
    upper = place[0] == 1

    @pl.when(step == 0)
    def _():
        for total in (u, v, x):
            total[...] = jnp.zeros_like(total)

    s[...] = jnp.where(upper, near[...], own[...])
    w[...] = jnp.where(upper, own[...], near[...])
    u[...] += nt(partner[...], s[...])
    v[...] += nt(w[...], partner[...])

    @pl.when(place[1] == 0)
    def _():
        x[...] += nt(w[...], other[...])

    @pl.when(place[1] == 1)
    def _():
        x[...] += nt(other[...], s[...])

    @pl.when(step == pl.num_programs(0) - 1)
    def _():
        u_out[...] = u[...].astype(u_out.dtype)
        v_out[...] = v[...].astype(v_out.dtype)
        x_out[...] = x[...].astype(x_out.dtype)


def early_tiles(place, own, partner, near, other):
    early, half = partner.shape
    steps = half // DEPTH
    block = pl.BlockSpec((early, DEPTH), lambda k, place: (0, k))
    mine = pl.BlockSpec((early, DEPTH), lambda k, place: (0, place[0] * steps + k))
    whole = pl.BlockSpec((early, early), lambda k, place: (0, 0))
    tile = jax.ShapeDtypeStruct((early, early), jnp.bfloat16)
    return pl.pallas_call(
        early_kernel,
        grid_spec=pltpu.PrefetchScalarGridSpec(
            num_scalar_prefetch=1,
            grid=(steps,),
            in_specs=[mine, block, block, block],
            out_specs=[whole] * 3,
            scratch_shapes=[pltpu.VMEM((early, DEPTH), jnp.bfloat16)] * 2
            + [pltpu.VMEM((early, early), jnp.float32)] * 3,
        ),
        out_shape=[tile] * 3,
        compiler_params=pltpu.CompilerParams(vmem_limit_bytes=40 * 2**20),
        cost_estimate=pl.CostEstimate(
            flops=6 * early * early * half, bytes_accessed=8 * early * half, transcendentals=0
        ),
    )(place, own, partner, near, other)


def late_kernel(
    place, own1, own2, partner1, partner2, near1, near2, other1, other2,
    u_out, v_out, x_out, s, w, ur, uc, vr, vc, xr, xc,
):
    step = pl.program_id(0)
    upper = place[0] == 1
    early = own1.shape[0]

    @pl.when(step == 0)
    def _():
        for total in (ur, uc, vr, vc, xr, xc):
            total[...] = jnp.zeros_like(total)

    s[:early] = jnp.where(upper, near1[...], own1[...])
    s[early:] = jnp.where(upper, near2[...], own2[...])
    w[:early] = jnp.where(upper, own1[...], near1[...])
    w[early:] = jnp.where(upper, own2[...], near2[...])
    ur[...] += nt(partner2[...], s[...])
    uc[...] += nt(partner1[...], s[early:])
    vr[:, :early] += nt(w[early:], partner1[...])
    vr[:, early:] += nt(w[early:], partner2[...])
    vc[...] += nt(w[:early], partner2[...])

    @pl.when(place[1] == 0)
    def _():
        xr[:, :early] += nt(w[early:], other1[...])
        xr[:, early:] += nt(w[early:], other2[...])
        xc[...] += nt(w[:early], other2[...])

    @pl.when(place[1] == 1)
    def _():
        xr[...] += nt(other2[...], s[...])
        xc[...] += nt(other1[...], s[early:])

    @pl.when(step == pl.num_programs(0) - 1)
    def _():
        for out, rows, columns in ((u_out, ur, uc), (v_out, vr, vc), (x_out, xr, xc)):
            late, width = rows.shape
            out[:, :width] = rows[...].astype(out.dtype)
            for j in range(early // late):
                out[:, width + j * late : width + (j + 1) * late] = columns[
                    j * late : (j + 1) * late
                ].astype(out.dtype)


def late_tiles(place, own, partner1, partner2, near1, near2, other1, other2):
    early, half = partner1.shape
    late = partner2.shape[0]
    rows = early + late
    steps = half // DEPTH
    block1 = pl.BlockSpec((early, DEPTH), lambda k, place: (0, k))
    block2 = pl.BlockSpec((late, DEPTH), lambda k, place: (0, k))
    mine1 = pl.BlockSpec((early, DEPTH), lambda k, place: (0, place[0] * steps + k))
    mine2 = pl.BlockSpec((late, DEPTH), lambda k, place: (early // late, place[0] * steps + k))
    whole = pl.BlockSpec((late, rows + early), lambda k, place: (0, 0))
    out = jax.ShapeDtypeStruct((late, rows + early), jnp.bfloat16)
    totals = [pltpu.VMEM((late, rows), jnp.float32), pltpu.VMEM((early, late), jnp.float32)]
    return pl.pallas_call(
        late_kernel,
        grid_spec=pltpu.PrefetchScalarGridSpec(
            num_scalar_prefetch=1,
            grid=(steps,),
            in_specs=[mine1, mine2] + [block1, block2] * 3,
            out_specs=[whole] * 3,
            scratch_shapes=[pltpu.VMEM((rows, DEPTH), jnp.bfloat16)] * 2 + totals * 3,
        ),
        out_shape=[out] * 3,
        compiler_params=pltpu.CompilerParams(vmem_limit_bytes=40 * 2**20),
        cost_estimate=pl.CostEstimate(
            flops=6 * late * (rows + early) * half, bytes_accessed=8 * rows * half, transcendentals=0
        ),
    )(place, own, own, partner1, partner2, near1, near2, other1, other2)


def join_kernel(
    scale, place, u1, u2r, u2c, v1, v2r, v2c, y1, y2r, y2c, z1, z2r, z2c, local,
    inverse, behind1, behind2, gram, row_mass, column_mass,
):
    step = pl.program_id(0)
    last = pl.num_programs(0) - 1
    early = u1.shape[1]

    @pl.when(step == 0)
    def _():
        column_mass[...] = jnp.zeros_like(column_mass)

    def f32(ref):
        return ref[...].astype(jnp.float32)

    @pl.when(step < last)
    def _():
        gram[0, :, :early] = f32(y1) + f32(z1)
        gram[0, :, early:] = f32(y2c) + f32(z2c)
        gram[1, :, :early] = f32(u1) + f32(v1)
        gram[1, :, early:] = f32(u2c) + f32(v2c)

    @pl.when(step == last)
    def _():
        gram[0] = f32(y2r) + f32(z2r)
        gram[1] = f32(u2r) + f32(v2r)

    first = jnp.where(place[1] == 1, local[...], gram[0])
    left = inverse[...]
    first = first * left * behind1[...] * scale
    second = gram[1] * left * behind2[...] * scale
    gram[0] = first
    gram[1] = second
    first2 = first * first
    second2 = second * second
    column_mass[0:1] += jnp.sum(first2, axis=0, keepdims=True)
    column_mass[1:2] += jnp.sum(second2, axis=0, keepdims=True)
    sums = jnp.sum(first2 + second2, axis=1, keepdims=True)
    size = sums.shape[0]
    row_mass[...] = jnp.broadcast_to(sums, (size, size)).T[0:1]


def join(scale, place, u, v, y, z, local, inverse, behind1, behind2):
    early = u[0].shape[0]
    late = u[1].shape[0]
    rows = early + late
    last = early // late - 1
    first = pl.BlockSpec((late, early), lambda j, place: (jnp.minimum(j, last), 0))
    bottom = pl.BlockSpec((late, rows), lambda j, place: (0, 0))
    side = pl.BlockSpec((late, late), lambda j, place: (0, rows // late + jnp.minimum(j, last)))
    by_rows = pl.BlockSpec((late, rows), lambda j, place: (j, 0))
    column = pl.BlockSpec((late, 1), lambda j, place: (j, 0))
    row = pl.BlockSpec((1, rows), lambda j, place: (0, 0))
    operands = [part for first_, second_ in (u, v, y, z) for part in (first_, second_, second_)]
    return pl.pallas_call(
        functools.partial(join_kernel, scale),
        grid_spec=pltpu.PrefetchScalarGridSpec(
            num_scalar_prefetch=1,
            grid=(rows // late,),
            in_specs=[first, bottom, side] * 4 + [by_rows, column, row, row],
            out_specs=[
                pl.BlockSpec((2, late, rows), lambda j, place: (0, j, 0)),
                pl.BlockSpec((1, late), lambda j, place: (0, j)),
                pl.BlockSpec((2, rows), lambda j, place: (0, 0)),
            ],
        ),
        out_shape=[
            jax.ShapeDtypeStruct((2, rows, rows), jnp.float32),
            jax.ShapeDtypeStruct((1, rows), jnp.float32),
            jax.ShapeDtypeStruct((2, rows), jnp.float32),
        ],
        compiler_params=pltpu.CompilerParams(vmem_limit_bytes=40 * 2**20),
        cost_estimate=pl.CostEstimate(
            flops=20 * rows * rows, bytes_accessed=20 * rows * rows, transcendentals=0
        ),
    )(place, *operands, local, inverse[:, None], behind1[None, :], behind2[None, :])


def scatter_sum(value, index, size, waits):
    bit = size // 2
    for wait in waits:
        half = value.shape[0] // 2
        mine = (index // bit) % 2
        away = lax.dynamic_slice_in_dim(value, (1 - mine) * half, half)
        kept = lax.dynamic_slice_in_dim(value, mine * half, half)
        if wait is not None:
            away, _ = lax.optimization_barrier((away, wait))
        value = kept + send(away, [(i, i ^ bit) for i in range(size)])
        bit //= 2
    return value


def local(sketches, test_sketches, domain_map):
    rows, depth = sketches.shape
    size = lax.axis_size("blocks")
    index = lax.axis_index("blocks")
    half = depth // 2
    early = rows - LATE
    blocks = range(size)
    upper = (index // 2) % 2
    core = index % 2
    place = jnp.stack([upper, core]).astype(jnp.int32)

    across = [(i, i ^ 2) for i in blocks]
    along = [(i, (i + (4 if i & 2 else -4)) % size) for i in blocks]
    swap = [(i, i ^ 1) for i in blocks]

    def part(start, count, side):
        return lax.dynamic_slice(sketches, (start, side * half), (count, half))

    partner1 = send(part(0, early, 1 - upper), across)
    near1 = send(part(0, early, upper), along)
    partner2 = send(part(early, LATE, 1 - upper), across)
    near2 = send(part(early, LATE, upper), along)
    even = send(sketches, [(i, i + 1) for i in blocks if i % 2 == 0])

    inverse = inverse_norm(sketches)
    behind1 = send(inverse, [(i, (i + 1) % size) for i in blocks])
    behind2 = send(inverse, [(i, (i + 2) % size) for i in blocks])
    scale = 1.0 / math.sqrt(depth)

    test_inverse = inverse_norm(test_sketches)
    similarity = (
        nt(sketches, test_sketches) * inverse[:, None] * test_inverse[None, :] * scale
    ).astype(jnp.bfloat16)
    members = (
        domain_map[:, None] == lax.iota(jnp.int32, DOM_DEV * size)[None, :]
    ).astype(jnp.bfloat16)
    sums = lax.dot_general(
        members, similarity, (((0,), (0,)), ((), ())), preferred_element_type=jnp.float32
    )
    inside = nt(sketches, even)

    other1 = send(partner1, swap)
    other2 = send(partner2, swap)

    u1, v1, x1 = early_tiles(place, sketches, partner1, near1, other1)
    u2, v2, x2 = late_tiles(
        place, sketches, partner1, partner2, near1, near2, other1, other2
    )

    back_v = [(i, i) if i & 2 else (i, (i + 4) % size) for i in blocks]
    back_y = [(i, i ^ 3) for i in blocks if i & 1]
    back_z = [pair for pair in back_v if pair[0] % 2 == 0]
    u1r, y1, v1r, z1 = send(u1, across), send(x1, back_y), send(v1, back_v), send(x1, back_z)
    u2r, y2, v2r, z2 = send(u2, across), send(x2, back_y), send(v2, back_v), send(x2, back_z)

    bits = size.bit_length() - 1
    waits = ([None, partner1, partner2, u1r] + [u1r] * bits)[:bits]
    domain_scores = scatter_sum(sums, index, size, waits) * (1.0 / math.sqrt(rows / DOM_DEV))

    gram, row_mass, column_mass = join(
        scale, place, (u1r, u2r), (v1r, v2r), (y1, y2), (z1, z2), inside, inverse, behind1, behind2
    )
    mass = (
        row_mass[0]
        + send(column_mass[0], [(i, (i - 1) % size) for i in blocks])
        + send(column_mass[1], [(i, (i - 2) % size) for i in blocks])
    )
    redundancy = mass / float(2 * ROUNDS * rows)
    return (gram, redundancy, domain_scores)


def solution(mesh):
    in_specs = (P(("groups", "blocks"), None), P(), P(("groups", "blocks")))
    out_specs = (
        P(None, ("groups", "blocks"), None),
        P(("groups", "blocks")),
        P(("groups", "blocks"), None),
    )
    return jax.shard_map(local, mesh=mesh, in_specs=in_specs, out_specs=out_specs, check_vma=False)
```

time: 517 us -> 259 us (0.50)
  blocking collectives: 441 us -> 0 us
  waiting for transfers between devices: 0.01 us -> 130 us
  Pallas kernels: 0 us -> 41.2 us
  starting transfers between devices: 3.03 us -> 42.1 us
  matrix products: 41.8 us -> 21.6 us
  other arithmetic: 28.9 us -> 8.9 us
  local copies, waits for them, and re-layouts: 1.25 us -> 13 us
    unnamed x1 -> x0, blocking collectives: 441 us -> none
    ppermute x4 -> x23, waiting for transfers between devices: 0.01 us -> 130 us  [send(): return lax.ppermute(value, 'blocks', pairs)]
    pallas_call x0 -> x3, Pallas kernels: none -> 41.2 us  [the longest x1 19.6 us: early_tiles(): pl.pallas_call(early_kernel, grid_spec=pltpu.PrefetchScalarGridSpec(num_s...]
    ppermute x4 -> x23, starting transfers between devices: 3.03 us -> 42.1 us  [send(): return lax.ppermute(value, 'blocks', pairs)]
    dot_general x2 -> x1, matrix products: 34.7 us -> 14.8 us  [nt(): return lax.dot_general(left, right, NT, preferred_element_type=jnp.float32)]
    reduce_sum x4 -> x2, other arithmetic: 23.5 us -> 7.59 us  [inverse_norm(): return lax.rsqrt(jnp.mean(values * values, axis=1) + 1e-06)]
    dynamic_slice x0 -> x6, local copies, waits for them, and re-layouts: none -> 12.8 us  [the longest x2 12.7 us: part(): return lax.dynamic_slice(sketches, (start, side * half), (count, half))]
  transfers between devices with their start and end apart: 4 -> 23, of which waited for: 0 -> 8; matrix products, arithmetic and copies ran while one was open for 6% -> 17% of each run, Pallas kernels for 0% -> 16%
where the time goes in v1:
time: 259 us; the launch traced here: 258 us
  waiting for transfers between devices  130 us (50%)
  starting transfers between devices  42.1 us (16%)
  Pallas kernels  41.2 us (16%)
  matrix products  21.6 us (8%)
  local copies, waits for them, and re-layouts  13 us (5%)
  other arithmetic  8.9 us (3%)
    ppermute x23, waiting for transfers between devices, send(): return lax.ppermute(value, 'blocks', pairs)  130 us
    ppermute x23, starting transfers between devices, send(): return lax.ppermute(value, 'blocks', pairs)  42.1 us
    pallas_call x1, Pallas kernels, early_tiles(): pl.pallas_call(early_kernel, grid_spec=pltpu.PrefetchScalarGridSpec(num_s...  19.6 us
    pallas_call x1, Pallas kernels, late_tiles(): pl.pallas_call(late_kernel, grid_spec=pltpu.PrefetchScalarGridSpec(num_sc...  16.4 us
    dot_general x1, matrix products, nt(): return lax.dot_general(left, right, NT, preferred_element_type=jnp.float32)  14.8 us
    dynamic_slice x2, local copies, waits for them, and re-layouts, part(): return lax.dynamic_slice(sketches, (start, side * half), (count, half))  12.7 us
    reduce_sum x2, other arithmetic, inverse_norm(): return lax.rsqrt(jnp.mean(values * values, axis=1) + 1e-06)  7.59 us
    dot_general x1, matrix products, local(): lax.dot_general(members, similarity, (((0,), (0,)), ((), ())), preferred_...  6.88 us
  transfers between devices with their start and end apart: 23, of which 8 were waited for; matrix products, arithmetic and copies ran while one was open for 17% of the time, Pallas kernels for 16%

profile of v1, /device:TPU:0, one launch (start us, length us, event | category | flops | bytes accessed | tf_op | source)
XLA Modules:
  0.0 258.2 jit_solution(390699546372845842)
XLA Ops:
  0.6 6.9 %collective-permute-start.14 = (bf16[768,8192]{1,0:T(8,128)(2,1)}, bf16[768,8192]{1,0:T(8,128)(2,1)}, u32[]{:S(2)}, u32[]{:S(2)}) collective-permute-start(bf16[768,8192]{1,0:T(8,128)(2,1)} %own2.1), channel_id=1, source_target_pairs={{0,1},{2,3},{4,5},{6,7},{8,9},{10,11},{12,13},{14,15},{16,17},{18,... | collective-permute-start | bytes 37748744 | tf_op jit(solution)/shard_map/ppermute | solution.py:19
  7.5 9.7 %constant_dynamic-slice_fusion.5 = (bf16[640,4096]{1,0:T(8,128)(2,1)}, bf16[640,4096]{1,0:T(8,128)(2,1)}) fusion(bf16[768,8192]{1,0:T(8,128)(2,1)} %own2.1, s32[]{:T(128)S(6)} %select_n.71, s32[]{:T(128)S(6)} %select_n.70), kind=kLoop, calls=%fused_computation.24 | loop fusion | bytes 20971528 | tf_op jit(solution)/shard_map/dynamic_slice | solution.py:267
  17.2 2.3 collective-permute-start
  19.5 3.6 %collective-permute-start.1 = (bf16[640,4096]{1,0:T(8,128)(2,1)}, bf16[640,4096]{1,0:T(8,128)(2,1)}, u32[]{:S(2)}, u32[]{:S(2)}) collective-permute-start(bf16[640,4096]{1,0:T(8,128)(2,1)} %get-tuple-element.31), channel_id=1, source_target_pairs={{0,12},{1,13},{2,6},{3,7},{4,0},{5,1},{6,10},{7,11},{8,4},{9,5},{1... | collective-permute-start | bytes 15728648 | tf_op jit(solution)/shard_map/ppermute | solution.py:19
  23.1 104.8 %collective-permute-done.partner.partner1 = bf16[640,4096]{1,0:T(8,128)(2,1)} collective-permute-done((bf16[640,4096]{1,0:T(8,128)(2,1)}, bf16[640,4096]{1,0:T(8,128)(2,1)}, u32[]{:S(2)}, u32[]{:S(2)}) %collective-permute-start) | collective-permute-done | bytes 5242912 | tf_op jit(solution)/shard_map/ppermute | solution.py:19
  128.0 3.1 %constant_dynamic-slice_fusion.7 = (bf16[128,4096]{1,0:T(8,128)(2,1)}, bf16[128,4096]{1,0:T(8,128)(2,1)}) fusion(bf16[768,8192]{1,0:T(8,128)(2,1)} %own2.1, s32[]{:T(128)S(6)} %select_n.71, s32[]{:T(128)S(6)} %select_n.70), kind=kLoop, calls=%fused_computation.28 | loop fusion | bytes 4194312 | tf_op jit(solution)/shard_map/dynamic_slice | solution.py:267
  133.3 7.1 %multiply_reduce_fusion = f32[768]{0:T(1024)S(1)} fusion(bf16[768,8192]{1,0:T(8,128)(2,1)} %own2.1), kind=kLoop, calls=%fused_computation | loop fusion | flops 18873600 | bytes 12585984 | tf_op jit(solution)/shard_map/reduce_sum | solution.py:24
  140.4 6.9 %fusion.3 = f32[64,128]{1,0:T(8,128)S(1)} fusion(bf16[768,8192]{1,0:T(8,128)(2,1)} %own2.1, bf16[128,8192]{1,0:T(8,128)(2,1)S(1)} %copy-done.1, f32[128]{0:T(128)S(1)} %add_rsqrt_fusion.1, f32[768]{0:T(1024)S(1)} %add_rsqrt_fusion, s32[768]{0:T(1024)S(1)} %copy-done.2), kind=kOutput, calls=%fused_computation.6 | convolution fusion | flops 1623638016 | bytes 14719488 | tf_op jit(solution)/shard_map/dot_general | solution.py:287
  147.3 2.7 %collective-permute-start.19 = (f32[32,128]{1,0:T(8,128)S(1)}, f32[32,128]{1,0:T(8,128)S(1)}, u32[]{:S(2)}, u32[]{:S(2)}) collective-permute-start(f32[32,128]{1,0:T(8,128)S(1)} %constant_dynamic-slice_fusion.4), channel_id=1, source_target_pairs={{0,8},{1,9},{2,10},{3,11},{4,12},{5,13},{6,14},{7,15},{8,0},{9,1},... | collective-permute-start | bytes 49160 | tf_op jit(solution)/shard_map/ppermute | solution.py:19
  150.0 2.0 collective-permute-done.19
  153.7 3.1 %collective-permute-done.4.partner2 = bf16[128,4096]{1,0:T(8,128)(2,1)S(1)} collective-permute-done((bf16[128,4096]{1,0:T(8,128)(2,1)}, bf16[128,4096]{1,0:T(8,128)(2,1)S(1)}, u32[]{:S(2)}, u32[]{:S(2)}) %collective-permute-start.4) | collective-permute-done | bytes 1048608 | tf_op jit(solution)/shard_map/ppermute | solution.py:19
  156.8 3.8 %collective-permute-start.5 = (bf16[128,4096]{1,0:T(8,128)(2,1)}, bf16[128,4096]{1,0:T(8,128)(2,1)S(1)}, u32[]{:S(2)}, u32[]{:S(2)}) collective-permute-start(bf16[128,4096]{1,0:T(8,128)(2,1)} %get-tuple-element.29), channel_id=1, source_target_pairs={{0,12},{1,13},{2,6},{3,7},{4,0},{5,1},{6,10},{7,11},{8,4},{9,5},{1... | collective-permute-start | bytes 3145736 | tf_op jit(solution)/shard_map/ppermute | solution.py:19
  161.4 19.6 %shard_map.58 = (bf16[640,640]{1,0:T(8,128)(2,1)}, bf16[640,640]{1,0:T(8,128)(2,1)S(1)}, bf16[640,640]{1,0:T(8,128)(2,1)S(1)}) custom-call(s32[2]{0:T(128)S(1)} %pad_add_fusion.place, bf16[768,8192]{1,0:T(8,128)(2,1)} %own2.1, bf16[640,4096]{1,0:T(8,128)(2,1)} %collective-permute-done.partner.partner1, bf16[640,4096]{1,0:T(8,128)(2,1)} %collective-permute-done.1.near.near1, ...), custom_call_target="tpu_custom_call" | custom-call | flops 10066329600 | bytes 20971520 | tf_op jit(solution)/shard_map/pallas_call | solution.py:67
  181.0 2.2 collective-permute-done.5.near2
  183.3 2.2 collective-permute-start.3
  185.5 16.4 %shard_map.59 = (bf16[128,1408]{1,0:T(8,128)(2,1)}, bf16[128,1408]{1,0:T(8,128)(2,1)}, bf16[128,1408]{1,0:T(8,128)(2,1)S(1)}) custom-call(s32[2]{0:T(128)S(1)} %pad_add_fusion.place, bf16[768,8192]{1,0:T(8,128)(2,1)} %own2.1, bf16[768,8192]{1,0:T(8,128)(2,1)} %own2.1, bf16[640,4096]{1,0:T(8,128)(2,1)} %collective-permute-done.partner.partner1, ...), custom_call_target="tpu_custom_call" | custom-call | flops 4429185024 | bytes 25165824 | tf_op jit(solution)/shard_map/pallas_call | solution.py:142
  205.8 5.4 %collective-permute-done.21 = f32[8,128]{1,0:T(8,128)S(1)} collective-permute-done((f32[8,128]{1,0:T(8,128)S(1)}, f32[8,128]{1,0:T(8,128)S(1)}, u32[]{:S(2)}, u32[]{:S(2)}) %collective-permute-start.21) | collective-permute-done | bytes 4128 | tf_op jit(solution)/shard_map/ppermute | solution.py:19
  211.2 2.3 collective-permute-start.13
  214.8 3.0 %collective-permute-start.12 = (bf16[640,640]{1,0:T(8,128)(2,1)S(1)}, bf16[640,640]{1,0:T(8,128)(2,1)S(1)}, u32[]{:S(2)}, u32[]{:S(2)}) collective-permute-start(bf16[640,640]{1,0:T(8,128)(2,1)S(1)} %get-tuple-element.19), channel_id=1, source_target_pairs={{0,4},{2,2},{4,8},{6,6},{8,12},{10,10},{12,0},{14,14},{16,20},{18,... | collective-permute-start | bytes 2457608 | tf_op jit(solution)/shard_map/ppermute | solution.py:19
  219.1 4.9 %collective-permute-start.8 = (bf16[640,640]{1,0:T(8,128)(2,1)}, bf16[640,640]{1,0:T(8,128)(2,1)S(1)}, u32[]{:S(2)}, u32[]{:S(2)}) collective-permute-start(bf16[640,640]{1,0:T(8,128)(2,1)} %copy-done), channel_id=1, source_target_pairs={{0,4},{1,5},{2,2},{3,3},{4,8},{5,9},{6,6},{7,7},{8,12},{9,13},{10,... | collective-permute-start | bytes 2457608 | tf_op jit(solution)/shard_map/ppermute | solution.py:19
  224.0 14.8 %fusion.11.local = f32[768,768]{1,0:T(8,128)S(1)} fusion(bf16[768,8192]{1,0:T(8,128)(2,1)} %own2.1, bf16[768,8192]{1,0:T(8,128)(2,1)} %collective-permute-done.14), kind=kOutput, calls=%fused_computation.33 | convolution fusion | flops 9663676416 | bytes 27525120 | tf_op jit(solution)/shard_map/dot_general | solution.py:28
  238.9 9.8 %collective-permute-done.8.v1 = bf16[640,640]{1,0:T(8,128)(2,1)S(1)} collective-permute-done((bf16[640,640]{1,0:T(8,128)(2,1)}, bf16[640,640]{1,0:T(8,128)(2,1)S(1)}, u32[]{:S(2)}, u32[]{:S(2)}) %collective-permute-start.8) | collective-permute-done | bytes 819232 | tf_op jit(solution)/shard_map/ppermute | solution.py:19
  248.6 5.2 %shard_map.60 = (f32[2,768,768]{2,1,0:T(8,128)}, f32[1,768]{1,0:T(1,128)S(1)}, f32[2,768]{1,0:T(2,128)S(1)}) custom-call(s32[2]{0:T(128)S(1)} %pad_add_fusion.place, bf16[640,640]{1,0:T(8,128)(2,1)S(1)} %collective-permute-done.3.u1, bf16[128,1408]{1,0:T(8,128)(2,1)S(1)} %collective-permute-done.7.u2r.u2c, ...), custom_call_target="tpu_custom_call" | custom-call | flops 11796480 | bytes 11796480 | tf_op jit(solution)/shard_map/pallas_call | solution.py:213
  255.3 2.3 collective-permute-done.18
  (54 shorter events, 13.2 us)
Async XLA Ops:
  0.6 218.5 %collective-permute-start.14 = (bf16[768,8192]{1,0:T(8,128)(2,1)}, bf16[768,8192]{1,0:T(8,128)(2,1)}, u32[]{:S(2)}, u32[]{:S(2)}) collective-permute-start(bf16[768,8192]{1,0:T(8,128)(2,1)} %own2.1), channel_id=1, source_target_pairs={{0,1},{2,3},{4,5},{6,7},{8,9},{10,11},{12,13},{14,15},{16,17},{18,... | collective-permute-start | bytes 37748744 | tf_op jit(solution)/shard_map/ppermute | solution.py:19
  17.2 115.6 %copy-start.1 = (bf16[128,8192]{1,0:T(8,128)(2,1)S(1)}, bf16[128,8192]{1,0:T(8,128)(2,1)}, u32[]{:S(2)}) copy-start(bf16[128,8192]{1,0:T(8,128)(2,1)} %param.4) | copy-start | bytes 6291460
  17.2 110.8 %collective-permute-start = (bf16[640,4096]{1,0:T(8,128)(2,1)}, bf16[640,4096]{1,0:T(8,128)(2,1)}, u32[]{:S(2)}, u32[]{:S(2)}) collective-permute-start(bf16[640,4096]{1,0:T(8,128)(2,1)} %get-tuple-element.32), channel_id=1, source_target_pairs={{0,2},{1,3},{2,0},{3,1},{4,6},{5,7},{6,4},{7,5},{8,10},{9,11},{10,... | collective-permute-start | bytes 15728648 | tf_op jit(solution)/shard_map/ppermute | solution.py:19
  19.5 141.1 %collective-permute-start.1 = (bf16[640,4096]{1,0:T(8,128)(2,1)}, bf16[640,4096]{1,0:T(8,128)(2,1)}, u32[]{:S(2)}, u32[]{:S(2)}) collective-permute-start(bf16[640,4096]{1,0:T(8,128)(2,1)} %get-tuple-element.31), channel_id=1, source_target_pairs={{0,12},{1,13},{2,6},{3,7},{4,0},{5,1},{6,10},{7,11},{8,4},{9,5},{1... | collective-permute-start | bytes 15728648 | tf_op jit(solution)/shard_map/ppermute | solution.py:19
  128.0 32.8 %collective-permute-start.2 = (bf16[640,4096]{1,0:T(8,128)(2,1)}, bf16[640,4096]{1,0:T(8,128)(2,1)}, u32[]{:S(2)}, u32[]{:S(2)}) collective-permute-start(bf16[640,4096]{1,0:T(8,128)(2,1)} %collective-permute-done.partner.partner1), channel_id=1, source_target_pairs={{0,1},{1,0},{2,3},{3,2},{4,5},{5,4},{6,7},{7,6},{8,9},{9,8},{10,11... | collective-permute-start | bytes 15728648 | tf_op jit(solution)/shard_map/ppermute | solution.py:19
  131.0 25.8 %collective-permute-start.4 = (bf16[128,4096]{1,0:T(8,128)(2,1)}, bf16[128,4096]{1,0:T(8,128)(2,1)S(1)}, u32[]{:S(2)}, u32[]{:S(2)}) collective-permute-start(bf16[128,4096]{1,0:T(8,128)(2,1)} %get-tuple-element.30), channel_id=1, source_target_pairs={{0,2},{1,3},{2,0},{3,1},{4,6},{5,7},{6,4},{7,5},{8,10},{9,11},{10,... | collective-permute-start | bytes 3145736 | tf_op jit(solution)/shard_map/ppermute | solution.py:19
  147.3 4.7 %collective-permute-start.19 = (f32[32,128]{1,0:T(8,128)S(1)}, f32[32,128]{1,0:T(8,128)S(1)}, u32[]{:S(2)}, u32[]{:S(2)}) collective-permute-start(f32[32,128]{1,0:T(8,128)S(1)} %constant_dynamic-slice_fusion.4), channel_id=1, source_target_pairs={{0,8},{1,9},{2,10},{3,11},{4,12},{5,13},{6,14},{7,15},{8,0},{9,1},... | collective-permute-start | bytes 49160 | tf_op jit(solution)/shard_map/ppermute | solution.py:19
  152.0 8.6 %collective-permute-start.20 = (f32[16,128]{1,0:T(8,128)S(1)}, f32[16,128]{1,0:T(8,128)S(1)}, u32[]{:S(2)}, u32[]{:S(2)}) collective-permute-start(f32[16,128]{1,0:T(8,128)S(1)} %constant_dynamic-slice_fusion.3), channel_id=1, source_target_pairs={{0,4},{1,5},{2,6},{3,7},{4,0},{5,1},{6,2},{7,3},{8,12},{9,13},{10,... | collective-permute-start | bytes 24584 | tf_op jit(solution)/shard_map/ppermute | solution.py:19
  156.8 26.4 %collective-permute-start.5 = (bf16[128,4096]{1,0:T(8,128)(2,1)}, bf16[128,4096]{1,0:T(8,128)(2,1)S(1)}, u32[]{:S(2)}, u32[]{:S(2)}) collective-permute-start(bf16[128,4096]{1,0:T(8,128)(2,1)} %get-tuple-element.29), channel_id=1, source_target_pairs={{0,12},{1,13},{2,6},{3,7},{4,0},{5,1},{6,10},{7,11},{8,4},{9,5},{1... | collective-permute-start | bytes 3145736 | tf_op jit(solution)/shard_map/ppermute | solution.py:19
  160.7 24.9 %collective-permute-start.6 = (bf16[128,4096]{1,0:T(8,128)(2,1)S(1)}, bf16[128,4096]{1,0:T(8,128)(2,1)S(1)}, u32[]{:S(2)}, u32[]{:S(2)}) collective-permute-start(bf16[128,4096]{1,0:T(8,128)(2,1)S(1)} %collective-permute-done.4.partner2), channel_id=1, source_target_pairs={{0,1},{1,0},{2,3},{3,2},{4,5},{5,4},{6,7},{7,6},{8,9},{9,8},{10,11... | collective-permute-start | bytes 3145736 | tf_op jit(solution)/shard_map/ppermute | solution.py:19
  160.7 41.3 %collective-permute-start.16 = (f32[768]{0:T(1024)S(1)}, f32[768]{0:T(1024)S(1)}, u32[]{:S(2)}, u32[]{:S(2)}) collective-permute-start(f32[768]{0:T(1024)S(1)} %add_rsqrt_fusion), channel_id=1, source_target_pairs={{0,2},{1,3},{2,4},{3,5},{4,6},{5,7},{6,8},{7,9},{8,10},{9,11},{10,... | collective-permute-start | bytes 9224 | tf_op jit(solution)/shard_map/ppermute | solution.py:19
  160.8 43.2 %collective-permute-start.15 = (f32[768]{0:T(1024)S(1)}, f32[768]{0:T(1024)S(1)}, u32[]{:S(2)}, u32[]{:S(2)}) collective-permute-start(f32[768]{0:T(1024)S(1)} %add_rsqrt_fusion), channel_id=1, source_target_pairs={{0,1},{1,2},{2,3},{3,4},{4,5},{5,6},{6,7},{7,8},{8,9},{9,10},{10,1... | collective-permute-start | bytes 9224 | tf_op jit(solution)/shard_map/ppermute | solution.py:19
  183.3 30.2 %collective-permute-start.3 = (bf16[640,640]{1,0:T(8,128)(2,1)}, bf16[640,640]{1,0:T(8,128)(2,1)S(1)}, u32[]{:S(2)}, u32[]{:S(2)}) collective-permute-start(bf16[640,640]{1,0:T(8,128)(2,1)} %get-tuple-element.15), channel_id=1, source_target_pairs={{0,2},{1,3},{2,0},{3,1},{4,6},{5,7},{6,4},{7,5},{8,10},{9,11},{10,... | collective-permute-start | bytes 2457608 | tf_op jit(solution)/shard_map/ppermute | solution.py:19
  201.9 12.9 %collective-permute-start.7 = (bf16[128,1408]{1,0:T(8,128)(2,1)}, bf16[128,1408]{1,0:T(8,128)(2,1)S(1)}, u32[]{:S(2)}, u32[]{:S(2)}) collective-permute-start(bf16[128,1408]{1,0:T(8,128)(2,1)} %get-tuple-element.16), channel_id=1, source_target_pairs={{0,2},{1,3},{2,0},{3,1},{4,6},{5,7},{6,4},{7,5},{8,10},{9,11},{10,... | collective-permute-start | bytes 1081352 | tf_op jit(solution)/shard_map/ppermute | solution.py:19
  201.9 15.9 %collective-permute-start.9 = (bf16[128,1408]{1,0:T(8,128)(2,1)}, bf16[128,1408]{1,0:T(8,128)(2,1)S(1)}, u32[]{:S(2)}, u32[]{:S(2)}) collective-permute-start(bf16[128,1408]{1,0:T(8,128)(2,1)} %get-tuple-element.18), channel_id=1, source_target_pairs={{0,4},{1,5},{2,2},{3,3},{4,8},{5,9},{6,6},{7,7},{8,12},{9,13},{10,... | collective-permute-start | bytes 1081352 | tf_op jit(solution)/shard_map/ppermute | solution.py:19
  204.0 7.2 %collective-permute-start.21 = (f32[8,128]{1,0:T(8,128)S(1)}, f32[8,128]{1,0:T(8,128)S(1)}, u32[]{:S(2)}, u32[]{:S(2)}) collective-permute-start(f32[8,128]{1,0:T(8,128)S(1)} %constant_dynamic-slice_fusion.2), channel_id=1, source_target_pairs={{0,2},{1,3},{2,0},{3,1},{4,6},{5,7},{6,4},{7,5},{8,10},{9,11},{10,... | collective-permute-start | bytes 12296 | tf_op jit(solution)/shard_map/ppermute | solution.py:19
  211.2 27.6 %collective-permute-start.13 = (bf16[128,1408]{1,0:T(8,128)(2,1)S(1)}, bf16[128,1408]{1,0:T(8,128)(2,1)S(1)}, u32[]{:S(2)}, u32[]{:S(2)}) collective-permute-start(bf16[128,1408]{1,0:T(8,128)(2,1)S(1)} %get-tuple-element.20), channel_id=1, source_target_pairs={{0,4},{2,2},{4,8},{6,6},{8,12},{10,10},{12,0},{14,14},{16,20},{18,... | collective-permute-start | bytes 1081352 | tf_op jit(solution)/shard_map/ppermute | solution.py:19
  213.5 25.4 %collective-permute-start.11 = (bf16[128,1408]{1,0:T(8,128)(2,1)S(1)}, bf16[128,1408]{1,0:T(8,128)(2,1)S(1)}, u32[]{:S(2)}, u32[]{:S(2)}) collective-permute-start(bf16[128,1408]{1,0:T(8,128)(2,1)S(1)} %get-tuple-element.20), channel_id=1, source_target_pairs={{1,2},{3,0},{5,6},{7,4},{9,10},{11,8},{13,14},{15,12},{17,18},{19,... | collective-permute-start | bytes 1081352 | tf_op jit(solution)/shard_map/ppermute | solution.py:19
  214.8 33.8 %collective-permute-start.12 = (bf16[640,640]{1,0:T(8,128)(2,1)S(1)}, bf16[640,640]{1,0:T(8,128)(2,1)S(1)}, u32[]{:S(2)}, u32[]{:S(2)}) collective-permute-start(bf16[640,640]{1,0:T(8,128)(2,1)S(1)} %get-tuple-element.19), channel_id=1, source_target_pairs={{0,4},{2,2},{4,8},{6,6},{8,12},{10,10},{12,0},{14,14},{16,20},{18,... | collective-permute-start | bytes 2457608 | tf_op jit(solution)/shard_map/ppermute | solution.py:19
  217.8 30.8 %collective-permute-start.10 = (bf16[640,640]{1,0:T(8,128)(2,1)S(1)}, bf16[640,640]{1,0:T(8,128)(2,1)S(1)}, u32[]{:S(2)}, u32[]{:S(2)}) collective-permute-start(bf16[640,640]{1,0:T(8,128)(2,1)S(1)} %get-tuple-element.19), channel_id=1, source_target_pairs={{1,2},{3,0},{5,6},{7,4},{9,10},{11,8},{13,14},{15,12},{17,18},{19,... | collective-permute-start | bytes 2457608 | tf_op jit(solution)/shard_map/ppermute | solution.py:19
  219.1 29.5 %collective-permute-start.8 = (bf16[640,640]{1,0:T(8,128)(2,1)}, bf16[640,640]{1,0:T(8,128)(2,1)S(1)}, u32[]{:S(2)}, u32[]{:S(2)}) collective-permute-start(bf16[640,640]{1,0:T(8,128)(2,1)} %copy-done), channel_id=1, source_target_pairs={{0,4},{1,5},{2,2},{3,3},{4,8},{5,9},{6,6},{7,7},{8,12},{9,13},{10,... | collective-permute-start | bytes 2457608 | tf_op jit(solution)/shard_map/ppermute | solution.py:19
  238.8 15.3 %collective-permute-start.22 = (f32[4,128]{1,0:T(4,128)S(1)}, f32[4,128]{1,0:T(4,128)S(1)}, u32[]{:S(2)}, u32[]{:S(2)}) collective-permute-start(f32[4,128]{1,0:T(4,128)S(1)} %constant_dynamic-slice_fusion), channel_id=1, source_target_pairs={{0,1},{1,0},{2,3},{3,2},{4,5},{5,4},{6,7},{7,6},{8,9},{9,8},{10,11... | collective-permute-start | bytes 6152 | tf_op jit(solution)/shard_map/ppermute | solution.py:19
  253.9 1.4 collective-permute-start.17
  254.0 3.7 %collective-permute-start.18 = (f32[768]{0:T(1024)S(1)}, f32[768]{0:T(1024)S(1)}, u32[]{:S(2)}, u32[]{:S(2)}) collective-permute-start(f32[768]{0:T(1024)S(1)} %get-tuple-element.28), channel_id=1, source_target_pairs={{0,14},{1,15},{2,0},{3,1},{4,2},{5,3},{6,4},{7,5},{8,6},{9,7},{10,... | collective-permute-start | bytes 9224 | tf_op jit(solution)/shard_map/ppermute | solution.py:19
  (2 other events, 28.0 us)

commit v2 on v1

v2 whole, which is shorter than its diff:
```python
import functools
import math

import jax
import jax.numpy as jnp
from jax import lax
from jax.experimental import pallas as pl
from jax.experimental.pallas import tpu as pltpu
from jax.sharding import PartitionSpec as P

ROUNDS = 2
DOM_DEV = 4
LATE = 256
DEPTH = 1024
NT = (((1,), (1,)), ((), ()))
VMEM_LIMIT = 48 * 2**20


def send(value, pairs):
    return lax.ppermute(value, "blocks", pairs)


def after(value, *others):
    return lax.optimization_barrier((value, *others))[0]


def inverse_norm(matrix):
    values = matrix.astype(jnp.float32)
    return lax.rsqrt(jnp.mean(values * values, axis=1) + 1e-06)


def nt(left, right):
    return lax.dot_general(left, right, NT, preferred_element_type=jnp.float32)


def params():
    return pltpu.CompilerParams(vmem_limit_bytes=VMEM_LIMIT)


def cost(flops, bytes_accessed):
    return pl.CostEstimate(flops=flops, bytes_accessed=bytes_accessed, transcendentals=0)


def clear(*totals):
    @pl.when(pl.program_id(0) == 0)
    def _():
        for total in totals:
            total[...] = jnp.zeros_like(total)


def at_end(body):
    pl.when(pl.program_id(0) == pl.num_programs(0) - 1)(body)


def early_kernel(place, own, partner, near, u_out, v_out, u, v):
    clear(u, v)

    @pl.when(place[0] == 0)
    def _():
        u[...] += nt(partner[...], own[...])
        v[...] += nt(near[...], partner[...])

    @pl.when(place[0] == 1)
    def _():
        u[...] += nt(partner[...], near[...])
        v[...] += nt(own[...], partner[...])

    @at_end
    def _():
        u_out[...] = u[...].astype(u_out.dtype)
        v_out[...] = v[...].astype(v_out.dtype)


def early_tiles(place, own, partner, near):
    early, half = partner.shape
    steps = half // DEPTH
    block = pl.BlockSpec((early, DEPTH), lambda k, place: (0, k))
    mine = pl.BlockSpec((early, DEPTH), lambda k, place: (0, place[0] * steps + k))
    whole = pl.BlockSpec((early, early), lambda k, place: (0, 0))
    return pl.pallas_call(
        early_kernel,
        grid_spec=pltpu.PrefetchScalarGridSpec(
            num_scalar_prefetch=1,
            grid=(steps,),
            in_specs=[mine, block, block],
            out_specs=[whole] * 2,
            scratch_shapes=[pltpu.VMEM((early, early), jnp.float32)] * 2,
        ),
        out_shape=[jax.ShapeDtypeStruct((early, early), jnp.bfloat16)] * 2,
        compiler_params=params(),
        cost_estimate=cost(early, early),
    )(place, own, partner, near)


def late_kernel(
    place, own1, own2, partner1, partner2, near1, near2, u_out, v_out, ur, uc, vr, vc
):
    clear(ur, uc, vr, vc)
    early = own1.shape[0]

    def add(s1, s2, w1, w2):
        ur[:, :early] += nt(partner2[...], s1[...])
        ur[:, early:] += nt(partner2[...], s2[...])
        uc[...] += nt(partner1[...], s2[...])
        vr[:, :early] += nt(w2[...], partner1[...])
        vr[:, early:] += nt(w2[...], partner2[...])
        vc[...] += nt(w1[...], partner2[...])

    @pl.when(place[0] == 0)
    def _():
        add(own1, own2, near1, near2)

    @pl.when(place[0] == 1)
    def _():
        add(near1, near2, own1, own2)

    @at_end
    def _():
        for out, rows, columns in ((u_out, ur, uc), (v_out, vr, vc)):
            late, width = rows.shape
            out[:, :width] = rows[...].astype(out.dtype)
            for j in range(early // late):
                out[:, width + j * late : width + (j + 1) * late] = columns[
                    j * late : (j + 1) * late
                ].astype(out.dtype)


def late_tiles(place, own, partner1, partner2, near1, near2):
    early, half = partner1.shape
    late = partner2.shape[0]
    rows = early + late
    steps = half // DEPTH
    block1 = pl.BlockSpec((early, DEPTH), lambda k, place: (0, k))
    block2 = pl.BlockSpec((late, DEPTH), lambda k, place: (0, k))
    mine1 = pl.BlockSpec((early, DEPTH), lambda k, place: (0, place[0] * steps + k))
    mine2 = pl.BlockSpec((late, DEPTH), lambda k, place: (early // late, place[0] * steps + k))
    whole = pl.BlockSpec((late, rows + early), lambda k, place: (0, 0))
    totals = [pltpu.VMEM((late, rows), jnp.float32), pltpu.VMEM((early, late), jnp.float32)]
    return pl.pallas_call(
        late_kernel,
        grid_spec=pltpu.PrefetchScalarGridSpec(
            num_scalar_prefetch=1,
            grid=(steps,),
            in_specs=[mine1, mine2] + [block1, block2] * 2,
            out_specs=[whole] * 2,
            scratch_shapes=totals * 2,
        ),
        out_shape=[jax.ShapeDtypeStruct((late, rows + early), jnp.bfloat16)] * 2,
        compiler_params=params(),
        cost_estimate=cost(4 * late * (rows + early) * half, 6 * rows * half),
    )(place, own, own, partner1, partner2, near1, near2)


def cross_kernel(place, own, near1, near2, other1, other2, out, x):
    clear(x)
    early = near1.shape[0]
    first, second = slice(None, early), slice(early, None)
    near = ((first, near1), (second, near2))
    other = ((first, other1), (second, other2))
    mine = ((slice(None), own),)

    def add(left, right):
        for rows, left_ref in left:
            for columns, right_ref in right:
                x[rows, columns] += nt(left_ref[...], right_ref[...])

    code = place[0] * 2 + place[1]
    for number, pair in enumerate(((near, other), (other, mine), (mine, other), (other, near))):

        @pl.when(code == number)
        def _(pair=pair):
            add(*pair)

    @at_end
    def _():
        out[...] = x[...].astype(out.dtype)


def cross_tile(place, own, near1, near2, other1, other2):
    early, half = near1.shape
    late = near2.shape[0]
    rows = early + late
    steps = half // DEPTH
    block1 = pl.BlockSpec((early, DEPTH), lambda k, place: (0, k))
    block2 = pl.BlockSpec((late, DEPTH), lambda k, place: (0, k))
    mine = pl.BlockSpec((rows, DEPTH), lambda k, place: (0, place[0] * steps + k))
    return pl.pallas_call(
        cross_kernel,
        grid_spec=pltpu.PrefetchScalarGridSpec(
            num_scalar_prefetch=1,
            grid=(steps,),
            in_specs=[mine] + [block1, block2] * 2,
            out_specs=pl.BlockSpec((rows, rows), lambda k, place: (0, 0)),
            scratch_shapes=[pltpu.VMEM((rows, rows), jnp.float32)],
        ),
        out_shape=jax.ShapeDtypeStruct((rows, rows), jnp.bfloat16),
        compiler_params=params(),
        cost_estimate=cost(2 * rows * rows * half, 6 * rows * half),
    )(place, own, near1, near2, other1, other2)


def finish(tile, row_mass, column_mass):
    @pl.when(pl.program_id(0) == 0)
    def _():
        column_mass[...] = jnp.zeros_like(column_mass)

    squared = tile * tile
    column_mass[...] += jnp.sum(squared, axis=0, keepdims=True)
    sums = jnp.sum(squared, axis=1, keepdims=True)
    size = sums.shape[0]
    row_mass[...] = jnp.broadcast_to(sums, (size, size)).T[0:1]


def second_kernel(
    scale, u1, u2r, u2c, v1, v2r, v2c, inverse, behind, gram, row_mass, column_mass
):
    step = pl.program_id(0)
    last = pl.num_programs(0) - 1
    early = u1.shape[1]

    def f32(ref):
        return ref[...].astype(jnp.float32)

    @pl.when(step < last)
    def _():
        gram[0, :, :early] = f32(u1) + f32(v1)
        gram[0, :, early:] = f32(u2c) + f32(v2c)

    @pl.when(step == last)
    def _():
        gram[0] = f32(u2r) + f32(v2r)

    tile = gram[0] * inverse[...] * behind[...] * scale
    gram[0] = tile
    finish(tile, row_mass, column_mass)


def mass_shapes(rows, late):
    specs = [
        pl.BlockSpec((1, late), lambda j, *_: (0, j)),
        pl.BlockSpec((1, rows), lambda j, *_: (0, 0)),
    ]
    return specs, [jax.ShapeDtypeStruct((1, rows), jnp.float32)] * 2


def second_tiles(scale, u1, u2, v1, v2, inverse, behind):
    early = u1.shape[0]
    late = u2.shape[0]
    rows = early + late
    last = early // late - 1
    first = pl.BlockSpec((late, early), lambda j: (jnp.minimum(j, last), 0))
    bottom = pl.BlockSpec((late, rows), lambda j: (0, 0))
    side = pl.BlockSpec((late, late), lambda j: (0, rows // late + jnp.minimum(j, last)))
    mass_specs, mass_types = mass_shapes(rows, late)
    return pl.pallas_call(
        functools.partial(second_kernel, scale),
        grid=(rows // late,),
        in_specs=[first, bottom, side] * 2
        + [
            pl.BlockSpec((late, 1), lambda j: (j, 0)),
            pl.BlockSpec((1, rows), lambda j: (0, 0)),
        ],
        out_specs=[pl.BlockSpec((1, late, rows), lambda j: (1, j, 0))] + mass_specs,
        out_shape=[jax.ShapeDtypeStruct((2, rows, rows), jnp.float32)] + mass_types,
        compiler_params=params(),
        cost_estimate=cost(8 * rows * rows, 160 * rows * rows),
    )(u1, u2, u2, v1, v2, v2, inverse[:, None], behind[None, :])


def first_kernel(
    scale, place, y, z, local, inverse, behind, gram_in, gram, row_mass, column_mass
):
    del gram_in
    summed = y[...].astype(jnp.float32) + z[...].astype(jnp.float32)
    tile = jnp.where(place[1] == 1, local[...], summed)
    tile = tile * inverse[...] * behind[...] * scale
    gram[0] = tile
    finish(tile, row_mass, column_mass)


def first_tiles(scale, place, y, z, local, inverse, behind, gram, late):
    rows = y.shape[0]
    block = pl.BlockSpec((late, rows), lambda j, place: (j, 0))
    mass_specs, mass_types = mass_shapes(rows, late)
    return pl.pallas_call(
        functools.partial(first_kernel, scale),
        grid_spec=pltpu.PrefetchScalarGridSpec(
            num_scalar_prefetch=1,
            grid=(rows // late,),
            in_specs=[block] * 3
            + [
                pl.BlockSpec((late, 1), lambda j, place: (j, 0)),
                pl.BlockSpec((1, rows), lambda j, place: (0, 0)),
                pl.BlockSpec(memory_space=pl.ANY),
            ],
            out_specs=[pl.BlockSpec((1, late, rows), lambda j, place: (0, j, 0))] + mass_specs,
        ),
        out_shape=[jax.ShapeDtypeStruct((2, rows, rows), jnp.float32)] + mass_types,
        input_output_aliases={6: 0},
        compiler_params=params(),
        cost_estimate=cost(8 * rows * rows, 12 * rows * rows),
    )(place, y, z, local, inverse[:, None], behind[None, :], gram)


def scatter_sum(value, index, size, waits):
    bit = size // 2
    for wait in waits:
        half = value.shape[0] // 2
        mine = (index // bit) % 2
        away = lax.dynamic_slice_in_dim(value, (1 - mine) * half, half)
        kept = lax.dynamic_slice_in_dim(value, mine * half, half)
        if wait is not None:
            away = after(away, wait)
        value = kept + send(away, [(i, i ^ bit) for i in range(size)])
        bit //= 2
    return value


def local(sketches, test_sketches, domain_map):
    rows, depth = sketches.shape
    size = lax.axis_size("blocks")
    index = lax.axis_index("blocks")
    half = depth // 2
    early = rows - LATE
    blocks = range(size)
    upper = (index // 2) % 2
    core = index % 2
    place = jnp.stack([upper, core]).astype(jnp.int32)

    across = [(i, i ^ 2) for i in blocks]
    along = [(i, (i + (4 if i & 2 else -4)) % size) for i in blocks]
    swap = [(i, i ^ 1) for i in blocks]

    def part(source, start, count, side):
        return lax.dynamic_slice(source, (start, side * half), (count, half))

    out1 = part(sketches, 0, early, 1 - upper)
    partner1 = send(out1, across)
    source = after(sketches, out1)
    side1 = part(source, 0, early, upper)
    near1 = send(side1, along)
    source = after(source, side1)
    partner2 = send(part(source, early, LATE, 1 - upper), across)
    near2 = send(part(source, early, LATE, upper), along)
    even = send(sketches, [(i, i + 1) for i in blocks if i % 2 == 0])

    inverse = inverse_norm(sketches)
    behind1 = send(inverse, [(i, (i + 1) % size) for i in blocks])
    behind2 = send(inverse, [(i, (i + 2) % size) for i in blocks])
    scale = 1.0 / math.sqrt(depth)

    test_inverse = inverse_norm(test_sketches)
    similarity = (
        nt(sketches, test_sketches) * inverse[:, None] * test_inverse[None, :] * scale
    ).astype(jnp.bfloat16)
    members = (
        domain_map[:, None] == lax.iota(jnp.int32, DOM_DEV * size)[None, :]
    ).astype(jnp.bfloat16)
    sums = lax.dot_general(
        members, similarity, (((0,), (0,)), ((), ())), preferred_element_type=jnp.float32
    )
    inside = nt(sketches, even)

    partner1 = after(partner1, inside, sums)
    u1, v1 = early_tiles(place, sketches, partner1, near1)
    other1 = send(partner1, swap)
    partner2 = after(partner2, u1, behind1, behind2)
    other2 = send(partner2, swap)
    u2, v2 = late_tiles(place, sketches, partner1, partner2, near1, after(near2, u1))
    x = cross_tile(place, sketches, near1, near2, other1, after(other2, u2))

    back_v = [(i, i) if i & 2 else (i, (i + 4) % size) for i in blocks]
    back_y = [(i, i ^ 3) for i in blocks if i & 1]
    back_z = [pair for pair in back_v if pair[0] % 2 == 0]
    u1r, v1r = send(u1, across), send(v1, back_v)
    u2r, v2r = send(u2, across), send(v2, back_v)
    y, z = send(x, back_y), send(x, back_z)

    bits = size.bit_length() - 1
    waits = ([None, u1, u2, x] + [x] * bits)[:bits]
    domain_scores = scatter_sum(sums, index, size, waits) * (1.0 / math.sqrt(rows / DOM_DEV))

    gram, row_mass2, column_mass2 = second_tiles(scale, u1r, u2r, v1r, v2r, inverse, behind2)
    gram, row_mass1, column_mass1 = first_tiles(
        scale, place, y, z, inside, inverse, behind1, gram, LATE
    )
    mass = (
        row_mass1[0]
        + row_mass2[0]
        + send(column_mass1[0], [(i, (i - 1) % size) for i in blocks])
        + send(column_mass2[0], [(i, (i - 2) % size) for i in blocks])
    )
    redundancy = mass / float(2 * ROUNDS * rows)
    return (gram, redundancy, domain_scores)


def solution(mesh):
    in_specs = (P(("groups", "blocks"), None), P(), P(("groups", "blocks")))
    out_specs = (
        P(None, ("groups", "blocks"), None),
        P(("groups", "blocks")),
        P(("groups", "blocks"), None),
    )
    return jax.shard_map(local, mesh=mesh, in_specs=in_specs, out_specs=out_specs, check_vma=False)
```

time: 259 us -> 247 us (0.954)
  waiting for transfers between devices: 130 us -> 111 us
  starting transfers between devices: 42.1 us -> 46.5 us
  local copies, waits for them, and re-layouts: 13 us -> 15.9 us
    ppermute x23 -> x21, waiting for transfers between devices: 130 us -> 111 us  [send(): return lax.ppermute(value, 'blocks', pairs)]
    pallas_call x1 -> x3, Pallas kernels: 5.23 us -> 18.1 us  [the longest x1 10.8 us: cross_tile(): pl.pallas_call(cross_kernel, grid_spec=pltpu.PrefetchScalarGridSpec(num_s...]
    pallas_call x1, Pallas kernels: 19.6 us -> 9.57 us  [early_tiles(): pl.pallas_call(early_kernel, grid_spec=pltpu.PrefetchScalarGridSpec(num_s...]
    pallas_call x1, Pallas kernels: 16.4 us -> 11.3 us  [late_tiles(): pl.pallas_call(late_kernel, grid_spec=pltpu.PrefetchScalarGridSpec(num_sc...]
    ppermute x23 -> x21, starting transfers between devices: 42.1 us -> 46.5 us  [send(): return lax.ppermute(value, 'blocks', pairs)]
    dynamic_slice x2 -> x3, local copies, waits for them, and re-layouts: 12.7 us -> 14 us  [part(): return lax.dynamic_slice(source, (start, side * half), (count, half))]
  transfers between devices with their start and end apart: 23 -> 21, of which waited for: 8 -> 7; matrix products, arithmetic and copies ran while one was open for 17% -> 19% of each run, Pallas kernels for 16% -> 16%
where the time goes in v2:
time: 247 us; the launch traced here: 246 us
  waiting for transfers between devices  111 us (45%)
  starting transfers between devices  46.5 us (19%)
  Pallas kernels  39 us (16%)
  matrix products  23.1 us (9%)
  local copies, waits for them, and re-layouts  15.9 us (6%)
  other arithmetic  8.94 us (4%)
    ppermute x21, waiting for transfers between devices, send(): return lax.ppermute(value, 'blocks', pairs)  111 us
    ppermute x21, starting transfers between devices, send(): return lax.ppermute(value, 'blocks', pairs)  46.5 us
    dot_general x1, matrix products, nt(): return lax.dot_general(left, right, NT, preferred_element_type=jnp.float32)  16.2 us
    dynamic_slice x3, local copies, waits for them, and re-layouts, part(): return lax.dynamic_slice(source, (start, side * half), (count, half))  14 us
    pallas_call x1, Pallas kernels, late_tiles(): pl.pallas_call(late_kernel, grid_spec=pltpu.PrefetchScalarGridSpec(num_sc...  11.3 us
    pallas_call x1, Pallas kernels, cross_tile(): pl.pallas_call(cross_kernel, grid_spec=pltpu.PrefetchScalarGridSpec(num_s...  10.8 us
    pallas_call x1, Pallas kernels, early_tiles(): pl.pallas_call(early_kernel, grid_spec=pltpu.PrefetchScalarGridSpec(num_s...  9.57 us
    reduce_sum x2, other arithmetic, inverse_norm(): return lax.rsqrt(jnp.mean(values * values, axis=1) + 1e-06)  7.59 us
  transfers between devices with their start and end apart: 21, of which 7 were waited for; matrix products, arithmetic and copies ran while one was open for 19% of the time, Pallas kernels for 16%

profile of v2, /device:TPU:0, one launch (start us, length us, event | category | flops | bytes accessed | tf_op | source)
XLA Modules:
  0.0 245.7 jit_solution(1228296817988674245)
XLA Ops:
  0.6 6.9 %collective-permute-start.3 = (bf16[768,8192]{1,0:T(8,128)(2,1)}, bf16[768,8192]{1,0:T(8,128)(2,1)}, u32[]{:S(2)}, u32[]{:S(2)}) collective-permute-start(bf16[768,8192]{1,0:T(8,128)(2,1)} %own.3), channel_id=1, source_target_pairs={{0,1},{2,3},{4,5},{6,7},{8,9},{10,11},{12,13},{14,15},{16,17},{18,... | collective-permute-start | bytes 37748744 | tf_op jit(solution)/shard_map/ppermute | solution.py:20
  7.5 4.7 %constant_dynamic-slice_fusion.6 = bf16[512,4096]{1,0:T(8,128)(2,1)} fusion(bf16[768,8192]{1,0:T(8,128)(2,1)} %own.3, s32[]{:T(128)S(6)} %select_n.70), kind=kLoop, calls=%fused_computation.24 | loop fusion | bytes 8388612 | tf_op jit(solution)/shard_map/dynamic_slice | solution.py:335
  12.2 2.3 collective-permute-start.2
  14.5 4.7 %constant_dynamic-slice_fusion.5 = bf16[512,4096]{1,0:T(8,128)(2,1)} fusion(bf16[768,8192]{1,0:T(8,128)(2,1)} %own.3, s32[]{:T(128)S(6)} %select_n.71), kind=kLoop, calls=%fused_computation.23 | loop fusion | bytes 8388612 | tf_op jit(solution)/shard_map/dynamic_slice | solution.py:335
  19.2 3.6 %collective-permute-start = (bf16[512,4096]{1,0:T(8,128)(2,1)}, bf16[512,4096]{1,0:T(8,128)(2,1)}, u32[]{:S(2)}, u32[]{:S(2)}) collective-permute-start(bf16[512,4096]{1,0:T(8,128)(2,1)} %constant_dynamic-slice_fusion.5), channel_id=1, source_target_pairs={{0,12},{1,13},{2,6},{3,7},{4,0},{5,1},{6,10},{7,11},{8,4},{9,5},{1... | collective-permute-start | bytes 12582920 | tf_op jit(solution)/shard_map/ppermute | solution.py:20
  22.8 4.7 %constant_dynamic-slice_fusion.7 = (bf16[256,4096]{1,0:T(8,128)(2,1)}, bf16[256,4096]{1,0:T(8,128)(2,1)}) fusion(bf16[768,8192]{1,0:T(8,128)(2,1)} %own.3, s32[]{:T(128)S(6)} %select_n.70, s32[]{:T(128)S(6)} %select_n.71), kind=kLoop, calls=%fused_computation.27 | loop fusion | bytes 8388616 | tf_op jit(solution)/shard_map/dynamic_slice | solution.py:335
  28.0 7.1 %multiply_reduce_fusion = f32[768]{0:T(1024)S(1)} fusion(bf16[768,8192]{1,0:T(8,128)(2,1)} %own.3), kind=kLoop, calls=%fused_computation | loop fusion | flops 18873600 | bytes 12585984 | tf_op jit(solution)/shard_map/reduce_sum | solution.py:29
  35.2 6.9 %fusion.3 = f32[64,128]{1,0:T(8,128)S(1)} fusion(bf16[768,8192]{1,0:T(8,128)(2,1)} %own.3, bf16[128,8192]{1,0:T(8,128)(2,1)S(1)} %copy-done.1, f32[128]{0:T(128)S(1)} %add_rsqrt_fusion.1, f32[768]{0:T(1024)S(1)} %add_rsqrt_fusion, s32[768]{0:T(1024)S(1)} %copy-done.2), kind=kOutput, calls=%fused_computation.6 | convolution fusion | flops 1623638016 | bytes 14719488 | tf_op jit(solution)/shard_map/dot_general | solution.py:359
  42.1 16.2 %fusion.11.local = f32[768,768]{1,0:T(8,128)} fusion(bf16[768,8192]{1,0:T(8,128)(2,1)} %own.3, bf16[768,8192]{1,0:T(8,128)(2,1)} %collective-permute-done.3), kind=kOutput, calls=%fused_computation.32 | convolution fusion | flops 9663676416 | bytes 27525120 | tf_op jit(solution)/shard_map/dot_general | solution.py:33
  58.3 48.0 %collective-permute-done.2.partner.partner1 = bf16[512,4096]{1,0:T(8,128)(2,1)} collective-permute-done((bf16[512,4096]{1,0:T(8,128)(2,1)}, bf16[512,4096]{1,0:T(8,128)(2,1)}, u32[]{:S(2)}, u32[]{:S(2)}) %collective-permute-start.2) | collective-permute-done | bytes 4194336 | tf_op jit(solution)/shard_map/ppermute | solution.py:20
  106.3 4.1 %collective-permute-start.1 = (bf16[256,4096]{1,0:T(8,128)(2,1)}, bf16[256,4096]{1,0:T(8,128)(2,1)S(1)}, u32[]{:S(2)}, u32[]{:S(2)}) collective-permute-start(bf16[256,4096]{1,0:T(8,128)(2,1)} %get-tuple-element.42), channel_id=1, source_target_pairs={{0,12},{1,13},{2,6},{3,7},{4,0},{5,1},{6,10},{7,11},{8,4},{9,5},{1... | collective-permute-start | bytes 6291464 | tf_op jit(solution)/shard_map/ppermute | solution.py:20
  110.8 9.6 %shard_map.58 = (bf16[512,512]{1,0:T(8,128)(2,1)}, bf16[512,512]{1,0:T(8,128)(2,1)}) custom-call(s32[2]{0:T(128)S(1)} %pad_add_fusion.place, bf16[768,8192]{1,0:T(8,128)(2,1)} %own.3, bf16[512,4096]{1,0:T(8,128)(2,1)} %collective-permute-done.2.partner.partner1, bf16[512,4096]{1,0:T(8,128)(2,1)} %collective-permute-done.near.near1), custom_call_target="tpu_custom_call" | custom-call | flops 512 | bytes 512 | tf_op jit(solution)/shard_map/pallas_call | solution.py:80
  120.3 37.4 %collective-permute-done.6 = f32[768]{0:T(1024)S(1)} collective-permute-done((f32[768]{0:T(1024)S(1)}, f32[768]{0:T(1024)S(1)}, u32[]{:S(2)}, u32[]{:S(2)}) %collective-permute-start.6) | collective-permute-done | bytes 3104 | tf_op jit(solution)/shard_map/ppermute | solution.py:20
  158.9 3.9 %collective-permute-done.17 = f32[32,128]{1,0:T(8,128)S(1)} collective-permute-done((f32[32,128]{1,0:T(8,128)S(1)}, f32[32,128]{1,0:T(8,128)S(1)}, u32[]{:S(2)}, u32[]{:S(2)}) %collective-permute-start.17) | collective-permute-done | bytes 16416 | tf_op jit(solution)/shard_map/ppermute | solution.py:20
  162.9 11.3 %shard_map.59 = (bf16[256,1280]{1,0:T(8,128)(2,1)}, bf16[256,1280]{1,0:T(8,128)(2,1)}) custom-call(s32[2]{0:T(128)S(1)} %pad_add_fusion.place, bf16[768,8192]{1,0:T(8,128)(2,1)} %own.3, bf16[768,8192]{1,0:T(8,128)(2,1)} %own.3, bf16[512,4096]{1,0:T(8,128)(2,1)} %collective-permute-done.2.partner.partner1, bf16[256,4096]{1,0:T(8,128)(2,1)} %collective-permute-done.5.partner2, ...), custom_call_target="tpu_custom_call" | custom-call | flops 5368709120 | bytes 18874368 | tf_op jit(solution)/shard_map/pallas_call | solution.py:139
  174.2 10.8 %shard_map.60 = bf16[768,768]{1,0:T(8,128)(2,1)} custom-call(s32[2]{0:T(128)S(1)} %pad_add_fusion.place, bf16[768,8192]{1,0:T(8,128)(2,1)} %own.3, bf16[512,4096]{1,0:T(8,128)(2,1)} %collective-permute-done.near.near1, bf16[256,4096]{1,0:T(8,128)(2,1)S(1)} %collective-permute-done.1.near2, bf16[512,4096]{1,0:T(8,128)(2,1)} %collective-permute-done.4.other1, ...), custom_call_target="tpu_custom_call" | custom-call | flops 4831838208 | bytes 18874368 | tf_op jit(solution)/shard_map/pallas_call | solution.py:187
  184.9 3.9 %collective-permute-start.10 = (bf16[768,768]{1,0:T(8,128)(2,1)}, bf16[768,768]{1,0:T(8,128)(2,1)S(1)}, u32[]{:S(2)}, u32[]{:S(2)}) collective-permute-start(bf16[768,768]{1,0:T(8,128)(2,1)} %shard_map.60), channel_id=1, source_target_pairs={{0,4},{2,2},{4,8},{6,6},{8,12},{10,10},{12,0},{14,14},{16,20},{18,... | collective-permute-start | bytes 3538952 | tf_op jit(solution)/shard_map/ppermute | solution.py:20
  190.2 2.0 collective-permute-start.12
  193.8 2.8 %collective-permute-start.14 = (bf16[256,1280]{1,0:T(8,128)(2,1)}, bf16[256,1280]{1,0:T(8,128)(2,1)S(1)}, u32[]{:S(2)}, u32[]{:S(2)}) collective-permute-start(bf16[256,1280]{1,0:T(8,128)(2,1)} %get-tuple-element.31), channel_id=1, source_target_pairs={{0,4},{1,5},{2,2},{3,3},{4,8},{5,9},{6,6},{7,7},{8,12},{9,13},{10,... | collective-permute-start | bytes 1966088 | tf_op jit(solution)/shard_map/ppermute | solution.py:20
  196.6 2.3 collective-permute-start.13
  199.0 18.8 %collective-permute-done.13.v1 = bf16[512,512]{1,0:T(8,128)(2,1)} collective-permute-done((bf16[512,512]{1,0:T(8,128)(2,1)}, bf16[512,512]{1,0:T(8,128)(2,1)}, u32[]{:S(2)}, u32[]{:S(2)}) %collective-permute-start.13) | collective-permute-done | bytes 524320 | tf_op jit(solution)/shard_map/ppermute | solution.py:20
  217.8 15.1 %collective-permute-start.20 = (f32[4,128]{1,0:T(4,128)S(1)}, f32[4,128]{1,0:T(4,128)S(1)}, u32[]{:S(2)}, u32[]{:S(2)}) collective-permute-start(f32[4,128]{1,0:T(4,128)S(1)} %constant_dynamic-slice_fusion), channel_id=1, source_target_pairs={{0,1},{1,0},{2,3},{3,2},{4,5},{5,4},{6,7},{7,6},{8,9},{9,8},{10,11... | collective-permute-start | bytes 6152 | tf_op jit(solution)/shard_map/ppermute | solution.py:20
  233.1 3.2 %shard_map.61 = (f32[2,768,768]{2,1,0:T(8,128)}, f32[1,768]{1,0:T(1,128)S(1)}, f32[1,768]{1,0:T(1,128)S(1)}) custom-call(bf16[512,512]{1,0:T(8,128)(2,1)S(1)} %collective-permute-done.11.u1, bf16[256,1280]{1,0:T(8,128)(2,1)S(1)} %collective-permute-done.12.u2r.u2c, bf16[256,1280]{1,0:T(8,128)(2,1)S(1)} %collective-permute-done.12.u2r.u2c, ...), custom_call_target="tpu_custom_call" | custom-call | flops 4718592 | bytes 94371840 | tf_op jit(solution)/shard_map/pallas_call | solution.py:255
  238.7 4.1 %shard_map.62 = (f32[2,768,768]{2,1,0:T(8,128)}, f32[1,768]{1,0:T(1,128)S(1)}, f32[1,768]{1,0:T(1,128)S(1)}) custom-call(s32[2]{0:T(128)S(1)} %pad_add_fusion.place, bf16[768,768]{1,0:T(8,128)(2,1)} %collective-permute-done.9.y, bf16[768,768]{1,0:T(8,128)(2,1)S(1)} %collective-permute-done.10.z, ...), custom_call_target="tpu_custom_call", output_to_operand_aliasing={{0}: (6, {})} | custom-call | flops 4718592 | bytes 7077888 | tf_op jit(solution)/shard_map/pallas_call | solution.py:285
  (54 shorter events, 10.4 us)
Async XLA Ops:
  0.6 41.4 %collective-permute-start.3 = (bf16[768,8192]{1,0:T(8,128)(2,1)}, bf16[768,8192]{1,0:T(8,128)(2,1)}, u32[]{:S(2)}, u32[]{:S(2)}) collective-permute-start(bf16[768,8192]{1,0:T(8,128)(2,1)} %own.3), channel_id=1, source_target_pairs={{0,1},{2,3},{4,5},{6,7},{8,9},{10,11},{12,13},{14,15},{16,17},{18,... | collective-permute-start | bytes 37748744 | tf_op jit(solution)/shard_map/ppermute | solution.py:20
  12.2 94.2 %collective-permute-start.2 = (bf16[512,4096]{1,0:T(8,128)(2,1)}, bf16[512,4096]{1,0:T(8,128)(2,1)}, u32[]{:S(2)}, u32[]{:S(2)}) collective-permute-start(bf16[512,4096]{1,0:T(8,128)(2,1)} %constant_dynamic-slice_fusion.6), channel_id=1, source_target_pairs={{0,2},{1,3},{2,0},{3,1},{4,6},{5,7},{6,4},{7,5},{8,10},{9,11},{10,... | collective-permute-start | bytes 12582920 | tf_op jit(solution)/shard_map/ppermute | solution.py:20
  19.2 8.3 %copy-start.1 = (bf16[128,8192]{1,0:T(8,128)(2,1)S(1)}, bf16[128,8192]{1,0:T(8,128)(2,1)}, u32[]{:S(2)}) copy-start(bf16[128,8192]{1,0:T(8,128)(2,1)} %param.4) | copy-start | bytes 6291460
  19.2 91.4 %collective-permute-start = (bf16[512,4096]{1,0:T(8,128)(2,1)}, bf16[512,4096]{1,0:T(8,128)(2,1)}, u32[]{:S(2)}, u32[]{:S(2)}) collective-permute-start(bf16[512,4096]{1,0:T(8,128)(2,1)} %constant_dynamic-slice_fusion.5), channel_id=1, source_target_pairs={{0,12},{1,13},{2,6},{3,7},{4,0},{5,1},{6,10},{7,11},{8,4},{9,5},{1... | collective-permute-start | bytes 12582920 | tf_op jit(solution)/shard_map/ppermute | solution.py:20
  27.5 130.5 %collective-permute-start.5 = (bf16[256,4096]{1,0:T(8,128)(2,1)}, bf16[256,4096]{1,0:T(8,128)(2,1)}, u32[]{:S(2)}, u32[]{:S(2)}) collective-permute-start(bf16[256,4096]{1,0:T(8,128)(2,1)} %get-tuple-element.41), channel_id=1, source_target_pairs={{0,2},{1,3},{2,0},{3,1},{4,6},{5,7},{6,4},{7,5},{8,10},{9,11},{10,... | collective-permute-start | bytes 6291464 | tf_op jit(solution)/shard_map/ppermute | solution.py:20
  28.0 7.1 %copy-start.2 = (s32[768]{0:T(1024)S(1)}, s32[768]{0:T(1024)}, u32[]{:S(2)}) copy-start(s32[768]{0:T(1024)} %param.5) | copy-start | bytes 9220
  106.3 67.8 %collective-permute-start.4 = (bf16[512,4096]{1,0:T(8,128)(2,1)}, bf16[512,4096]{1,0:T(8,128)(2,1)}, u32[]{:S(2)}, u32[]{:S(2)}) collective-permute-start(bf16[512,4096]{1,0:T(8,128)(2,1)} %collective-permute-done.2.partner.partner1), channel_id=1, source_target_pairs={{0,1},{1,0},{2,3},{3,2},{4,5},{5,4},{6,7},{7,6},{8,9},{9,8},{10,11... | collective-permute-start | bytes 12582920 | tf_op jit(solution)/shard_map/ppermute | solution.py:20
  106.3 56.5 %collective-permute-start.1 = (bf16[256,4096]{1,0:T(8,128)(2,1)}, bf16[256,4096]{1,0:T(8,128)(2,1)S(1)}, u32[]{:S(2)}, u32[]{:S(2)}) collective-permute-start(bf16[256,4096]{1,0:T(8,128)(2,1)} %get-tuple-element.42), channel_id=1, source_target_pairs={{0,12},{1,13},{2,6},{3,7},{4,0},{5,1},{6,10},{7,11},{8,4},{9,5},{1... | collective-permute-start | bytes 6291464 | tf_op jit(solution)/shard_map/ppermute | solution.py:20
  110.4 47.2 %collective-permute-start.6 = (f32[768]{0:T(1024)S(1)}, f32[768]{0:T(1024)S(1)}, u32[]{:S(2)}, u32[]{:S(2)}) collective-permute-start(f32[768]{0:T(1024)S(1)} %add_rsqrt_fusion), channel_id=1, source_target_pairs={{0,1},{1,2},{2,3},{3,4},{4,5},{5,6},{6,7},{7,8},{8,9},{9,10},{10,1... | collective-permute-start | bytes 9224 | tf_op jit(solution)/shard_map/ppermute | solution.py:20
  110.7 47.4 %collective-permute-start.7 = (f32[768]{0:T(1024)S(1)}, f32[768]{0:T(1024)S(1)}, u32[]{:S(2)}, u32[]{:S(2)}) collective-permute-start(f32[768]{0:T(1024)S(1)} %add_rsqrt_fusion), channel_id=1, source_target_pairs={{0,2},{1,3},{2,4},{3,5},{4,6},{5,7},{6,8},{7,9},{8,10},{9,11},{10,... | collective-permute-start | bytes 9224 | tf_op jit(solution)/shard_map/ppermute | solution.py:20
  158.0 16.1 %collective-permute-start.8 = (bf16[256,4096]{1,0:T(8,128)(2,1)}, bf16[256,4096]{1,0:T(8,128)(2,1)}, u32[]{:S(2)}, u32[]{:S(2)}) collective-permute-start(bf16[256,4096]{1,0:T(8,128)(2,1)} %collective-permute-done.5.partner2), channel_id=1, source_target_pairs={{0,1},{1,0},{2,3},{3,2},{4,5},{5,4},{6,7},{7,6},{8,9},{9,8},{10,11... | collective-permute-start | bytes 6291464 | tf_op jit(solution)/shard_map/ppermute | solution.py:20
  158.1 4.7 %collective-permute-start.17 = (f32[32,128]{1,0:T(8,128)S(1)}, f32[32,128]{1,0:T(8,128)S(1)}, u32[]{:S(2)}, u32[]{:S(2)}) collective-permute-start(f32[32,128]{1,0:T(8,128)S(1)} %constant_dynamic-slice_fusion.4), channel_id=1, source_target_pairs={{0,8},{1,9},{2,10},{3,11},{4,12},{5,13},{6,14},{7,15},{8,0},{9,1},... | collective-permute-start | bytes 49160 | tf_op jit(solution)/shard_map/ppermute | solution.py:20
  162.8 33.9 %collective-permute-start.11 = (bf16[512,512]{1,0:T(8,128)(2,1)}, bf16[512,512]{1,0:T(8,128)(2,1)S(1)}, u32[]{:S(2)}, u32[]{:S(2)}) collective-permute-start(bf16[512,512]{1,0:T(8,128)(2,1)} %get-tuple-element.25), channel_id=1, source_target_pairs={{0,2},{1,3},{2,0},{3,1},{4,6},{5,7},{6,4},{7,5},{8,10},{9,11},{10,... | collective-permute-start | bytes 1572872 | tf_op jit(solution)/shard_map/ppermute | solution.py:20
  162.8 27.3 %collective-permute-start.18 = (f32[16,128]{1,0:T(8,128)S(1)}, f32[16,128]{1,0:T(8,128)S(1)}, u32[]{:S(2)}, u32[]{:S(2)}) collective-permute-start(f32[16,128]{1,0:T(8,128)S(1)} %constant_dynamic-slice_fusion.3), channel_id=1, source_target_pairs={{0,4},{1,5},{2,6},{3,7},{4,0},{5,1},{6,2},{7,3},{8,12},{9,13},{10,... | collective-permute-start | bytes 24584 | tf_op jit(solution)/shard_map/ppermute | solution.py:20
  184.9 52.1 %collective-permute-start.10 = (bf16[768,768]{1,0:T(8,128)(2,1)}, bf16[768,768]{1,0:T(8,128)(2,1)S(1)}, u32[]{:S(2)}, u32[]{:S(2)}) collective-permute-start(bf16[768,768]{1,0:T(8,128)(2,1)} %shard_map.60), channel_id=1, source_target_pairs={{0,4},{2,2},{4,8},{6,6},{8,12},{10,10},{12,0},{14,14},{16,20},{18,... | collective-permute-start | bytes 3538952 | tf_op jit(solution)/shard_map/ppermute | solution.py:20
  188.8 48.2 %collective-permute-start.9 = (bf16[768,768]{1,0:T(8,128)(2,1)}, bf16[768,768]{1,0:T(8,128)(2,1)}, u32[]{:S(2)}, u32[]{:S(2)}) collective-permute-start(bf16[768,768]{1,0:T(8,128)(2,1)} %shard_map.60), channel_id=1, source_target_pairs={{1,2},{3,0},{5,6},{7,4},{9,10},{11,8},{13,14},{15,12},{17,18},{19,... | collective-permute-start | bytes 3538952 | tf_op jit(solution)/shard_map/ppermute | solution.py:20
  190.2 3.7 %collective-permute-start.19 = (f32[8,128]{1,0:T(8,128)S(1)}, f32[8,128]{1,0:T(8,128)S(1)}, u32[]{:S(2)}, u32[]{:S(2)}) collective-permute-start(f32[8,128]{1,0:T(8,128)S(1)} %constant_dynamic-slice_fusion.2), channel_id=1, source_target_pairs={{0,2},{1,3},{2,0},{3,1},{4,6},{5,7},{6,4},{7,5},{8,10},{9,11},{10,... | collective-permute-start | bytes 12296 | tf_op jit(solution)/shard_map/ppermute | solution.py:20
  190.2 42.8 %collective-permute-start.12 = (bf16[256,1280]{1,0:T(8,128)(2,1)}, bf16[256,1280]{1,0:T(8,128)(2,1)S(1)}, u32[]{:S(2)}, u32[]{:S(2)}) collective-permute-start(bf16[256,1280]{1,0:T(8,128)(2,1)} %get-tuple-element.28), channel_id=1, source_target_pairs={{0,2},{1,3},{2,0},{3,1},{4,6},{5,7},{6,4},{7,5},{8,10},{9,11},{10,... | collective-permute-start | bytes 1966088 | tf_op jit(solution)/shard_map/ppermute | solution.py:20
  193.8 39.3 %collective-permute-start.14 = (bf16[256,1280]{1,0:T(8,128)(2,1)}, bf16[256,1280]{1,0:T(8,128)(2,1)S(1)}, u32[]{:S(2)}, u32[]{:S(2)}) collective-permute-start(bf16[256,1280]{1,0:T(8,128)(2,1)} %get-tuple-element.31), channel_id=1, source_target_pairs={{0,4},{1,5},{2,2},{3,3},{4,8},{5,9},{6,6},{7,7},{8,12},{9,13},{10,... | collective-permute-start | bytes 1966088 | tf_op jit(solution)/shard_map/ppermute | solution.py:20
  196.6 21.1 %collective-permute-start.13 = (bf16[512,512]{1,0:T(8,128)(2,1)}, bf16[512,512]{1,0:T(8,128)(2,1)}, u32[]{:S(2)}, u32[]{:S(2)}) collective-permute-start(bf16[512,512]{1,0:T(8,128)(2,1)} %get-tuple-element.30), channel_id=1, source_target_pairs={{0,4},{1,5},{2,2},{3,3},{4,8},{5,9},{6,6},{7,7},{8,12},{9,13},{10,... | collective-permute-start | bytes 1572872 | tf_op jit(solution)/shard_map/ppermute | solution.py:20
  217.8 18.7 %collective-permute-start.20 = (f32[4,128]{1,0:T(4,128)S(1)}, f32[4,128]{1,0:T(4,128)S(1)}, u32[]{:S(2)}, u32[]{:S(2)}) collective-permute-start(f32[4,128]{1,0:T(4,128)S(1)} %constant_dynamic-slice_fusion), channel_id=1, source_target_pairs={{0,1},{1,0},{2,3},{3,2},{4,5},{5,4},{6,7},{7,6},{8,9},{9,8},{10,11... | collective-permute-start | bytes 6152 | tf_op jit(solution)/shard_map/ppermute | solution.py:20
  236.4 7.4 %collective-permute-start.16 = (f32[768]{0:T(1024)S(1)}, f32[768]{0:T(1024)S(1)}, u32[]{:S(2)}, u32[]{:S(2)}) collective-permute-start(f32[768]{0:T(1024)S(1)} %reduce.2), channel_id=1, source_target_pairs={{0,14},{1,15},{2,0},{3,1},{4,2},{5,3},{6,4},{7,5},{8,6},{9,7},{10,... | collective-permute-start | bytes 9224 | tf_op jit(solution)/shard_map/ppermute | solution.py:20
  237.0 1.7 copy-start
  242.9 2.2 collective-permute-start.15

commit v3 on v2

--- a/solution.py
+++ b/solution.py
@@ -199,6 +199,35 @@
     )(place, own, near1, near2, other1, other2)
 
 
+def copy_kernel(place, *refs):
+    del place
+    count = len(refs) // 2
+    for source, target in zip(refs[:count], refs[count:]):
+        target[...] = source[...]
+
+
+def halves(place, own, start, count, sides):
+    half = own.shape[1] // 2
+    tall = 64
+    first = start // tall
+
+    def source(side):
+        return pl.BlockSpec((tall, half), lambda i, place: (first + i, (place[0] + side) % 2))
+
+    return pl.pallas_call(
+        copy_kernel,
+        grid_spec=pltpu.PrefetchScalarGridSpec(
+            num_scalar_prefetch=1,
+            grid=(count // tall,),
+            in_specs=[source(side) for side in sides],
+            out_specs=[pl.BlockSpec((tall, half), lambda i, place: (i, 0)) for _ in sides],
+        ),
+        out_shape=[jax.ShapeDtypeStruct((count, half), own.dtype) for _ in sides],
+        compiler_params=params(),
+        cost_estimate=cost(0, 4 * count * half * len(sides)),
+    )(place, *([own] * len(sides)))
+
+
 def finish(tile, row_mass, column_mass):
     @pl.when(pl.program_id(0) == 0)
     def _():
@@ -263,7 +292,7 @@
         out_specs=[pl.BlockSpec((1, late, rows), lambda j: (1, j, 0))] + mass_specs,
         out_shape=[jax.ShapeDtypeStruct((2, rows, rows), jnp.float32)] + mass_types,
         compiler_params=params(),
-        cost_estimate=cost(8 * rows * rows, 160 * rows * rows),
+        cost_estimate=cost(60000 * rows * rows, 160 * rows * rows),
     )(u1, u2, u2, v1, v2, v2, inverse[:, None], behind[None, :])
 
 
@@ -302,20 +331,6 @@
     )(place, y, z, local, inverse[:, None], behind[None, :], gram)
 
 
-def scatter_sum(value, index, size, waits):
-    bit = size // 2
-    for wait in waits:
-        half = value.shape[0] // 2
-        mine = (index // bit) % 2
-        away = lax.dynamic_slice_in_dim(value, (1 - mine) * half, half)
-        kept = lax.dynamic_slice_in_dim(value, mine * half, half)
-        if wait is not None:
-            away = after(away, wait)
-        value = kept + send(away, [(i, i ^ bit) for i in range(size)])
-        bit //= 2
-    return value
-
-
 def local(sketches, test_sketches, domain_map):
     rows, depth = sketches.shape
     size = lax.axis_size("blocks")
@@ -331,22 +346,17 @@
     along = [(i, (i + (4 if i & 2 else -4)) % size) for i in blocks]
     swap = [(i, i ^ 1) for i in blocks]
 
-    def part(source, start, count, side):
-        return lax.dynamic_slice(source, (start, side * half), (count, half))
-
-    out1 = part(sketches, 0, early, 1 - upper)
+    even = send(sketches, swap)
+    (out1,) = halves(place, sketches, 0, early, (1,))
     partner1 = send(out1, across)
-    source = after(sketches, out1)
-    side1 = part(source, 0, early, upper)
+    (side1,) = halves(place, after(sketches, out1), 0, early, (0,))
     near1 = send(side1, along)
-    source = after(source, side1)
-    partner2 = send(part(source, early, LATE, 1 - upper), across)
-    near2 = send(part(source, early, LATE, upper), along)
-    even = send(sketches, [(i, i + 1) for i in blocks if i % 2 == 0])
+    out2, side2 = halves(place, after(sketches, side1), early, LATE, (1, 0))
+    partner2 = send(out2, across)
+    near2 = send(side2, along)
 
     inverse = inverse_norm(sketches)
-    behind1 = send(inverse, [(i, (i + 1) % size) for i in blocks])
-    behind2 = send(inverse, [(i, (i + 2) % size) for i in blocks])
+    inverses = lax.all_gather(inverse, "blocks")
     scale = 1.0 / math.sqrt(depth)
 
     test_inverse = inverse_norm(test_sketches)
@@ -361,24 +371,30 @@
     )
     inside = nt(sketches, even)
 
-    partner1 = after(partner1, inside, sums)
-    u1, v1 = early_tiles(place, sketches, partner1, near1)
-    other1 = send(partner1, swap)
-    partner2 = after(partner2, u1, behind1, behind2)
-    other2 = send(partner2, swap)
-    u2, v2 = late_tiles(place, sketches, partner1, partner2, near1, after(near2, u1))
-    x = cross_tile(place, sketches, near1, near2, other1, after(other2, u2))
+    grouped = jnp.pad(sums.reshape(size, DOM_DEV, -1), ((0, 0), (0, DOM_DEV), (0, 0)))
+    total = lax.psum_scatter(
+        grouped.reshape(2 * DOM_DEV * size, -1), "blocks", scatter_dimension=0, tiled=True
+    )
 
     back_v = [(i, i) if i & 2 else (i, (i + 4) % size) for i in blocks]
     back_y = [(i, i ^ 3) for i in blocks if i & 1]
     back_z = [pair for pair in back_v if pair[0] % 2 == 0]
+    partner1 = after(partner1, inside, sums)
+    u1, v1 = early_tiles(place, sketches, partner1, near1)
     u1r, v1r = send(u1, across), send(v1, back_v)
+    other1 = send(partner1, swap)
+    partner2, near2, inverses, total, _ = lax.optimization_barrier(
+        (partner2, near2, inverses, total, u1)
+    )
+    behind1 = lax.dynamic_index_in_dim(inverses, (index - 1) % size, 0, False)
+    behind2 = lax.dynamic_index_in_dim(inverses, (index - 2) % size, 0, False)
+    domain_scores = total[:DOM_DEV] * (1.0 / math.sqrt(rows / DOM_DEV))
+    other2 = send(partner2, swap)
+    u2, v2 = late_tiles(place, sketches, partner1, partner2, near1, near2)
     u2r, v2r = send(u2, across), send(v2, back_v)
+    other2 = lax.optimization_barrier((other2, u2, u1r, v1r))[0]
+    x = cross_tile(place, sketches, near1, near2, other1, other2)
     y, z = send(x, back_y), send(x, back_z)
-
-    bits = size.bit_length() - 1
-    waits = ([None, u1, u2, x] + [x] * bits)[:bits]
-    domain_scores = scatter_sum(sums, index, size, waits) * (1.0 / math.sqrt(rows / DOM_DEV))
 
     gram, row_mass2, column_mass2 = second_tiles(scale, u1r, u2r, v1r, v2r, inverse, behind2)
     gram, row_mass1, column_mass1 = first_tiles(

time: 247 us -> 294 us (1.19)
  blocking collectives: 0 us -> 70.3 us
  waiting for transfers between devices: 111 us -> 83.9 us
  Pallas kernels: 39 us -> 56.3 us
  starting transfers between devices: 46.5 us -> 29.5 us
  between operations: 0.89 us -> 14.9 us
  local copies, waits for them, and re-layouts: 15.9 us -> 2.48 us
    all_gather x0 -> x1, blocking collectives: none -> 70.3 us  [local(): inverses = lax.all_gather(inverse, 'blocks')]
    ppermute x21 -> x15, waiting for transfers between devices: 111 us -> 55.3 us  [send(): return lax.ppermute(value, 'blocks', pairs)]
    unnamed x0 -> x2, waiting for transfers between devices: none -> 28.6 us
    pallas_call x0 -> x3, Pallas kernels: none -> 19.7 us  [halves(): pl.pallas_call(copy_kernel, grid_spec=pltpu.PrefetchScalarGridSpec(num_sc...]
    ppermute x21 -> x15, starting transfers between devices: 46.5 us -> 29.5 us  [send(): return lax.ppermute(value, 'blocks', pairs)]
    dynamic_slice x7 -> x1, local copies, waits for them, and re-layouts: 14.1 us -> 0.02 us  [local(): behind2 = lax.dynamic_index_in_dim(inverses, (index - 2) % size, 0, False)]
  transfers between devices with their start and end apart: 21 -> 16, of which waited for: 7 -> 6; matrix products, arithmetic and copies ran while one was open for 19% -> 12% of each run, Pallas kernels for 16% -> 19%
where the time goes in v3:
time: 294 us; the launch traced here: 290 us
  waiting for transfers between devices  83.9 us (29%)
  blocking collectives  70.3 us (24%)
  Pallas kernels  56.3 us (19%)
  starting transfers between devices  29.5 us (10%)
  matrix products  23.7 us (8%)
  between operations  14.9 us (5%)
  other arithmetic  8.91 us (3%)
    all_gather x1, blocking collectives, local(): inverses = lax.all_gather(inverse, 'blocks')  70.3 us
    ppermute x15, waiting for transfers between devices, send(): return lax.ppermute(value, 'blocks', pairs)  55.3 us
    ppermute x15, starting transfers between devices, send(): return lax.ppermute(value, 'blocks', pairs)  29.5 us
    unnamed x2, waiting for transfers between devices  28.6 us
    pallas_call x3, Pallas kernels, halves(): pl.pallas_call(copy_kernel, grid_spec=pltpu.PrefetchScalarGridSpec(num_sc...  19.7 us
    dot_general x1, matrix products, nt(): return lax.dot_general(left, right, NT, preferred_element_type=jnp.float32)  16.2 us
    pallas_call x1, Pallas kernels, cross_tile(): pl.pallas_call(cross_kernel, grid_spec=pltpu.PrefetchScalarGridSpec(num_s...  10.8 us
    pallas_call x1, Pallas kernels, late_tiles(): pl.pallas_call(late_kernel, grid_spec=pltpu.PrefetchScalarGridSpec(num_sc...  10.2 us
  transfers between devices with their start and end apart: 16, of which 6 were waited for; matrix products, arithmetic and copies ran while one was open for 12% of the time, Pallas kernels for 19%

profile of v3, /device:TPU:0, one launch (start us, length us, event | category | flops | bytes accessed | tf_op | source)
XLA Modules:
  0.0 290.0 jit_solution(2657586449693305046)
XLA Ops:
  7.8 7.2 %shard_map.58 = bf16[512,4096]{1,0:T(8,128)(2,1)} custom-call(s32[2]{0:T(128)S(1)} %pad_add_fusion.place, bf16[768,8192]{1,0:T(8,128)(2,1)} %own.3), custom_call_target="tpu_custom_call" | custom-call | bytes 8388608 | tf_op jit(solution)/shard_map/pallas_call | solution.py:217
  15.0 2.6 collective-permute-start.3
  17.6 7.1 %shard_map.59 = bf16[512,4096]{1,0:T(8,128)(2,1)} custom-call(s32[2]{0:T(128)S(1)} %pad_add_fusion.place, bf16[768,8192]{1,0:T(8,128)(2,1)} %own.3), custom_call_target="tpu_custom_call" | custom-call | bytes 8388608 | tf_op jit(solution)/shard_map/pallas_call | solution.py:217
  24.7 3.6 %collective-permute-start = (bf16[512,4096]{1,0:T(8,128)(2,1)}, bf16[512,4096]{1,0:T(8,128)(2,1)}, u32[]{:S(2)}, u32[]{:S(2)}) collective-permute-start(bf16[512,4096]{1,0:T(8,128)(2,1)} %shard_map.59), channel_id=1, source_target_pairs={{0,12},{1,13},{2,6},{3,7},{4,0},{5,1},{6,10},{7,11},{8,4},{9,5},{1... | collective-permute-start | bytes 12582920 | tf_op jit(solution)/shard_map/ppermute | solution.py:20
  28.4 5.3 %shard_map.60 = (bf16[256,4096]{1,0:T(8,128)(2,1)}, bf16[256,4096]{1,0:T(8,128)(2,1)}) custom-call(s32[2]{0:T(128)S(1)} %pad_add_fusion.place, bf16[768,8192]{1,0:T(8,128)(2,1)} %own.3, bf16[768,8192]{1,0:T(8,128)(2,1)} %own.3), custom_call_target="tpu_custom_call" | custom-call | bytes 8388608 | tf_op jit(solution)/shard_map/pallas_call | solution.py:217
  34.8 7.1 %multiply_reduce_fusion = f32[768]{0:T(1024)S(1)} fusion(bf16[768,8192]{1,0:T(8,128)(2,1)} %own.3), kind=kLoop, calls=%fused_computation | loop fusion | flops 18873600 | bytes 12585984 | tf_op jit(solution)/shard_map/reduce_sum | solution.py:29
  41.9 7.5 %fusion.3 = f32[64,128]{1,0:T(8,128)S(1)} fusion(bf16[768,8192]{1,0:T(8,128)(2,1)} %own.3, bf16[128,8192]{1,0:T(8,128)(2,1)} %param.4, f32[128]{0:T(128)S(1)} %add_rsqrt_fusion.1, f32[768]{0:T(1024)S(1)} %add_rsqrt_fusion, s32[768]{0:T(1024)S(1)} %copy-done.3), kind=kOutput, calls=%fused_computation.6 | convolution fusion | flops 1623638016 | bytes 14719488 | tf_op jit(solution)/shard_map/dot_general | solution.py:369
  49.4 16.2 %fusion.9.local = f32[768,768]{1,0:T(8,128)} fusion(bf16[768,8192]{1,0:T(8,128)(2,1)} %own.3, bf16[768,8192]{1,0:T(8,128)(2,1)} %collective-permute-done.4), kind=kOutput, calls=%fused_computation.24 | convolution fusion | flops 9663676416 | bytes 27525120 | tf_op jit(solution)/shard_map/dot_general | solution.py:33
  65.7 43.7 %collective-permute-done.3.partner.partner1 = bf16[512,4096]{1,0:T(8,128)(2,1)} collective-permute-done((bf16[512,4096]{1,0:T(8,128)(2,1)}, bf16[512,4096]{1,0:T(8,128)(2,1)}, u32[]{:S(2)}, u32[]{:S(2)}) %collective-permute-start.3) | collective-permute-done | bytes 4194336 | tf_op jit(solution)/shard_map/ppermute | solution.py:20
  110.0 70.3 %all-gather.1 = f32[16,1,768]{2,1,0:T(1,128)S(1)} all-gather(f32[1,1,768]{2,1,0:T(1,128)S(1)} %reshape.58), channel_id=2, replica_groups=mesh['groups'=2,'blocks'=16] {'blocks'}, dimensions={0}, use_global_device_ids=true | all-gather | bytes 52224 | tf_op jit(solution)/shard_map/all_gather | solution.py:359
  181.5 28.6 %all-reduce.4.cloned.1.call-done = f32[128,128]{1,0:T(8,128)} async-done(((f32[128,128]{1,0:T(8,128)}), f32[128,128]{1,0:T(8,128)}) %all-reduce.4.cloned.1.call-update) | async-done | bytes 65552
  210.8 8.6 %shard_map.61 = (bf16[512,512]{1,0:T(8,128)(2,1)S(1)}, bf16[512,512]{1,0:T(8,128)(2,1)S(1)}) custom-call(s32[2]{0:T(128)S(1)} %pad_add_fusion.place, bf16[768,8192]{1,0:T(8,128)(2,1)} %own.3, bf16[512,4096]{1,0:T(8,128)(2,1)} %collective-permute-done.3.partner.partner1, bf16[512,4096]{1,0:T(8,128)(2,1)} %collective-permute-done.near.near1), custom_call_target="tpu_custom_call" | custom-call | flops 512 | bytes 512 | tf_op jit(solution)/shard_map/pallas_call | solution.py:80
  221.4 5.6 %collective-permute-start.8 = (bf16[512,512]{1,0:T(8,128)(2,1)S(1)}, bf16[512,512]{1,0:T(8,128)(2,1)S(1)}, u32[]{:S(2)}, u32[]{:S(2)}) collective-permute-start(bf16[512,512]{1,0:T(8,128)(2,1)S(1)} %get-tuple-element.32), channel_id=1, source_target_pairs={{0,4},{1,5},{2,2},{3,3},{4,8},{5,9},{6,6},{7,7},{8,12},{9,13},{10,... | collective-permute-start | bytes 1572872 | tf_op jit(solution)/shard_map/ppermute | solution.py:20
  226.9 10.2 %shard_map.62 = (bf16[256,1280]{1,0:T(8,128)(2,1)S(1)}, bf16[256,1280]{1,0:T(8,128)(2,1)S(1)}) custom-call(s32[2]{0:T(128)S(1)} %pad_add_fusion.place, bf16[768,8192]{1,0:T(8,128)(2,1)} %own.3, bf16[768,8192]{1,0:T(8,128)(2,1)} %own.3, bf16[512,4096]{1,0:T(8,128)(2,1)} %collective-permute-done.3.partner.partner1, ...), custom_call_target="tpu_custom_call" | custom-call | flops 5368709120 | bytes 18874368 | tf_op jit(solution)/shard_map/pallas_call | solution.py:139
  237.3 2.9 %collective-permute-start.12 = (bf16[256,1280]{1,0:T(8,128)(2,1)S(1)}, bf16[256,1280]{1,0:T(8,128)(2,1)S(1)}, u32[]{:S(2)}, u32[]{:S(2)}) collective-permute-start(bf16[256,1280]{1,0:T(8,128)(2,1)S(1)} %get-tuple-element.35), channel_id=1, source_target_pairs={{0,4},{1,5},{2,2},{3,3},{4,8},{5,9},{6,6},{7,7},{8,12},{9,13},{10,... | collective-permute-start | bytes 1966088 | tf_op jit(solution)/shard_map/ppermute | solution.py:20
  240.8 10.8 %shard_map.63 = bf16[768,768]{1,0:T(8,128)(2,1)} custom-call(s32[2]{0:T(128)S(1)} %pad_add_fusion.place, bf16[768,8192]{1,0:T(8,128)(2,1)} %own.3, bf16[512,4096]{1,0:T(8,128)(2,1)} %collective-permute-done.near.near1, bf16[256,4096]{1,0:T(8,128)(2,1)S(1)} %collective-permute-done.2.near2, bf16[512,4096]{1,0:T(8,128)(2,1)} %collective-permute-done.5.other1, ...), custom_call_target="tpu_custom_call" | custom-call | flops 4831838208 | bytes 18874368 | tf_op jit(solution)/shard_map/pallas_call | solution.py:187
  251.6 2.9 collective-permute-start.10
  254.5 1.3 collective-permute-start.9
  256.9 2.4 shard_map.64
  259.3 6.5 %collective-permute-start.14 = (f32[768]{0:T(1024)S(1)}, f32[768]{0:T(1024)S(1)}, u32[]{:S(2)}, u32[]{:S(2)}) collective-permute-start(f32[768]{0:T(1024)S(1)} %reduce.2), channel_id=1, source_target_pairs={{0,14},{1,15},{2,0},{3,1},{4,2},{5,3},{6,4},{7,5},{8,6},{9,7},{10,... | collective-permute-start | bytes 9224 | tf_op jit(solution)/shard_map/ppermute | solution.py:20
  265.8 6.1 %collective-permute-done.10.z = bf16[768,768]{1,0:T(8,128)(2,1)} collective-permute-done((bf16[768,768]{1,0:T(8,128)(2,1)}, bf16[768,768]{1,0:T(8,128)(2,1)}, u32[]{:S(2)}, u32[]{:S(2)}) %collective-permute-start.10) | collective-permute-done | bytes 1179680 | tf_op jit(solution)/shard_map/ppermute | solution.py:20
  272.3 4.6 %shard_map.65 = (f32[2,768,768]{2,1,0:T(8,128)}, f32[1,768]{1,0:T(1,128)S(1)}, f32[1,768]{1,0:T(1,128)S(1)}) custom-call(s32[2]{0:T(128)S(1)} %pad_add_fusion.place, bf16[768,768]{1,0:T(8,128)(2,1)} %collective-permute-done.9.y, bf16[768,768]{1,0:T(8,128)(2,1)} %collective-permute-done.10.z, ...), custom_call_target="tpu_custom_call", output_to_operand_aliasing={{0}: (6, {})} | custom-call | flops 4718592 | bytes 7077888 | tf_op jit(solution)/shard_map/pallas_call | solution.py:314
  276.9 1.6 collective-permute-start.13
  278.6 3.9 %collective-permute-done.13 = f32[768]{0:T(1024)S(1)} collective-permute-done((f32[768]{0:T(1024)S(1)}, f32[768]{0:T(1024)S(1)}, u32[]{:S(2)}, u32[]{:S(2)}) %collective-permute-start.13) | collective-permute-done | bytes 3104 | tf_op jit(solution)/shard_map/ppermute | solution.py:20
  (47 shorter events, 8.5 us)
Async XLA Ops:
  7.2 202.9 %all-reduce.4.cloned.1.call-start = ((), (), s32[]{:S(2)}) async-start(), calls=%async_computation | async-start | bytes 131072
  7.2 42.2 %collective-permute-start.4 = (bf16[768,8192]{1,0:T(8,128)(2,1)}, bf16[768,8192]{1,0:T(8,128)(2,1)}, u32[]{:S(2)}, u32[]{:S(2)}) collective-permute-start(bf16[768,8192]{1,0:T(8,128)(2,1)} %own.3), channel_id=1, source_target_pairs={{0,1},{1,0},{2,3},{3,2},{4,5},{5,4},{6,7},{7,6},{8,9},{9,8},{10,11... | collective-permute-start | bytes 37748744 | tf_op jit(solution)/shard_map/ppermute | solution.py:20
  15.0 94.3 %collective-permute-start.3 = (bf16[512,4096]{1,0:T(8,128)(2,1)}, bf16[512,4096]{1,0:T(8,128)(2,1)}, u32[]{:S(2)}, u32[]{:S(2)}) collective-permute-start(bf16[512,4096]{1,0:T(8,128)(2,1)} %shard_map.58), channel_id=1, source_target_pairs={{0,2},{1,3},{2,0},{3,1},{4,6},{5,7},{6,4},{7,5},{8,10},{9,11},{10,... | collective-permute-start | bytes 12582920 | tf_op jit(solution)/shard_map/ppermute | solution.py:20
  24.7 9.5 %copy-start.2 = (bf16[128,8192]{1,0:T(8,128)(2,1)S(1)}, bf16[128,8192]{1,0:T(8,128)(2,1)}, u32[]{:S(2)}) copy-start(bf16[128,8192]{1,0:T(8,128)(2,1)} %param.4) | copy-start | bytes 6291460
  24.7 186.0 %collective-permute-start = (bf16[512,4096]{1,0:T(8,128)(2,1)}, bf16[512,4096]{1,0:T(8,128)(2,1)}, u32[]{:S(2)}, u32[]{:S(2)}) collective-permute-start(bf16[512,4096]{1,0:T(8,128)(2,1)} %shard_map.59), channel_id=1, source_target_pairs={{0,12},{1,13},{2,6},{3,7},{4,0},{5,1},{6,10},{7,11},{8,4},{9,5},{1... | collective-permute-start | bytes 12582920 | tf_op jit(solution)/shard_map/ppermute | solution.py:20
  33.7 185.7 %collective-permute-start.1 = (bf16[256,4096]{1,0:T(8,128)(2,1)}, bf16[256,4096]{1,0:T(8,128)(2,1)}, u32[]{:S(2)}, u32[]{:S(2)}) collective-permute-start(bf16[256,4096]{1,0:T(8,128)(2,1)} %get-tuple-element.25), channel_id=1, source_target_pairs={{0,2},{1,3},{2,0},{3,1},{4,6},{5,7},{6,4},{7,5},{8,10},{9,11},{10,... | collective-permute-start | bytes 6291464 | tf_op jit(solution)/shard_map/ppermute | solution.py:20
  33.7 185.7 %collective-permute-start.2 = (bf16[256,4096]{1,0:T(8,128)(2,1)}, bf16[256,4096]{1,0:T(8,128)(2,1)S(1)}, u32[]{:S(2)}, u32[]{:S(2)}) collective-permute-start(bf16[256,4096]{1,0:T(8,128)(2,1)} %get-tuple-element.26), channel_id=1, source_target_pairs={{0,12},{1,13},{2,6},{3,7},{4,0},{5,1},{6,10},{7,11},{8,4},{9,5},{1... | collective-permute-start | bytes 6291464 | tf_op jit(solution)/shard_map/ppermute | solution.py:20
  34.7 7.1 %copy-start.3 = (s32[768]{0:T(1024)S(1)}, s32[768]{0:T(1024)}, u32[]{:S(2)}) copy-start(s32[768]{0:T(1024)} %param.5) | copy-start | bytes 9220
  49.4 130.9 %copy-start.4 = (u32[32]{0:T(128)S(1)}, u32[32]{0:T(128)}, u32[]{:S(2)}) copy-start(u32[32]{0:T(128)} %constant.79) | copy-start | bytes 388
  109.3 131.5 %collective-permute-start.5 = (bf16[512,4096]{1,0:T(8,128)(2,1)}, bf16[512,4096]{1,0:T(8,128)(2,1)}, u32[]{:S(2)}, u32[]{:S(2)}) collective-permute-start(bf16[512,4096]{1,0:T(8,128)(2,1)} %collective-permute-done.3.partner.partner1), channel_id=1, source_target_pairs={{0,1},{1,0},{2,3},{3,2},{4,5},{5,4},{6,7},{7,6},{8,9},{9,8},{10,11... | collective-permute-start | bytes 12582920 | tf_op jit(solution)/shard_map/ppermute | solution.py:20
  219.4 0.8 copy-start.1
  219.4 21.4 %collective-permute-start.6 = (bf16[256,4096]{1,0:T(8,128)(2,1)}, bf16[256,4096]{1,0:T(8,128)(2,1)}, u32[]{:S(2)}, u32[]{:S(2)}) collective-permute-start(bf16[256,4096]{1,0:T(8,128)(2,1)} %collective-permute-done.1.partner2), channel_id=1, source_target_pairs={{0,1},{1,0},{2,3},{3,2},{4,5},{5,4},{6,7},{7,6},{8,9},{9,8},{10,11... | collective-permute-start | bytes 6291464 | tf_op jit(solution)/shard_map/ppermute | solution.py:20
  220.4 16.9 %collective-permute-start.7 = (bf16[512,512]{1,0:T(8,128)(2,1)}, bf16[512,512]{1,0:T(8,128)(2,1)S(1)}, u32[]{:S(2)}, u32[]{:S(2)}) collective-permute-start(bf16[512,512]{1,0:T(8,128)(2,1)} %copy-done.1), channel_id=1, source_target_pairs={{0,2},{1,3},{2,0},{3,1},{4,6},{5,7},{6,4},{7,5},{8,10},{9,11},{10,... | collective-permute-start | bytes 1572872 | tf_op jit(solution)/shard_map/ppermute | solution.py:20
  221.4 19.4 %collective-permute-start.8 = (bf16[512,512]{1,0:T(8,128)(2,1)S(1)}, bf16[512,512]{1,0:T(8,128)(2,1)S(1)}, u32[]{:S(2)}, u32[]{:S(2)}) collective-permute-start(bf16[512,512]{1,0:T(8,128)(2,1)S(1)} %get-tuple-element.32), channel_id=1, source_target_pairs={{0,4},{1,5},{2,2},{3,3},{4,8},{5,9},{6,6},{7,7},{8,12},{9,13},{10,... | collective-permute-start | bytes 1572872 | tf_op jit(solution)/shard_map/ppermute | solution.py:20
  237.2 18.6 %collective-permute-start.11 = (bf16[256,1280]{1,0:T(8,128)(2,1)S(1)}, bf16[256,1280]{1,0:T(8,128)(2,1)S(1)}, u32[]{:S(2)}, u32[]{:S(2)}) collective-permute-start(bf16[256,1280]{1,0:T(8,128)(2,1)S(1)} %get-tuple-element.31), channel_id=1, source_target_pairs={{0,2},{1,3},{2,0},{3,1},{4,6},{5,7},{6,4},{7,5},{8,10},{9,11},{10,... | collective-permute-start | bytes 1966088 | tf_op jit(solution)/shard_map/ppermute | solution.py:20
  237.3 19.6 %collective-permute-start.12 = (bf16[256,1280]{1,0:T(8,128)(2,1)S(1)}, bf16[256,1280]{1,0:T(8,128)(2,1)S(1)}, u32[]{:S(2)}, u32[]{:S(2)}) collective-permute-start(bf16[256,1280]{1,0:T(8,128)(2,1)S(1)} %get-tuple-element.35), channel_id=1, source_target_pairs={{0,4},{1,5},{2,2},{3,3},{4,8},{5,9},{6,6},{7,7},{8,12},{9,13},{10,... | collective-permute-start | bytes 1966088 | tf_op jit(solution)/shard_map/ppermute | solution.py:20
  251.6 20.3 %collective-permute-start.10 = (bf16[768,768]{1,0:T(8,128)(2,1)}, bf16[768,768]{1,0:T(8,128)(2,1)}, u32[]{:S(2)}, u32[]{:S(2)}) collective-permute-start(bf16[768,768]{1,0:T(8,128)(2,1)} %shard_map.63), channel_id=1, source_target_pairs={{0,4},{2,2},{4,8},{6,6},{8,12},{10,10},{12,0},{14,14},{16,20},{18,... | collective-permute-start | bytes 3538952 | tf_op jit(solution)/shard_map/ppermute | solution.py:20
  254.5 17.9 %collective-permute-start.9 = (bf16[768,768]{1,0:T(8,128)(2,1)}, bf16[768,768]{1,0:T(8,128)(2,1)}, u32[]{:S(2)}, u32[]{:S(2)}) collective-permute-start(bf16[768,768]{1,0:T(8,128)(2,1)} %shard_map.63), channel_id=1, source_target_pairs={{1,2},{3,0},{5,6},{7,4},{9,10},{11,8},{13,14},{15,12},{17,18},{19,... | collective-permute-start | bytes 3538952 | tf_op jit(solution)/shard_map/ppermute | solution.py:20
  256.9 15.5 %copy-start = (f32[768,768]{1,0:T(8,128)S(1)}, f32[768,768]{1,0:T(8,128)}, u32[]{:S(2)}) copy-start(f32[768,768]{1,0:T(8,128)} %fusion.9.local) | copy-start | bytes 7077892
  259.3 19.3 %collective-permute-start.14 = (f32[768]{0:T(1024)S(1)}, f32[768]{0:T(1024)S(1)}, u32[]{:S(2)}, u32[]{:S(2)}) collective-permute-start(f32[768]{0:T(1024)S(1)} %reduce.2), channel_id=1, source_target_pairs={{0,14},{1,15},{2,0},{3,1},{4,2},{5,3},{6,4},{7,5},{8,6},{9,7},{10,... | collective-permute-start | bytes 9224 | tf_op jit(solution)/shard_map/ppermute | solution.py:20
  276.9 5.6 %collective-permute-start.13 = (f32[768]{0:T(1024)S(1)}, f32[768]{0:T(1024)S(1)}, u32[]{:S(2)}, u32[]{:S(2)}) collective-permute-start(f32[768]{0:T(1024)S(1)} %reduce.1), channel_id=1, source_target_pairs={{0,15},{1,0},{2,1},{3,2},{4,3},{5,4},{6,5},{7,6},{8,7},{9,8},{10,9... | collective-permute-start | bytes 9224 | tf_op jit(solution)/shard_map/ppermute | solution.py:20
Sparse Core Ops, SparseCore 0:
  110.1 99.9 all-reduce.3

commit v4 on v3

--- a/solution.py
+++ b/solution.py
@@ -13,7 +13,8 @@
 LATE = 256
 DEPTH = 1024
 NT = (((1,), (1,)), ((), ()))
-VMEM_LIMIT = 48 * 2**20
+VMEM_LIMIT = 52 * 2**20
+PIECES = 4
 
 
 def send(value, pairs):
@@ -199,33 +200,39 @@
     )(place, own, near1, near2, other1, other2)
 
 
-def copy_kernel(place, *refs):
-    del place
-    count = len(refs) // 2
-    for source, target in zip(refs[:count], refs[count:]):
-        target[...] = source[...]
+def halves_kernel(start, sides, place, own, *rest):
+    outs, sems = rest[: len(sides)], rest[len(sides)]
+    copies = []
+    for number, (side, out) in enumerate(zip(sides, outs)):
+        count, half = out.shape
+        left = pl.multiple_of(((place[0] + side) % 2) * half, half)
+        piece = count // PIECES
+        for i in range(PIECES):
+            copies.append(
+                pltpu.make_async_copy(
+                    own.at[pl.ds(start + i * piece, piece), pl.ds(left, half)],
+                    out.at[pl.ds(i * piece, piece)],
+                    sems.at[number * PIECES + i],
+                )
+            )
+    for copy in copies:
+        copy.start()
+    for copy in copies:
+        copy.wait()
 
 
 def halves(place, own, start, count, sides):
     half = own.shape[1] // 2
-    tall = 64
-    first = start // tall
-
-    def source(side):
-        return pl.BlockSpec((tall, half), lambda i, place: (first + i, (place[0] + side) % 2))
-
-    return pl.pallas_call(
-        copy_kernel,
-        grid_spec=pltpu.PrefetchScalarGridSpec(
-            num_scalar_prefetch=1,
-            grid=(count // tall,),
-            in_specs=[source(side) for side in sides],
-            out_specs=[pl.BlockSpec((tall, half), lambda i, place: (i, 0)) for _ in sides],
-        ),
+    anywhere = pl.BlockSpec(memory_space=pltpu.HBM)
+    return pl.pallas_call(
+        functools.partial(halves_kernel, start, sides),
+        in_specs=[pl.BlockSpec(memory_space=pltpu.SMEM), anywhere],
+        out_specs=[anywhere] * len(sides),
         out_shape=[jax.ShapeDtypeStruct((count, half), own.dtype) for _ in sides],
+        scratch_shapes=[pltpu.SemaphoreType.DMA((PIECES * len(sides),))],
         compiler_params=params(),
         cost_estimate=cost(0, 4 * count * half * len(sides)),
-    )(place, *([own] * len(sides)))
+    )(place, own)
 
 
 def finish(tile, row_mass, column_mass):
@@ -356,7 +363,6 @@
     near2 = send(side2, along)
 
     inverse = inverse_norm(sketches)
-    inverses = lax.all_gather(inverse, "blocks")
     scale = 1.0 / math.sqrt(depth)
 
     test_inverse = inverse_norm(test_sketches)
@@ -371,11 +377,15 @@
     )
     inside = nt(sketches, even)
 
-    grouped = jnp.pad(sums.reshape(size, DOM_DEV, -1), ((0, 0), (0, DOM_DEV), (0, 0)))
-    total = lax.psum_scatter(
-        grouped.reshape(2 * DOM_DEV * size, -1), "blocks", scatter_dimension=0, tiled=True
-    )
-
+
+    def halve(value, bit, *waits):
+        count = value.shape[0] // 2
+        mine = (index // bit) % 2
+        away = lax.dynamic_slice_in_dim(value, (1 - mine) * count, count)
+        kept = lax.dynamic_slice_in_dim(value, mine * count, count)
+        return kept, send(after(away, *waits), [(i, i ^ bit) for i in blocks])
+
+    bits = [size >> (step + 1) for step in range(size.bit_length() - 1)]
     back_v = [(i, i) if i & 2 else (i, (i + 4) % size) for i in blocks]
     back_y = [(i, i ^ 3) for i in blocks if i & 1]
     back_z = [pair for pair in back_v if pair[0] % 2 == 0]
@@ -383,23 +393,33 @@
     u1, v1 = early_tiles(place, sketches, partner1, near1)
     u1r, v1r = send(u1, across), send(v1, back_v)
     other1 = send(partner1, swap)
-    partner2, near2, inverses, total, _ = lax.optimization_barrier(
-        (partner2, near2, inverses, total, u1)
+    behind1 = send(after(inverse, partner1), [(i, (i + 1) % size) for i in blocks])
+    behind2 = send(after(inverse, partner1), [(i, (i + 2) % size) for i in blocks])
+    partner2, near2, behind1, behind2, _ = lax.optimization_barrier(
+        (partner2, near2, behind1, behind2, u1)
     )
-    behind1 = lax.dynamic_index_in_dim(inverses, (index - 1) % size, 0, False)
-    behind2 = lax.dynamic_index_in_dim(inverses, (index - 2) % size, 0, False)
-    domain_scores = total[:DOM_DEV] * (1.0 / math.sqrt(rows / DOM_DEV))
     other2 = send(partner2, swap)
+    for bit in bits[:-4]:
+        kept, came = halve(sums, bit, partner2)
+        sums = kept + came
+    kept, came = halve(sums, bits[-4], partner2)
     u2, v2 = late_tiles(place, sketches, partner1, partner2, near1, near2)
     u2r, v2r = send(u2, across), send(v2, back_v)
-    other2 = lax.optimization_barrier((other2, u2, u1r, v1r))[0]
+    sums = kept + came
+    other2, sums, _, _, _ = lax.optimization_barrier((other2, sums, u2, u1r, v1r))
+    kept, came = halve(sums, bits[-3], u2)
     x = cross_tile(place, sketches, near1, near2, other1, other2)
     y, z = send(x, back_y), send(x, back_z)
+    sums = kept + came
 
     gram, row_mass2, column_mass2 = second_tiles(scale, u1r, u2r, v1r, v2r, inverse, behind2)
+    kept, came = halve(sums, bits[-2], row_mass2)
+    y, sums = lax.optimization_barrier((y, kept + came))
     gram, row_mass1, column_mass1 = first_tiles(
         scale, place, y, z, inside, inverse, behind1, gram, LATE
     )
+    kept, came = halve(sums, bits[-1], row_mass1)
+    domain_scores = (kept + came) * (1.0 / math.sqrt(rows / DOM_DEV))
     mass = (
         row_mass1[0]
         + row_mass2[0]

time: 294 us -> 507 us (1.72)
  Pallas kernels: 56.3 us -> 424 us
  blocking collectives: 70.3 us -> 0 us
  waiting for transfers between devices: 83.9 us -> 23 us
  between operations: 14.9 us -> 0.99 us
  starting transfers between devices: 29.5 us -> 23.3 us
    pallas_call x3, Pallas kernels: 19.7 us -> 386 us  [halves(): pl.pallas_call(functools.partial(halves_kernel, start, sides), in_specs=[...]
    all_gather x1 -> x0, blocking collectives: 70.3 us -> none  [local(): inverses = lax.all_gather(inverse, 'blocks')]
    ppermute x15 -> x21, waiting for transfers between devices: 55.3 us -> 23 us  [send(): return lax.ppermute(value, 'blocks', pairs)]
    unnamed x2 -> x0, waiting for transfers between devices: 28.6 us -> none
    ppermute x15 -> x21, starting transfers between devices: 29.5 us -> 23.3 us  [send(): return lax.ppermute(value, 'blocks', pairs)]
  transfers between devices with their start and end apart: 16 -> 21, of which waited for: 6 -> 9; matrix products, arithmetic and copies ran while one was open for 12% -> 6% of each run, Pallas kernels for 19% -> 84%
where the time goes in v4:
time: 507 us; the launch traced here: 505 us
  Pallas kernels  424 us (84%)
  starting transfers between devices  23.3 us (5%)
  matrix products  23.1 us (5%)
  waiting for transfers between devices  23 us (5%)
  other arithmetic  8.93 us (2%)
    pallas_call x3, Pallas kernels, halves(): pl.pallas_call(functools.partial(halves_kernel, start, sides), in_specs=[...  386 us
    ppermute x21, starting transfers between devices, send(): return lax.ppermute(value, 'blocks', pairs)  23.3 us
    ppermute x21, waiting for transfers between devices, send(): return lax.ppermute(value, 'blocks', pairs)  23 us
    dot_general x1, matrix products, nt(): return lax.dot_general(left, right, NT, preferred_element_type=jnp.float32)  16.2 us
    pallas_call x1, Pallas kernels, late_tiles(): pl.pallas_call(late_kernel, grid_spec=pltpu.PrefetchScalarGridSpec(num_sc...  10.5 us
  transfers between devices with their start and end apart: 21, of which 9 were waited for; matrix products, arithmetic and copies ran while one was open for 6% of the time, Pallas kernels for 84%

profile of v4, /device:TPU:0, one launch (start us, length us, event | category | flops | bytes accessed | tf_op | source)
XLA Modules:
  0.0 505.1 jit_solution(17041245968571359494)
XLA Ops:
  1.2 128.7 %shard_map.58 = bf16[512,4096]{1,0:T(8,128)(2,1)} custom-call(s32[2]{0:T(128)S(1)} %pad_add_fusion.place, bf16[768,8192]{1,0:T(8,128)(2,1)} %own.7), custom_call_target="tpu_custom_call" | custom-call | bytes 8388608 | tf_op jit(solution)/shard_map/pallas_call | solution.py:227
  130.0 2.6 collective-permute-start.3
  132.6 128.7 %shard_map.59 = bf16[512,4096]{1,0:T(8,128)(2,1)} custom-call(s32[2]{0:T(128)S(1)} %pad_add_fusion.place, bf16[768,8192]{1,0:T(8,128)(2,1)} %own.7), custom_call_target="tpu_custom_call" | custom-call | bytes 8388608 | tf_op jit(solution)/shard_map/pallas_call | solution.py:227
  261.4 3.7 collective-permute-start
  265.0 128.8 %shard_map.60 = (bf16[256,4096]{1,0:T(8,128)(2,1)}, bf16[256,4096]{1,0:T(8,128)(2,1)}) custom-call(s32[2]{0:T(128)S(1)} %pad_add_fusion.place, bf16[768,8192]{1,0:T(8,128)(2,1)} %own.7), custom_call_target="tpu_custom_call" | custom-call | bytes 8388608 | tf_op jit(solution)/shard_map/pallas_call | solution.py:227
  394.9 7.1 %multiply_reduce_fusion = f32[768]{0:T(1024)S(1)} fusion(bf16[768,8192]{1,0:T(8,128)(2,1)} %own.7), kind=kLoop, calls=%fused_computation | loop fusion | flops 18873600 | bytes 12585984 | tf_op jit(solution)/shard_map/reduce_sum | solution.py:30
  402.0 6.9 %fusion.3 = f32[64,128]{1,0:T(8,128)S(1)} fusion(bf16[768,8192]{1,0:T(8,128)(2,1)} %own.7, bf16[128,8192]{1,0:T(8,128)(2,1)S(1)} %copy-done, f32[128]{0:T(128)S(1)} %add_rsqrt_fusion.1, f32[768]{0:T(1024)S(1)} %add_rsqrt_fusion, s32[768]{0:T(1024)S(1)} %copy-done.3), kind=kOutput, calls=%fused_computation.6 | convolution fusion | flops 1623638016 | bytes 14719488 | tf_op jit(solution)/shard_map/dot_general | solution.py:375
  408.9 16.2 %fusion.9.local = f32[768,768]{1,0:T(8,128)} fusion(bf16[768,8192]{1,0:T(8,128)(2,1)} %own.7, bf16[768,8192]{1,0:T(8,128)(2,1)} %collective-permute-done.4), kind=kOutput, calls=%fused_computation.26 | convolution fusion | flops 9663676416 | bytes 27525120 | tf_op jit(solution)/shard_map/dot_general | solution.py:34
  425.7 1.5 collective-permute-start.6
  427.2 8.6 %shard_map.61 = (bf16[512,512]{1,0:T(8,128)(2,1)S(1)}, bf16[512,512]{1,0:T(8,128)(2,1)S(1)}) custom-call(s32[2]{0:T(128)S(1)} %pad_add_fusion.place, bf16[768,8192]{1,0:T(8,128)(2,1)} %own.7, bf16[512,4096]{1,0:T(8,128)(2,1)} %collective-permute-done.3.partner.partner1, bf16[512,4096]{1,0:T(8,128)(2,1)} %collective-permute-done.near.near1), custom_call_target="tpu_custom_call" | custom-call | flops 512 | bytes 512 | tf_op jit(solution)/shard_map/pallas_call | solution.py:81
  435.8 5.8 %collective-permute-done.1.partner2 = bf16[256,4096]{1,0:T(8,128)(2,1)} collective-permute-done((bf16[256,4096]{1,0:T(8,128)(2,1)}, bf16[256,4096]{1,0:T(8,128)(2,1)}, u32[]{:S(2)}, u32[]{:S(2)}) %collective-permute-start.1) | collective-permute-done | bytes 2097184 | tf_op jit(solution)/shard_map/ppermute | solution.py:21
  441.7 1.5 collective-permute-done.5
  443.2 1.4 collective-permute-done.6
  445.6 1.9 collective-permute-start.11
  447.7 10.5 %shard_map.62 = (bf16[256,1280]{1,0:T(8,128)(2,1)S(1)}, bf16[256,1280]{1,0:T(8,128)(2,1)S(1)}) custom-call(s32[2]{0:T(128)S(1)} %pad_add_fusion.place, bf16[768,8192]{1,0:T(8,128)(2,1)} %own.7, bf16[768,8192]{1,0:T(8,128)(2,1)} %own.7, bf16[512,4096]{1,0:T(8,128)(2,1)} %collective-permute-done.3.partner.partner1, ...), custom_call_target="tpu_custom_call" | custom-call | flops 5368709120 | bytes 18874368 | tf_op jit(solution)/shard_map/pallas_call | solution.py:140
  458.2 5.6 %collective-permute-done.9 = f32[32,128]{1,0:T(8,128)S(1)} collective-permute-done((f32[32,128]{1,0:T(8,128)S(1)}, f32[32,128]{1,0:T(8,128)S(1)}, u32[]{:S(2)}, u32[]{:S(2)}) %collective-permute-start.9) | collective-permute-done | bytes 16416 | tf_op jit(solution)/shard_map/ppermute | solution.py:21
  463.8 2.4 collective-permute-start.15
  466.3 10.1 %shard_map.63 = bf16[768,768]{1,0:T(8,128)(2,1)S(1)} custom-call(s32[2]{0:T(128)S(1)} %pad_add_fusion.place, bf16[768,8192]{1,0:T(8,128)(2,1)} %own.7, bf16[512,4096]{1,0:T(8,128)(2,1)} %collective-permute-done.near.near1, bf16[256,4096]{1,0:T(8,128)(2,1)} %collective-permute-done.2.near2, bf16[512,4096]{1,0:T(8,128)(2,1)} %collective-permute-done.7.other1, ...), custom_call_target="tpu_custom_call" | custom-call | flops 4831838208 | bytes 18874368 | tf_op jit(solution)/shard_map/pallas_call | solution.py:188
  477.7 3.9 collective-permute-start.17
  483.4 3.5 shard_map.64
  487.0 3.3 collective-permute-start.19
  490.7 3.3 collective-permute-done.12.y
  494.0 3.8 collective-permute-done.17.z
  497.8 4.9 shard_map.65
  (56 shorter events, 9.2 us)
Async XLA Ops:
  0.6 408.3 %collective-permute-start.4 = (bf16[768,8192]{1,0:T(8,128)(2,1)}, bf16[768,8192]{1,0:T(8,128)(2,1)}, u32[]{:S(2)}, u32[]{:S(2)}) collective-permute-start(bf16[768,8192]{1,0:T(8,128)(2,1)} %own.7), channel_id=1, source_target_pairs={{0,1},{1,0},{2,3},{3,2},{4,5},{5,4},{6,7},{7,6},{8,9},{9,8},{10,11... | collective-permute-start | bytes 37748744 | tf_op jit(solution)/shard_map/ppermute | solution.py:21
  130.0 295.2 %collective-permute-start.3 = (bf16[512,4096]{1,0:T(8,128)(2,1)}, bf16[512,4096]{1,0:T(8,128)(2,1)}, u32[]{:S(2)}, u32[]{:S(2)}) collective-permute-start(bf16[512,4096]{1,0:T(8,128)(2,1)} %shard_map.58), channel_id=1, source_target_pairs={{0,2},{1,3},{2,0},{3,1},{4,6},{5,7},{6,4},{7,5},{8,10},{9,11},{10,... | collective-permute-start | bytes 12582920 | tf_op jit(solution)/shard_map/ppermute | solution.py:21
  261.4 133.0 %copy-start = (bf16[128,8192]{1,0:T(8,128)(2,1)S(1)}, bf16[128,8192]{1,0:T(8,128)(2,1)}, u32[]{:S(2)}) copy-start(bf16[128,8192]{1,0:T(8,128)(2,1)} %param.4) | copy-start | bytes 6291460
  261.4 164.3 %collective-permute-start = (bf16[512,4096]{1,0:T(8,128)(2,1)}, bf16[512,4096]{1,0:T(8,128)(2,1)}, u32[]{:S(2)}, u32[]{:S(2)}) collective-permute-start(bf16[512,4096]{1,0:T(8,128)(2,1)} %shard_map.59), channel_id=1, source_target_pairs={{0,12},{1,13},{2,6},{3,7},{4,0},{5,1},{6,10},{7,11},{8,4},{9,5},{1... | collective-permute-start | bytes 12582920 | tf_op jit(solution)/shard_map/ppermute | solution.py:21
  393.8 47.8 %collective-permute-start.1 = (bf16[256,4096]{1,0:T(8,128)(2,1)}, bf16[256,4096]{1,0:T(8,128)(2,1)}, u32[]{:S(2)}, u32[]{:S(2)}) collective-permute-start(bf16[256,4096]{1,0:T(8,128)(2,1)} %get-tuple-element.33), channel_id=1, source_target_pairs={{0,2},{1,3},{2,0},{3,1},{4,6},{5,7},{6,4},{7,5},{8,10},{9,11},{10,... | collective-permute-start | bytes 6291464 | tf_op jit(solution)/shard_map/ppermute | solution.py:21
  393.9 47.8 %collective-permute-start.2 = (bf16[256,4096]{1,0:T(8,128)(2,1)}, bf16[256,4096]{1,0:T(8,128)(2,1)}, u32[]{:S(2)}, u32[]{:S(2)}) collective-permute-start(bf16[256,4096]{1,0:T(8,128)(2,1)} %get-tuple-element.34), channel_id=1, source_target_pairs={{0,12},{1,13},{2,6},{3,7},{4,0},{5,1},{6,10},{7,11},{8,4},{9,5},{1... | collective-permute-start | bytes 6291464 | tf_op jit(solution)/shard_map/ppermute | solution.py:21
  394.9 7.1 %copy-start.3 = (s32[768]{0:T(1024)S(1)}, s32[768]{0:T(1024)}, u32[]{:S(2)}) copy-start(s32[768]{0:T(1024)} %param.5) | copy-start | bytes 9220
  425.2 41.2 %collective-permute-start.7 = (bf16[512,4096]{1,0:T(8,128)(2,1)}, bf16[512,4096]{1,0:T(8,128)(2,1)}, u32[]{:S(2)}, u32[]{:S(2)}) collective-permute-start(bf16[512,4096]{1,0:T(8,128)(2,1)} %collective-permute-done.3.partner.partner1), channel_id=1, source_target_pairs={{0,1},{1,0},{2,3},{3,2},{4,5},{5,4},{6,7},{7,6},{8,9},{9,8},{10,11... | collective-permute-start | bytes 12582920 | tf_op jit(solution)/shard_map/ppermute | solution.py:21
  425.2 18.0 %collective-permute-start.5 = (f32[768]{0:T(1024)S(1)}, f32[768]{0:T(1024)S(1)}, u32[]{:S(2)}, u32[]{:S(2)}) collective-permute-start(f32[768]{0:T(1024)S(1)} %add_rsqrt_fusion), channel_id=1, source_target_pairs={{0,1},{1,2},{2,3},{3,4},{4,5},{5,6},{6,7},{7,8},{8,9},{9,10},{10,1... | collective-permute-start | bytes 9224 | tf_op jit(solution)/shard_map/ppermute | solution.py:21
  425.7 18.9 %collective-permute-start.6 = (f32[768]{0:T(1024)S(1)}, f32[768]{0:T(1024)S(1)}, u32[]{:S(2)}, u32[]{:S(2)}) collective-permute-start(f32[768]{0:T(1024)S(1)} %add_rsqrt_fusion), channel_id=1, source_target_pairs={{0,2},{1,3},{2,4},{3,5},{4,6},{5,7},{6,8},{7,9},{8,10},{9,11},{10,... | collective-permute-start | bytes 9224 | tf_op jit(solution)/shard_map/ppermute | solution.py:21
  444.6 21.6 %collective-permute-start.8 = (bf16[256,4096]{1,0:T(8,128)(2,1)}, bf16[256,4096]{1,0:T(8,128)(2,1)}, u32[]{:S(2)}, u32[]{:S(2)}) collective-permute-start(bf16[256,4096]{1,0:T(8,128)(2,1)} %collective-permute-done.1.partner2), channel_id=1, source_target_pairs={{0,1},{1,0},{2,3},{3,2},{4,5},{5,4},{6,7},{7,6},{8,9},{9,8},{10,11... | collective-permute-start | bytes 6291464 | tf_op jit(solution)/shard_map/ppermute | solution.py:21
  444.6 19.2 %collective-permute-start.10 = (bf16[512,512]{1,0:T(8,128)(2,1)S(1)}, bf16[512,512]{1,0:T(8,128)(2,1)S(1)}, u32[]{:S(2)}, u32[]{:S(2)}) collective-permute-start(bf16[512,512]{1,0:T(8,128)(2,1)S(1)} %get-tuple-element.37), channel_id=1, source_target_pairs={{0,2},{1,3},{2,0},{3,1},{4,6},{5,7},{6,4},{7,5},{8,10},{9,11},{10,... | collective-permute-start | bytes 1572872 | tf_op jit(solution)/shard_map/ppermute | solution.py:21
  445.6 20.6 %collective-permute-start.11 = (bf16[512,512]{1,0:T(8,128)(2,1)S(1)}, bf16[512,512]{1,0:T(8,128)(2,1)S(1)}, u32[]{:S(2)}, u32[]{:S(2)}) collective-permute-start(bf16[512,512]{1,0:T(8,128)(2,1)S(1)} %get-tuple-element.42), channel_id=1, source_target_pairs={{0,4},{1,5},{2,2},{3,3},{4,8},{5,9},{6,6},{7,7},{8,12},{9,13},{10,... | collective-permute-start | bytes 1572872 | tf_op jit(solution)/shard_map/ppermute | solution.py:21
  447.5 16.3 %collective-permute-start.9 = (f32[32,128]{1,0:T(8,128)S(1)}, f32[32,128]{1,0:T(8,128)S(1)}, u32[]{:S(2)}, u32[]{:S(2)}) collective-permute-start(f32[32,128]{1,0:T(8,128)S(1)} %constant_dynamic-slice_fusion.3), channel_id=1, source_target_pairs={{0,8},{1,9},{2,10},{3,11},{4,12},{5,13},{6,14},{7,15},{8,0},{9,1},... | collective-permute-start | bytes 49160 | tf_op jit(solution)/shard_map/ppermute | solution.py:21
  463.8 17.9 %collective-permute-start.14 = (bf16[256,1280]{1,0:T(8,128)(2,1)S(1)}, bf16[256,1280]{1,0:T(8,128)(2,1)S(1)}, u32[]{:S(2)}, u32[]{:S(2)}) collective-permute-start(bf16[256,1280]{1,0:T(8,128)(2,1)S(1)} %get-tuple-element.41), channel_id=1, source_target_pairs={{0,2},{1,3},{2,0},{3,1},{4,6},{5,7},{6,4},{7,5},{8,10},{9,11},{10,... | collective-permute-start | bytes 1966088 | tf_op jit(solution)/shard_map/ppermute | solution.py:21
  463.8 17.9 %collective-permute-start.15 = (bf16[256,1280]{1,0:T(8,128)(2,1)S(1)}, bf16[256,1280]{1,0:T(8,128)(2,1)S(1)}, u32[]{:S(2)}, u32[]{:S(2)}) collective-permute-start(bf16[256,1280]{1,0:T(8,128)(2,1)S(1)} %get-tuple-element.46), channel_id=1, source_target_pairs={{0,4},{1,5},{2,2},{3,3},{4,8},{5,9},{6,6},{7,7},{8,12},{9,13},{10,... | collective-permute-start | bytes 1966088 | tf_op jit(solution)/shard_map/ppermute | solution.py:21
  466.2 20.6 %collective-permute-start.13 = (f32[16,128]{1,0:T(8,128)S(1)}, f32[16,128]{1,0:T(8,128)S(1)}, u32[]{:S(2)}, u32[]{:S(2)}) collective-permute-start(f32[16,128]{1,0:T(8,128)S(1)} %constant_dynamic-slice_fusion.2), channel_id=1, source_target_pairs={{0,4},{1,5},{2,6},{3,7},{4,0},{5,1},{6,2},{7,3},{8,12},{9,13},{10,... | collective-permute-start | bytes 24584 | tf_op jit(solution)/shard_map/ppermute | solution.py:21
  476.4 17.6 %collective-permute-start.12 = (bf16[768,768]{1,0:T(8,128)(2,1)S(1)}, bf16[768,768]{1,0:T(8,128)(2,1)S(1)}, u32[]{:S(2)}, u32[]{:S(2)}) collective-permute-start(bf16[768,768]{1,0:T(8,128)(2,1)S(1)} %shard_map.63), channel_id=1, source_target_pairs={{1,2},{3,0},{5,6},{7,4},{9,10},{11,8},{13,14},{15,12},{17,18},{19,... | collective-permute-start | bytes 3538952 | tf_op jit(solution)/shard_map/ppermute | solution.py:21
  477.7 20.1 %collective-permute-start.17 = (bf16[768,768]{1,0:T(8,128)(2,1)S(1)}, bf16[768,768]{1,0:T(8,128)(2,1)}, u32[]{:S(2)}, u32[]{:S(2)}) collective-permute-start(bf16[768,768]{1,0:T(8,128)(2,1)S(1)} %shard_map.63), channel_id=1, source_target_pairs={{0,4},{2,2},{4,8},{6,6},{8,12},{10,10},{12,0},{14,14},{16,20},{18,... | collective-permute-start | bytes 3538952 | tf_op jit(solution)/shard_map/ppermute | solution.py:21
  481.6 0.9 copy-start.1
  486.9 3.8 collective-permute-start.16
  487.0 17.4 %collective-permute-start.19 = (f32[768]{0:T(1024)S(1)}, f32[768]{0:T(1024)S(1)}, u32[]{:S(2)}, u32[]{:S(2)}) collective-permute-start(f32[768]{0:T(1024)S(1)} %reduce.2), channel_id=1, source_target_pairs={{0,14},{1,15},{2,0},{3,1},{4,2},{5,3},{6,4},{7,5},{8,6},{9,7},{10,... | collective-permute-start | bytes 9224 | tf_op jit(solution)/shard_map/ppermute | solution.py:21
  502.7 1.2 collective-permute-start.20
  502.8 1.7 collective-permute-start.18
  (1 other events, 0.8 us)

commit v5 on v0

v5 whole, which is shorter than its diff:
```python
import functools
import math

import jax
import jax.numpy as jnp
from jax import lax
from jax.experimental import pallas as pl
from jax.experimental.pallas import tpu as pltpu
from jax.sharding import PartitionSpec as P

ROUNDS = 2
DOM_DEV = 4
DEPTH = 1024
TALL = 256
PIECES = 4
NT = (((1,), (1,)), ((), ()))
VMEM_LIMIT = 40 * 2**20


def send(value, pairs):
    return lax.ppermute(value, "blocks", pairs)


def after(value, *others):
    return lax.optimization_barrier((value, *others))[0]


def inverse_norm(matrix):
    values = matrix.astype(jnp.float32)
    return lax.rsqrt(jnp.mean(values * values, axis=1) + 1e-06)


def nt(left, right):
    return lax.dot_general(left, right, NT, preferred_element_type=jnp.float32)


def params():
    return pltpu.CompilerParams(vmem_limit_bytes=VMEM_LIMIT)


def cost(flops, bytes_accessed):
    return pl.CostEstimate(flops=flops, bytes_accessed=bytes_accessed, transcendentals=0)


def clear(*totals):
    @pl.when(pl.program_id(0) == 0)
    def _():
        for total in totals:
            total[...] = jnp.zeros_like(total)


def halves_kernel(start, sides, place, own, *rest):
    count = len(sides)
    outs, (buffer, reads, writes) = rest[:count], rest[count:]
    rows, width = outs[0].shape
    half = own.shape[1] // 2
    piece = rows // PIECES
    inward, outward = [], []
    for number, (side, out) in enumerate(zip(sides, outs)):
        left = pl.multiple_of(((place[0] + side) % 2) * half + start, 128)
        for i in range(PIECES):
            part = pl.ds(i * piece, piece)
            slot = number * PIECES + i
            held = buffer.at[number, part]
            inward.append(
                pltpu.make_async_copy(own.at[part, pl.ds(left, width)], held, reads.at[slot])
            )
            outward.append(pltpu.make_async_copy(held, out.at[part], writes.at[slot]))
    for copy in inward:
        copy.start()
    for arrived, copy in zip(inward, outward):
        arrived.wait()
        copy.start()
    for copy in outward:
        copy.wait()


def halves(place, own, start, width, sides):
    rows = own.shape[0]
    slots = PIECES * len(sides)
    anywhere = pl.BlockSpec(memory_space=pltpu.HBM)
    return pl.pallas_call(
        functools.partial(halves_kernel, start, sides),
        in_specs=[pl.BlockSpec(memory_space=pltpu.SMEM), anywhere],
        out_specs=[anywhere] * len(sides),
        out_shape=[jax.ShapeDtypeStruct((rows, width), own.dtype) for _ in sides],
        scratch_shapes=[
            pltpu.VMEM((len(sides), rows, width), own.dtype),
            pltpu.SemaphoreType.DMA((slots,)),
            pltpu.SemaphoreType.DMA((slots,)),
        ],
        compiler_params=params(),
        cost_estimate=cost(0, 4 * rows * width * len(sides)),
    )(place, own)


def early_kernel(place, own, partner, near, u, v):
    clear(u, v)

    @pl.when(place[0] == 0)
    def _():
        u[...] += nt(partner[...], own[...])
        v[...] += nt(near[...], partner[...])

    @pl.when(place[0] == 1)
    def _():
        u[...] += nt(partner[...], near[...])
        v[...] += nt(own[...], partner[...])


def early_tiles(place, own, partner, near):
    rows, width = partner.shape
    half = own.shape[1] // 2
    block = pl.BlockSpec((rows, DEPTH), lambda k, place: (0, k))
    mine = pl.BlockSpec((rows, DEPTH), lambda k, place: (0, place[0] * (half // DEPTH) + k))
    whole = pl.BlockSpec((rows, rows), lambda k, place: (0, 0))
    return pl.pallas_call(
        early_kernel,
        grid_spec=pltpu.PrefetchScalarGridSpec(
            num_scalar_prefetch=1,
            grid=(width // DEPTH,),
            in_specs=[mine, block, block],
            out_specs=[whole] * 2,
        ),
        out_shape=[jax.ShapeDtypeStruct((rows, rows), jnp.float32)] * 2,
        compiler_params=params(),
        cost_estimate=cost(rows, rows),
    )(place, own, partner, near)


def late_kernel(place, own, partner, near, u, v, u_out, v_out):
    rows = pl.ds(pl.program_id(0) * TALL, TALL)

    @pl.when(place[0] == 0)
    def _():
        u_out[...] = (u[...] + nt(partner[rows, :], own[...])).astype(u_out.dtype)
        v_out[...] = (v[...] + nt(near[rows, :], partner[...])).astype(v_out.dtype)

    @pl.when(place[0] == 1)
    def _():
        u_out[...] = (u[...] + nt(partner[rows, :], near[...])).astype(u_out.dtype)
        v_out[...] = (v[...] + nt(own[rows, :], partner[...])).astype(v_out.dtype)


def late_tiles(place, own, partner, near, u, v):
    rows, width = partner.shape
    half = own.shape[1] // 2
    block = pl.BlockSpec((rows, width), lambda j, place: (0, 0))
    mine = pl.BlockSpec((rows, width), lambda j, place: (0, (place[0] + 1) * (half // width) - 1))
    part = pl.BlockSpec((TALL, rows), lambda j, place: (j, 0))
    return pl.pallas_call(
        late_kernel,
        grid_spec=pltpu.PrefetchScalarGridSpec(
            num_scalar_prefetch=1,
            grid=(rows // TALL,),
            in_specs=[mine, block, block, part, part],
            out_specs=[part] * 2,
        ),
        out_shape=[jax.ShapeDtypeStruct((rows, rows), jnp.bfloat16)] * 2,
        compiler_params=params(),
        cost_estimate=cost(60000 * rows * rows, 160 * rows * rows),
    )(place, own, partner, near, u, v)


def cross_kernel(place, own, near1, near2, other1, other2, out, x):
    clear(x)
    step = pl.program_id(0)
    last = pl.num_programs(0) - 1
    code = place[0] * 2 + place[1]

    def add(near, other):
        pairs = ((near, other), (other, own), (own, other), (other, near))
        for number, (left, right) in enumerate(pairs):

            @pl.when(code == number)
            def _(left=left, right=right):
                x[...] += nt(left[...], right[...])

    pl.when(step < last)(functools.partial(add, near1, other1))
    pl.when(step == last)(functools.partial(add, near2, other2))

    @pl.when(step == last)
    def _():
        out[...] = x[...].astype(out.dtype)


def cross_tile(place, own, near1, near2, other1, other2):
    rows, width = near1.shape
    steps = own.shape[1] // 2 // DEPTH
    block1 = pl.BlockSpec((rows, DEPTH), lambda k, place: (0, jnp.minimum(k, steps - 2)))
    block2 = pl.BlockSpec((rows, DEPTH), lambda k, place: (0, 0))
    mine = pl.BlockSpec((rows, DEPTH), lambda k, place: (0, place[0] * steps + k))
    return pl.pallas_call(
        cross_kernel,
        grid_spec=pltpu.PrefetchScalarGridSpec(
            num_scalar_prefetch=1,
            grid=(steps,),
            in_specs=[mine] + [block1, block2] * 2,
            out_specs=pl.BlockSpec((rows, rows), lambda k, place: (0, 0)),
            scratch_shapes=[pltpu.VMEM((rows, rows), jnp.float32)],
        ),
        out_shape=jax.ShapeDtypeStruct((rows, rows), jnp.bfloat16),
        compiler_params=params(),
        cost_estimate=cost(2 * rows * rows * width, 6 * rows * width),
    )(place, own, near1, near2, other1, other2)


def finish(tile, gram, row_mass, column_mass):
    @pl.when(pl.program_id(0) == 0)
    def _():
        column_mass[...] = jnp.zeros_like(column_mass)

    gram[0] = tile
    squared = tile * tile
    column_mass[...] += jnp.sum(squared, axis=0, keepdims=True)
    sums = jnp.sum(squared, axis=1, keepdims=True)
    size = sums.shape[0]
    row_mass[...] = jnp.broadcast_to(sums, (size, size)).T[0:1]


def second_kernel(scale, u, v, inverse, behind, gram, row_mass, column_mass):
    tile = u[...].astype(jnp.float32) + v[...].astype(jnp.float32)
    finish(tile * inverse[...] * behind[...] * scale, gram, row_mass, column_mass)


def first_kernel(
    scale, place, y, z, local, inverse, behind, gram_in, gram, row_mass, column_mass
):
    del gram_in
    tile = y[...].astype(jnp.float32) + z[...].astype(jnp.float32)
    tile = jnp.where(place[1] == 1, local[...], tile)
    finish(tile * inverse[...] * behind[...] * scale, gram, row_mass, column_mass)


def mass_shapes(rows):
    specs = [
        pl.BlockSpec((1, TALL), lambda j, *_: (0, j)),
        pl.BlockSpec((1, rows), lambda j, *_: (0, 0)),
    ]
    return specs, [jax.ShapeDtypeStruct((1, rows), jnp.float32)] * 2


def second_tiles(scale, u, v, inverse, behind):
    rows = u.shape[0]
    block = pl.BlockSpec((TALL, rows), lambda j: (j, 0))
    mass_specs, mass_types = mass_shapes(rows)
    return pl.pallas_call(
        functools.partial(second_kernel, scale),
        grid=(rows // TALL,),
        in_specs=[
            block,
            block,
            pl.BlockSpec((TALL, 1), lambda j: (j, 0)),
            pl.BlockSpec((1, rows), lambda j: (0, 0)),
        ],
        out_specs=[pl.BlockSpec((1, TALL, rows), lambda j: (1, j, 0))] + mass_specs,
        out_shape=[jax.ShapeDtypeStruct((2, rows, rows), jnp.float32)] + mass_types,
        compiler_params=params(),
        cost_estimate=cost(60000 * rows * rows, 160 * rows * rows),
    )(u, v, inverse[:, None], behind[None, :])


def first_tiles(scale, place, y, z, local, inverse, behind, gram):
    rows = y.shape[0]
    block = pl.BlockSpec((TALL, rows), lambda j, place: (j, 0))
    mass_specs, mass_types = mass_shapes(rows)
    return pl.pallas_call(
        functools.partial(first_kernel, scale),
        grid_spec=pltpu.PrefetchScalarGridSpec(
            num_scalar_prefetch=1,
            grid=(rows // TALL,),
            in_specs=[block] * 3
            + [
                pl.BlockSpec((TALL, 1), lambda j, place: (j, 0)),
                pl.BlockSpec((1, rows), lambda j, place: (0, 0)),
                pl.BlockSpec(memory_space=pl.ANY),
            ],
            out_specs=[pl.BlockSpec((1, TALL, rows), lambda j, place: (0, j, 0))] + mass_specs,
        ),
        out_shape=[jax.ShapeDtypeStruct((2, rows, rows), jnp.float32)] + mass_types,
        input_output_aliases={6: 0},
        compiler_params=params(),
        cost_estimate=cost(8 * rows * rows, 12 * rows * rows),
    )(place, y, z, local, inverse[:, None], behind[None, :], gram)


def local(sketches, test_sketches, domain_map):
    rows, depth = sketches.shape
    size = lax.axis_size("blocks")
    index = lax.axis_index("blocks")
    half = depth // 2
    first = half - DEPTH
    blocks = range(size)
    upper = (index // 2) % 2
    core = index % 2
    place = jnp.stack([upper, core]).astype(jnp.int32)

    across = [(i, i ^ 2) for i in blocks]
    along = [(i, (i + (4 if i & 2 else -4)) % size) for i in blocks]
    swap = [(i, i ^ 1) for i in blocks]

    even = send(sketches, swap)
    (out1,) = halves(place, sketches, 0, first, (1,))
    partner1 = send(out1, across)
    (side1,) = halves(place, after(sketches, out1), 0, first, (0,))
    near1 = send(side1, along)
    out2, side2 = halves(place, after(sketches, side1), first, DEPTH, (1, 0))
    partner2 = send(out2, across)
    near2 = send(side2, along)

    inverse = inverse_norm(sketches)
    scale = 1.0 / math.sqrt(depth)

    test_inverse = inverse_norm(test_sketches)
    similarity = (
        nt(sketches, test_sketches) * inverse[:, None] * test_inverse[None, :] * scale
    ).astype(jnp.bfloat16)
    members = (
        domain_map[:, None] == lax.iota(jnp.int32, DOM_DEV * size)[None, :]
    ).astype(jnp.bfloat16)
    sums = lax.dot_general(
        members, similarity, (((0,), (0,)), ((), ())), preferred_element_type=jnp.float32
    )
    inside = nt(sketches, even)


    def halve(value, bit, *waits):
        count = value.shape[0] // 2
        mine = (index // bit) % 2
        away = lax.dynamic_slice_in_dim(value, (1 - mine) * count, count)
        kept = lax.dynamic_slice_in_dim(value, mine * count, count)
        return kept, send(after(away, *waits), [(i, i ^ bit) for i in blocks])

    bits = [size >> (step + 1) for step in range(size.bit_length() - 1)]
    back_v = [(i, i) if i & 2 else (i, (i + 4) % size) for i in blocks]
    back_y = [(i, i ^ 3) for i in blocks if i & 1]
    back_z = [pair for pair in back_v if pair[0] % 2 == 0]
    partner1 = after(partner1, inside, sums)
    u, v = early_tiles(place, sketches, partner1, near1)
    other1 = send(partner1, swap)
    partner2, near2, u, v = lax.optimization_barrier((partner2, near2, u, v))
    behind1 = send(after(inverse, partner2), [(i, (i + 1) % size) for i in blocks])
    behind2 = send(after(inverse, partner2), [(i, (i + 2) % size) for i in blocks])
    other2 = send(partner2, swap)
    for bit in bits[:-4]:
        kept, came = halve(sums, bit, partner2)
        sums = kept + came
    kept, came = halve(sums, bits[-4], partner2)
    u, v = late_tiles(place, sketches, partner2, near2, u, v)
    u, v, sums, behind1, behind2 = lax.optimization_barrier((u, v, kept + came, behind1, behind2))
    ur, vr = send(u, across), send(v, back_v)
    kept, came = halve(sums, bits[-3], u)
    x = cross_tile(place, sketches, near1, near2, after(other1, u), after(other2, u))
    y, z = send(x, back_y), send(x, back_z)

    gram, row_mass2, column_mass2 = second_tiles(scale, ur, vr, inverse, behind2)
    kept, came = halve(kept + after(came, row_mass2), bits[-2])
    kept, came = halve(kept + came, bits[-1])
    y, domain_sums = lax.optimization_barrier((y, kept + came))
    domain_scores = domain_sums * (1.0 / math.sqrt(rows / DOM_DEV))
    gram, row_mass1, column_mass1 = first_tiles(
        scale, place, y, z, inside, inverse, behind1, gram
    )
    mass = (
        row_mass1[0]
        + row_mass2[0]
        + send(column_mass1[0], [(i, (i - 1) % size) for i in blocks])
        + send(column_mass2[0], [(i, (i - 2) % size) for i in blocks])
    )
    redundancy = mass / float(2 * ROUNDS * rows)
    return (gram, redundancy, domain_scores)


def solution(mesh):
    in_specs = (P(("groups", "blocks"), None), P(), P(("groups", "blocks")))
    out_specs = (
        P(None, ("groups", "blocks"), None),
        P(("groups", "blocks")),
        P(("groups", "blocks"), None),
    )
    return jax.shard_map(local, mesh=mesh, in_specs=in_specs, out_specs=out_specs, check_vma=False)
```

time: 517 us -> 220 us (0.43)
  blocking collectives: 441 us -> 0 us
  waiting for transfers between devices: 0.01 us -> 104 us
  Pallas kernels: 0 us -> 51.6 us
  starting transfers between devices: 3.03 us -> 30.1 us
  matrix products: 41.8 us -> 21.9 us
  other arithmetic: 28.9 us -> 9.03 us
    unnamed x1 -> x0, blocking collectives: 441 us -> none
    ppermute x4 -> x19, waiting for transfers between devices: 0.01 us -> 104 us  [send(): return lax.ppermute(value, 'blocks', pairs)]
    pallas_call x0 -> x8, Pallas kernels: none -> 51.6 us  [the longest x1 12.4 us: cross_tile(): pl.pallas_call(cross_kernel, grid_spec=pltpu.PrefetchScalarGridSpec(num_s...]
    ppermute x4 -> x19, starting transfers between devices: 3.03 us -> 30.1 us  [send(): return lax.ppermute(value, 'blocks', pairs)]
    dot_general x2 -> x1, matrix products: 34.7 us -> 14.8 us  [nt(): return lax.dot_general(left, right, NT, preferred_element_type=jnp.float32)]
    reduce_sum x4 -> x2, other arithmetic: 23.5 us -> 7.7 us  [inverse_norm(): return lax.rsqrt(jnp.mean(values * values, axis=1) + 1e-06)]
  transfers between devices with their start and end apart: 4 -> 19, of which waited for: 0 -> 8; matrix products, arithmetic and copies ran while one was open for 6% -> 14% of each run, Pallas kernels for 0% -> 24%
where the time goes in v5:
time: 220 us; the launch traced here: 218 us
  waiting for transfers between devices  104 us (47%)
  Pallas kernels  51.6 us (23%)
  starting transfers between devices  30.1 us (14%)
  matrix products  21.9 us (10%)
  other arithmetic  9.03 us (4%)
    ppermute x19, waiting for transfers between devices, send(): return lax.ppermute(value, 'blocks', pairs)  104 us
    ppermute x19, starting transfers between devices, send(): return lax.ppermute(value, 'blocks', pairs)  30.1 us
    dot_general x1, matrix products, nt(): return lax.dot_general(left, right, NT, preferred_element_type=jnp.float32)  14.8 us
    pallas_call x1, Pallas kernels, cross_tile(): pl.pallas_call(cross_kernel, grid_spec=pltpu.PrefetchScalarGridSpec(num_s...  12.4 us
    pallas_call x3, Pallas kernels, halves(): pl.pallas_call(functools.partial(halves_kernel, start, sides), in_specs=[...  11.9 us
    pallas_call x1, Pallas kernels, early_tiles(): pl.pallas_call(early_kernel, grid_spec=pltpu.PrefetchScalarGridSpec(num_s...  11.4 us
    reduce_sum x2, other arithmetic, inverse_norm(): return lax.rsqrt(jnp.mean(values * values, axis=1) + 1e-06)  7.7 us
    pallas_call x1, Pallas kernels, late_tiles(): pl.pallas_call(late_kernel, grid_spec=pltpu.PrefetchScalarGridSpec(num_sc...  7.21 us
  transfers between devices with their start and end apart: 19, of which 8 were waited for; matrix products, arithmetic and copies ran while one was open for 14% of the time, Pallas kernels for 24%

profile of v5, /device:TPU:0, one launch (start us, length us, event | category | flops | bytes accessed | tf_op | source)
XLA Modules:
  0.0 218.0 jit_solution(2033640789445329188)
XLA Ops:
  1.2 4.3 %shard_map.58 = bf16[768,3072]{1,0:T(8,128)(2,1)} custom-call(s32[2]{0:T(128)S(1)} %pad_add_fusion.place, bf16[768,8192]{1,0:T(8,128)(2,1)} %own.9), custom_call_target="tpu_custom_call" | custom-call | bytes 9437184 | tf_op jit(solution)/shard_map/pallas_call | solution.py:82
  5.5 2.6 %collective-permute-start.3 = (bf16[768,3072]{1,0:T(8,128)(2,1)}, bf16[768,3072]{1,0:T(8,128)(2,1)}, u32[]{:S(2)}, u32[]{:S(2)}) collective-permute-start(bf16[768,3072]{1,0:T(8,128)(2,1)} %shard_map.58), channel_id=1, source_target_pairs={{0,2},{1,3},{2,0},{3,1},{4,6},{5,7},{6,4},{7,5},{8,10},{9,11},{10,... | collective-permute-start | bytes 14155784 | tf_op jit(solution)/shard_map/ppermute | solution.py:21
  8.2 4.3 %shard_map.59 = bf16[768,3072]{1,0:T(8,128)(2,1)} custom-call(s32[2]{0:T(128)S(1)} %pad_add_fusion.place, bf16[768,8192]{1,0:T(8,128)(2,1)} %own.9), custom_call_target="tpu_custom_call" | custom-call | bytes 9437184 | tf_op jit(solution)/shard_map/pallas_call | solution.py:82
  12.5 3.7 %collective-permute-start = (bf16[768,3072]{1,0:T(8,128)(2,1)}, bf16[768,3072]{1,0:T(8,128)(2,1)}, u32[]{:S(2)}, u32[]{:S(2)}) collective-permute-start(bf16[768,3072]{1,0:T(8,128)(2,1)} %shard_map.59), channel_id=1, source_target_pairs={{0,12},{1,13},{2,6},{3,7},{4,0},{5,1},{6,10},{7,11},{8,4},{9,5},{1... | collective-permute-start | bytes 14155784 | tf_op jit(solution)/shard_map/ppermute | solution.py:21
  16.1 3.3 %shard_map.60 = (bf16[768,1024]{1,0:T(8,128)(2,1)}, bf16[768,1024]{1,0:T(8,128)(2,1)}) custom-call(s32[2]{0:T(128)S(1)} %pad_add_fusion.place, bf16[768,8192]{1,0:T(8,128)(2,1)} %own.9), custom_call_target="tpu_custom_call" | custom-call | bytes 6291456 | tf_op jit(solution)/shard_map/pallas_call | solution.py:82
  20.1 7.2 %multiply_reduce_fusion = f32[768]{0:T(1024)S(1)} fusion(bf16[768,8192]{1,0:T(8,128)(2,1)} %own.9), kind=kLoop, calls=%fused_computation | loop fusion | flops 18873600 | bytes 12585984 | tf_op jit(solution)/shard_map/reduce_sum | solution.py:30
  27.8 7.1 %fusion.3 = f32[64,128]{1,0:T(8,128)S(1)} fusion(bf16[768,8192]{1,0:T(8,128)(2,1)} %own.9, bf16[128,8192]{1,0:T(8,128)(2,1)S(1)} %copy-done, f32[128]{0:T(128)S(1)} %add_rsqrt_fusion.1, f32[768]{0:T(1024)S(1)} %add_rsqrt_fusion, s32[768]{0:T(1024)S(1)} %copy-done.1), kind=kOutput, calls=%fused_computation.6 | convolution fusion | flops 1623638016 | bytes 14719488 | tf_op jit(solution)/shard_map/dot_general | solution.py:321
  35.0 14.8 %fusion.9.local = f32[768,768]{1,0:T(8,128)S(1)} fusion(bf16[768,8192]{1,0:T(8,128)(2,1)} %own.9, bf16[768,8192]{1,0:T(8,128)(2,1)} %collective-permute-done.4), kind=kOutput, calls=%fused_computation.27 | convolution fusion | flops 9663676416 | bytes 27525120 | tf_op jit(solution)/shard_map/dot_general | solution.py:34
  49.8 61.4 %collective-permute-done.3.partner = bf16[768,3072]{1,0:T(8,128)(2,1)} collective-permute-done((bf16[768,3072]{1,0:T(8,128)(2,1)}, bf16[768,3072]{1,0:T(8,128)(2,1)}, u32[]{:S(2)}, u32[]{:S(2)}) %collective-permute-start.3) | collective-permute-done | bytes 4718624 | tf_op jit(solution)/shard_map/ppermute | solution.py:21
  111.2 7.5 %collective-permute-done.near.near1 = bf16[768,3072]{1,0:T(8,128)(2,1)} collective-permute-done((bf16[768,3072]{1,0:T(8,128)(2,1)}, bf16[768,3072]{1,0:T(8,128)(2,1)}, u32[]{:S(2)}, u32[]{:S(2)}) %collective-permute-start) | collective-permute-done | bytes 4718624 | tf_op jit(solution)/shard_map/ppermute | solution.py:21
  118.6 11.4 %shard_map.61 = (f32[768,768]{1,0:T(8,128)S(1)}, f32[768,768]{1,0:T(8,128)S(1)}) custom-call(s32[2]{0:T(128)S(1)} %pad_add_fusion.place, bf16[768,8192]{1,0:T(8,128)(2,1)} %own.9, bf16[768,3072]{1,0:T(8,128)(2,1)} %collective-permute-done.3.partner, bf16[768,3072]{1,0:T(8,128)(2,1)} %collective-permute-done.near.near1), custom_call_target="tpu_custom_call" | custom-call | flops 768 | bytes 768 | tf_op jit(solution)/shard_map/pallas_call | solution.py:117
  130.0 14.6 %collective-permute-done.1.partner = bf16[768,1024]{1,0:T(8,128)(2,1)} collective-permute-done((bf16[768,1024]{1,0:T(8,128)(2,1)}, bf16[768,1024]{1,0:T(8,128)(2,1)}, u32[]{:S(2)}, u32[]{:S(2)}) %collective-permute-start.1) | collective-permute-done | bytes 1572896 | tf_op jit(solution)/shard_map/ppermute | solution.py:21
  144.6 6.9 %collective-permute-done.2.near.near2 = bf16[768,1024]{1,0:T(8,128)(2,1)} collective-permute-done((bf16[768,1024]{1,0:T(8,128)(2,1)}, bf16[768,1024]{1,0:T(8,128)(2,1)}, u32[]{:S(2)}, u32[]{:S(2)}) %collective-permute-start.2) | collective-permute-done | bytes 1572896 | tf_op jit(solution)/shard_map/ppermute | solution.py:21
  153.3 4.4 %collective-permute-start.6 = (f32[32,128]{1,0:T(8,128)S(1)}, f32[32,128]{1,0:T(8,128)S(1)}, u32[]{:S(2)}, u32[]{:S(2)}) collective-permute-start(f32[32,128]{1,0:T(8,128)S(1)} %constant_dynamic-slice_fusion.3), channel_id=1, source_target_pairs={{0,8},{1,9},{2,10},{3,11},{4,12},{5,13},{6,14},{7,15},{8,0},{9,1},... | collective-permute-start | bytes 49160 | tf_op jit(solution)/shard_map/ppermute | solution.py:21
  157.7 7.2 %shard_map.62 = (bf16[768,768]{1,0:T(8,128)(2,1)}, bf16[768,768]{1,0:T(8,128)(2,1)}) custom-call(s32[2]{0:T(128)S(1)} %pad_add_fusion.place, bf16[768,8192]{1,0:T(8,128)(2,1)} %own.9, bf16[768,1024]{1,0:T(8,128)(2,1)} %collective-permute-done.1.partner, bf16[768,1024]{1,0:T(8,128)(2,1)} %collective-permute-done.2.near.near2, ...), custom_call_target="tpu_custom_call" | custom-call | flops 35389440000 | bytes 94371840 | tf_op jit(solution)/shard_map/pallas_call | solution.py:151
  165.3 2.4 %collective-permute-start.13 = (bf16[768,768]{1,0:T(8,128)(2,1)}, bf16[768,768]{1,0:T(8,128)(2,1)}, u32[]{:S(2)}, u32[]{:S(2)}) collective-permute-start(bf16[768,768]{1,0:T(8,128)(2,1)} %get-tuple-element.55), channel_id=1, source_target_pairs={{0,4},{1,5},{2,2},{3,3},{4,8},{5,9},{6,6},{7,7},{8,12},{9,13},{10,... | collective-permute-start | bytes 3538952 | tf_op jit(solution)/shard_map/ppermute | solution.py:21
  168.1 12.4 %shard_map.63 = bf16[768,768]{1,0:T(8,128)(2,1)} custom-call(s32[2]{0:T(128)S(1)} %pad_add_fusion.place, bf16[768,8192]{1,0:T(8,128)(2,1)} %own.9, bf16[768,3072]{1,0:T(8,128)(2,1)} %collective-permute-done.near.near1, bf16[768,1024]{1,0:T(8,128)(2,1)} %collective-permute-done.2.near.near2, bf16[768,3072]{1,0:T(8,128)(2,1)} %collective-permute-done.5.other1, ...), custom_call_target="tpu_custom_call" | custom-call | flops 3623878656 | bytes 14155776 | tf_op jit(solution)/shard_map/pallas_call | solution.py:193
  181.8 3.9 %collective-permute-start.16 = (bf16[768,768]{1,0:T(8,128)(2,1)}, bf16[768,768]{1,0:T(8,128)(2,1)}, u32[]{:S(2)}, u32[]{:S(2)}) collective-permute-start(bf16[768,768]{1,0:T(8,128)(2,1)} %shard_map.63), channel_id=1, source_target_pairs={{0,4},{2,2},{4,8},{6,6},{8,12},{10,10},{12,0},{14,14},{16,20},{18,... | collective-permute-start | bytes 3538952 | tf_op jit(solution)/shard_map/ppermute | solution.py:21
  185.7 8.2 %collective-permute-done.12.u = bf16[768,768]{1,0:T(8,128)(2,1)} collective-permute-done((bf16[768,768]{1,0:T(8,128)(2,1)}, bf16[768,768]{1,0:T(8,128)(2,1)}, u32[]{:S(2)}, u32[]{:S(2)}) %collective-permute-start.12) | collective-permute-done | bytes 1179680 | tf_op jit(solution)/shard_map/ppermute | solution.py:21
  193.8 3.3 %collective-permute-done.13.v = bf16[768,768]{1,0:T(8,128)(2,1)} collective-permute-done((bf16[768,768]{1,0:T(8,128)(2,1)}, bf16[768,768]{1,0:T(8,128)(2,1)}, u32[]{:S(2)}, u32[]{:S(2)}) %collective-permute-start.13) | collective-permute-done | bytes 1179680 | tf_op jit(solution)/shard_map/ppermute | solution.py:21
  197.1 4.0 %shard_map.64 = (f32[2,768,768]{2,1,0:T(8,128)}, f32[1,768]{1,0:T(1,128)S(1)}, f32[1,768]{1,0:T(1,128)S(1)}) custom-call(bf16[768,768]{1,0:T(8,128)(2,1)} %collective-permute-done.12.u, bf16[768,768]{1,0:T(8,128)(2,1)} %collective-permute-done.13.v, f32[768,1]{1,0:T(8,128)S(1)} %rsqrt.24.inverse, f32[1,768]{1,0:T(1,128)S(1)} %broadcast_in_dim.4.behind), custom_call_target="tpu_custom_call" | custom-call | flops 35389440000 | bytes 94371840 | tf_op jit(solution)/shard_map/pallas_call | solution.py:247
  201.2 4.7 %collective-permute-start.14 = (f32[8,128]{1,0:T(8,128)S(1)}, f32[8,128]{1,0:T(8,128)S(1)}, u32[]{:S(2)}, u32[]{:S(2)}) collective-permute-start(f32[8,128]{1,0:T(8,128)S(1)} %constant_dynamic-slice_fusion.1), channel_id=1, source_target_pairs={{0,2},{1,3},{2,0},{3,1},{4,6},{5,7},{6,4},{7,5},{8,10},{9,11},{10,... | collective-permute-start | bytes 12296 | tf_op jit(solution)/shard_map/ppermute | solution.py:21
  207.6 2.9 %collective-permute-start.18 = (f32[768]{0:T(1024)S(1)}, f32[768]{0:T(1024)S(1)}, u32[]{:S(2)}, u32[]{:S(2)}) collective-permute-start(f32[768]{0:T(1024)S(1)} %reduce.2), channel_id=1, source_target_pairs={{0,14},{1,15},{2,0},{3,1},{4,2},{5,3},{6,4},{7,5},{8,6},{9,7},{10,... | collective-permute-start | bytes 9224 | tf_op jit(solution)/shard_map/ppermute | solution.py:21
  210.6 4.6 %shard_map.65 = (f32[2,768,768]{2,1,0:T(8,128)}, f32[1,768]{1,0:T(1,128)S(1)}, f32[1,768]{1,0:T(1,128)S(1)}) custom-call(s32[2]{0:T(128)S(1)} %pad_add_fusion.place, bf16[768,768]{1,0:T(8,128)(2,1)} %collective-permute-done.10.y, bf16[768,768]{1,0:T(8,128)(2,1)} %collective-permute-done.16.z, ...), custom_call_target="tpu_custom_call", output_to_operand_aliasing={{0}: (6, {})} | custom-call | flops 4718592 | bytes 7077888 | tf_op jit(solution)/shard_map/pallas_call | solution.py:267
  (49 shorter events, 9.9 us)
Async XLA Ops:
  0.6 34.3 %collective-permute-start.4 = (bf16[768,8192]{1,0:T(8,128)(2,1)}, bf16[768,8192]{1,0:T(8,128)(2,1)}, u32[]{:S(2)}, u32[]{:S(2)}) collective-permute-start(bf16[768,8192]{1,0:T(8,128)(2,1)} %own.9), channel_id=1, source_target_pairs={{0,1},{1,0},{2,3},{3,2},{4,5},{5,4},{6,7},{7,6},{8,9},{9,8},{10,11... | collective-permute-start | bytes 37748744 | tf_op jit(solution)/shard_map/ppermute | solution.py:21
  5.5 105.6 %collective-permute-start.3 = (bf16[768,3072]{1,0:T(8,128)(2,1)}, bf16[768,3072]{1,0:T(8,128)(2,1)}, u32[]{:S(2)}, u32[]{:S(2)}) collective-permute-start(bf16[768,3072]{1,0:T(8,128)(2,1)} %shard_map.58), channel_id=1, source_target_pairs={{0,2},{1,3},{2,0},{3,1},{4,6},{5,7},{6,4},{7,5},{8,10},{9,11},{10,... | collective-permute-start | bytes 14155784 | tf_op jit(solution)/shard_map/ppermute | solution.py:21
  12.5 106.1 %collective-permute-start = (bf16[768,3072]{1,0:T(8,128)(2,1)}, bf16[768,3072]{1,0:T(8,128)(2,1)}, u32[]{:S(2)}, u32[]{:S(2)}) collective-permute-start(bf16[768,3072]{1,0:T(8,128)(2,1)} %shard_map.59), channel_id=1, source_target_pairs={{0,12},{1,13},{2,6},{3,7},{4,0},{5,1},{6,10},{7,11},{8,4},{9,5},{1... | collective-permute-start | bytes 14155784 | tf_op jit(solution)/shard_map/ppermute | solution.py:21
  19.5 125.1 %collective-permute-start.1 = (bf16[768,1024]{1,0:T(8,128)(2,1)}, bf16[768,1024]{1,0:T(8,128)(2,1)}, u32[]{:S(2)}, u32[]{:S(2)}) collective-permute-start(bf16[768,1024]{1,0:T(8,128)(2,1)} %get-tuple-element.37), channel_id=1, source_target_pairs={{0,2},{1,3},{2,0},{3,1},{4,6},{5,7},{6,4},{7,5},{8,10},{9,11},{10,... | collective-permute-start | bytes 4718600 | tf_op jit(solution)/shard_map/ppermute | solution.py:21
  19.6 7.8 %copy-start = (bf16[128,8192]{1,0:T(8,128)(2,1)S(1)}, bf16[128,8192]{1,0:T(8,128)(2,1)}, u32[]{:S(2)}) copy-start(bf16[128,8192]{1,0:T(8,128)(2,1)} %param.4) | copy-start | bytes 6291460
  19.6 8.2 %copy-start.1 = (s32[768]{0:T(1024)S(1)}, s32[768]{0:T(1024)}, u32[]{:S(2)}) copy-start(s32[768]{0:T(1024)} %param.5) | copy-start | bytes 9220
  19.6 132.0 %collective-permute-start.2 = (bf16[768,1024]{1,0:T(8,128)(2,1)}, bf16[768,1024]{1,0:T(8,128)(2,1)}, u32[]{:S(2)}, u32[]{:S(2)}) collective-permute-start(bf16[768,1024]{1,0:T(8,128)(2,1)} %get-tuple-element.38), channel_id=1, source_target_pairs={{0,12},{1,13},{2,6},{3,7},{4,0},{5,1},{6,10},{7,11},{8,4},{9,5},{1... | collective-permute-start | bytes 4718600 | tf_op jit(solution)/shard_map/ppermute | solution.py:21
  111.2 56.9 %collective-permute-start.5 = (bf16[768,3072]{1,0:T(8,128)(2,1)}, bf16[768,3072]{1,0:T(8,128)(2,1)}, u32[]{:S(2)}, u32[]{:S(2)}) collective-permute-start(bf16[768,3072]{1,0:T(8,128)(2,1)} %collective-permute-done.3.partner), channel_id=1, source_target_pairs={{0,1},{1,0},{2,3},{3,2},{4,5},{5,4},{6,7},{7,6},{8,9},{9,8},{10,11... | collective-permute-start | bytes 14155784 | tf_op jit(solution)/shard_map/ppermute | solution.py:21
  151.6 13.4 %collective-permute-start.7 = (f32[768]{0:T(1024)S(1)}, f32[768]{0:T(1024)S(1)}, u32[]{:S(2)}, u32[]{:S(2)}) collective-permute-start(f32[768]{0:T(1024)S(1)} %add_rsqrt_fusion), channel_id=1, source_target_pairs={{0,1},{1,2},{2,3},{3,4},{4,5},{5,6},{6,7},{7,8},{8,9},{9,10},{10,1... | collective-permute-start | bytes 9224 | tf_op jit(solution)/shard_map/ppermute | solution.py:21
  151.6 13.4 %collective-permute-start.8 = (f32[768]{0:T(1024)S(1)}, f32[768]{0:T(1024)S(1)}, u32[]{:S(2)}, u32[]{:S(2)}) collective-permute-start(f32[768]{0:T(1024)S(1)} %add_rsqrt_fusion), channel_id=1, source_target_pairs={{0,2},{1,3},{2,4},{3,5},{4,6},{5,7},{6,8},{7,9},{8,10},{9,11},{10,... | collective-permute-start | bytes 9224 | tf_op jit(solution)/shard_map/ppermute | solution.py:21
  152.9 15.2 %collective-permute-start.9 = (bf16[768,1024]{1,0:T(8,128)(2,1)}, bf16[768,1024]{1,0:T(8,128)(2,1)}, u32[]{:S(2)}, u32[]{:S(2)}) collective-permute-start(bf16[768,1024]{1,0:T(8,128)(2,1)} %collective-permute-done.1.partner), channel_id=1, source_target_pairs={{0,1},{1,0},{2,3},{3,2},{4,5},{5,4},{6,7},{7,6},{8,9},{9,8},{10,11... | collective-permute-start | bytes 4718600 | tf_op jit(solution)/shard_map/ppermute | solution.py:21
  153.3 11.6 %collective-permute-start.6 = (f32[32,128]{1,0:T(8,128)S(1)}, f32[32,128]{1,0:T(8,128)S(1)}, u32[]{:S(2)}, u32[]{:S(2)}) collective-permute-start(f32[32,128]{1,0:T(8,128)S(1)} %constant_dynamic-slice_fusion.3), channel_id=1, source_target_pairs={{0,8},{1,9},{2,10},{3,11},{4,12},{5,13},{6,14},{7,15},{8,0},{9,1},... | collective-permute-start | bytes 49160 | tf_op jit(solution)/shard_map/ppermute | solution.py:21
  165.0 28.9 %collective-permute-start.12 = (bf16[768,768]{1,0:T(8,128)(2,1)}, bf16[768,768]{1,0:T(8,128)(2,1)}, u32[]{:S(2)}, u32[]{:S(2)}) collective-permute-start(bf16[768,768]{1,0:T(8,128)(2,1)} %get-tuple-element.50), channel_id=1, source_target_pairs={{0,2},{1,3},{2,0},{3,1},{4,6},{5,7},{6,4},{7,5},{8,10},{9,11},{10,... | collective-permute-start | bytes 3538952 | tf_op jit(solution)/shard_map/ppermute | solution.py:21
  165.3 31.8 %collective-permute-start.13 = (bf16[768,768]{1,0:T(8,128)(2,1)}, bf16[768,768]{1,0:T(8,128)(2,1)}, u32[]{:S(2)}, u32[]{:S(2)}) collective-permute-start(bf16[768,768]{1,0:T(8,128)(2,1)} %get-tuple-element.55), channel_id=1, source_target_pairs={{0,4},{1,5},{2,2},{3,3},{4,8},{5,9},{6,6},{7,7},{8,12},{9,13},{10,... | collective-permute-start | bytes 3538952 | tf_op jit(solution)/shard_map/ppermute | solution.py:21
  168.0 33.2 %collective-permute-start.11 = (f32[16,128]{1,0:T(8,128)S(1)}, f32[16,128]{1,0:T(8,128)S(1)}, u32[]{:S(2)}, u32[]{:S(2)}) collective-permute-start(f32[16,128]{1,0:T(8,128)S(1)} %constant_dynamic-slice_fusion.2), channel_id=1, source_target_pairs={{0,4},{1,5},{2,6},{3,7},{4,0},{5,1},{6,2},{7,3},{8,12},{9,13},{10,... | collective-permute-start | bytes 24584 | tf_op jit(solution)/shard_map/ppermute | solution.py:21
  180.5 30.1 %collective-permute-start.10 = (bf16[768,768]{1,0:T(8,128)(2,1)}, bf16[768,768]{1,0:T(8,128)(2,1)}, u32[]{:S(2)}, u32[]{:S(2)}) collective-permute-start(bf16[768,768]{1,0:T(8,128)(2,1)} %shard_map.63), channel_id=1, source_target_pairs={{1,2},{3,0},{5,6},{7,4},{9,10},{11,8},{13,14},{15,12},{17,18},{19,... | collective-permute-start | bytes 3538952 | tf_op jit(solution)/shard_map/ppermute | solution.py:21
  181.8 28.8 %collective-permute-start.16 = (bf16[768,768]{1,0:T(8,128)(2,1)}, bf16[768,768]{1,0:T(8,128)(2,1)}, u32[]{:S(2)}, u32[]{:S(2)}) collective-permute-start(bf16[768,768]{1,0:T(8,128)(2,1)} %shard_map.63), channel_id=1, source_target_pairs={{0,4},{2,2},{4,8},{6,6},{8,12},{10,10},{12,0},{14,14},{16,20},{18,... | collective-permute-start | bytes 3538952 | tf_op jit(solution)/shard_map/ppermute | solution.py:21
  201.2 6.3 %collective-permute-start.14 = (f32[8,128]{1,0:T(8,128)S(1)}, f32[8,128]{1,0:T(8,128)S(1)}, u32[]{:S(2)}, u32[]{:S(2)}) collective-permute-start(f32[8,128]{1,0:T(8,128)S(1)} %constant_dynamic-slice_fusion.1), channel_id=1, source_target_pairs={{0,2},{1,3},{2,0},{3,1},{4,6},{5,7},{6,4},{7,5},{8,10},{9,11},{10,... | collective-permute-start | bytes 12296 | tf_op jit(solution)/shard_map/ppermute | solution.py:21
  207.5 3.1 %collective-permute-start.15 = (f32[4,128]{1,0:T(4,128)S(1)}, f32[4,128]{1,0:T(4,128)S(1)}, u32[]{:S(2)}, u32[]{:S(2)}) collective-permute-start(f32[4,128]{1,0:T(4,128)S(1)} %constant_dynamic-slice_fusion), channel_id=1, source_target_pairs={{0,1},{1,0},{2,3},{3,2},{4,5},{5,4},{6,7},{7,6},{8,9},{9,8},{10,11... | collective-permute-start | bytes 6152 | tf_op jit(solution)/shard_map/ppermute | solution.py:21
  207.6 9.1 %collective-permute-start.18 = (f32[768]{0:T(1024)S(1)}, f32[768]{0:T(1024)S(1)}, u32[]{:S(2)}, u32[]{:S(2)}) collective-permute-start(f32[768]{0:T(1024)S(1)} %reduce.2), channel_id=1, source_target_pairs={{0,14},{1,15},{2,0},{3,1},{4,2},{5,3},{6,4},{7,5},{8,6},{9,7},{10,... | collective-permute-start | bytes 9224 | tf_op jit(solution)/shard_map/ppermute | solution.py:21
  215.2 2.2 %collective-permute-start.17 = (f32[768]{0:T(1024)S(1)}, f32[768]{0:T(1024)S(1)}, u32[]{:S(2)}, u32[]{:S(2)}) collective-permute-start(f32[768]{0:T(1024)S(1)} %reduce.1), channel_id=1, source_target_pairs={{0,15},{1,0},{2,1},{3,2},{4,3},{5,4},{6,5},{7,6},{8,7},{9,8},{10,9... | collective-permute-start | bytes 9224 | tf_op jit(solution)/shard_map/ppermute | solution.py:21

commit v6 on v5

--- a/solution.py
+++ b/solution.py
@@ -11,10 +11,11 @@
 ROUNDS = 2
 DOM_DEV = 4
 DEPTH = 1024
-TALL = 256
+TALL = 128
+BAND = 256
 PIECES = 4
 NT = (((1,), (1,)), ((), ()))
-VMEM_LIMIT = 40 * 2**20
+VMEM_LIMIT = 36 * 2**20
 
 
 def send(value, pairs):
@@ -51,46 +52,38 @@
 
 def halves_kernel(start, sides, place, own, *rest):
     count = len(sides)
-    outs, (buffer, reads, writes) = rest[:count], rest[count:]
+    outs, reads = rest[:count], rest[count]
     rows, width = outs[0].shape
     half = own.shape[1] // 2
     piece = rows // PIECES
-    inward, outward = [], []
+    copies = []
     for number, (side, out) in enumerate(zip(sides, outs)):
         left = pl.multiple_of(((place[0] + side) % 2) * half + start, 128)
         for i in range(PIECES):
             part = pl.ds(i * piece, piece)
-            slot = number * PIECES + i
-            held = buffer.at[number, part]
-            inward.append(
-                pltpu.make_async_copy(own.at[part, pl.ds(left, width)], held, reads.at[slot])
+            copies.append(
+                pltpu.make_async_copy(
+                    own.at[part, pl.ds(left, width)],
+                    out.at[part],
+                    reads.at[number * PIECES + i],
+                )
             )
-            outward.append(pltpu.make_async_copy(held, out.at[part], writes.at[slot]))
-    for copy in inward:
+    for copy in copies:
         copy.start()
-    for arrived, copy in zip(inward, outward):
-        arrived.wait()
-        copy.start()
-    for copy in outward:
+    for copy in copies:
         copy.wait()
 
 
 def halves(place, own, start, width, sides):
     rows = own.shape[0]
-    slots = PIECES * len(sides)
-    anywhere = pl.BlockSpec(memory_space=pltpu.HBM)
     return pl.pallas_call(
         functools.partial(halves_kernel, start, sides),
-        in_specs=[pl.BlockSpec(memory_space=pltpu.SMEM), anywhere],
-        out_specs=[anywhere] * len(sides),
-        out_shape=[jax.ShapeDtypeStruct((rows, width), own.dtype) for _ in sides],
-        scratch_shapes=[
-            pltpu.VMEM((len(sides), rows, width), own.dtype),
-            pltpu.SemaphoreType.DMA((slots,)),
-            pltpu.SemaphoreType.DMA((slots,)),
-        ],
-        compiler_params=params(),
-        cost_estimate=cost(0, 4 * rows * width * len(sides)),
+        in_specs=[pl.BlockSpec(memory_space=pltpu.SMEM), pl.BlockSpec(memory_space=pltpu.HBM)],
+        out_specs=[pl.BlockSpec(memory_space=pltpu.VMEM)] * len(sides),
+        out_shape=[pltpu.VMEM((rows, width), own.dtype) for _ in sides],
+        scratch_shapes=[pltpu.SemaphoreType.DMA((PIECES * len(sides),))],
+        compiler_params=params(),
+        cost_estimate=cost(0, 2 * rows * width * len(sides)),
     )(place, own)
 
 
@@ -128,38 +121,33 @@
     )(place, own, partner, near)
 
 
-def late_kernel(place, own, partner, near, u, v, u_out, v_out):
-    rows = pl.ds(pl.program_id(0) * TALL, TALL)
+def late_kernel(place, mine, partner, near, u, v, u_out, v_out):
+    def add(s, w):
+        for start in range(0, u.shape[0], BAND):
+            rows = pl.ds(start, BAND)
+            u_out[rows, :] = (u[rows, :] + nt(partner[rows, :], s[...])).astype(u_out.dtype)
+            v_out[rows, :] = (v[rows, :] + nt(w[rows, :], partner[...])).astype(v_out.dtype)
 
     @pl.when(place[0] == 0)
     def _():
-        u_out[...] = (u[...] + nt(partner[rows, :], own[...])).astype(u_out.dtype)
-        v_out[...] = (v[...] + nt(near[rows, :], partner[...])).astype(v_out.dtype)
+        add(mine, near)
 
     @pl.when(place[0] == 1)
     def _():
-        u_out[...] = (u[...] + nt(partner[rows, :], near[...])).astype(u_out.dtype)
-        v_out[...] = (v[...] + nt(own[rows, :], partner[...])).astype(v_out.dtype)
-
-
-def late_tiles(place, own, partner, near, u, v):
+        add(near, mine)
+
+
+def late_tiles(place, mine, partner, near, u, v):
     rows, width = partner.shape
-    half = own.shape[1] // 2
-    block = pl.BlockSpec((rows, width), lambda j, place: (0, 0))
-    mine = pl.BlockSpec((rows, width), lambda j, place: (0, (place[0] + 1) * (half // width) - 1))
-    part = pl.BlockSpec((TALL, rows), lambda j, place: (j, 0))
     return pl.pallas_call(
         late_kernel,
-        grid_spec=pltpu.PrefetchScalarGridSpec(
-            num_scalar_prefetch=1,
-            grid=(rows // TALL,),
-            in_specs=[mine, block, block, part, part],
-            out_specs=[part] * 2,
-        ),
-        out_shape=[jax.ShapeDtypeStruct((rows, rows), jnp.bfloat16)] * 2,
+        in_specs=[pl.BlockSpec(memory_space=pltpu.SMEM)]
+        + [pl.BlockSpec(memory_space=pltpu.VMEM)] * 5,
+        out_specs=[pl.BlockSpec(memory_space=pltpu.VMEM)] * 2,
+        out_shape=[pltpu.VMEM((rows, rows), jnp.bfloat16)] * 2,
         compiler_params=params(),
         cost_estimate=cost(60000 * rows * rows, 160 * rows * rows),
-    )(place, own, partner, near, u, v)
+    )(place, mine, partner, near, u, v)
 
 
 def cross_kernel(place, own, near1, near2, other1, other2, out, x):
@@ -338,34 +326,35 @@
     partner1 = after(partner1, inside, sums)
     u, v = early_tiles(place, sketches, partner1, near1)
     other1 = send(partner1, swap)
-    partner2, near2, u, v = lax.optimization_barrier((partner2, near2, u, v))
-    behind1 = send(after(inverse, partner2), [(i, (i + 1) % size) for i in blocks])
-    behind2 = send(after(inverse, partner2), [(i, (i + 2) % size) for i in blocks])
+    behind1 = send(after(inverse, partner1), [(i, (i + 1) % size) for i in blocks])
+    behind2 = send(after(inverse, partner1), [(i, (i + 2) % size) for i in blocks])
+    for bit in bits[:-4]:
+        kept, came = halve(sums, bit, partner1)
+        sums = kept + came
+    kept, came = halve(sums, bits[-4], u)
+    partner2, near2, u, v, behind1, behind2, came = lax.optimization_barrier(
+        (partner2, near2, u, v, behind1, behind2, came)
+    )
     other2 = send(partner2, swap)
-    for bit in bits[:-4]:
-        kept, came = halve(sums, bit, partner2)
-        sums = kept + came
-    kept, came = halve(sums, bits[-4], partner2)
-    u, v = late_tiles(place, sketches, partner2, near2, u, v)
-    u, v, sums, behind1, behind2 = lax.optimization_barrier((u, v, kept + came, behind1, behind2))
+    u, v = late_tiles(place, side2, partner2, near2, u, v)
     ur, vr = send(u, across), send(v, back_v)
-    kept, came = halve(sums, bits[-3], u)
+    kept, came = halve(kept + came, bits[-3], u)
     x = cross_tile(place, sketches, near1, near2, after(other1, u), after(other2, u))
     y, z = send(x, back_y), send(x, back_z)
 
     gram, row_mass2, column_mass2 = second_tiles(scale, ur, vr, inverse, behind2)
     kept, came = halve(kept + after(came, row_mass2), bits[-2])
-    kept, came = halve(kept + came, bits[-1])
-    y, domain_sums = lax.optimization_barrier((y, kept + came))
-    domain_scores = domain_sums * (1.0 / math.sqrt(rows / DOM_DEV))
+    y, sums = lax.optimization_barrier((y, kept + came))
     gram, row_mass1, column_mass1 = first_tiles(
         scale, place, y, z, inside, inverse, behind1, gram
     )
+    kept, came = halve(sums, bits[-1], row_mass1)
+    domain_scores = (kept + came) * (1.0 / math.sqrt(rows / DOM_DEV))
     mass = (
         row_mass1[0]
         + row_mass2[0]
         + send(column_mass1[0], [(i, (i - 1) % size) for i in blocks])
-        + send(column_mass2[0], [(i, (i - 2) % size) for i in blocks])
+        + send(after(column_mass2[0], row_mass1), [(i, (i - 2) % size) for i in blocks])
     )
     redundancy = mass / float(2 * ROUNDS * rows)
     return (gram, redundancy, domain_scores)

time: 220 us -> 222 us (level)
  local copies, waits for them, and re-layouts: 0.21 us -> 4.78 us
  starting transfers between devices: 30.1 us -> 27.6 us
    unnamed x4 -> x6, local copies, waits for them, and re-layouts: 0.01 us -> 4.59 us
    pallas_call x3, Pallas kernels: 11.9 us -> 8.75 us  [halves(): pl.pallas_call(functools.partial(halves_kernel, start, sides), in_specs=[...]
    ppermute x19, starting transfers between devices: 30.1 us -> 27.6 us  [send(): return lax.ppermute(value, 'blocks', pairs)]
  transfers between devices with their start and end apart: 19 -> 19, of which waited for: 8 -> 12; matrix products, arithmetic and copies ran while one was open for 14% -> 14% of each run, Pallas kernels for 24% -> 20%
where the time goes in v6:
time: 222 us; the launch traced here: 219 us
  waiting for transfers between devices  105 us (47%)
  Pallas kernels  50 us (23%)
  starting transfers between devices  27.6 us (12%)
  matrix products  21.8 us (10%)
  other arithmetic  9.04 us (4%)
  local copies, waits for them, and re-layouts  4.78 us (2%)
    ppermute x19, waiting for transfers between devices, send(): return lax.ppermute(value, 'blocks', pairs)  105 us
    ppermute x19, starting transfers between devices, send(): return lax.ppermute(value, 'blocks', pairs)  27.6 us
    dot_general x1, matrix products, nt(): return lax.dot_general(left, right, NT, preferred_element_type=jnp.float32)  14.8 us
    pallas_call x1, Pallas kernels, cross_tile(): pl.pallas_call(cross_kernel, grid_spec=pltpu.PrefetchScalarGridSpec(num_s...  12.4 us
    pallas_call x1, Pallas kernels, early_tiles(): pl.pallas_call(early_kernel, grid_spec=pltpu.PrefetchScalarGridSpec(num_s...  11.3 us
    pallas_call x3, Pallas kernels, halves(): pl.pallas_call(functools.partial(halves_kernel, start, sides), in_specs=[...  8.75 us
    reduce_sum x2, other arithmetic, inverse_norm(): return lax.rsqrt(jnp.mean(values * values, axis=1) + 1e-06)  7.7 us
    dot_general x1, matrix products, local(): lax.dot_general(members, similarity, (((0,), (0,)), ((), ())), preferred_...  7.06 us
  transfers between devices with their start and end apart: 19, of which 12 were waited for; matrix products, arithmetic and copies ran while one was open for 14% of the time, Pallas kernels for 20%

profile of v6, /device:TPU:0, one launch (start us, length us, event | category | flops | bytes accessed | tf_op | source)
XLA Modules:
  0.0 218.7 jit_solution(16395482722981751517)
XLA Ops:
  1.2 4.6 %copy-done = bf16[768,8192]{1,0:T(8,128)(2,1)S(1)} copy-done((bf16[768,8192]{1,0:T(8,128)(2,1)S(1)}, bf16[768,8192]{1,0:T(8,128)(2,1)}, u32[]{:S(2)}) %copy-start) | copy-done | bytes 12582936
  5.8 3.1 %shard_map.58 = bf16[768,3072]{1,0:T(8,128)(2,1)} custom-call(s32[2]{0:T(128)S(1)} %pad_add_fusion.place, bf16[768,8192]{1,0:T(8,128)(2,1)S(1)} %copy-done), custom_call_target="tpu_custom_call" | custom-call | bytes 4718592 | tf_op jit(solution)/shard_map/pallas_call | solution.py:79
  8.9 2.6 %collective-permute-start.3 = (bf16[768,3072]{1,0:T(8,128)(2,1)}, bf16[768,3072]{1,0:T(8,128)(2,1)}, u32[]{:S(2)}, u32[]{:S(2)}) collective-permute-start(bf16[768,3072]{1,0:T(8,128)(2,1)} %shard_map.58), channel_id=1, source_target_pairs={{0,2},{1,3},{2,0},{3,1},{4,6},{5,7},{6,4},{7,5},{8,10},{9,11},{10,... | collective-permute-start | bytes 14155784 | tf_op jit(solution)/shard_map/ppermute | solution.py:22
  11.5 3.1 %shard_map.59 = bf16[768,3072]{1,0:T(8,128)(2,1)} custom-call(s32[2]{0:T(128)S(1)} %pad_add_fusion.place, bf16[768,8192]{1,0:T(8,128)(2,1)S(1)} %copy-done), custom_call_target="tpu_custom_call" | custom-call | bytes 4718592 | tf_op jit(solution)/shard_map/pallas_call | solution.py:79
  14.6 3.7 %collective-permute-start = (bf16[768,3072]{1,0:T(8,128)(2,1)}, bf16[768,3072]{1,0:T(8,128)(2,1)}, u32[]{:S(2)}, u32[]{:S(2)}) collective-permute-start(bf16[768,3072]{1,0:T(8,128)(2,1)} %shard_map.59), channel_id=1, source_target_pairs={{0,12},{1,13},{2,6},{3,7},{4,0},{5,1},{6,10},{7,11},{8,4},{9,5},{1... | collective-permute-start | bytes 14155784 | tf_op jit(solution)/shard_map/ppermute | solution.py:22
  18.2 2.6 %shard_map.60 = (bf16[768,1024]{1,0:T(8,128)(2,1)}, bf16[768,1024]{1,0:T(8,128)(2,1)}) custom-call(s32[2]{0:T(128)S(1)} %pad_add_fusion.place, bf16[768,8192]{1,0:T(8,128)(2,1)S(1)} %copy-done), custom_call_target="tpu_custom_call" | custom-call | bytes 3145728 | tf_op jit(solution)/shard_map/pallas_call | solution.py:79
  21.5 7.2 %multiply_reduce_fusion = f32[768]{0:T(1024)S(1)} fusion(bf16[768,8192]{1,0:T(8,128)(2,1)} %own.7), kind=kLoop, calls=%fused_computation | loop fusion | flops 18873600 | bytes 12585984 | tf_op jit(solution)/shard_map/reduce_sum | solution.py:31
  29.2 7.1 %fusion.3 = f32[64,128]{1,0:T(8,128)S(1)} fusion(bf16[768,8192]{1,0:T(8,128)(2,1)} %own.7, bf16[128,8192]{1,0:T(8,128)(2,1)S(1)} %copy-done.1, f32[128]{0:T(128)S(1)} %add_rsqrt_fusion.1, f32[768]{0:T(1024)S(1)} %add_rsqrt_fusion, s32[768]{0:T(1024)S(1)} %copy-done.2), kind=kOutput, calls=%fused_computation.6 | convolution fusion | flops 1623638016 | bytes 14719488 | tf_op jit(solution)/shard_map/dot_general | solution.py:309
  36.3 14.8 %fusion.9.local = f32[768,768]{1,0:T(8,128)S(1)} fusion(bf16[768,8192]{1,0:T(8,128)(2,1)} %own.7, bf16[768,8192]{1,0:T(8,128)(2,1)} %collective-permute-done.4), kind=kOutput, calls=%fused_computation.26 | convolution fusion | flops 9663676416 | bytes 27525120 | tf_op jit(solution)/shard_map/dot_general | solution.py:35
  51.1 63.4 %collective-permute-done.3.partner = bf16[768,3072]{1,0:T(8,128)(2,1)} collective-permute-done((bf16[768,3072]{1,0:T(8,128)(2,1)}, bf16[768,3072]{1,0:T(8,128)(2,1)}, u32[]{:S(2)}, u32[]{:S(2)}) %collective-permute-start.3) | collective-permute-done | bytes 4718624 | tf_op jit(solution)/shard_map/ppermute | solution.py:22
  114.5 6.3 %collective-permute-done.near.near1 = bf16[768,3072]{1,0:T(8,128)(2,1)} collective-permute-done((bf16[768,3072]{1,0:T(8,128)(2,1)}, bf16[768,3072]{1,0:T(8,128)(2,1)}, u32[]{:S(2)}, u32[]{:S(2)}) %collective-permute-start) | collective-permute-done | bytes 4718624 | tf_op jit(solution)/shard_map/ppermute | solution.py:22
  120.7 11.3 %shard_map.61 = (f32[768,768]{1,0:T(8,128)S(1)}, f32[768,768]{1,0:T(8,128)S(1)}) custom-call(s32[2]{0:T(128)S(1)} %pad_add_fusion.place, bf16[768,8192]{1,0:T(8,128)(2,1)} %own.7, bf16[768,3072]{1,0:T(8,128)(2,1)} %collective-permute-done.3.partner, bf16[768,3072]{1,0:T(8,128)(2,1)} %collective-permute-done.near.near1), custom_call_target="tpu_custom_call" | custom-call | flops 768 | bytes 768 | tf_op jit(solution)/shard_map/pallas_call | solution.py:110
  133.5 14.4 %collective-permute-done.1.partner = bf16[768,1024]{1,0:T(8,128)(2,1)} collective-permute-done((bf16[768,1024]{1,0:T(8,128)(2,1)}, bf16[768,1024]{1,0:T(8,128)(2,1)}, u32[]{:S(2)}, u32[]{:S(2)}) %collective-permute-start.1) | collective-permute-done | bytes 1572896 | tf_op jit(solution)/shard_map/ppermute | solution.py:22
  149.7 4.2 %collective-permute-done.2.near.near2 = bf16[768,1024]{1,0:T(8,128)(2,1)} collective-permute-done((bf16[768,1024]{1,0:T(8,128)(2,1)}, bf16[768,1024]{1,0:T(8,128)(2,1)}, u32[]{:S(2)}, u32[]{:S(2)}) %collective-permute-start.2) | collective-permute-done | bytes 1572896 | tf_op jit(solution)/shard_map/ppermute | solution.py:22
  154.8 6.6 %shard_map.62 = (bf16[768,768]{1,0:T(8,128)(2,1)}, bf16[768,768]{1,0:T(8,128)(2,1)}) custom-call(s32[2]{0:T(128)S(1)} %pad_add_fusion.place, bf16[768,1024]{1,0:T(8,128)(2,1)} %get-tuple-element.38.mine, bf16[768,1024]{1,0:T(8,128)(2,1)} %collective-permute-done.1.partner, bf16[768,1024]{1,0:T(8,128)(2,1)} %collective-permute-done.2.near.near2, ...), custom_call_target="tpu_custom_call" | custom-call | flops 35389440000 | bytes 94371840 | tf_op jit(solution)/shard_map/pallas_call | solution.py:142
  162.3 2.2 collective-permute-start.13
  164.7 2.1 collective-permute-start.11
  166.9 12.4 %shard_map.63 = bf16[768,768]{1,0:T(8,128)(2,1)} custom-call(s32[2]{0:T(128)S(1)} %pad_add_fusion.place, bf16[768,8192]{1,0:T(8,128)(2,1)} %own.7, bf16[768,3072]{1,0:T(8,128)(2,1)} %collective-permute-done.near.near1, bf16[768,1024]{1,0:T(8,128)(2,1)} %collective-permute-done.2.near.near2, bf16[768,3072]{1,0:T(8,128)(2,1)} %collective-permute-done.8.other1, ...), custom_call_target="tpu_custom_call" | custom-call | flops 3623878656 | bytes 14155776 | tf_op jit(solution)/shard_map/pallas_call | solution.py:181
  182.5 7.9 %collective-permute-done.12.u = bf16[768,768]{1,0:T(8,128)(2,1)} collective-permute-done((bf16[768,768]{1,0:T(8,128)(2,1)}, bf16[768,768]{1,0:T(8,128)(2,1)}, u32[]{:S(2)}, u32[]{:S(2)}) %collective-permute-start.12) | collective-permute-done | bytes 1179680 | tf_op jit(solution)/shard_map/ppermute | solution.py:22
  190.3 4.1 %collective-permute-done.13.v = bf16[768,768]{1,0:T(8,128)(2,1)} collective-permute-done((bf16[768,768]{1,0:T(8,128)(2,1)}, bf16[768,768]{1,0:T(8,128)(2,1)}, u32[]{:S(2)}, u32[]{:S(2)}) %collective-permute-start.13) | collective-permute-done | bytes 1179680 | tf_op jit(solution)/shard_map/ppermute | solution.py:22
  194.5 5.2 %shard_map.64 = (f32[2,768,768]{2,1,0:T(8,128)}, f32[1,768]{1,0:T(1,128)S(1)}, f32[1,768]{1,0:T(1,128)S(1)}) custom-call(bf16[768,768]{1,0:T(8,128)(2,1)} %collective-permute-done.12.u, bf16[768,768]{1,0:T(8,128)(2,1)} %collective-permute-done.13.v, f32[768,1]{1,0:T(8,128)S(1)} %rsqrt.24.inverse, f32[1,768]{1,0:T(1,128)S(1)} %broadcast_in_dim.4.behind), custom_call_target="tpu_custom_call" | custom-call | flops 35389440000 | bytes 94371840 | tf_op jit(solution)/shard_map/pallas_call | solution.py:235
  199.7 4.9 %collective-permute-start.14 = (f32[8,128]{1,0:T(8,128)S(1)}, f32[8,128]{1,0:T(8,128)S(1)}, u32[]{:S(2)}, u32[]{:S(2)}) collective-permute-start(f32[8,128]{1,0:T(8,128)S(1)} %constant_dynamic-slice_fusion.1), channel_id=1, source_target_pairs={{0,2},{1,3},{2,0},{3,1},{4,6},{5,7},{6,4},{7,5},{8,10},{9,11},{10,... | collective-permute-start | bytes 12296 | tf_op jit(solution)/shard_map/ppermute | solution.py:22
  207.2 5.8 %shard_map.65 = (f32[2,768,768]{2,1,0:T(8,128)}, f32[1,768]{1,0:T(1,128)S(1)}, f32[1,768]{1,0:T(1,128)S(1)}) custom-call(s32[2]{0:T(128)S(1)} %pad_add_fusion.place, bf16[768,768]{1,0:T(8,128)(2,1)} %collective-permute-done.10.y, bf16[768,768]{1,0:T(8,128)(2,1)} %collective-permute-done.15.z, ...), custom_call_target="tpu_custom_call", output_to_operand_aliasing={{0}: (6, {})} | custom-call | flops 4718592 | bytes 7077888 | tf_op jit(solution)/shard_map/pallas_call | solution.py:255
  213.0 3.6 %collective-permute-start.17 = (f32[768]{0:T(1024)S(1)}, f32[768]{0:T(1024)S(1)}, u32[]{:S(2)}, u32[]{:S(2)}) collective-permute-start(f32[768]{0:T(1024)S(1)} %reduce.2), channel_id=1, source_target_pairs={{0,14},{1,15},{2,0},{3,1},{4,2},{5,3},{6,4},{7,5},{8,6},{9,7},{10,... | collective-permute-start | bytes 9224 | tf_op jit(solution)/shard_map/ppermute | solution.py:22
  (50 shorter events, 15.0 us)
Async XLA Ops:
  0.6 35.7 %collective-permute-start.4 = (bf16[768,8192]{1,0:T(8,128)(2,1)}, bf16[768,8192]{1,0:T(8,128)(2,1)}, u32[]{:S(2)}, u32[]{:S(2)}) collective-permute-start(bf16[768,8192]{1,0:T(8,128)(2,1)} %own.7), channel_id=1, source_target_pairs={{0,1},{1,0},{2,3},{3,2},{4,5},{5,4},{6,7},{7,6},{8,9},{9,8},{10,11... | collective-permute-start | bytes 37748744 | tf_op jit(solution)/shard_map/ppermute | solution.py:22
  1.2 4.6 %copy-start = (bf16[768,8192]{1,0:T(8,128)(2,1)S(1)}, bf16[768,8192]{1,0:T(8,128)(2,1)}, u32[]{:S(2)}) copy-start(bf16[768,8192]{1,0:T(8,128)(2,1)} %own.7) | copy-start | bytes 37748740
  8.9 105.6 %collective-permute-start.3 = (bf16[768,3072]{1,0:T(8,128)(2,1)}, bf16[768,3072]{1,0:T(8,128)(2,1)}, u32[]{:S(2)}, u32[]{:S(2)}) collective-permute-start(bf16[768,3072]{1,0:T(8,128)(2,1)} %shard_map.58), channel_id=1, source_target_pairs={{0,2},{1,3},{2,0},{3,1},{4,6},{5,7},{6,4},{7,5},{8,10},{9,11},{10,... | collective-permute-start | bytes 14155784 | tf_op jit(solution)/shard_map/ppermute | solution.py:22
  14.6 106.1 %collective-permute-start = (bf16[768,3072]{1,0:T(8,128)(2,1)}, bf16[768,3072]{1,0:T(8,128)(2,1)}, u32[]{:S(2)}, u32[]{:S(2)}) collective-permute-start(bf16[768,3072]{1,0:T(8,128)(2,1)} %shard_map.59), channel_id=1, source_target_pairs={{0,12},{1,13},{2,6},{3,7},{4,0},{5,1},{6,10},{7,11},{8,4},{9,5},{1... | collective-permute-start | bytes 14155784 | tf_op jit(solution)/shard_map/ppermute | solution.py:22
  20.9 127.1 %collective-permute-start.1 = (bf16[768,1024]{1,0:T(8,128)(2,1)}, bf16[768,1024]{1,0:T(8,128)(2,1)}, u32[]{:S(2)}, u32[]{:S(2)}) collective-permute-start(bf16[768,1024]{1,0:T(8,128)(2,1)} %get-tuple-element.37), channel_id=1, source_target_pairs={{0,2},{1,3},{2,0},{3,1},{4,6},{5,7},{6,4},{7,5},{8,10},{9,11},{10,... | collective-permute-start | bytes 4718600 | tf_op jit(solution)/shard_map/ppermute | solution.py:22
  20.9 7.8 %copy-start.1 = (bf16[128,8192]{1,0:T(8,128)(2,1)S(1)}, bf16[128,8192]{1,0:T(8,128)(2,1)}, u32[]{:S(2)}) copy-start(bf16[128,8192]{1,0:T(8,128)(2,1)} %param.4) | copy-start | bytes 6291460
  21.0 8.2 %copy-start.2 = (s32[768]{0:T(1024)S(1)}, s32[768]{0:T(1024)}, u32[]{:S(2)}) copy-start(s32[768]{0:T(1024)} %param.5) | copy-start | bytes 9220
  21.0 132.9 %collective-permute-start.2 = (bf16[768,1024]{1,0:T(8,128)(2,1)}, bf16[768,1024]{1,0:T(8,128)(2,1)}, u32[]{:S(2)}, u32[]{:S(2)}) collective-permute-start(bf16[768,1024]{1,0:T(8,128)(2,1)} %get-tuple-element.38.mine), channel_id=1, source_target_pairs={{0,12},{1,13},{2,6},{3,7},{4,0},{5,1},{6,10},{7,11},{8,4},{9,5},{1... | collective-permute-start | bytes 4718600 | tf_op jit(solution)/shard_map/ppermute | solution.py:22
  114.5 52.4 %collective-permute-start.8 = (bf16[768,3072]{1,0:T(8,128)(2,1)}, bf16[768,3072]{1,0:T(8,128)(2,1)}, u32[]{:S(2)}, u32[]{:S(2)}) collective-permute-start(bf16[768,3072]{1,0:T(8,128)(2,1)} %collective-permute-done.3.partner), channel_id=1, source_target_pairs={{0,1},{1,0},{2,3},{3,2},{4,5},{5,4},{6,7},{7,6},{8,9},{9,8},{10,11... | collective-permute-start | bytes 14155784 | tf_op jit(solution)/shard_map/ppermute | solution.py:22
  132.0 22.8 %collective-permute-start.7 = (f32[32,128]{1,0:T(8,128)S(1)}, f32[32,128]{1,0:T(8,128)S(1)}, u32[]{:S(2)}, u32[]{:S(2)}) collective-permute-start(f32[32,128]{1,0:T(8,128)S(1)} %constant_dynamic-slice_fusion.3), channel_id=1, source_target_pairs={{0,8},{1,9},{2,10},{3,11},{4,12},{5,13},{6,14},{7,15},{8,0},{9,1},... | collective-permute-start | bytes 49160 | tf_op jit(solution)/shard_map/ppermute | solution.py:22
  133.5 20.8 %collective-permute-start.5 = (f32[768]{0:T(1024)S(1)}, f32[768]{0:T(1024)S(1)}, u32[]{:S(2)}, u32[]{:S(2)}) collective-permute-start(f32[768]{0:T(1024)S(1)} %add_rsqrt_fusion), channel_id=1, source_target_pairs={{0,1},{1,2},{2,3},{3,4},{4,5},{5,6},{6,7},{7,8},{8,9},{9,10},{10,1... | collective-permute-start | bytes 9224 | tf_op jit(solution)/shard_map/ppermute | solution.py:22
  147.9 6.9 %collective-permute-start.6 = (f32[768]{0:T(1024)S(1)}, f32[768]{0:T(1024)S(1)}, u32[]{:S(2)}, u32[]{:S(2)}) collective-permute-start(f32[768]{0:T(1024)S(1)} %add_rsqrt_fusion), channel_id=1, source_target_pairs={{0,2},{1,3},{2,4},{3,5},{4,6},{5,7},{6,8},{7,9},{8,10},{9,11},{10,... | collective-permute-start | bytes 9224 | tf_op jit(solution)/shard_map/ppermute | solution.py:22
  154.8 12.0 %collective-permute-start.9 = (bf16[768,1024]{1,0:T(8,128)(2,1)}, bf16[768,1024]{1,0:T(8,128)(2,1)}, u32[]{:S(2)}, u32[]{:S(2)}) collective-permute-start(bf16[768,1024]{1,0:T(8,128)(2,1)} %collective-permute-done.1.partner), channel_id=1, source_target_pairs={{0,1},{1,0},{2,3},{3,2},{4,5},{5,4},{6,7},{7,6},{8,9},{9,8},{10,11... | collective-permute-start | bytes 4718600 | tf_op jit(solution)/shard_map/ppermute | solution.py:22
  161.5 28.9 %collective-permute-start.12 = (bf16[768,768]{1,0:T(8,128)(2,1)}, bf16[768,768]{1,0:T(8,128)(2,1)}, u32[]{:S(2)}, u32[]{:S(2)}) collective-permute-start(bf16[768,768]{1,0:T(8,128)(2,1)} %get-tuple-element.48), channel_id=1, source_target_pairs={{0,2},{1,3},{2,0},{3,1},{4,6},{5,7},{6,4},{7,5},{8,10},{9,11},{10,... | collective-permute-start | bytes 3538952 | tf_op jit(solution)/shard_map/ppermute | solution.py:22
  162.3 32.2 %collective-permute-start.13 = (bf16[768,768]{1,0:T(8,128)(2,1)}, bf16[768,768]{1,0:T(8,128)(2,1)}, u32[]{:S(2)}, u32[]{:S(2)}) collective-permute-start(bf16[768,768]{1,0:T(8,128)(2,1)} %get-tuple-element.53), channel_id=1, source_target_pairs={{0,4},{1,5},{2,2},{3,3},{4,8},{5,9},{6,6},{7,7},{8,12},{9,13},{10,... | collective-permute-start | bytes 3538952 | tf_op jit(solution)/shard_map/ppermute | solution.py:22
  164.7 35.0 %collective-permute-start.11 = (f32[16,128]{1,0:T(8,128)S(1)}, f32[16,128]{1,0:T(8,128)S(1)}, u32[]{:S(2)}, u32[]{:S(2)}) collective-permute-start(f32[16,128]{1,0:T(8,128)S(1)} %constant_dynamic-slice_fusion.2), channel_id=1, source_target_pairs={{0,4},{1,5},{2,6},{3,7},{4,0},{5,1},{6,2},{7,3},{8,12},{9,13},{10,... | collective-permute-start | bytes 24584 | tf_op jit(solution)/shard_map/ppermute | solution.py:22
  179.3 26.9 %collective-permute-start.10 = (bf16[768,768]{1,0:T(8,128)(2,1)}, bf16[768,768]{1,0:T(8,128)(2,1)}, u32[]{:S(2)}, u32[]{:S(2)}) collective-permute-start(bf16[768,768]{1,0:T(8,128)(2,1)} %shard_map.63), channel_id=1, source_target_pairs={{1,2},{3,0},{5,6},{7,4},{9,10},{11,8},{13,14},{15,12},{17,18},{19,... | collective-permute-start | bytes 3538952 | tf_op jit(solution)/shard_map/ppermute | solution.py:22
  180.5 26.7 %collective-permute-start.15 = (bf16[768,768]{1,0:T(8,128)(2,1)}, bf16[768,768]{1,0:T(8,128)(2,1)}, u32[]{:S(2)}, u32[]{:S(2)}) collective-permute-start(bf16[768,768]{1,0:T(8,128)(2,1)} %shard_map.63), channel_id=1, source_target_pairs={{0,4},{2,2},{4,8},{6,6},{8,12},{10,10},{12,0},{14,14},{16,20},{18,... | collective-permute-start | bytes 3538952 | tf_op jit(solution)/shard_map/ppermute | solution.py:22
  199.7 6.4 %collective-permute-start.14 = (f32[8,128]{1,0:T(8,128)S(1)}, f32[8,128]{1,0:T(8,128)S(1)}, u32[]{:S(2)}, u32[]{:S(2)}) collective-permute-start(f32[8,128]{1,0:T(8,128)S(1)} %constant_dynamic-slice_fusion.1), channel_id=1, source_target_pairs={{0,2},{1,3},{2,0},{3,1},{4,6},{5,7},{6,4},{7,5},{8,10},{9,11},{10,... | collective-permute-start | bytes 12296 | tf_op jit(solution)/shard_map/ppermute | solution.py:22
  213.0 3.8 %collective-permute-start.18 = (f32[4,128]{1,0:T(4,128)S(1)}, f32[4,128]{1,0:T(4,128)S(1)}, u32[]{:S(2)}, u32[]{:S(2)}) collective-permute-start(f32[4,128]{1,0:T(4,128)S(1)} %constant_dynamic-slice_fusion), channel_id=1, source_target_pairs={{0,1},{1,0},{2,3},{3,2},{4,5},{5,4},{6,7},{7,6},{8,9},{9,8},{10,11... | collective-permute-start | bytes 6152 | tf_op jit(solution)/shard_map/ppermute | solution.py:22
  213.0 4.9 %collective-permute-start.17 = (f32[768]{0:T(1024)S(1)}, f32[768]{0:T(1024)S(1)}, u32[]{:S(2)}, u32[]{:S(2)}) collective-permute-start(f32[768]{0:T(1024)S(1)} %reduce.2), channel_id=1, source_target_pairs={{0,14},{1,15},{2,0},{3,1},{4,2},{5,3},{6,4},{7,5},{8,6},{9,7},{10,... | collective-permute-start | bytes 9224 | tf_op jit(solution)/shard_map/ppermute | solution.py:22
  216.6 1.5 collective-permute-start.16

commit v7 on v6

--- a/solution.py
+++ b/solution.py
@@ -11,11 +11,11 @@
 ROUNDS = 2
 DOM_DEV = 4
 DEPTH = 1024
-TALL = 128
+TALL = 384
 BAND = 256
 PIECES = 4
 NT = (((1,), (1,)), ((), ()))
-VMEM_LIMIT = 36 * 2**20
+VMEM_LIMIT = 40 * 2**20
 
 
 def send(value, pairs):
@@ -52,38 +52,46 @@
 
 def halves_kernel(start, sides, place, own, *rest):
     count = len(sides)
-    outs, reads = rest[:count], rest[count]
+    outs, (buffer, reads, writes) = rest[:count], rest[count:]
     rows, width = outs[0].shape
     half = own.shape[1] // 2
     piece = rows // PIECES
-    copies = []
+    inward, outward = [], []
     for number, (side, out) in enumerate(zip(sides, outs)):
         left = pl.multiple_of(((place[0] + side) % 2) * half + start, 128)
         for i in range(PIECES):
             part = pl.ds(i * piece, piece)
-            copies.append(
-                pltpu.make_async_copy(
-                    own.at[part, pl.ds(left, width)],
-                    out.at[part],
-                    reads.at[number * PIECES + i],
-                )
+            slot = number * PIECES + i
+            held = buffer.at[number, part]
+            inward.append(
+                pltpu.make_async_copy(own.at[part, pl.ds(left, width)], held, reads.at[slot])
             )
-    for copy in copies:
+            outward.append(pltpu.make_async_copy(held, out.at[part], writes.at[slot]))
+    for copy in inward:
         copy.start()
-    for copy in copies:
+    for arrived, copy in zip(inward, outward):
+        arrived.wait()
+        copy.start()
+    for copy in outward:
         copy.wait()
 
 
 def halves(place, own, start, width, sides):
     rows = own.shape[0]
+    slots = PIECES * len(sides)
+    anywhere = pl.BlockSpec(memory_space=pltpu.HBM)
     return pl.pallas_call(
         functools.partial(halves_kernel, start, sides),
-        in_specs=[pl.BlockSpec(memory_space=pltpu.SMEM), pl.BlockSpec(memory_space=pltpu.HBM)],
-        out_specs=[pl.BlockSpec(memory_space=pltpu.VMEM)] * len(sides),
-        out_shape=[pltpu.VMEM((rows, width), own.dtype) for _ in sides],
-        scratch_shapes=[pltpu.SemaphoreType.DMA((PIECES * len(sides),))],
-        compiler_params=params(),
-        cost_estimate=cost(0, 2 * rows * width * len(sides)),
+        in_specs=[pl.BlockSpec(memory_space=pltpu.SMEM), anywhere],
+        out_specs=[anywhere] * len(sides),
+        out_shape=[jax.ShapeDtypeStruct((rows, width), own.dtype) for _ in sides],
+        scratch_shapes=[
+            pltpu.VMEM((len(sides), rows, width), own.dtype),
+            pltpu.SemaphoreType.DMA((slots,)),
+            pltpu.SemaphoreType.DMA((slots,)),
+        ],
+        compiler_params=params(),
+        cost_estimate=cost(0, 4 * rows * width * len(sides)),
     )(place, own)
 
 
@@ -206,16 +214,18 @@
     row_mass[...] = jnp.broadcast_to(sums, (size, size)).T[0:1]
 
 
-def second_kernel(scale, u, v, inverse, behind, gram, row_mass, column_mass):
-    tile = u[...].astype(jnp.float32) + v[...].astype(jnp.float32)
+def second_kernel(scale, place, u, v, kept, inverse, behind, gram, row_mass, column_mass):
+    other = jnp.where(place[0] == 1, kept[...], v[...])
+    tile = u[...].astype(jnp.float32) + other.astype(jnp.float32)
     finish(tile * inverse[...] * behind[...] * scale, gram, row_mass, column_mass)
 
 
 def first_kernel(
-    scale, place, y, z, local, inverse, behind, gram_in, gram, row_mass, column_mass
+    scale, place, y, z, kept, local, inverse, behind, gram_in, gram, row_mass, column_mass
 ):
     del gram_in
-    tile = y[...].astype(jnp.float32) + z[...].astype(jnp.float32)
+    other = jnp.where(place[0] == 1, kept[...], z[...])
+    tile = y[...].astype(jnp.float32) + other.astype(jnp.float32)
     tile = jnp.where(place[1] == 1, local[...], tile)
     finish(tile * inverse[...] * behind[...] * scale, gram, row_mass, column_mass)
 
@@ -228,48 +238,29 @@
     return specs, [jax.ShapeDtypeStruct((1, rows), jnp.float32)] * 2
 
 
-def second_tiles(scale, u, v, inverse, behind):
-    rows = u.shape[0]
-    block = pl.BlockSpec((TALL, rows), lambda j: (j, 0))
+def join(kernel, index, scale, place, tiles, inverse, behind, gram=()):
+    rows = tiles[0].shape[0]
     mass_specs, mass_types = mass_shapes(rows)
     return pl.pallas_call(
-        functools.partial(second_kernel, scale),
-        grid=(rows // TALL,),
-        in_specs=[
-            block,
-            block,
-            pl.BlockSpec((TALL, 1), lambda j: (j, 0)),
-            pl.BlockSpec((1, rows), lambda j: (0, 0)),
-        ],
-        out_specs=[pl.BlockSpec((1, TALL, rows), lambda j: (1, j, 0))] + mass_specs,
-        out_shape=[jax.ShapeDtypeStruct((2, rows, rows), jnp.float32)] + mass_types,
-        compiler_params=params(),
-        cost_estimate=cost(60000 * rows * rows, 160 * rows * rows),
-    )(u, v, inverse[:, None], behind[None, :])
-
-
-def first_tiles(scale, place, y, z, local, inverse, behind, gram):
-    rows = y.shape[0]
-    block = pl.BlockSpec((TALL, rows), lambda j, place: (j, 0))
-    mass_specs, mass_types = mass_shapes(rows)
-    return pl.pallas_call(
-        functools.partial(first_kernel, scale),
+        functools.partial(kernel, scale),
         grid_spec=pltpu.PrefetchScalarGridSpec(
             num_scalar_prefetch=1,
             grid=(rows // TALL,),
-            in_specs=[block] * 3
+            in_specs=[pl.BlockSpec((TALL, rows), lambda j, place: (j, 0))] * len(tiles)
             + [
                 pl.BlockSpec((TALL, 1), lambda j, place: (j, 0)),
                 pl.BlockSpec((1, rows), lambda j, place: (0, 0)),
-                pl.BlockSpec(memory_space=pl.ANY),
-            ],
-            out_specs=[pl.BlockSpec((1, TALL, rows), lambda j, place: (0, j, 0))] + mass_specs,
+            ]
+            + [pl.BlockSpec(memory_space=pl.ANY)] * len(gram),
+            out_specs=[pl.BlockSpec((1, TALL, rows), lambda j, place: (index, j, 0))] + mass_specs,
         ),
         out_shape=[jax.ShapeDtypeStruct((2, rows, rows), jnp.float32)] + mass_types,
-        input_output_aliases={6: 0},
-        compiler_params=params(),
-        cost_estimate=cost(8 * rows * rows, 12 * rows * rows),
-    )(place, y, z, local, inverse[:, None], behind[None, :], gram)
+        input_output_aliases={len(tiles) + 3: 0} if gram else {},
+        compiler_params=params(),
+        cost_estimate=cost(60000 * rows * rows, 160 * rows * rows)
+        if index
+        else cost(8 * rows * rows, 12 * rows * rows),
+    )(place, *tiles, inverse[:, None], behind[None, :], *gram)
 
 
 def local(sketches, test_sketches, domain_map):
@@ -288,9 +279,8 @@
     swap = [(i, i ^ 1) for i in blocks]
 
     even = send(sketches, swap)
-    (out1,) = halves(place, sketches, 0, first, (1,))
+    out1, side1 = halves(place, sketches, 0, first, (1, 0))
     partner1 = send(out1, across)
-    (side1,) = halves(place, after(sketches, out1), 0, first, (0,))
     near1 = send(side1, along)
     out2, side2 = halves(place, after(sketches, side1), first, DEPTH, (1, 0))
     partner2 = send(out2, across)
@@ -311,7 +301,6 @@
     )
     inside = nt(sketches, even)
 
-
     def halve(value, bit, *waits):
         count = value.shape[0] // 2
         mine = (index // bit) % 2
@@ -320,7 +309,7 @@
         return kept, send(after(away, *waits), [(i, i ^ bit) for i in blocks])
 
     bits = [size >> (step + 1) for step in range(size.bit_length() - 1)]
-    back_v = [(i, i) if i & 2 else (i, (i + 4) % size) for i in blocks]
+    back_v = [(i, (i + 4) % size) for i in blocks if not i & 2]
     back_y = [(i, i ^ 3) for i in blocks if i & 1]
     back_z = [pair for pair in back_v if pair[0] % 2 == 0]
     partner1 = after(partner1, inside, sums)
@@ -342,11 +331,13 @@
     x = cross_tile(place, sketches, near1, near2, after(other1, u), after(other2, u))
     y, z = send(x, back_y), send(x, back_z)
 
-    gram, row_mass2, column_mass2 = second_tiles(scale, ur, vr, inverse, behind2)
+    gram, row_mass2, column_mass2 = join(
+        second_kernel, 1, scale, place, (ur, vr, v), inverse, behind2
+    )
     kept, came = halve(kept + after(came, row_mass2), bits[-2])
     y, sums = lax.optimization_barrier((y, kept + came))
-    gram, row_mass1, column_mass1 = first_tiles(
-        scale, place, y, z, inside, inverse, behind1, gram
+    gram, row_mass1, column_mass1 = join(
+        first_kernel, 0, scale, place, (y, z, x, inside), inverse, behind1, (gram,)
     )
     kept, came = halve(sums, bits[-1], row_mass1)
     domain_scores = (kept + came) * (1.0 / math.sqrt(rows / DOM_DEV))

time: 222 us -> 216 us (0.973); the launches traced: 219 us -> 216 us
  starting transfers between devices: 27.6 us -> 20.3 us
  waiting for transfers between devices: 105 us -> 109 us
    ppermute x19, starting transfers between devices: 27.6 us -> 20.3 us  [send(): return lax.ppermute(value, 'blocks', pairs)]
    ppermute x19, waiting for transfers between devices: 105 us -> 109 us  [send(): return lax.ppermute(value, 'blocks', pairs)]
    pallas_call x2, Pallas kernels: 11 us -> 7.81 us  [join(): pl.pallas_call(functools.partial(kernel, scale), grid_spec=pltpu.Prefetch...]
    unnamed x6 -> x14, local copies, waits for them, and re-layouts: 4.59 us -> 1.6 us
    pallas_call x3 -> x2, Pallas kernels: 8.75 us -> 11.2 us  [halves(): pl.pallas_call(functools.partial(halves_kernel, start, sides), in_specs=[...]
  transfers between devices with their start and end apart: 19 -> 19, of which waited for: 12 -> 11; matrix products, arithmetic and copies ran while one was open for 14% -> 16% of each run, Pallas kernels for 20% -> 21%
where the time goes in v7:
time: 216 us
  waiting for transfers between devices  109 us (50%)
  Pallas kernels  48.6 us (22%)
  matrix products  21.9 us (10%)
  starting transfers between devices  20.3 us (9%)
  other arithmetic  11 us (5%)
  local copies, waits for them, and re-layouts  4.4 us (2%)
    ppermute x19, waiting for transfers between devices, send(): return lax.ppermute(value, 'blocks', pairs)  109 us
    ppermute x19, starting transfers between devices, send(): return lax.ppermute(value, 'blocks', pairs)  20.3 us
    dot_general x1, matrix products, nt(): return lax.dot_general(left, right, NT, preferred_element_type=jnp.float32)  14.8 us
    pallas_call x1, Pallas kernels, cross_tile(): pl.pallas_call(cross_kernel, grid_spec=pltpu.PrefetchScalarGridSpec(num_s...  11.4 us
    pallas_call x1, Pallas kernels, early_tiles(): pl.pallas_call(early_kernel, grid_spec=pltpu.PrefetchScalarGridSpec(num_s...  11.4 us
    pallas_call x2, Pallas kernels, halves(): pl.pallas_call(functools.partial(halves_kernel, start, sides), in_specs=[...  11.2 us
    pallas_call x2, Pallas kernels, join(): pl.pallas_call(functools.partial(kernel, scale), grid_spec=pltpu.Prefetch...  7.81 us
    reduce_sum x2, other arithmetic, inverse_norm(): return lax.rsqrt(jnp.mean(values * values, axis=1) + 1e-06)  7.7 us
  transfers between devices with their start and end apart: 19, of which 11 were waited for; matrix products, arithmetic and copies ran while one was open for 16% of the time, Pallas kernels for 21%

profile of v7, /device:TPU:0, one launch (start us, length us, event | category | flops | bytes accessed | tf_op | source)
XLA Modules:
  0.0 216.0 jit_solution(14336541085594152592)
XLA Ops:
  1.2 7.9 %shard_map.58 = (bf16[768,3072]{1,0:T(8,128)(2,1)}, bf16[768,3072]{1,0:T(8,128)(2,1)}) custom-call(s32[2]{0:T(128)S(1)} %pad_add_fusion.place, bf16[768,8192]{1,0:T(8,128)(2,1)} %own.6), custom_call_target="tpu_custom_call" | custom-call | bytes 18874368 | tf_op jit(solution)/shard_map/pallas_call | solution.py:83
  9.1 2.6 %collective-permute-start.3 = (bf16[768,3072]{1,0:T(8,128)(2,1)}, bf16[768,3072]{1,0:T(8,128)(2,1)}, u32[]{:S(2)}, u32[]{:S(2)}) collective-permute-start(bf16[768,3072]{1,0:T(8,128)(2,1)} %get-tuple-element.40), channel_id=1, source_target_pairs={{0,2},{1,3},{2,0},{3,1},{4,6},{5,7},{6,4},{7,5},{8,10},{9,11},{10,... | collective-permute-start | bytes 14155784 | tf_op jit(solution)/shard_map/ppermute | solution.py:22
  11.8 3.6 %collective-permute-start = (bf16[768,3072]{1,0:T(8,128)(2,1)}, bf16[768,3072]{1,0:T(8,128)(2,1)}, u32[]{:S(2)}, u32[]{:S(2)}) collective-permute-start(bf16[768,3072]{1,0:T(8,128)(2,1)} %get-tuple-element.36), channel_id=1, source_target_pairs={{0,12},{1,13},{2,6},{3,7},{4,0},{5,1},{6,10},{7,11},{8,4},{9,5},{1... | collective-permute-start | bytes 14155784 | tf_op jit(solution)/shard_map/ppermute | solution.py:22
  15.4 3.3 %shard_map.59 = (bf16[768,1024]{1,0:T(8,128)(2,1)}, bf16[768,1024]{1,0:T(8,128)(2,1)}) custom-call(s32[2]{0:T(128)S(1)} %pad_add_fusion.place, bf16[768,8192]{1,0:T(8,128)(2,1)} %own.6), custom_call_target="tpu_custom_call" | custom-call | bytes 6291456 | tf_op jit(solution)/shard_map/pallas_call | solution.py:83
  19.3 7.2 %multiply_reduce_fusion = f32[768]{0:T(1024)S(1)} fusion(bf16[768,8192]{1,0:T(8,128)(2,1)} %own.6), kind=kLoop, calls=%fused_computation | loop fusion | flops 18873600 | bytes 12585984 | tf_op jit(solution)/shard_map/reduce_sum | solution.py:31
  27.1 7.1 %fusion.3 = f32[64,128]{1,0:T(8,128)S(1)} fusion(bf16[768,8192]{1,0:T(8,128)(2,1)} %own.6, bf16[128,8192]{1,0:T(8,128)(2,1)S(1)} %copy-done.2, f32[128]{0:T(128)S(1)} %add_rsqrt_fusion.1, f32[768]{0:T(1024)S(1)} %add_rsqrt_fusion, s32[768]{0:T(1024)S(1)} %copy-done.6), kind=kOutput, calls=%fused_computation.6 | convolution fusion | flops 1623638016 | bytes 14719488 | tf_op jit(solution)/shard_map/dot_general | solution.py:299
  34.2 14.8 %fusion.9.local = f32[768,768]{1,0:T(8,128)S(1)} fusion(bf16[768,8192]{1,0:T(8,128)(2,1)} %own.6, bf16[768,8192]{1,0:T(8,128)(2,1)} %collective-permute-done.4), kind=kOutput, calls=%fused_computation.26 | convolution fusion | flops 9663676416 | bytes 27525120 | tf_op jit(solution)/shard_map/dot_general | solution.py:35
  49.0 65.7 %collective-permute-done.3.partner = bf16[768,3072]{1,0:T(8,128)(2,1)} collective-permute-done((bf16[768,3072]{1,0:T(8,128)(2,1)}, bf16[768,3072]{1,0:T(8,128)(2,1)}, u32[]{:S(2)}, u32[]{:S(2)}) %collective-permute-start.3) | collective-permute-done | bytes 4718624 | tf_op jit(solution)/shard_map/ppermute | solution.py:22
  114.8 3.1 %collective-permute-done.near.near1 = bf16[768,3072]{1,0:T(8,128)(2,1)} collective-permute-done((bf16[768,3072]{1,0:T(8,128)(2,1)}, bf16[768,3072]{1,0:T(8,128)(2,1)}, u32[]{:S(2)}, u32[]{:S(2)}) %collective-permute-start) | collective-permute-done | bytes 4718624 | tf_op jit(solution)/shard_map/ppermute | solution.py:22
  117.9 11.4 %shard_map.60 = (f32[768,768]{1,0:T(8,128)S(1)}, f32[768,768]{1,0:T(8,128)S(1)}) custom-call(s32[2]{0:T(128)S(1)} %pad_add_fusion.place, bf16[768,8192]{1,0:T(8,128)(2,1)} %own.6, bf16[768,3072]{1,0:T(8,128)(2,1)} %collective-permute-done.3.partner, bf16[768,3072]{1,0:T(8,128)(2,1)} %collective-permute-done.near.near1), custom_call_target="tpu_custom_call" | custom-call | flops 768 | bytes 768 | tf_op jit(solution)/shard_map/pallas_call | solution.py:118
  130.8 17.4 %collective-permute-done.1.partner = bf16[768,1024]{1,0:T(8,128)(2,1)} collective-permute-done((bf16[768,1024]{1,0:T(8,128)(2,1)}, bf16[768,1024]{1,0:T(8,128)(2,1)}, u32[]{:S(2)}, u32[]{:S(2)}) %collective-permute-start.1) | collective-permute-done | bytes 1572896 | tf_op jit(solution)/shard_map/ppermute | solution.py:22
  148.2 1.8 collective-permute-start.6
  151.5 3.2 %collective-permute-done.6 = f32[768]{0:T(1024)S(1)} collective-permute-done((f32[768]{0:T(1024)S(1)}, f32[768]{0:T(1024)S(1)}, u32[]{:S(2)}, u32[]{:S(2)}) %collective-permute-start.6) | collective-permute-done | bytes 3104 | tf_op jit(solution)/shard_map/ppermute | solution.py:22
  154.7 6.8 %shard_map.61 = (bf16[768,768]{1,0:T(8,128)(2,1)}, bf16[768,768]{1,0:T(8,128)(2,1)}) custom-call(s32[2]{0:T(128)S(1)} %pad_add_fusion.place, bf16[768,1024]{1,0:T(8,128)(2,1)} %get-tuple-element.39.mine, bf16[768,1024]{1,0:T(8,128)(2,1)} %collective-permute-done.1.partner, bf16[768,1024]{1,0:T(8,128)(2,1)} %collective-permute-done.2.near.near2, ...), custom_call_target="tpu_custom_call" | custom-call | flops 35389440000 | bytes 94371840 | tf_op jit(solution)/shard_map/pallas_call | solution.py:150
  161.4 2.5 %collective-permute-start.13 = (bf16[768,768]{1,0:T(8,128)(2,1)}, bf16[768,768]{1,0:T(8,128)(2,1)}, u32[]{:S(2)}, u32[]{:S(2)}) collective-permute-start(bf16[768,768]{1,0:T(8,128)(2,1)} %get-tuple-element.55.kept), channel_id=1, source_target_pairs={{0,4},{1,5},{4,8},{5,9},{8,12},{9,13},{12,0},{13,1},{16,20},{17,21... | collective-permute-start | bytes 3538952 | tf_op jit(solution)/shard_map/ppermute | solution.py:22
  166.5 11.4 %shard_map.62.kept = bf16[768,768]{1,0:T(8,128)(2,1)S(1)} custom-call(s32[2]{0:T(128)S(1)} %pad_add_fusion.place, bf16[768,8192]{1,0:T(8,128)(2,1)} %own.6, bf16[768,3072]{1,0:T(8,128)(2,1)} %collective-permute-done.near.near1, bf16[768,1024]{1,0:T(8,128)(2,1)} %collective-permute-done.2.near.near2, bf16[768,3072]{1,0:T(8,128)(2,1)} %collective-permute-done.8.other1, ...), custom_call_target="tpu_custom_call" | custom-call | flops 3623878656 | bytes 14155776 | tf_op jit(solution)/shard_map/pallas_call | solution.py:189
  179.2 2.4 %collective-permute-start.15 = (bf16[768,768]{1,0:T(8,128)(2,1)S(1)}, bf16[768,768]{1,0:T(8,128)(2,1)}, u32[]{:S(2)}, u32[]{:S(2)}) collective-permute-start(bf16[768,768]{1,0:T(8,128)(2,1)S(1)} %shard_map.62.kept), channel_id=1, source_target_pairs={{0,4},{4,8},{8,12},{12,0},{16,20},{20,24},{24,28},{28,16}} | collective-permute-start | bytes 3538952 | tf_op jit(solution)/shard_map/ppermute | solution.py:22
  181.5 8.9 %collective-permute-done.12.u = bf16[768,768]{1,0:T(8,128)(2,1)} collective-permute-done((bf16[768,768]{1,0:T(8,128)(2,1)}, bf16[768,768]{1,0:T(8,128)(2,1)}, u32[]{:S(2)}, u32[]{:S(2)}) %collective-permute-start.12) | collective-permute-done | bytes 1179680 | tf_op jit(solution)/shard_map/ppermute | solution.py:22
  190.5 3.4 %collective-permute-done.13.v = bf16[768,768]{1,0:T(8,128)(2,1)} collective-permute-done((bf16[768,768]{1,0:T(8,128)(2,1)}, bf16[768,768]{1,0:T(8,128)(2,1)}, u32[]{:S(2)}, u32[]{:S(2)}) %collective-permute-start.13) | collective-permute-done | bytes 1179680 | tf_op jit(solution)/shard_map/ppermute | solution.py:22
  193.9 3.9 %shard_map.63 = (f32[2,768,768]{2,1,0:T(8,128)}, f32[1,768]{1,0:T(1,128)S(1)}, f32[1,768]{1,0:T(1,128)S(1)}) custom-call(s32[2]{0:T(128)S(1)} %pad_add_fusion.place, bf16[768,768]{1,0:T(8,128)(2,1)} %collective-permute-done.12.u, bf16[768,768]{1,0:T(8,128)(2,1)} %collective-permute-done.13.v, bf16[768,768]{1,0:T(8,128)(2,1)} %get-tuple-element.55.kept, ...), custom_call_target="tpu_custom_call" | custom-call | flops 35389440000 | bytes 94371840 | tf_op jit(solution)/shard_map/pallas_call | solution.py:244
  200.3 2.6 %collective-permute-done.14 = f32[8,128]{1,0:T(8,128)} collective-permute-done((f32[8,128]{1,0:T(8,128)}, f32[8,128]{1,0:T(8,128)}, u32[]{:S(2)}, u32[]{:S(2)}) %collective-permute-start.14) | collective-permute-done | bytes 4128 | tf_op jit(solution)/shard_map/ppermute | solution.py:22
  204.2 2.4 %collective-permute-done.15.z = bf16[768,768]{1,0:T(8,128)(2,1)} collective-permute-done((bf16[768,768]{1,0:T(8,128)(2,1)S(1)}, bf16[768,768]{1,0:T(8,128)(2,1)}, u32[]{:S(2)}, u32[]{:S(2)}) %collective-permute-start.15) | collective-permute-done | bytes 1179680 | tf_op jit(solution)/shard_map/ppermute | solution.py:22
  207.6 3.9 %shard_map.64 = (f32[2,768,768]{2,1,0:T(8,128)}, f32[1,768]{1,0:T(1,128)S(1)}, f32[1,768]{1,0:T(1,128)S(1)}) custom-call(s32[2]{0:T(128)S(1)} %pad_add_fusion.place, bf16[768,768]{1,0:T(8,128)(2,1)} %collective-permute-done.10.y, bf16[768,768]{1,0:T(8,128)(2,1)} %collective-permute-done.15.z, ...), custom_call_target="tpu_custom_call", output_to_operand_aliasing={{0}: (7, {})} | custom-call | flops 4718592 | bytes 7077888 | tf_op jit(solution)/shard_map/pallas_call | solution.py:244
  211.6 1.8 collective-permute-start.16
  (57 shorter events, 16.0 us)
Async XLA Ops:
  0.6 33.6 %collective-permute-start.4 = (bf16[768,8192]{1,0:T(8,128)(2,1)}, bf16[768,8192]{1,0:T(8,128)(2,1)}, u32[]{:S(2)}, u32[]{:S(2)}) collective-permute-start(bf16[768,8192]{1,0:T(8,128)(2,1)} %own.6), channel_id=1, source_target_pairs={{0,1},{1,0},{2,3},{3,2},{4,5},{5,4},{6,7},{7,6},{8,9},{9,8},{10,11... | collective-permute-start | bytes 37748744 | tf_op jit(solution)/shard_map/ppermute | solution.py:22
  9.1 105.6 %collective-permute-start.3 = (bf16[768,3072]{1,0:T(8,128)(2,1)}, bf16[768,3072]{1,0:T(8,128)(2,1)}, u32[]{:S(2)}, u32[]{:S(2)}) collective-permute-start(bf16[768,3072]{1,0:T(8,128)(2,1)} %get-tuple-element.40), channel_id=1, source_target_pairs={{0,2},{1,3},{2,0},{3,1},{4,6},{5,7},{6,4},{7,5},{8,10},{9,11},{10,... | collective-permute-start | bytes 14155784 | tf_op jit(solution)/shard_map/ppermute | solution.py:22
  11.8 106.1 %collective-permute-start = (bf16[768,3072]{1,0:T(8,128)(2,1)}, bf16[768,3072]{1,0:T(8,128)(2,1)}, u32[]{:S(2)}, u32[]{:S(2)}) collective-permute-start(bf16[768,3072]{1,0:T(8,128)(2,1)} %get-tuple-element.36), channel_id=1, source_target_pairs={{0,12},{1,13},{2,6},{3,7},{4,0},{5,1},{6,10},{7,11},{8,4},{9,5},{1... | collective-permute-start | bytes 14155784 | tf_op jit(solution)/shard_map/ppermute | solution.py:22
  18.7 129.5 %collective-permute-start.1 = (bf16[768,1024]{1,0:T(8,128)(2,1)}, bf16[768,1024]{1,0:T(8,128)(2,1)}, u32[]{:S(2)}, u32[]{:S(2)}) collective-permute-start(bf16[768,1024]{1,0:T(8,128)(2,1)} %get-tuple-element.38), channel_id=1, source_target_pairs={{0,2},{1,3},{2,0},{3,1},{4,6},{5,7},{6,4},{7,5},{8,10},{9,11},{10,... | collective-permute-start | bytes 4718600 | tf_op jit(solution)/shard_map/ppermute | solution.py:22
  18.8 7.8 %copy-start.2 = (bf16[128,8192]{1,0:T(8,128)(2,1)S(1)}, bf16[128,8192]{1,0:T(8,128)(2,1)}, u32[]{:S(2)}) copy-start(bf16[128,8192]{1,0:T(8,128)(2,1)} %param.4) | copy-start | bytes 6291460
  18.8 8.2 %copy-start.6 = (s32[768]{0:T(1024)S(1)}, s32[768]{0:T(1024)}, u32[]{:S(2)}) copy-start(s32[768]{0:T(1024)} %param.5) | copy-start | bytes 9220
  18.8 132.2 %collective-permute-start.2 = (bf16[768,1024]{1,0:T(8,128)(2,1)}, bf16[768,1024]{1,0:T(8,128)(2,1)}, u32[]{:S(2)}, u32[]{:S(2)}) collective-permute-start(bf16[768,1024]{1,0:T(8,128)(2,1)} %get-tuple-element.39.mine), channel_id=1, source_target_pairs={{0,12},{1,13},{2,6},{3,7},{4,0},{5,1},{6,10},{7,11},{8,4},{9,5},{1... | collective-permute-start | bytes 4718600 | tf_op jit(solution)/shard_map/ppermute | solution.py:22
  114.8 51.7 %collective-permute-start.8 = (bf16[768,3072]{1,0:T(8,128)(2,1)}, bf16[768,3072]{1,0:T(8,128)(2,1)}, u32[]{:S(2)}, u32[]{:S(2)}) collective-permute-start(bf16[768,3072]{1,0:T(8,128)(2,1)} %collective-permute-done.3.partner), channel_id=1, source_target_pairs={{0,1},{1,0},{2,3},{3,2},{4,5},{5,4},{6,7},{7,6},{8,9},{9,8},{10,11... | collective-permute-start | bytes 14155784 | tf_op jit(solution)/shard_map/ppermute | solution.py:22
  129.3 25.4 %collective-permute-start.7 = (f32[32,128]{1,0:T(8,128)S(1)}, f32[32,128]{1,0:T(8,128)S(1)}, u32[]{:S(2)}, u32[]{:S(2)}) collective-permute-start(f32[32,128]{1,0:T(8,128)S(1)} %constant_dynamic-slice_fusion.3), channel_id=1, source_target_pairs={{0,8},{1,9},{2,10},{3,11},{4,12},{5,13},{6,14},{7,15},{8,0},{9,1},... | collective-permute-start | bytes 49160 | tf_op jit(solution)/shard_map/ppermute | solution.py:22
  130.8 20.7 %collective-permute-start.5 = (f32[768]{0:T(1024)S(1)}, f32[768]{0:T(1024)S(1)}, u32[]{:S(2)}, u32[]{:S(2)}) collective-permute-start(f32[768]{0:T(1024)S(1)} %add_rsqrt_fusion), channel_id=1, source_target_pairs={{0,1},{1,2},{2,3},{3,4},{4,5},{5,6},{6,7},{7,8},{8,9},{9,10},{10,1... | collective-permute-start | bytes 9224 | tf_op jit(solution)/shard_map/ppermute | solution.py:22
  148.2 6.4 %collective-permute-start.6 = (f32[768]{0:T(1024)S(1)}, f32[768]{0:T(1024)S(1)}, u32[]{:S(2)}, u32[]{:S(2)}) collective-permute-start(f32[768]{0:T(1024)S(1)} %add_rsqrt_fusion), channel_id=1, source_target_pairs={{0,2},{1,3},{2,4},{3,5},{4,6},{5,7},{6,8},{7,9},{8,10},{9,11},{10,... | collective-permute-start | bytes 9224 | tf_op jit(solution)/shard_map/ppermute | solution.py:22
  151.5 3.2 %copy-start.5 = (f32[768]{0:T(1024)}, f32[768]{0:T(1024)S(1)}, u32[]{:S(2)}) copy-start(f32[768]{0:T(1024)S(1)} %collective-permute-done.5) | copy-start | bytes 9220
  154.6 11.8 %collective-permute-start.9 = (bf16[768,1024]{1,0:T(8,128)(2,1)}, bf16[768,1024]{1,0:T(8,128)(2,1)}, u32[]{:S(2)}, u32[]{:S(2)}) collective-permute-start(bf16[768,1024]{1,0:T(8,128)(2,1)} %collective-permute-done.1.partner), channel_id=1, source_target_pairs={{0,1},{1,0},{2,3},{3,2},{4,5},{5,4},{6,7},{7,6},{8,9},{9,8},{10,11... | collective-permute-start | bytes 4718600 | tf_op jit(solution)/shard_map/ppermute | solution.py:22
  161.4 29.1 %collective-permute-start.12 = (bf16[768,768]{1,0:T(8,128)(2,1)}, bf16[768,768]{1,0:T(8,128)(2,1)}, u32[]{:S(2)}, u32[]{:S(2)}) collective-permute-start(bf16[768,768]{1,0:T(8,128)(2,1)} %get-tuple-element.50), channel_id=1, source_target_pairs={{0,2},{1,3},{2,0},{3,1},{4,6},{5,7},{6,4},{7,5},{8,10},{9,11},{10,... | collective-permute-start | bytes 3538952 | tf_op jit(solution)/shard_map/ppermute | solution.py:22
  161.4 32.5 %collective-permute-start.13 = (bf16[768,768]{1,0:T(8,128)(2,1)}, bf16[768,768]{1,0:T(8,128)(2,1)}, u32[]{:S(2)}, u32[]{:S(2)}) collective-permute-start(bf16[768,768]{1,0:T(8,128)(2,1)} %get-tuple-element.55.kept), channel_id=1, source_target_pairs={{0,4},{1,5},{4,8},{5,9},{8,12},{9,13},{12,0},{13,1},{16,20},{17,21... | collective-permute-start | bytes 3538952 | tf_op jit(solution)/shard_map/ppermute | solution.py:22
  164.8 29.0 %copy-start = (f32[768,1]{1,0:T(8,128)S(1)}, f32[768,1]{1,0:T(8,128)}, u32[]{:S(2)}) copy-start(f32[768,1]{1,0:T(8,128)} %rsqrt.24.inverse) | copy-start | bytes 9220
  164.8 32.9 %collective-permute-start.11 = (f32[16,128]{1,0:T(8,128)S(1)}, f32[16,128]{1,0:T(8,128)S(1)}, u32[]{:S(2)}, u32[]{:S(2)}) collective-permute-start(f32[16,128]{1,0:T(8,128)S(1)} %constant_dynamic-slice_fusion.2), channel_id=1, source_target_pairs={{0,4},{1,5},{2,6},{3,7},{4,0},{5,1},{6,2},{7,3},{8,12},{9,13},{10,... | collective-permute-start | bytes 24584 | tf_op jit(solution)/shard_map/ppermute | solution.py:22
  177.9 25.7 %collective-permute-start.10 = (bf16[768,768]{1,0:T(8,128)(2,1)S(1)}, bf16[768,768]{1,0:T(8,128)(2,1)}, u32[]{:S(2)}, u32[]{:S(2)}) collective-permute-start(bf16[768,768]{1,0:T(8,128)(2,1)S(1)} %shard_map.62.kept), channel_id=1, source_target_pairs={{1,2},{3,0},{5,6},{7,4},{9,10},{11,8},{13,14},{15,12},{17,18},{19,... | collective-permute-start | bytes 3538952 | tf_op jit(solution)/shard_map/ppermute | solution.py:22
  179.2 27.4 %collective-permute-start.15 = (bf16[768,768]{1,0:T(8,128)(2,1)S(1)}, bf16[768,768]{1,0:T(8,128)(2,1)}, u32[]{:S(2)}, u32[]{:S(2)}) collective-permute-start(bf16[768,768]{1,0:T(8,128)(2,1)S(1)} %shard_map.62.kept), channel_id=1, source_target_pairs={{0,4},{4,8},{8,12},{12,0},{16,20},{20,24},{24,28},{28,16}} | collective-permute-start | bytes 3538952 | tf_op jit(solution)/shard_map/ppermute | solution.py:22
  199.0 3.9 %collective-permute-start.14 = (f32[8,128]{1,0:T(8,128)}, f32[8,128]{1,0:T(8,128)}, u32[]{:S(2)}, u32[]{:S(2)}) collective-permute-start(f32[8,128]{1,0:T(8,128)} %constant_dynamic-slice_fusion.1), channel_id=1, source_target_pairs={{0,2},{1,3},{2,0},{3,1},{4,6},{5,7},{6,4},{7,5},{8,10},{9,11},{10,... | collective-permute-start | bytes 12296 | tf_op jit(solution)/shard_map/ppermute | solution.py:22
  203.6 3.0 %copy-start.4 = (f32[8,128]{1,0:T(8,128)}, f32[8,128]{1,0:T(8,128)S(1)}, u32[]{:S(2)}) copy-start(f32[8,128]{1,0:T(8,128)S(1)} %dynamic-slice_add_fusion.2) | copy-start | bytes 12292
  211.5 1.9 collective-permute-start.18
  211.5 3.9 %collective-permute-start.17 = (f32[768]{0:T(1024)}, f32[768]{0:T(1024)S(1)}, u32[]{:S(2)}, u32[]{:S(2)}) collective-permute-start(f32[768]{0:T(1024)} %reduce.2), channel_id=1, source_target_pairs={{0,14},{1,15},{2,0},{3,1},{4,2},{5,3},{6,4},{7,5},{8,6},{9,7},{10,... | collective-permute-start | bytes 9224 | tf_op jit(solution)/shard_map/ppermute | solution.py:22
  211.6 3.8 %collective-permute-start.16 = (f32[768]{0:T(1024)S(1)}, f32[768]{0:T(1024)S(1)}, u32[]{:S(2)}, u32[]{:S(2)}) collective-permute-start(f32[768]{0:T(1024)S(1)} %reduce.1), channel_id=1, source_target_pairs={{0,15},{1,0},{2,1},{3,2},{4,3},{5,4},{6,5},{7,6},{8,7},{9,8},{10,9... | collective-permute-start | bytes 9224 | tf_op jit(solution)/shard_map/ppermute | solution.py:22
  (2 other events, 1.6 us)

commit v8 on v7

--- a/solution.py
+++ b/solution.py
@@ -316,31 +316,32 @@
     u, v = early_tiles(place, sketches, partner1, near1)
     other1 = send(partner1, swap)
     behind1 = send(after(inverse, partner1), [(i, (i + 1) % size) for i in blocks])
-    behind2 = send(after(inverse, partner1), [(i, (i + 2) % size) for i in blocks])
     for bit in bits[:-4]:
         kept, came = halve(sums, bit, partner1)
         sums = kept + came
     kept, came = halve(sums, bits[-4], u)
-    partner2, near2, u, v, behind1, behind2, came = lax.optimization_barrier(
-        (partner2, near2, u, v, behind1, behind2, came)
-    )
-    other2 = send(partner2, swap)
+    partner2, near2, u, v, behind1, came = lax.optimization_barrier(
+        (partner2, near2, u, v, behind1, came)
+    )
+    behind2 = send(after(inverse, partner2), [(i, (i + 2) % size) for i in blocks])
     u, v = late_tiles(place, side2, partner2, near2, u, v)
+    u, v, behind2 = lax.optimization_barrier((u, v, behind2))
+    other2 = send(after(partner2, u), swap)
     ur, vr = send(u, across), send(v, back_v)
     kept, came = halve(kept + came, bits[-3], u)
-    x = cross_tile(place, sketches, near1, near2, after(other1, u), after(other2, u))
+    x = cross_tile(place, sketches, near1, near2, after(other1, u), other2)
     y, z = send(x, back_y), send(x, back_z)
 
     gram, row_mass2, column_mass2 = join(
         second_kernel, 1, scale, place, (ur, vr, v), inverse, behind2
     )
     kept, came = halve(kept + after(came, row_mass2), bits[-2])
+    kept, came = halve(kept + came, bits[-1])
     y, sums = lax.optimization_barrier((y, kept + came))
     gram, row_mass1, column_mass1 = join(
         first_kernel, 0, scale, place, (y, z, x, inside), inverse, behind1, (gram,)
     )
-    kept, came = halve(sums, bits[-1], row_mass1)
-    domain_scores = (kept + came) * (1.0 / math.sqrt(rows / DOM_DEV))
+    domain_scores = sums * (1.0 / math.sqrt(rows / DOM_DEV))
     mass = (
         row_mass1[0]
         + row_mass2[0]

time: 216 us -> 219 us (1.014)
  waiting for transfers between devices: 109 us -> 102 us
  starting transfers between devices: 20.3 us -> 24.4 us
  other arithmetic: 11 us -> 14.5 us
    ppermute x19, waiting for transfers between devices: 109 us -> 102 us  [send(): return lax.ppermute(value, 'blocks', pairs)]
    ppermute x19, starting transfers between devices: 20.3 us -> 24.4 us  [send(): return lax.ppermute(value, 'blocks', pairs)]
  transfers between devices with their start and end apart: 19 -> 19, of which waited for: 11 -> 9; matrix products, arithmetic and copies ran while one was open for 16% -> 18% of each run, Pallas kernels for 21% -> 21%
where the time goes in v8:
time: 219 us; the launch traced here: 218 us
  waiting for transfers between devices  102 us (47%)
  Pallas kernels  48.5 us (22%)
  starting transfers between devices  24.4 us (11%)
  matrix products  21.9 us (10%)
  other arithmetic  14.5 us (7%)
  local copies, waits for them, and re-layouts  5.57 us (3%)
    ppermute x19, waiting for transfers between devices, send(): return lax.ppermute(value, 'blocks', pairs)  102 us
    ppermute x19, starting transfers between devices, send(): return lax.ppermute(value, 'blocks', pairs)  24.4 us
    dot_general x1, matrix products, nt(): return lax.dot_general(left, right, NT, preferred_element_type=jnp.float32)  14.8 us
    pallas_call x1, Pallas kernels, cross_tile(): pl.pallas_call(cross_kernel, grid_spec=pltpu.PrefetchScalarGridSpec(num_s...  11.4 us
    pallas_call x1, Pallas kernels, early_tiles(): pl.pallas_call(early_kernel, grid_spec=pltpu.PrefetchScalarGridSpec(num_s...  11.4 us
    pallas_call x2, Pallas kernels, halves(): pl.pallas_call(functools.partial(halves_kernel, start, sides), in_specs=[...  11.2 us
    reduce_sum x2, other arithmetic, inverse_norm(): return lax.rsqrt(jnp.mean(values * values, axis=1) + 1e-06)  9.32 us
    pallas_call x2, Pallas kernels, join(): pl.pallas_call(functools.partial(kernel, scale), grid_spec=pltpu.Prefetch...  7.77 us
  transfers between devices with their start and end apart: 19, of which 9 were waited for; matrix products, arithmetic and copies ran while one was open for 18% of the time, Pallas kernels for 21%

profile of v8, /device:TPU:0, one launch (start us, length us, event | category | flops | bytes accessed | tf_op | source)
XLA Modules:
  0.0 217.6 jit_solution(4511803175337156581)
XLA Ops:
  1.2 7.9 %shard_map.58 = (bf16[768,3072]{1,0:T(8,128)(2,1)}, bf16[768,3072]{1,0:T(8,128)(2,1)}) custom-call(s32[2]{0:T(128)S(1)} %pad_add_fusion.place, bf16[768,8192]{1,0:T(8,128)(2,1)} %own.6), custom_call_target="tpu_custom_call" | custom-call | bytes 18874368 | tf_op jit(solution)/shard_map/pallas_call | solution.py:83
  9.1 2.6 %collective-permute-start.3 = (bf16[768,3072]{1,0:T(8,128)(2,1)}, bf16[768,3072]{1,0:T(8,128)(2,1)}, u32[]{:S(2)}, u32[]{:S(2)}) collective-permute-start(bf16[768,3072]{1,0:T(8,128)(2,1)} %get-tuple-element.42), channel_id=1, source_target_pairs={{0,2},{1,3},{2,0},{3,1},{4,6},{5,7},{6,4},{7,5},{8,10},{9,11},{10,... | collective-permute-start | bytes 14155784 | tf_op jit(solution)/shard_map/ppermute | solution.py:22
  11.8 3.6 %collective-permute-start = (bf16[768,3072]{1,0:T(8,128)(2,1)}, bf16[768,3072]{1,0:T(8,128)(2,1)}, u32[]{:S(2)}, u32[]{:S(2)}) collective-permute-start(bf16[768,3072]{1,0:T(8,128)(2,1)} %get-tuple-element.38), channel_id=1, source_target_pairs={{0,12},{1,13},{2,6},{3,7},{4,0},{5,1},{6,10},{7,11},{8,4},{9,5},{1... | collective-permute-start | bytes 14155784 | tf_op jit(solution)/shard_map/ppermute | solution.py:22
  15.4 3.3 %shard_map.59 = (bf16[768,1024]{1,0:T(8,128)(2,1)}, bf16[768,1024]{1,0:T(8,128)(2,1)}) custom-call(s32[2]{0:T(128)S(1)} %pad_add_fusion.place, bf16[768,8192]{1,0:T(8,128)(2,1)} %own.6), custom_call_target="tpu_custom_call" | custom-call | bytes 6291456 | tf_op jit(solution)/shard_map/pallas_call | solution.py:83
  19.3 2.1 multiply_reduce_fusion.1
  21.4 7.2 %multiply_reduce_fusion = f32[768]{0:T(1024)S(1)} fusion(bf16[768,8192]{1,0:T(8,128)(2,1)} %own.6), kind=kLoop, calls=%fused_computation | loop fusion | flops 18873600 | bytes 12585984 | tf_op jit(solution)/shard_map/reduce_sum | solution.py:31
  28.7 7.1 %fusion.3 = f32[64,128]{1,0:T(8,128)S(1)} fusion(bf16[768,8192]{1,0:T(8,128)(2,1)} %own.6, bf16[128,8192]{1,0:T(8,128)(2,1)S(1)} %copy-done.3, f32[128]{0:T(128)S(1)} %add_rsqrt_fusion.1, f32[768]{0:T(1024)S(1)} %add_rsqrt_fusion, s32[768]{0:T(1024)S(1)} %copy-done.7), kind=kOutput, calls=%fused_computation.6 | convolution fusion | flops 1623638016 | bytes 14719488 | tf_op jit(solution)/shard_map/dot_general | solution.py:299
  35.8 14.8 %fusion.9.local = f32[768,768]{1,0:T(8,128)S(1)} fusion(bf16[768,8192]{1,0:T(8,128)(2,1)} %own.6, bf16[768,8192]{1,0:T(8,128)(2,1)} %collective-permute-done.4), kind=kOutput, calls=%fused_computation.27 | convolution fusion | flops 9663676416 | bytes 27525120 | tf_op jit(solution)/shard_map/dot_general | solution.py:35
  50.6 64.1 %collective-permute-done.3.partner = bf16[768,3072]{1,0:T(8,128)(2,1)} collective-permute-done((bf16[768,3072]{1,0:T(8,128)(2,1)}, bf16[768,3072]{1,0:T(8,128)(2,1)}, u32[]{:S(2)}, u32[]{:S(2)}) %collective-permute-start.3) | collective-permute-done | bytes 4718624 | tf_op jit(solution)/shard_map/ppermute | solution.py:22
  114.8 3.1 %collective-permute-done.near.near1 = bf16[768,3072]{1,0:T(8,128)(2,1)} collective-permute-done((bf16[768,3072]{1,0:T(8,128)(2,1)}, bf16[768,3072]{1,0:T(8,128)(2,1)}, u32[]{:S(2)}, u32[]{:S(2)}) %collective-permute-start) | collective-permute-done | bytes 4718624 | tf_op jit(solution)/shard_map/ppermute | solution.py:22
  117.9 11.4 %shard_map.60 = (f32[768,768]{1,0:T(8,128)S(1)}, f32[768,768]{1,0:T(8,128)S(1)}) custom-call(s32[2]{0:T(128)S(1)} %pad_add_fusion.place, bf16[768,8192]{1,0:T(8,128)(2,1)} %own.6, bf16[768,3072]{1,0:T(8,128)(2,1)} %collective-permute-done.3.partner, bf16[768,3072]{1,0:T(8,128)(2,1)} %collective-permute-done.near.near1), custom_call_target="tpu_custom_call" | custom-call | flops 768 | bytes 768 | tf_op jit(solution)/shard_map/pallas_call | solution.py:118
  131.4 16.8 %collective-permute-done.1.partner = bf16[768,1024]{1,0:T(8,128)(2,1)} collective-permute-done((bf16[768,1024]{1,0:T(8,128)(2,1)}, bf16[768,1024]{1,0:T(8,128)(2,1)}, u32[]{:S(2)}, u32[]{:S(2)}) %collective-permute-start.1) | collective-permute-done | bytes 1572896 | tf_op jit(solution)/shard_map/ppermute | solution.py:22
  148.2 2.8 %collective-permute-done.2.near.near2 = bf16[768,1024]{1,0:T(8,128)(2,1)} collective-permute-done((bf16[768,1024]{1,0:T(8,128)(2,1)}, bf16[768,1024]{1,0:T(8,128)(2,1)}, u32[]{:S(2)}, u32[]{:S(2)}) %collective-permute-start.2) | collective-permute-done | bytes 1572896 | tf_op jit(solution)/shard_map/ppermute | solution.py:22
  152.7 6.8 %shard_map.61 = (bf16[768,768]{1,0:T(8,128)(2,1)}, bf16[768,768]{1,0:T(8,128)(2,1)}) custom-call(s32[2]{0:T(128)S(1)} %pad_add_fusion.place, bf16[768,1024]{1,0:T(8,128)(2,1)} %get-tuple-element.41.mine, bf16[768,1024]{1,0:T(8,128)(2,1)} %collective-permute-done.1.partner, bf16[768,1024]{1,0:T(8,128)(2,1)} %collective-permute-done.2.near.near2, ...), custom_call_target="tpu_custom_call" | custom-call | flops 35389440000 | bytes 94371840 | tf_op jit(solution)/shard_map/pallas_call | solution.py:150
  161.3 4.1 %collective-permute-start.13 = (bf16[768,768]{1,0:T(8,128)(2,1)}, bf16[768,768]{1,0:T(8,128)(2,1)}, u32[]{:S(2)}, u32[]{:S(2)}) collective-permute-start(bf16[768,768]{1,0:T(8,128)(2,1)} %get-tuple-element.60.kept), channel_id=1, source_target_pairs={{0,4},{1,5},{4,8},{5,9},{8,12},{9,13},{12,0},{13,1},{16,20},{17,21... | collective-permute-start | bytes 3538952 | tf_op jit(solution)/shard_map/ppermute | solution.py:22
  166.3 1.8 collective-permute-start.11
  168.1 11.4 %shard_map.62.kept = bf16[768,768]{1,0:T(8,128)(2,1)S(1)} custom-call(s32[2]{0:T(128)S(1)} %pad_add_fusion.place, bf16[768,8192]{1,0:T(8,128)(2,1)} %own.6, bf16[768,3072]{1,0:T(8,128)(2,1)} %collective-permute-done.near.near1, bf16[768,1024]{1,0:T(8,128)(2,1)} %collective-permute-done.2.near.near2, bf16[768,3072]{1,0:T(8,128)(2,1)} %collective-permute-done.7.other1, ...), custom_call_target="tpu_custom_call" | custom-call | flops 3623878656 | bytes 14155776 | tf_op jit(solution)/shard_map/pallas_call | solution.py:189
  180.8 2.2 %collective-permute-start.16 = (bf16[768,768]{1,0:T(8,128)(2,1)S(1)}, bf16[768,768]{1,0:T(8,128)(2,1)}, u32[]{:S(2)}, u32[]{:S(2)}) collective-permute-start(bf16[768,768]{1,0:T(8,128)(2,1)S(1)} %shard_map.62.kept), channel_id=1, source_target_pairs={{0,4},{4,8},{8,12},{12,0},{16,20},{20,24},{24,28},{28,16}} | collective-permute-start | bytes 3538952 | tf_op jit(solution)/shard_map/ppermute | solution.py:22
  183.0 5.7 %collective-permute-done.12.u = bf16[768,768]{1,0:T(8,128)(2,1)} collective-permute-done((bf16[768,768]{1,0:T(8,128)(2,1)}, bf16[768,768]{1,0:T(8,128)(2,1)}, u32[]{:S(2)}, u32[]{:S(2)}) %collective-permute-start.12) | collective-permute-done | bytes 1179680 | tf_op jit(solution)/shard_map/ppermute | solution.py:22
  188.7 4.8 %collective-permute-done.13.v = bf16[768,768]{1,0:T(8,128)(2,1)} collective-permute-done((bf16[768,768]{1,0:T(8,128)(2,1)}, bf16[768,768]{1,0:T(8,128)(2,1)}, u32[]{:S(2)}, u32[]{:S(2)}) %collective-permute-start.13) | collective-permute-done | bytes 1179680 | tf_op jit(solution)/shard_map/ppermute | solution.py:22
  193.5 3.9 %shard_map.63 = (f32[2,768,768]{2,1,0:T(8,128)}, f32[1,768]{1,0:T(1,128)S(1)}, f32[1,768]{1,0:T(1,128)S(1)}) custom-call(s32[2]{0:T(128)S(1)} %pad_add_fusion.place, bf16[768,768]{1,0:T(8,128)(2,1)} %collective-permute-done.12.u, bf16[768,768]{1,0:T(8,128)(2,1)} %collective-permute-done.13.v, bf16[768,768]{1,0:T(8,128)(2,1)} %get-tuple-element.60.kept, ...), custom_call_target="tpu_custom_call" | custom-call | flops 35389440000 | bytes 94371840 | tf_op jit(solution)/shard_map/pallas_call | solution.py:244
  198.6 3.8 %collective-permute-done.14 = f32[8,128]{1,0:T(8,128)S(1)} collective-permute-done((f32[8,128]{1,0:T(8,128)}, f32[8,128]{1,0:T(8,128)S(1)}, u32[]{:S(2)}, u32[]{:S(2)}) %collective-permute-start.14) | collective-permute-done | bytes 4128 | tf_op jit(solution)/shard_map/ppermute | solution.py:22
  208.0 3.9 %shard_map.64 = (f32[2,768,768]{2,1,0:T(8,128)}, f32[1,768]{1,0:T(1,128)S(1)}, f32[1,768]{1,0:T(1,128)S(1)}) custom-call(s32[2]{0:T(128)S(1)} %pad_add_fusion.place, bf16[768,768]{1,0:T(8,128)(2,1)} %collective-permute-done.10.y, bf16[768,768]{1,0:T(8,128)(2,1)} %collective-permute-done.16.z, ...), custom_call_target="tpu_custom_call", output_to_operand_aliasing={{0}: (7, {})} | custom-call | flops 4718592 | bytes 7077888 | tf_op jit(solution)/shard_map/pallas_call | solution.py:244
  212.5 2.0 collective-permute-start.18
  (60 shorter events, 19.6 us)
Async XLA Ops:
  0.6 35.2 %collective-permute-start.4 = (bf16[768,8192]{1,0:T(8,128)(2,1)}, bf16[768,8192]{1,0:T(8,128)(2,1)}, u32[]{:S(2)}, u32[]{:S(2)}) collective-permute-start(bf16[768,8192]{1,0:T(8,128)(2,1)} %own.6), channel_id=1, source_target_pairs={{0,1},{1,0},{2,3},{3,2},{4,5},{5,4},{6,7},{7,6},{8,9},{9,8},{10,11... | collective-permute-start | bytes 37748744 | tf_op jit(solution)/shard_map/ppermute | solution.py:22
  9.1 105.6 %collective-permute-start.3 = (bf16[768,3072]{1,0:T(8,128)(2,1)}, bf16[768,3072]{1,0:T(8,128)(2,1)}, u32[]{:S(2)}, u32[]{:S(2)}) collective-permute-start(bf16[768,3072]{1,0:T(8,128)(2,1)} %get-tuple-element.42), channel_id=1, source_target_pairs={{0,2},{1,3},{2,0},{3,1},{4,6},{5,7},{6,4},{7,5},{8,10},{9,11},{10,... | collective-permute-start | bytes 14155784 | tf_op jit(solution)/shard_map/ppermute | solution.py:22
  11.8 106.1 %collective-permute-start = (bf16[768,3072]{1,0:T(8,128)(2,1)}, bf16[768,3072]{1,0:T(8,128)(2,1)}, u32[]{:S(2)}, u32[]{:S(2)}) collective-permute-start(bf16[768,3072]{1,0:T(8,128)(2,1)} %get-tuple-element.38), channel_id=1, source_target_pairs={{0,12},{1,13},{2,6},{3,7},{4,0},{5,1},{6,10},{7,11},{8,4},{9,5},{1... | collective-permute-start | bytes 14155784 | tf_op jit(solution)/shard_map/ppermute | solution.py:22
  18.7 129.5 %collective-permute-start.1 = (bf16[768,1024]{1,0:T(8,128)(2,1)}, bf16[768,1024]{1,0:T(8,128)(2,1)}, u32[]{:S(2)}, u32[]{:S(2)}) collective-permute-start(bf16[768,1024]{1,0:T(8,128)(2,1)} %get-tuple-element.40), channel_id=1, source_target_pairs={{0,2},{1,3},{2,0},{3,1},{4,6},{5,7},{6,4},{7,5},{8,10},{9,11},{10,... | collective-permute-start | bytes 4718600 | tf_op jit(solution)/shard_map/ppermute | solution.py:22
  18.8 132.2 %collective-permute-start.2 = (bf16[768,1024]{1,0:T(8,128)(2,1)}, bf16[768,1024]{1,0:T(8,128)(2,1)}, u32[]{:S(2)}, u32[]{:S(2)}) collective-permute-start(bf16[768,1024]{1,0:T(8,128)(2,1)} %get-tuple-element.41.mine), channel_id=1, source_target_pairs={{0,12},{1,13},{2,6},{3,7},{4,0},{5,1},{6,10},{7,11},{8,4},{9,5},{1... | collective-permute-start | bytes 4718600 | tf_op jit(solution)/shard_map/ppermute | solution.py:22
  21.4 7.3 %copy-start.3 = (bf16[128,8192]{1,0:T(8,128)(2,1)S(1)}, bf16[128,8192]{1,0:T(8,128)(2,1)}, u32[]{:S(2)}) copy-start(bf16[128,8192]{1,0:T(8,128)(2,1)} %param.4) | copy-start | bytes 6291460
  21.4 7.3 %copy-start.7 = (s32[768]{0:T(1024)S(1)}, s32[768]{0:T(1024)}, u32[]{:S(2)}) copy-start(s32[768]{0:T(1024)} %param.5) | copy-start | bytes 9220
  129.3 22.2 %collective-permute-start.6 = (f32[32,128]{1,0:T(8,128)S(1)}, f32[32,128]{1,0:T(8,128)S(1)}, u32[]{:S(2)}, u32[]{:S(2)}) collective-permute-start(f32[32,128]{1,0:T(8,128)S(1)} %constant_dynamic-slice_fusion.3), channel_id=1, source_target_pairs={{0,8},{1,9},{2,10},{3,11},{4,12},{5,13},{6,14},{7,15},{8,0},{9,1},... | collective-permute-start | bytes 49160 | tf_op jit(solution)/shard_map/ppermute | solution.py:22
  130.8 20.7 %collective-permute-start.5 = (f32[768]{0:T(1024)S(1)}, f32[768]{0:T(1024)S(1)}, u32[]{:S(2)}, u32[]{:S(2)}) collective-permute-start(f32[768]{0:T(1024)S(1)} %add_rsqrt_fusion), channel_id=1, source_target_pairs={{0,1},{1,2},{2,3},{3,4},{4,5},{5,6},{6,7},{7,8},{8,9},{9,10},{10,1... | collective-permute-start | bytes 9224 | tf_op jit(solution)/shard_map/ppermute | solution.py:22
  130.8 37.3 %collective-permute-start.7 = (bf16[768,3072]{1,0:T(8,128)(2,1)}, bf16[768,3072]{1,0:T(8,128)(2,1)}, u32[]{:S(2)}, u32[]{:S(2)}) collective-permute-start(bf16[768,3072]{1,0:T(8,128)(2,1)} %collective-permute-done.3.partner), channel_id=1, source_target_pairs={{0,1},{1,0},{2,3},{3,2},{4,5},{5,4},{6,7},{7,6},{8,9},{9,8},{10,11... | collective-permute-start | bytes 14155784 | tf_op jit(solution)/shard_map/ppermute | solution.py:22
  151.5 8.0 %copy-start.6 = (f32[768]{0:T(1024)}, f32[768]{0:T(1024)S(1)}, u32[]{:S(2)}) copy-start(f32[768]{0:T(1024)S(1)} %collective-permute-done.5) | copy-start | bytes 9220
  151.5 8.0 %collective-permute-start.8 = (f32[768]{0:T(1024)S(1)}, f32[768]{0:T(1024)S(1)}, u32[]{:S(2)}, u32[]{:S(2)}) collective-permute-start(f32[768]{0:T(1024)S(1)} %add_rsqrt_fusion), channel_id=1, source_target_pairs={{0,2},{1,3},{2,4},{3,5},{4,6},{5,7},{6,8},{7,9},{8,10},{9,11},{10,... | collective-permute-start | bytes 9224 | tf_op jit(solution)/shard_map/ppermute | solution.py:22
  159.5 8.6 %collective-permute-start.9 = (bf16[768,1024]{1,0:T(8,128)(2,1)}, bf16[768,1024]{1,0:T(8,128)(2,1)}, u32[]{:S(2)}, u32[]{:S(2)}) collective-permute-start(bf16[768,1024]{1,0:T(8,128)(2,1)} %collective-permute-done.1.partner), channel_id=1, source_target_pairs={{0,1},{1,0},{2,3},{3,2},{4,5},{5,4},{6,7},{7,6},{8,9},{9,8},{10,11... | collective-permute-start | bytes 4718600 | tf_op jit(solution)/shard_map/ppermute | solution.py:22
  159.5 29.1 %collective-permute-start.12 = (bf16[768,768]{1,0:T(8,128)(2,1)}, bf16[768,768]{1,0:T(8,128)(2,1)}, u32[]{:S(2)}, u32[]{:S(2)}) collective-permute-start(bf16[768,768]{1,0:T(8,128)(2,1)} %get-tuple-element.55), channel_id=1, source_target_pairs={{0,2},{1,3},{2,0},{3,1},{4,6},{5,7},{6,4},{7,5},{8,10},{9,11},{10,... | collective-permute-start | bytes 3538952 | tf_op jit(solution)/shard_map/ppermute | solution.py:22
  161.3 32.2 %collective-permute-start.13 = (bf16[768,768]{1,0:T(8,128)(2,1)}, bf16[768,768]{1,0:T(8,128)(2,1)}, u32[]{:S(2)}, u32[]{:S(2)}) collective-permute-start(bf16[768,768]{1,0:T(8,128)(2,1)} %get-tuple-element.60.kept), channel_id=1, source_target_pairs={{0,4},{1,5},{4,8},{5,9},{8,12},{9,13},{12,0},{13,1},{16,20},{17,21... | collective-permute-start | bytes 3538952 | tf_op jit(solution)/shard_map/ppermute | solution.py:22
  166.3 27.2 %copy-start = (f32[768,1]{1,0:T(8,128)S(1)}, f32[768,1]{1,0:T(8,128)}, u32[]{:S(2)}) copy-start(f32[768,1]{1,0:T(8,128)} %rsqrt.24.inverse) | copy-start | bytes 9220
  166.3 31.1 %collective-permute-start.11 = (f32[16,128]{1,0:T(8,128)S(1)}, f32[16,128]{1,0:T(8,128)S(1)}, u32[]{:S(2)}, u32[]{:S(2)}) collective-permute-start(f32[16,128]{1,0:T(8,128)S(1)} %constant_dynamic-slice_fusion.2), channel_id=1, source_target_pairs={{0,4},{1,5},{2,6},{3,7},{4,0},{5,1},{6,2},{7,3},{8,12},{9,13},{10,... | collective-permute-start | bytes 24584 | tf_op jit(solution)/shard_map/ppermute | solution.py:22
  179.5 27.5 %collective-permute-start.10 = (bf16[768,768]{1,0:T(8,128)(2,1)S(1)}, bf16[768,768]{1,0:T(8,128)(2,1)}, u32[]{:S(2)}, u32[]{:S(2)}) collective-permute-start(bf16[768,768]{1,0:T(8,128)(2,1)S(1)} %shard_map.62.kept), channel_id=1, source_target_pairs={{1,2},{3,0},{5,6},{7,4},{9,10},{11,8},{13,14},{15,12},{17,18},{19,... | collective-permute-start | bytes 3538952 | tf_op jit(solution)/shard_map/ppermute | solution.py:22
  180.8 26.2 %collective-permute-start.16 = (bf16[768,768]{1,0:T(8,128)(2,1)S(1)}, bf16[768,768]{1,0:T(8,128)(2,1)}, u32[]{:S(2)}, u32[]{:S(2)}) collective-permute-start(bf16[768,768]{1,0:T(8,128)(2,1)S(1)} %shard_map.62.kept), channel_id=1, source_target_pairs={{0,4},{4,8},{8,12},{12,0},{16,20},{20,24},{24,28},{28,16}} | collective-permute-start | bytes 3538952 | tf_op jit(solution)/shard_map/ppermute | solution.py:22
  198.6 3.8 %collective-permute-start.14 = (f32[8,128]{1,0:T(8,128)}, f32[8,128]{1,0:T(8,128)S(1)}, u32[]{:S(2)}, u32[]{:S(2)}) collective-permute-start(f32[8,128]{1,0:T(8,128)} %constant_dynamic-slice_fusion.1), channel_id=1, source_target_pairs={{0,2},{1,3},{2,0},{3,1},{4,6},{5,7},{6,4},{7,5},{8,10},{9,11},{10,... | collective-permute-start | bytes 12296 | tf_op jit(solution)/shard_map/ppermute | solution.py:22
  204.2 1.5 collective-permute-start.15
  207.0 1.0 copy-start.1
  212.5 4.5 %collective-permute-start.18 = (f32[768]{0:T(1024)}, f32[768]{0:T(1024)S(1)}, u32[]{:S(2)}, u32[]{:S(2)}) collective-permute-start(f32[768]{0:T(1024)} %reduce.2), channel_id=1, source_target_pairs={{0,14},{1,15},{2,0},{3,1},{4,2},{5,3},{6,4},{7,5},{8,6},{9,7},{10,... | collective-permute-start | bytes 9224 | tf_op jit(solution)/shard_map/ppermute | solution.py:22
  215.1 1.9 collective-permute-start.17
  (3 other events, 1.8 us)

commit v9 on v8

--- a/solution.py
+++ b/solution.py
@@ -201,6 +201,31 @@
     )(place, own, near1, near2, other1, other2)
 
 
+def inside_kernel(place, mine, other, out):
+    clear(out)
+
+    @pl.when(place[1] == 1)
+    def _():
+        out[...] += nt(mine[...], other[...])
+
+
+def inside_tile(place, mine, other):
+    rows, depth = mine.shape
+    block = pl.BlockSpec((rows, DEPTH), lambda k, place: (0, k))
+    return pl.pallas_call(
+        inside_kernel,
+        grid_spec=pltpu.PrefetchScalarGridSpec(
+            num_scalar_prefetch=1,
+            grid=(depth // DEPTH,),
+            in_specs=[block, block],
+            out_specs=pl.BlockSpec((rows, rows), lambda k, place: (0, 0)),
+        ),
+        out_shape=jax.ShapeDtypeStruct((rows, rows), jnp.float32),
+        compiler_params=params(),
+        cost_estimate=cost(2 * rows * rows * depth, 4 * rows * depth),
+    )(place, mine, other)
+
+
 def finish(tile, gram, row_mass, column_mass):
     @pl.when(pl.program_id(0) == 0)
     def _():
@@ -260,7 +285,7 @@
         cost_estimate=cost(60000 * rows * rows, 160 * rows * rows)
         if index
         else cost(8 * rows * rows, 12 * rows * rows),
-    )(place, *tiles, inverse[:, None], behind[None, :], *gram)
+    )(place, *tiles, inverse, behind, *gram)
 
 
 def local(sketches, test_sketches, domain_map):
@@ -278,8 +303,8 @@
     along = [(i, (i + (4 if i & 2 else -4)) % size) for i in blocks]
     swap = [(i, i ^ 1) for i in blocks]
 
-    even = send(sketches, swap)
     out1, side1 = halves(place, sketches, 0, first, (1, 0))
+    even = send(after(sketches, out1), swap)
     partner1 = send(out1, across)
     near1 = send(side1, along)
     out2, side2 = halves(place, after(sketches, side1), first, DEPTH, (1, 0))
@@ -299,56 +324,55 @@
     sums = lax.dot_general(
         members, similarity, (((0,), (0,)), ((), ())), preferred_element_type=jnp.float32
     )
-    inside = nt(sketches, even)
-
-    def halve(value, bit, *waits):
-        count = value.shape[0] // 2
-        mine = (index // bit) % 2
-        away = lax.dynamic_slice_in_dim(value, (1 - mine) * count, count)
-        kept = lax.dynamic_slice_in_dim(value, mine * count, count)
-        return kept, send(after(away, *waits), [(i, i ^ bit) for i in blocks])
+    inside = inside_tile(place, sketches, even)
+    across_lanes, down_rows = inverse[None, :], inverse[:, None]
+
+    def doubled(value, bit, *waits):
+        return send(after(value, *waits), [(i, i ^ bit) for i in blocks])
 
     bits = [size >> (step + 1) for step in range(size.bit_length() - 1)]
     back_v = [(i, (i + 4) % size) for i in blocks if not i & 2]
     back_y = [(i, i ^ 3) for i in blocks if i & 1]
     back_z = [pair for pair in back_v if pair[0] % 2 == 0]
-    partner1 = after(partner1, inside, sums)
+    partner1 = after(partner1, inside, sums, across_lanes, down_rows)
     u, v = early_tiles(place, sketches, partner1, near1)
     other1 = send(partner1, swap)
-    behind1 = send(after(inverse, partner1), [(i, (i + 1) % size) for i in blocks])
+    behind1 = send(after(across_lanes, partner1), [(i, (i + 1) % size) for i in blocks])
     for bit in bits[:-4]:
-        kept, came = halve(sums, bit, partner1)
-        sums = kept + came
-    kept, came = halve(sums, bits[-4], u)
+        sums = sums + doubled(sums, bit, partner1)
+    came = doubled(sums, bits[-4], u)
     partner2, near2, u, v, behind1, came = lax.optimization_barrier(
         (partner2, near2, u, v, behind1, came)
     )
-    behind2 = send(after(inverse, partner2), [(i, (i + 2) % size) for i in blocks])
+    behind2 = send(after(across_lanes, partner2), [(i, (i + 2) % size) for i in blocks])
     u, v = late_tiles(place, side2, partner2, near2, u, v)
     u, v, behind2 = lax.optimization_barrier((u, v, behind2))
     other2 = send(after(partner2, u), swap)
     ur, vr = send(u, across), send(v, back_v)
-    kept, came = halve(kept + came, bits[-3], u)
+    sums = sums + came
+    came = doubled(sums, bits[-3], u)
     x = cross_tile(place, sketches, near1, near2, after(other1, u), other2)
     y, z = send(x, back_y), send(x, back_z)
 
     gram, row_mass2, column_mass2 = join(
-        second_kernel, 1, scale, place, (ur, vr, v), inverse, behind2
-    )
-    kept, came = halve(kept + after(came, row_mass2), bits[-2])
-    kept, came = halve(kept + came, bits[-1])
-    y, sums = lax.optimization_barrier((y, kept + came))
+        second_kernel, 1, scale, place, (ur, vr, v), down_rows, behind2
+    )
+    sums = sums + after(came, row_mass2)
+    sums = sums + doubled(sums, bits[-2])
+    came = doubled(sums, bits[-1])
+    y, came = lax.optimization_barrier((y, came))
     gram, row_mass1, column_mass1 = join(
-        first_kernel, 0, scale, place, (y, z, x, inside), inverse, behind1, (gram,)
-    )
+        first_kernel, 0, scale, place, (y, z, x, inside), down_rows, behind1, (gram,)
+    )
+    sums = lax.dynamic_slice_in_dim(sums + came, index * DOM_DEV, DOM_DEV)
     domain_scores = sums * (1.0 / math.sqrt(rows / DOM_DEV))
     mass = (
-        row_mass1[0]
-        + row_mass2[0]
-        + send(column_mass1[0], [(i, (i - 1) % size) for i in blocks])
-        + send(after(column_mass2[0], row_mass1), [(i, (i - 2) % size) for i in blocks])
-    )
-    redundancy = mass / float(2 * ROUNDS * rows)
+        row_mass1
+        + row_mass2
+        + send(column_mass1, [(i, (i - 1) % size) for i in blocks])
+        + send(after(column_mass2, row_mass1), [(i, (i - 2) % size) for i in blocks])
+    )
+    redundancy = mass[0] / float(2 * ROUNDS * rows)
     return (gram, redundancy, domain_scores)
 
 

time: 219 us -> 217 us (level)
  matrix products: 21.9 us -> 7.46 us
  waiting for transfers between devices: 102 us -> 115 us
  Pallas kernels: 48.5 us -> 58.2 us
  other arithmetic: 14.5 us -> 10.3 us
  local copies, waits for them, and re-layouts: 5.57 us -> 2.55 us
    dot_general x1 -> x0, matrix products: 14.8 us -> none  [nt(): return lax.dot_general(left, right, NT, preferred_element_type=jnp.float32)]
    ppermute x19, waiting for transfers between devices: 102 us -> 115 us  [send(): return lax.ppermute(value, 'blocks', pairs)]
    pallas_call x0 -> x1, Pallas kernels: none -> 9.77 us  [inside_tile(): pl.pallas_call(inside_kernel, grid_spec=pltpu.PrefetchScalarGridSpec(num_...]
  transfers between devices with their start and end apart: 19 -> 19, of which waited for: 9 -> 11; matrix products, arithmetic and copies ran while one was open for 18% -> 8% of each run, Pallas kernels for 21% -> 21%
where the time goes in v9:
time: 217 us
  waiting for transfers between devices  115 us (53%)
  Pallas kernels  58.2 us (27%)
  starting transfers between devices  22.9 us (11%)
  other arithmetic  10.3 us (5%)
  matrix products  7.46 us (3%)
  local copies, waits for them, and re-layouts  2.55 us (1%)
    ppermute x19, waiting for transfers between devices, send(): return lax.ppermute(value, 'blocks', pairs)  115 us
    ppermute x19, starting transfers between devices, send(): return lax.ppermute(value, 'blocks', pairs)  22.9 us
    pallas_call x1, Pallas kernels, early_tiles(): pl.pallas_call(early_kernel, grid_spec=pltpu.PrefetchScalarGridSpec(num_s...  11.4 us
    pallas_call x1, Pallas kernels, cross_tile(): pl.pallas_call(cross_kernel, grid_spec=pltpu.PrefetchScalarGridSpec(num_s...  11.4 us
    pallas_call x2, Pallas kernels, halves(): pl.pallas_call(functools.partial(halves_kernel, start, sides), in_specs=[...  11.2 us
    pallas_call x1, Pallas kernels, inside_tile(): pl.pallas_call(inside_kernel, grid_spec=pltpu.PrefetchScalarGridSpec(num_...  9.77 us
    pallas_call x2, Pallas kernels, join(): pl.pallas_call(functools.partial(kernel, scale), grid_spec=pltpu.Prefetch...  7.71 us
    reduce_sum x2, other arithmetic, inverse_norm(): return lax.rsqrt(jnp.mean(values * values, axis=1) + 1e-06)  7.7 us
  transfers between devices with their start and end apart: 19, of which 11 were waited for; matrix products, arithmetic and copies ran while one was open for 8% of the time, Pallas kernels for 21%

profile of v9, /device:TPU:0, one launch (start us, length us, event | category | flops | bytes accessed | tf_op | source)
XLA Modules:
  0.0 216.8 jit_solution(146093346829687274)
XLA Ops:
  0.7 7.9 %shard_map.58 = (bf16[768,3072]{1,0:T(8,128)(2,1)}, bf16[768,3072]{1,0:T(8,128)(2,1)}) custom-call(s32[2]{0:T(128)S(1)} %pad_add_fusion.place, bf16[768,8192]{1,0:T(8,128)(2,1)} %own.6), custom_call_target="tpu_custom_call" | custom-call | bytes 18874368 | tf_op jit(solution)/shard_map/pallas_call | solution.py:83
  9.2 2.6 %collective-permute-start.3 = (bf16[768,3072]{1,0:T(8,128)(2,1)}, bf16[768,3072]{1,0:T(8,128)(2,1)}, u32[]{:S(2)}, u32[]{:S(2)}) collective-permute-start(bf16[768,3072]{1,0:T(8,128)(2,1)} %get-tuple-element.43), channel_id=1, source_target_pairs={{0,2},{1,3},{2,0},{3,1},{4,6},{5,7},{6,4},{7,5},{8,10},{9,11},{10,... | collective-permute-start | bytes 14155784 | tf_op jit(solution)/shard_map/ppermute | solution.py:22
  11.8 3.6 %collective-permute-start = (bf16[768,3072]{1,0:T(8,128)(2,1)}, bf16[768,3072]{1,0:T(8,128)(2,1)}, u32[]{:S(2)}, u32[]{:S(2)}) collective-permute-start(bf16[768,3072]{1,0:T(8,128)(2,1)} %get-tuple-element.39), channel_id=1, source_target_pairs={{0,12},{1,13},{2,6},{3,7},{4,0},{5,1},{6,10},{7,11},{8,4},{9,5},{1... | collective-permute-start | bytes 14155784 | tf_op jit(solution)/shard_map/ppermute | solution.py:22
  15.4 3.3 %shard_map.59 = (bf16[768,1024]{1,0:T(8,128)(2,1)}, bf16[768,1024]{1,0:T(8,128)(2,1)}) custom-call(s32[2]{0:T(128)S(1)} %pad_add_fusion.place, bf16[768,8192]{1,0:T(8,128)(2,1)} %own.6), custom_call_target="tpu_custom_call" | custom-call | bytes 6291456 | tf_op jit(solution)/shard_map/pallas_call | solution.py:83
  19.3 7.2 %multiply_reduce_fusion = f32[768]{0:T(1024)S(1)} fusion(bf16[768,8192]{1,0:T(8,128)(2,1)} %own.6), kind=kLoop, calls=%fused_computation | loop fusion | flops 18873600 | bytes 12585984 | tf_op jit(solution)/shard_map/reduce_sum | solution.py:31
  27.1 7.5 %fusion.3 = f32[64,128]{1,0:T(8,128)} fusion(bf16[768,8192]{1,0:T(8,128)(2,1)} %own.6, bf16[128,8192]{1,0:T(8,128)(2,1)S(1)} %copy-done.4, f32[128]{0:T(128)S(1)} %add_rsqrt_fusion.1, f32[768]{0:T(1024)S(1)} %add_rsqrt_fusion, s32[768]{0:T(1024)S(1)} %copy-done.6), kind=kOutput, calls=%fused_computation.6 | convolution fusion | flops 1623638016 | bytes 14719488 | tf_op jit(solution)/shard_map/dot_general | solution.py:324
  34.5 9.8 %shard_map.60.local = f32[768,768]{1,0:T(8,128)S(1)} custom-call(s32[2]{0:T(128)S(1)} %pad_add_fusion.place, bf16[768,8192]{1,0:T(8,128)(2,1)} %own.6, bf16[768,8192]{1,0:T(8,128)(2,1)} %collective-permute-done.4.other), custom_call_target="tpu_custom_call" | custom-call | flops 9663676416 | bytes 25165824 | tf_op jit(solution)/shard_map/pallas_call | solution.py:215
  44.3 70.4 %collective-permute-done.3.partner = bf16[768,3072]{1,0:T(8,128)(2,1)} collective-permute-done((bf16[768,3072]{1,0:T(8,128)(2,1)}, bf16[768,3072]{1,0:T(8,128)(2,1)}, u32[]{:S(2)}, u32[]{:S(2)}) %collective-permute-start.3) | collective-permute-done | bytes 4718624 | tf_op jit(solution)/shard_map/ppermute | solution.py:22
  114.7 3.1 %collective-permute-done.near.near1 = bf16[768,3072]{1,0:T(8,128)(2,1)} collective-permute-done((bf16[768,3072]{1,0:T(8,128)(2,1)}, bf16[768,3072]{1,0:T(8,128)(2,1)}, u32[]{:S(2)}, u32[]{:S(2)}) %collective-permute-start) | collective-permute-done | bytes 4718624 | tf_op jit(solution)/shard_map/ppermute | solution.py:22
  117.8 11.4 %shard_map.61 = (f32[768,768]{1,0:T(8,128)S(1)}, f32[768,768]{1,0:T(8,128)S(1)}) custom-call(s32[2]{0:T(128)S(1)} %pad_add_fusion.place, bf16[768,8192]{1,0:T(8,128)(2,1)} %own.6, bf16[768,3072]{1,0:T(8,128)(2,1)} %collective-permute-done.3.partner, bf16[768,3072]{1,0:T(8,128)(2,1)} %collective-permute-done.near.near1), custom_call_target="tpu_custom_call" | custom-call | flops 768 | bytes 768 | tf_op jit(solution)/shard_map/pallas_call | solution.py:118
  131.4 16.7 %collective-permute-done.1.partner = bf16[768,1024]{1,0:T(8,128)(2,1)} collective-permute-done((bf16[768,1024]{1,0:T(8,128)(2,1)}, bf16[768,1024]{1,0:T(8,128)(2,1)}, u32[]{:S(2)}, u32[]{:S(2)}) %collective-permute-start.1) | collective-permute-done | bytes 1572896 | tf_op jit(solution)/shard_map/ppermute | solution.py:22
  148.2 3.0 %collective-permute-done.2.near.near2 = bf16[768,1024]{1,0:T(8,128)(2,1)} collective-permute-done((bf16[768,1024]{1,0:T(8,128)(2,1)}, bf16[768,1024]{1,0:T(8,128)(2,1)}, u32[]{:S(2)}, u32[]{:S(2)}) %collective-permute-start.2) | collective-permute-done | bytes 1572896 | tf_op jit(solution)/shard_map/ppermute | solution.py:22
  153.4 6.7 %shard_map.62 = (bf16[768,768]{1,0:T(8,128)(2,1)}, bf16[768,768]{1,0:T(8,128)(2,1)}) custom-call(s32[2]{0:T(128)S(1)} %pad_add_fusion.place, bf16[768,1024]{1,0:T(8,128)(2,1)} %get-tuple-element.42.mine, bf16[768,1024]{1,0:T(8,128)(2,1)} %collective-permute-done.1.partner, bf16[768,1024]{1,0:T(8,128)(2,1)} %collective-permute-done.2.near.near2, ...), custom_call_target="tpu_custom_call" | custom-call | flops 35389440000 | bytes 94371840 | tf_op jit(solution)/shard_map/pallas_call | solution.py:150
  160.6 1.7 collective-permute-start.12
  162.3 3.7 %collective-permute-start.13 = (bf16[768,768]{1,0:T(8,128)(2,1)}, bf16[768,768]{1,0:T(8,128)(2,1)}, u32[]{:S(2)}, u32[]{:S(2)}) collective-permute-start(bf16[768,768]{1,0:T(8,128)(2,1)} %get-tuple-element.62.kept), channel_id=1, source_target_pairs={{0,4},{1,5},{4,8},{5,9},{8,12},{9,13},{12,0},{13,1},{16,20},{17,21... | collective-permute-start | bytes 3538952 | tf_op jit(solution)/shard_map/ppermute | solution.py:22
  167.0 2.1 collective-permute-start.11
  169.2 11.4 %shard_map.63.kept = bf16[768,768]{1,0:T(8,128)(2,1)S(1)} custom-call(s32[2]{0:T(128)S(1)} %pad_add_fusion.place, bf16[768,8192]{1,0:T(8,128)(2,1)} %own.6, bf16[768,3072]{1,0:T(8,128)(2,1)} %collective-permute-done.near.near1, bf16[768,1024]{1,0:T(8,128)(2,1)} %collective-permute-done.2.near.near2, bf16[768,3072]{1,0:T(8,128)(2,1)} %collective-permute-done.7.other1, ...), custom_call_target="tpu_custom_call" | custom-call | flops 3623878656 | bytes 14155776 | tf_op jit(solution)/shard_map/pallas_call | solution.py:189
  181.9 1.9 collective-permute-start.16
  183.8 5.9 %collective-permute-done.12.u = bf16[768,768]{1,0:T(8,128)(2,1)} collective-permute-done((bf16[768,768]{1,0:T(8,128)(2,1)}, bf16[768,768]{1,0:T(8,128)(2,1)}, u32[]{:S(2)}, u32[]{:S(2)}) %collective-permute-start.12) | collective-permute-done | bytes 1179680 | tf_op jit(solution)/shard_map/ppermute | solution.py:22
  189.7 5.1 %collective-permute-done.13.v = bf16[768,768]{1,0:T(8,128)(2,1)} collective-permute-done((bf16[768,768]{1,0:T(8,128)(2,1)}, bf16[768,768]{1,0:T(8,128)(2,1)}, u32[]{:S(2)}, u32[]{:S(2)}) %collective-permute-start.13) | collective-permute-done | bytes 1179680 | tf_op jit(solution)/shard_map/ppermute | solution.py:22
  194.8 3.9 %shard_map.64 = (f32[2,768,768]{2,1,0:T(8,128)}, f32[1,768]{1,0:T(1,128)S(1)}, f32[1,768]{1,0:T(1,128)S(1)}) custom-call(s32[2]{0:T(128)S(1)} %pad_add_fusion.place, bf16[768,768]{1,0:T(8,128)(2,1)} %collective-permute-done.12.u, bf16[768,768]{1,0:T(8,128)(2,1)} %collective-permute-done.13.v, bf16[768,768]{1,0:T(8,128)(2,1)} %get-tuple-element.62.kept, ...), custom_call_target="tpu_custom_call" | custom-call | flops 35389440000 | bytes 94371840 | tf_op jit(solution)/shard_map/pallas_call | solution.py:269
  198.8 3.9 %collective-permute-done.14 = f32[64,128]{1,0:T(8,128)S(1)} collective-permute-done((f32[64,128]{1,0:T(8,128)S(1)}, f32[64,128]{1,0:T(8,128)S(1)}, u32[]{:S(2)}, u32[]{:S(2)}) %collective-permute-start.14) | collective-permute-done | bytes 32800 | tf_op jit(solution)/shard_map/ppermute | solution.py:22
  204.9 2.9 %collective-permute-done.16.z = bf16[768,768]{1,0:T(8,128)(2,1)} collective-permute-done((bf16[768,768]{1,0:T(8,128)(2,1)S(1)}, bf16[768,768]{1,0:T(8,128)(2,1)}, u32[]{:S(2)}, u32[]{:S(2)}) %collective-permute-start.16) | collective-permute-done | bytes 1179680 | tf_op jit(solution)/shard_map/ppermute | solution.py:22
  208.8 3.8 %shard_map.65 = (f32[2,768,768]{2,1,0:T(8,128)}, f32[1,768]{1,0:T(1,128)S(1)}, f32[1,768]{1,0:T(1,128)S(1)}) custom-call(s32[2]{0:T(128)S(1)} %pad_add_fusion.place, bf16[768,768]{1,0:T(8,128)(2,1)} %collective-permute-done.10.y, bf16[768,768]{1,0:T(8,128)(2,1)} %collective-permute-done.16.z, ...), custom_call_target="tpu_custom_call", output_to_operand_aliasing={{0}: (7, {})} | custom-call | flops 4718592 | bytes 7077888 | tf_op jit(solution)/shard_map/pallas_call | solution.py:269
  (50 shorter events, 16.3 us)
Async XLA Ops:
  8.6 25.9 %collective-permute-start.4 = (bf16[768,8192]{1,0:T(8,128)(2,1)}, bf16[768,8192]{1,0:T(8,128)(2,1)}, u32[]{:S(2)}, u32[]{:S(2)}) collective-permute-start(bf16[768,8192]{1,0:T(8,128)(2,1)} %own.6), channel_id=1, source_target_pairs={{0,1},{1,0},{2,3},{3,2},{4,5},{5,4},{6,7},{7,6},{8,9},{9,8},{10,11... | collective-permute-start | bytes 37748744 | tf_op jit(solution)/shard_map/ppermute | solution.py:22
  9.2 105.6 %collective-permute-start.3 = (bf16[768,3072]{1,0:T(8,128)(2,1)}, bf16[768,3072]{1,0:T(8,128)(2,1)}, u32[]{:S(2)}, u32[]{:S(2)}) collective-permute-start(bf16[768,3072]{1,0:T(8,128)(2,1)} %get-tuple-element.43), channel_id=1, source_target_pairs={{0,2},{1,3},{2,0},{3,1},{4,6},{5,7},{6,4},{7,5},{8,10},{9,11},{10,... | collective-permute-start | bytes 14155784 | tf_op jit(solution)/shard_map/ppermute | solution.py:22
  11.8 106.1 %collective-permute-start = (bf16[768,3072]{1,0:T(8,128)(2,1)}, bf16[768,3072]{1,0:T(8,128)(2,1)}, u32[]{:S(2)}, u32[]{:S(2)}) collective-permute-start(bf16[768,3072]{1,0:T(8,128)(2,1)} %get-tuple-element.39), channel_id=1, source_target_pairs={{0,12},{1,13},{2,6},{3,7},{4,0},{5,1},{6,10},{7,11},{8,4},{9,5},{1... | collective-permute-start | bytes 14155784 | tf_op jit(solution)/shard_map/ppermute | solution.py:22
  18.7 129.5 %collective-permute-start.1 = (bf16[768,1024]{1,0:T(8,128)(2,1)}, bf16[768,1024]{1,0:T(8,128)(2,1)}, u32[]{:S(2)}, u32[]{:S(2)}) collective-permute-start(bf16[768,1024]{1,0:T(8,128)(2,1)} %get-tuple-element.41), channel_id=1, source_target_pairs={{0,2},{1,3},{2,0},{3,1},{4,6},{5,7},{6,4},{7,5},{8,10},{9,11},{10,... | collective-permute-start | bytes 4718600 | tf_op jit(solution)/shard_map/ppermute | solution.py:22
  18.8 7.8 %copy-start.4 = (bf16[128,8192]{1,0:T(8,128)(2,1)S(1)}, bf16[128,8192]{1,0:T(8,128)(2,1)}, u32[]{:S(2)}) copy-start(bf16[128,8192]{1,0:T(8,128)(2,1)} %param.4) | copy-start | bytes 6291460
  18.8 8.3 %copy-start.6 = (s32[768]{0:T(1024)S(1)}, s32[768]{0:T(1024)}, u32[]{:S(2)}) copy-start(s32[768]{0:T(1024)} %param.5) | copy-start | bytes 9220
  18.8 132.4 %collective-permute-start.2 = (bf16[768,1024]{1,0:T(8,128)(2,1)}, bf16[768,1024]{1,0:T(8,128)(2,1)}, u32[]{:S(2)}, u32[]{:S(2)}) collective-permute-start(bf16[768,1024]{1,0:T(8,128)(2,1)} %get-tuple-element.42.mine), channel_id=1, source_target_pairs={{0,12},{1,13},{2,6},{3,7},{4,0},{5,1},{6,10},{7,11},{8,4},{9,5},{1... | collective-permute-start | bytes 4718600 | tf_op jit(solution)/shard_map/ppermute | solution.py:22
  44.3 85.0 %copy-start.5 = (f32[64,128]{1,0:T(8,128)S(1)}, f32[64,128]{1,0:T(8,128)}, u32[]{:S(2)}) copy-start(f32[64,128]{1,0:T(8,128)} %fusion.3) | copy-start | bytes 98308
  129.3 22.5 %collective-permute-start.6 = (f32[64,128]{1,0:T(8,128)S(1)}, f32[64,128]{1,0:T(8,128)S(1)}, u32[]{:S(2)}, u32[]{:S(2)}) collective-permute-start(f32[64,128]{1,0:T(8,128)S(1)} %copy-done.5), channel_id=1, source_target_pairs={{0,8},{1,9},{2,10},{3,11},{4,12},{5,13},{6,14},{7,15},{8,0},{9,1},... | collective-permute-start | bytes 98312 | tf_op jit(solution)/shard_map/ppermute | solution.py:22
  130.8 20.9 %collective-permute-start.5 = (f32[1,768]{1,0:T(1,128)S(1)}, f32[1,768]{1,0:T(1,128)S(1)}, u32[]{:S(2)}, u32[]{:S(2)}) collective-permute-start(f32[1,768]{1,0:T(1,128)S(1)} %rsqrt.33), channel_id=1, source_target_pairs={{0,1},{1,2},{2,3},{3,4},{4,5},{5,6},{6,7},{7,8},{8,9},{9,10},{10,1... | collective-permute-start | bytes 9224 | tf_op jit(solution)/shard_map/ppermute | solution.py:22
  130.8 38.3 %collective-permute-start.7 = (bf16[768,3072]{1,0:T(8,128)(2,1)}, bf16[768,3072]{1,0:T(8,128)(2,1)}, u32[]{:S(2)}, u32[]{:S(2)}) collective-permute-start(bf16[768,3072]{1,0:T(8,128)(2,1)} %collective-permute-done.3.partner), channel_id=1, source_target_pairs={{0,1},{1,0},{2,3},{3,2},{4,5},{5,4},{6,7},{7,6},{8,9},{9,8},{10,11... | collective-permute-start | bytes 14155784 | tf_op jit(solution)/shard_map/ppermute | solution.py:22
  151.8 8.3 %collective-permute-start.8 = (f32[1,768]{1,0:T(1,128)S(1)}, f32[1,768]{1,0:T(1,128)S(1)}, u32[]{:S(2)}, u32[]{:S(2)}) collective-permute-start(f32[1,768]{1,0:T(1,128)S(1)} %rsqrt.33), channel_id=1, source_target_pairs={{0,2},{1,3},{2,4},{3,5},{4,6},{5,7},{6,8},{7,9},{8,10},{9,11},{10,... | collective-permute-start | bytes 9224 | tf_op jit(solution)/shard_map/ppermute | solution.py:22
  160.6 8.5 %collective-permute-start.9 = (bf16[768,1024]{1,0:T(8,128)(2,1)}, bf16[768,1024]{1,0:T(8,128)(2,1)}, u32[]{:S(2)}, u32[]{:S(2)}) collective-permute-start(bf16[768,1024]{1,0:T(8,128)(2,1)} %collective-permute-done.1.partner), channel_id=1, source_target_pairs={{0,1},{1,0},{2,3},{3,2},{4,5},{5,4},{6,7},{7,6},{8,9},{9,8},{10,11... | collective-permute-start | bytes 4718600 | tf_op jit(solution)/shard_map/ppermute | solution.py:22
  160.6 29.1 %collective-permute-start.12 = (bf16[768,768]{1,0:T(8,128)(2,1)}, bf16[768,768]{1,0:T(8,128)(2,1)}, u32[]{:S(2)}, u32[]{:S(2)}) collective-permute-start(bf16[768,768]{1,0:T(8,128)(2,1)} %get-tuple-element.57), channel_id=1, source_target_pairs={{0,2},{1,3},{2,0},{3,1},{4,6},{5,7},{6,4},{7,5},{8,10},{9,11},{10,... | collective-permute-start | bytes 3538952 | tf_op jit(solution)/shard_map/ppermute | solution.py:22
  162.3 32.5 %collective-permute-start.13 = (bf16[768,768]{1,0:T(8,128)(2,1)}, bf16[768,768]{1,0:T(8,128)(2,1)}, u32[]{:S(2)}, u32[]{:S(2)}) collective-permute-start(bf16[768,768]{1,0:T(8,128)(2,1)} %get-tuple-element.62.kept), channel_id=1, source_target_pairs={{0,4},{1,5},{4,8},{5,9},{8,12},{9,13},{12,0},{13,1},{16,20},{17,21... | collective-permute-start | bytes 3538952 | tf_op jit(solution)/shard_map/ppermute | solution.py:22
  167.0 27.8 %copy-start = (f32[768,1]{1,0:T(8,128)S(1)}, f32[768,1]{1,0:T(8,128)}, u32[]{:S(2)}) copy-start(f32[768,1]{1,0:T(8,128)} %copy.7.inverse) | copy-start | bytes 9220
  167.0 27.8 %copy-start.3 = (f32[1,768]{1,0:T(1,128)S(1)}, f32[1,768]{1,0:T(1,128)}, u32[]{:S(2)}) copy-start(f32[1,768]{1,0:T(1,128)} %copy-done.2) | copy-start | bytes 9220
  167.0 31.7 %collective-permute-start.11 = (f32[64,128]{1,0:T(8,128)S(1)}, f32[64,128]{1,0:T(8,128)S(1)}, u32[]{:S(2)}, u32[]{:S(2)}) collective-permute-start(f32[64,128]{1,0:T(8,128)S(1)} %add.71), channel_id=1, source_target_pairs={{0,4},{1,5},{2,6},{3,7},{4,0},{5,1},{6,2},{7,3},{8,12},{9,13},{10,... | collective-permute-start | bytes 98312 | tf_op jit(solution)/shard_map/ppermute | solution.py:22
  180.6 24.3 %collective-permute-start.10 = (bf16[768,768]{1,0:T(8,128)(2,1)S(1)}, bf16[768,768]{1,0:T(8,128)(2,1)}, u32[]{:S(2)}, u32[]{:S(2)}) collective-permute-start(bf16[768,768]{1,0:T(8,128)(2,1)S(1)} %shard_map.63.kept), channel_id=1, source_target_pairs={{1,2},{3,0},{5,6},{7,4},{9,10},{11,8},{13,14},{15,12},{17,18},{19,... | collective-permute-start | bytes 3538952 | tf_op jit(solution)/shard_map/ppermute | solution.py:22
  181.9 25.9 %collective-permute-start.16 = (bf16[768,768]{1,0:T(8,128)(2,1)S(1)}, bf16[768,768]{1,0:T(8,128)(2,1)}, u32[]{:S(2)}, u32[]{:S(2)}) collective-permute-start(bf16[768,768]{1,0:T(8,128)(2,1)S(1)} %shard_map.63.kept), channel_id=1, source_target_pairs={{0,4},{4,8},{8,12},{12,0},{16,20},{20,24},{24,28},{28,16}} | collective-permute-start | bytes 3538952 | tf_op jit(solution)/shard_map/ppermute | solution.py:22
  198.7 4.0 %collective-permute-start.14 = (f32[64,128]{1,0:T(8,128)S(1)}, f32[64,128]{1,0:T(8,128)S(1)}, u32[]{:S(2)}, u32[]{:S(2)}) collective-permute-start(f32[64,128]{1,0:T(8,128)S(1)} %add.72), channel_id=1, source_target_pairs={{0,2},{1,3},{2,0},{3,1},{4,6},{5,7},{6,4},{7,5},{8,10},{9,11},{10,... | collective-permute-start | bytes 98312 | tf_op jit(solution)/shard_map/ppermute | solution.py:22
  203.3 1.6 collective-permute-start.15
  212.6 3.6 %collective-permute-start.18 = (f32[1,768]{1,0:T(1,128)S(1)}, f32[1,768]{1,0:T(1,128)S(1)}, u32[]{:S(2)}, u32[]{:S(2)}) collective-permute-start(f32[1,768]{1,0:T(1,128)S(1)} %get-tuple-element.73), channel_id=1, source_target_pairs={{0,14},{1,15},{2,0},{3,1},{4,2},{5,3},{6,4},{7,5},{8,6},{9,7},{10,... | collective-permute-start | bytes 9224 | tf_op jit(solution)/shard_map/ppermute | solution.py:22
  212.6 3.6 %collective-permute-start.17 = (f32[1,768]{1,0:T(1,128)S(1)}, f32[1,768]{1,0:T(1,128)S(1)}, u32[]{:S(2)}, u32[]{:S(2)}) collective-permute-start(f32[1,768]{1,0:T(1,128)S(1)} %get-tuple-element.71), channel_id=1, source_target_pairs={{0,15},{1,0},{2,1},{3,2},{4,3},{5,4},{6,5},{7,6},{8,7},{9,8},{10,9... | collective-permute-start | bytes 9224 | tf_op jit(solution)/shard_map/ppermute | solution.py:22
  (2 other events, 1.6 us)

commit v10 on v9

--- a/solution.py
+++ b/solution.py
@@ -239,10 +239,14 @@
     row_mass[...] = jnp.broadcast_to(sums, (size, size)).T[0:1]
 
 
+def down(row):
+    return jnp.broadcast_to(row, (128, row.shape[1])).T[:, 0:1]
+
+
 def second_kernel(scale, place, u, v, kept, inverse, behind, gram, row_mass, column_mass):
     other = jnp.where(place[0] == 1, kept[...], v[...])
     tile = u[...].astype(jnp.float32) + other.astype(jnp.float32)
-    finish(tile * inverse[...] * behind[...] * scale, gram, row_mass, column_mass)
+    finish(tile * down(inverse[...]) * behind[...] * scale, gram, row_mass, column_mass)
 
 
 def first_kernel(
@@ -252,7 +256,7 @@
     other = jnp.where(place[0] == 1, kept[...], z[...])
     tile = y[...].astype(jnp.float32) + other.astype(jnp.float32)
     tile = jnp.where(place[1] == 1, local[...], tile)
-    finish(tile * inverse[...] * behind[...] * scale, gram, row_mass, column_mass)
+    finish(tile * down(inverse[...]) * behind[...] * scale, gram, row_mass, column_mass)
 
 
 def mass_shapes(rows):
@@ -273,7 +277,7 @@
             grid=(rows // TALL,),
             in_specs=[pl.BlockSpec((TALL, rows), lambda j, place: (j, 0))] * len(tiles)
             + [
-                pl.BlockSpec((TALL, 1), lambda j, place: (j, 0)),
+                pl.BlockSpec((1, TALL), lambda j, place: (0, j)),
                 pl.BlockSpec((1, rows), lambda j, place: (0, 0)),
             ]
             + [pl.BlockSpec(memory_space=pl.ANY)] * len(gram),
@@ -325,7 +329,7 @@
         members, similarity, (((0,), (0,)), ((), ())), preferred_element_type=jnp.float32
     )
     inside = inside_tile(place, sketches, even)
-    across_lanes, down_rows = inverse[None, :], inverse[:, None]
+    across_lanes = inverse[None, :]
 
     def doubled(value, bit, *waits):
         return send(after(value, *waits), [(i, i ^ bit) for i in blocks])
@@ -334,7 +338,7 @@
     back_v = [(i, (i + 4) % size) for i in blocks if not i & 2]
     back_y = [(i, i ^ 3) for i in blocks if i & 1]
     back_z = [pair for pair in back_v if pair[0] % 2 == 0]
-    partner1 = after(partner1, inside, sums, across_lanes, down_rows)
+    partner1 = after(partner1, inside, sums, across_lanes)
     u, v = early_tiles(place, sketches, partner1, near1)
     other1 = send(partner1, swap)
     behind1 = send(after(across_lanes, partner1), [(i, (i + 1) % size) for i in blocks])
@@ -346,23 +350,23 @@
     )
     behind2 = send(after(across_lanes, partner2), [(i, (i + 2) % size) for i in blocks])
     u, v = late_tiles(place, side2, partner2, near2, u, v)
-    u, v, behind2 = lax.optimization_barrier((u, v, behind2))
-    other2 = send(after(partner2, u), swap)
-    ur, vr = send(u, across), send(v, back_v)
+    vr = send(v, back_v)
+    ur = send(u, across)
+    other2 = send(after(partner2, u, behind2), swap)
     sums = sums + came
     came = doubled(sums, bits[-3], u)
     x = cross_tile(place, sketches, near1, near2, after(other1, u), other2)
     y, z = send(x, back_y), send(x, back_z)
 
     gram, row_mass2, column_mass2 = join(
-        second_kernel, 1, scale, place, (ur, vr, v), down_rows, behind2
+        second_kernel, 1, scale, place, (ur, vr, v), across_lanes, behind2
     )
     sums = sums + after(came, row_mass2)
     sums = sums + doubled(sums, bits[-2])
     came = doubled(sums, bits[-1])
     y, came = lax.optimization_barrier((y, came))
     gram, row_mass1, column_mass1 = join(
-        first_kernel, 0, scale, place, (y, z, x, inside), down_rows, behind1, (gram,)
+        first_kernel, 0, scale, place, (y, z, x, inside), across_lanes, behind1, (gram,)
     )
     sums = lax.dynamic_slice_in_dim(sums + came, index * DOM_DEV, DOM_DEV)
     domain_scores = sums * (1.0 / math.sqrt(rows / DOM_DEV))

time: 217 us -> 214 us (0.986)
  Pallas kernels: 58.2 us -> 53.9 us
    ppermute x19, waiting for transfers between devices: 115 us -> 117 us  [send(): return lax.ppermute(value, 'blocks', pairs)]
  transfers between devices with their start and end apart: 19 -> 19, of which waited for: 11 -> 11; matrix products, arithmetic and copies ran while one was open for 8% -> 8% of each run, Pallas kernels for 21% -> 20%
where the time goes in v10:
time: 214 us
  waiting for transfers between devices  117 us (55%)
  Pallas kernels  53.9 us (25%)
  starting transfers between devices  23.5 us (11%)
  other arithmetic  10.3 us (5%)
  matrix products  7.47 us (3%)
    ppermute x19, waiting for transfers between devices, send(): return lax.ppermute(value, 'blocks', pairs)  117 us
    ppermute x19, starting transfers between devices, send(): return lax.ppermute(value, 'blocks', pairs)  23.5 us
    pallas_call x1, Pallas kernels, early_tiles(): pl.pallas_call(early_kernel, grid_spec=pltpu.PrefetchScalarGridSpec(num_s...  11.4 us
    pallas_call x2, Pallas kernels, halves(): pl.pallas_call(functools.partial(halves_kernel, start, sides), in_specs=[...  11.2 us
    pallas_call x1, Pallas kernels, inside_tile(): pl.pallas_call(inside_kernel, grid_spec=pltpu.PrefetchScalarGridSpec(num_...  9.77 us
    pallas_call x1, Pallas kernels, cross_tile(): pl.pallas_call(cross_kernel, grid_spec=pltpu.PrefetchScalarGridSpec(num_s...  9.58 us
    reduce_sum x2, other arithmetic, inverse_norm(): return lax.rsqrt(jnp.mean(values * values, axis=1) + 1e-06)  7.7 us
    dot_general x1, matrix products, local(): lax.dot_general(members, similarity, (((0,), (0,)), ((), ())), preferred_...  7.47 us
  transfers between devices with their start and end apart: 19, of which 11 were waited for; matrix products, arithmetic and copies ran while one was open for 8% of the time, Pallas kernels for 20%

profile of v10, /device:TPU:0, one launch (start us, length us, event | category | flops | bytes accessed | tf_op | source)
XLA Modules:
  0.0 213.8 jit_solution(14662948210860291275)
XLA Ops:
  0.7 7.9 %shard_map.58 = (bf16[768,3072]{1,0:T(8,128)(2,1)}, bf16[768,3072]{1,0:T(8,128)(2,1)}) custom-call(s32[2]{0:T(128)S(1)} %pad_add_fusion.place, bf16[768,8192]{1,0:T(8,128)(2,1)} %own.6), custom_call_target="tpu_custom_call" | custom-call | bytes 18874368 | tf_op jit(solution)/shard_map/pallas_call | solution.py:83
  9.2 2.6 %collective-permute-start.3 = (bf16[768,3072]{1,0:T(8,128)(2,1)}, bf16[768,3072]{1,0:T(8,128)(2,1)}, u32[]{:S(2)}, u32[]{:S(2)}) collective-permute-start(bf16[768,3072]{1,0:T(8,128)(2,1)} %get-tuple-element.40), channel_id=1, source_target_pairs={{0,2},{1,3},{2,0},{3,1},{4,6},{5,7},{6,4},{7,5},{8,10},{9,11},{10,... | collective-permute-start | bytes 14155784 | tf_op jit(solution)/shard_map/ppermute | solution.py:22
  11.8 3.6 %collective-permute-start = (bf16[768,3072]{1,0:T(8,128)(2,1)}, bf16[768,3072]{1,0:T(8,128)(2,1)}, u32[]{:S(2)}, u32[]{:S(2)}) collective-permute-start(bf16[768,3072]{1,0:T(8,128)(2,1)} %get-tuple-element.36), channel_id=1, source_target_pairs={{0,12},{1,13},{2,6},{3,7},{4,0},{5,1},{6,10},{7,11},{8,4},{9,5},{1... | collective-permute-start | bytes 14155784 | tf_op jit(solution)/shard_map/ppermute | solution.py:22
  15.4 3.3 %shard_map.59 = (bf16[768,1024]{1,0:T(8,128)(2,1)}, bf16[768,1024]{1,0:T(8,128)(2,1)}) custom-call(s32[2]{0:T(128)S(1)} %pad_add_fusion.place, bf16[768,8192]{1,0:T(8,128)(2,1)} %own.6), custom_call_target="tpu_custom_call" | custom-call | bytes 6291456 | tf_op jit(solution)/shard_map/pallas_call | solution.py:83
  19.3 7.2 %multiply_reduce_fusion = f32[768]{0:T(1024)S(1)} fusion(bf16[768,8192]{1,0:T(8,128)(2,1)} %own.6), kind=kLoop, calls=%fused_computation | loop fusion | flops 18873600 | bytes 12585984 | tf_op jit(solution)/shard_map/reduce_sum | solution.py:31
  27.0 7.5 %fusion.3 = f32[64,128]{1,0:T(8,128)} fusion(bf16[768,8192]{1,0:T(8,128)(2,1)} %own.6, bf16[128,8192]{1,0:T(8,128)(2,1)S(1)} %copy-done.2, f32[128]{0:T(128)S(1)} %add_rsqrt_fusion.1, f32[768]{0:T(1024)S(1)} %add_rsqrt_fusion, s32[768]{0:T(1024)S(1)} %copy-done.4), kind=kOutput, calls=%fused_computation.6 | convolution fusion | flops 1623638016 | bytes 14719488 | tf_op jit(solution)/shard_map/dot_general | solution.py:328
  34.5 9.8 %shard_map.60.local = f32[768,768]{1,0:T(8,128)S(1)} custom-call(s32[2]{0:T(128)S(1)} %pad_add_fusion.place, bf16[768,8192]{1,0:T(8,128)(2,1)} %own.6, bf16[768,8192]{1,0:T(8,128)(2,1)} %collective-permute-done.4.other), custom_call_target="tpu_custom_call" | custom-call | flops 9663676416 | bytes 25165824 | tf_op jit(solution)/shard_map/pallas_call | solution.py:215
  44.3 70.4 %collective-permute-done.3.partner = bf16[768,3072]{1,0:T(8,128)(2,1)} collective-permute-done((bf16[768,3072]{1,0:T(8,128)(2,1)}, bf16[768,3072]{1,0:T(8,128)(2,1)}, u32[]{:S(2)}, u32[]{:S(2)}) %collective-permute-start.3) | collective-permute-done | bytes 4718624 | tf_op jit(solution)/shard_map/ppermute | solution.py:22
  114.7 3.1 %collective-permute-done.near.near1 = bf16[768,3072]{1,0:T(8,128)(2,1)} collective-permute-done((bf16[768,3072]{1,0:T(8,128)(2,1)}, bf16[768,3072]{1,0:T(8,128)(2,1)}, u32[]{:S(2)}, u32[]{:S(2)}) %collective-permute-start) | collective-permute-done | bytes 4718624 | tf_op jit(solution)/shard_map/ppermute | solution.py:22
  117.9 11.4 %shard_map.61 = (f32[768,768]{1,0:T(8,128)S(1)}, f32[768,768]{1,0:T(8,128)S(1)}) custom-call(s32[2]{0:T(128)S(1)} %pad_add_fusion.place, bf16[768,8192]{1,0:T(8,128)(2,1)} %own.6, bf16[768,3072]{1,0:T(8,128)(2,1)} %collective-permute-done.3.partner, bf16[768,3072]{1,0:T(8,128)(2,1)} %collective-permute-done.near.near1), custom_call_target="tpu_custom_call" | custom-call | flops 768 | bytes 768 | tf_op jit(solution)/shard_map/pallas_call | solution.py:118
  131.4 16.7 %collective-permute-done.1.partner = bf16[768,1024]{1,0:T(8,128)(2,1)} collective-permute-done((bf16[768,1024]{1,0:T(8,128)(2,1)}, bf16[768,1024]{1,0:T(8,128)(2,1)}, u32[]{:S(2)}, u32[]{:S(2)}) %collective-permute-start.1) | collective-permute-done | bytes 1572896 | tf_op jit(solution)/shard_map/ppermute | solution.py:22
  148.2 3.0 %collective-permute-done.2.near.near2 = bf16[768,1024]{1,0:T(8,128)(2,1)} collective-permute-done((bf16[768,1024]{1,0:T(8,128)(2,1)}, bf16[768,1024]{1,0:T(8,128)(2,1)}, u32[]{:S(2)}, u32[]{:S(2)}) %collective-permute-start.2) | collective-permute-done | bytes 1572896 | tf_op jit(solution)/shard_map/ppermute | solution.py:22
  153.4 5.3 %shard_map.62 = (bf16[768,768]{1,0:T(8,128)(2,1)S(1)}, bf16[768,768]{1,0:T(8,128)(2,1)S(1)}) custom-call(s32[2]{0:T(128)S(1)} %pad_add_fusion.place, bf16[768,1024]{1,0:T(8,128)(2,1)} %get-tuple-element.39.mine, bf16[768,1024]{1,0:T(8,128)(2,1)} %collective-permute-done.1.partner, bf16[768,1024]{1,0:T(8,128)(2,1)} %collective-permute-done.2.near.near2, ...), custom_call_target="tpu_custom_call" | custom-call | flops 35389440000 | bytes 94371840 | tf_op jit(solution)/shard_map/pallas_call | solution.py:150
  158.7 1.8 collective-permute-start.12
  160.5 3.7 %collective-permute-start.13 = (bf16[768,768]{1,0:T(8,128)(2,1)S(1)}, bf16[768,768]{1,0:T(8,128)(2,1)S(1)}, u32[]{:S(2)}, u32[]{:S(2)}) collective-permute-start(bf16[768,768]{1,0:T(8,128)(2,1)S(1)} %get-tuple-element.57.kept), channel_id=1, source_target_pairs={{0,4},{1,5},{4,8},{5,9},{8,12},{9,13},{12,0},{13,1},{16,20},{17,21... | collective-permute-start | bytes 3538952 | tf_op jit(solution)/shard_map/ppermute | solution.py:22
  164.3 2.1 collective-permute-start.11
  166.4 9.6 %shard_map.63.kept = bf16[768,768]{1,0:T(8,128)(2,1)S(1)} custom-call(s32[2]{0:T(128)S(1)} %pad_add_fusion.place, bf16[768,8192]{1,0:T(8,128)(2,1)} %own.6, bf16[768,3072]{1,0:T(8,128)(2,1)} %collective-permute-done.near.near1, bf16[768,1024]{1,0:T(8,128)(2,1)} %collective-permute-done.2.near.near2, bf16[768,3072]{1,0:T(8,128)(2,1)S(1)} %collective-permute-done.7.other1, ...), custom_call_target="tpu_custom_call" | custom-call | flops 3623878656 | bytes 14155776 | tf_op jit(solution)/shard_map/pallas_call | solution.py:189
  177.3 1.9 collective-permute-start.16
  179.2 8.4 %collective-permute-done.12.u = bf16[768,768]{1,0:T(8,128)(2,1)S(1)} collective-permute-done((bf16[768,768]{1,0:T(8,128)(2,1)S(1)}, bf16[768,768]{1,0:T(8,128)(2,1)S(1)}, u32[]{:S(2)}, u32[]{:S(2)}) %collective-permute-start.12) | collective-permute-done | bytes 1179680 | tf_op jit(solution)/shard_map/ppermute | solution.py:22
  187.6 5.0 %collective-permute-done.13.v = bf16[768,768]{1,0:T(8,128)(2,1)S(1)} collective-permute-done((bf16[768,768]{1,0:T(8,128)(2,1)S(1)}, bf16[768,768]{1,0:T(8,128)(2,1)S(1)}, u32[]{:S(2)}, u32[]{:S(2)}) %collective-permute-start.13) | collective-permute-done | bytes 1179680 | tf_op jit(solution)/shard_map/ppermute | solution.py:22
  192.6 2.6 %shard_map.64 = (f32[2,768,768]{2,1,0:T(8,128)}, f32[1,768]{1,0:T(1,128)S(1)}, f32[1,768]{1,0:T(1,128)S(1)}) custom-call(s32[2]{0:T(128)S(1)} %pad_add_fusion.place, bf16[768,768]{1,0:T(8,128)(2,1)S(1)} %collective-permute-done.12.u, bf16[768,768]{1,0:T(8,128)(2,1)S(1)} %collective-permute-done.13.v, bf16[768,768]{1,0:T(8,128)(2,1)S(1)} %get-tuple-element.57.kept, ...), custom_call_target="tpu_custom_call" | custom-call | flops 35389440000 | bytes 94371840 | tf_op jit(solution)/shard_map/pallas_call | solution.py:273
  195.9 4.3 %collective-permute-done.14 = f32[64,128]{1,0:T(8,128)S(1)} collective-permute-done((f32[64,128]{1,0:T(8,128)S(1)}, f32[64,128]{1,0:T(8,128)S(1)}, u32[]{:S(2)}, u32[]{:S(2)}) %collective-permute-start.14) | collective-permute-done | bytes 32800 | tf_op jit(solution)/shard_map/ppermute | solution.py:22
  202.5 3.2 %collective-permute-done.16.z = bf16[768,768]{1,0:T(8,128)(2,1)} collective-permute-done((bf16[768,768]{1,0:T(8,128)(2,1)S(1)}, bf16[768,768]{1,0:T(8,128)(2,1)}, u32[]{:S(2)}, u32[]{:S(2)}) %collective-permute-start.16) | collective-permute-done | bytes 1179680 | tf_op jit(solution)/shard_map/ppermute | solution.py:22
  205.7 4.0 %shard_map.65 = (f32[2,768,768]{2,1,0:T(8,128)}, f32[1,768]{1,0:T(1,128)S(1)}, f32[1,768]{1,0:T(1,128)S(1)}) custom-call(s32[2]{0:T(128)S(1)} %pad_add_fusion.place, bf16[768,768]{1,0:T(8,128)(2,1)} %collective-permute-done.10.y, bf16[768,768]{1,0:T(8,128)(2,1)} %collective-permute-done.16.z, ...), custom_call_target="tpu_custom_call", output_to_operand_aliasing={{0}: (7, {})} | custom-call | flops 4718592 | bytes 7077888 | tf_op jit(solution)/shard_map/pallas_call | solution.py:273
  (44 shorter events, 14.5 us)
Async XLA Ops:
  8.7 25.9 %collective-permute-start.4 = (bf16[768,8192]{1,0:T(8,128)(2,1)}, bf16[768,8192]{1,0:T(8,128)(2,1)}, u32[]{:S(2)}, u32[]{:S(2)}) collective-permute-start(bf16[768,8192]{1,0:T(8,128)(2,1)} %own.6), channel_id=1, source_target_pairs={{0,1},{1,0},{2,3},{3,2},{4,5},{5,4},{6,7},{7,6},{8,9},{9,8},{10,11... | collective-permute-start | bytes 37748744 | tf_op jit(solution)/shard_map/ppermute | solution.py:22
  9.2 105.6 %collective-permute-start.3 = (bf16[768,3072]{1,0:T(8,128)(2,1)}, bf16[768,3072]{1,0:T(8,128)(2,1)}, u32[]{:S(2)}, u32[]{:S(2)}) collective-permute-start(bf16[768,3072]{1,0:T(8,128)(2,1)} %get-tuple-element.40), channel_id=1, source_target_pairs={{0,2},{1,3},{2,0},{3,1},{4,6},{5,7},{6,4},{7,5},{8,10},{9,11},{10,... | collective-permute-start | bytes 14155784 | tf_op jit(solution)/shard_map/ppermute | solution.py:22
  11.8 106.1 %collective-permute-start = (bf16[768,3072]{1,0:T(8,128)(2,1)}, bf16[768,3072]{1,0:T(8,128)(2,1)}, u32[]{:S(2)}, u32[]{:S(2)}) collective-permute-start(bf16[768,3072]{1,0:T(8,128)(2,1)} %get-tuple-element.36), channel_id=1, source_target_pairs={{0,12},{1,13},{2,6},{3,7},{4,0},{5,1},{6,10},{7,11},{8,4},{9,5},{1... | collective-permute-start | bytes 14155784 | tf_op jit(solution)/shard_map/ppermute | solution.py:22
  18.7 129.5 %collective-permute-start.1 = (bf16[768,1024]{1,0:T(8,128)(2,1)}, bf16[768,1024]{1,0:T(8,128)(2,1)}, u32[]{:S(2)}, u32[]{:S(2)}) collective-permute-start(bf16[768,1024]{1,0:T(8,128)(2,1)} %get-tuple-element.38), channel_id=1, source_target_pairs={{0,2},{1,3},{2,0},{3,1},{4,6},{5,7},{6,4},{7,5},{8,10},{9,11},{10,... | collective-permute-start | bytes 4718600 | tf_op jit(solution)/shard_map/ppermute | solution.py:22
  18.8 7.8 %copy-start.2 = (bf16[128,8192]{1,0:T(8,128)(2,1)S(1)}, bf16[128,8192]{1,0:T(8,128)(2,1)}, u32[]{:S(2)}) copy-start(bf16[128,8192]{1,0:T(8,128)(2,1)} %param.4) | copy-start | bytes 6291460
  18.8 8.3 %copy-start.4 = (s32[768]{0:T(1024)S(1)}, s32[768]{0:T(1024)}, u32[]{:S(2)}) copy-start(s32[768]{0:T(1024)} %param.5) | copy-start | bytes 9220
  18.8 132.4 %collective-permute-start.2 = (bf16[768,1024]{1,0:T(8,128)(2,1)}, bf16[768,1024]{1,0:T(8,128)(2,1)}, u32[]{:S(2)}, u32[]{:S(2)}) collective-permute-start(bf16[768,1024]{1,0:T(8,128)(2,1)} %get-tuple-element.39.mine), channel_id=1, source_target_pairs={{0,12},{1,13},{2,6},{3,7},{4,0},{5,1},{6,10},{7,11},{8,4},{9,5},{1... | collective-permute-start | bytes 4718600 | tf_op jit(solution)/shard_map/ppermute | solution.py:22
  44.3 85.0 %copy-start.3 = (f32[64,128]{1,0:T(8,128)S(1)}, f32[64,128]{1,0:T(8,128)}, u32[]{:S(2)}) copy-start(f32[64,128]{1,0:T(8,128)} %fusion.3) | copy-start | bytes 98308
  129.3 22.5 %collective-permute-start.6 = (f32[64,128]{1,0:T(8,128)S(1)}, f32[64,128]{1,0:T(8,128)S(1)}, u32[]{:S(2)}, u32[]{:S(2)}) collective-permute-start(f32[64,128]{1,0:T(8,128)S(1)} %copy-done.3), channel_id=1, source_target_pairs={{0,8},{1,9},{2,10},{3,11},{4,12},{5,13},{6,14},{7,15},{8,0},{9,1},... | collective-permute-start | bytes 98312 | tf_op jit(solution)/shard_map/ppermute | solution.py:22
  130.8 20.9 %collective-permute-start.5 = (f32[1,768]{1,0:T(1,128)S(1)}, f32[1,768]{1,0:T(1,128)S(1)}, u32[]{:S(2)}, u32[]{:S(2)}) collective-permute-start(f32[1,768]{1,0:T(1,128)S(1)} %rsqrt.26.inverse), channel_id=1, source_target_pairs={{0,1},{1,2},{2,3},{3,4},{4,5},{5,6},{6,7},{7,8},{8,9},{9,10},{10,1... | collective-permute-start | bytes 9224 | tf_op jit(solution)/shard_map/ppermute | solution.py:22
  130.8 35.6 %collective-permute-start.7 = (bf16[768,3072]{1,0:T(8,128)(2,1)}, bf16[768,3072]{1,0:T(8,128)(2,1)S(1)}, u32[]{:S(2)}, u32[]{:S(2)}) collective-permute-start(bf16[768,3072]{1,0:T(8,128)(2,1)} %collective-permute-done.3.partner), channel_id=1, source_target_pairs={{0,1},{1,0},{2,3},{3,2},{4,5},{5,4},{6,7},{7,6},{8,9},{9,8},{10,11... | collective-permute-start | bytes 14155784 | tf_op jit(solution)/shard_map/ppermute | solution.py:22
  151.8 6.9 %collective-permute-start.8 = (f32[1,768]{1,0:T(1,128)S(1)}, f32[1,768]{1,0:T(1,128)S(1)}, u32[]{:S(2)}, u32[]{:S(2)}) collective-permute-start(f32[1,768]{1,0:T(1,128)S(1)} %rsqrt.26.inverse), channel_id=1, source_target_pairs={{0,2},{1,3},{2,4},{3,5},{4,6},{5,7},{6,8},{7,9},{8,10},{9,11},{10,... | collective-permute-start | bytes 9224 | tf_op jit(solution)/shard_map/ppermute | solution.py:22
  158.7 7.7 %collective-permute-start.9 = (bf16[768,1024]{1,0:T(8,128)(2,1)}, bf16[768,1024]{1,0:T(8,128)(2,1)S(1)}, u32[]{:S(2)}, u32[]{:S(2)}) collective-permute-start(bf16[768,1024]{1,0:T(8,128)(2,1)} %collective-permute-done.1.partner), channel_id=1, source_target_pairs={{0,1},{1,0},{2,3},{3,2},{4,5},{5,4},{6,7},{7,6},{8,9},{9,8},{10,11... | collective-permute-start | bytes 4718600 | tf_op jit(solution)/shard_map/ppermute | solution.py:22
  158.7 28.8 %collective-permute-start.12 = (bf16[768,768]{1,0:T(8,128)(2,1)S(1)}, bf16[768,768]{1,0:T(8,128)(2,1)S(1)}, u32[]{:S(2)}, u32[]{:S(2)}) collective-permute-start(bf16[768,768]{1,0:T(8,128)(2,1)S(1)} %get-tuple-element.51), channel_id=1, source_target_pairs={{0,2},{1,3},{2,0},{3,1},{4,6},{5,7},{6,4},{7,5},{8,10},{9,11},{10,... | collective-permute-start | bytes 3538952 | tf_op jit(solution)/shard_map/ppermute | solution.py:22
  160.5 32.1 %collective-permute-start.13 = (bf16[768,768]{1,0:T(8,128)(2,1)S(1)}, bf16[768,768]{1,0:T(8,128)(2,1)S(1)}, u32[]{:S(2)}, u32[]{:S(2)}) collective-permute-start(bf16[768,768]{1,0:T(8,128)(2,1)S(1)} %get-tuple-element.57.kept), channel_id=1, source_target_pairs={{0,4},{1,5},{4,8},{5,9},{8,12},{9,13},{12,0},{13,1},{16,20},{17,21... | collective-permute-start | bytes 3538952 | tf_op jit(solution)/shard_map/ppermute | solution.py:22
  164.3 31.6 %collective-permute-start.11 = (f32[64,128]{1,0:T(8,128)S(1)}, f32[64,128]{1,0:T(8,128)S(1)}, u32[]{:S(2)}, u32[]{:S(2)}) collective-permute-start(f32[64,128]{1,0:T(8,128)S(1)} %add.66), channel_id=1, source_target_pairs={{0,4},{1,5},{2,6},{3,7},{4,0},{5,1},{6,2},{7,3},{8,12},{9,13},{10,... | collective-permute-start | bytes 98312 | tf_op jit(solution)/shard_map/ppermute | solution.py:22
  176.0 26.5 %collective-permute-start.10 = (bf16[768,768]{1,0:T(8,128)(2,1)S(1)}, bf16[768,768]{1,0:T(8,128)(2,1)}, u32[]{:S(2)}, u32[]{:S(2)}) collective-permute-start(bf16[768,768]{1,0:T(8,128)(2,1)S(1)} %shard_map.63.kept), channel_id=1, source_target_pairs={{1,2},{3,0},{5,6},{7,4},{9,10},{11,8},{13,14},{15,12},{17,18},{19,... | collective-permute-start | bytes 3538952 | tf_op jit(solution)/shard_map/ppermute | solution.py:22
  177.3 28.4 %collective-permute-start.16 = (bf16[768,768]{1,0:T(8,128)(2,1)S(1)}, bf16[768,768]{1,0:T(8,128)(2,1)}, u32[]{:S(2)}, u32[]{:S(2)}) collective-permute-start(bf16[768,768]{1,0:T(8,128)(2,1)S(1)} %shard_map.63.kept), channel_id=1, source_target_pairs={{0,4},{4,8},{8,12},{12,0},{16,20},{20,24},{24,28},{28,16}} | collective-permute-start | bytes 3538952 | tf_op jit(solution)/shard_map/ppermute | solution.py:22
  195.3 0.6 copy-start
  195.8 4.4 %collective-permute-start.14 = (f32[64,128]{1,0:T(8,128)S(1)}, f32[64,128]{1,0:T(8,128)S(1)}, u32[]{:S(2)}, u32[]{:S(2)}) collective-permute-start(f32[64,128]{1,0:T(8,128)S(1)} %add.67), channel_id=1, source_target_pairs={{0,2},{1,3},{2,0},{3,1},{4,6},{5,7},{6,4},{7,5},{8,10},{9,11},{10,... | collective-permute-start | bytes 98312 | tf_op jit(solution)/shard_map/ppermute | solution.py:22
  200.8 1.7 collective-permute-start.15
  205.7 4.0 %copy-start.1 = (f32[1,768]{1,0:T(1,128)S(1)}, f32[1,768]{1,0:T(1,128)}, u32[]{:S(2)}) copy-start(f32[1,768]{1,0:T(1,128)} %copy-done) | copy-start | bytes 9220
  209.6 3.6 %collective-permute-start.18 = (f32[1,768]{1,0:T(1,128)S(1)}, f32[1,768]{1,0:T(1,128)S(1)}, u32[]{:S(2)}, u32[]{:S(2)}) collective-permute-start(f32[1,768]{1,0:T(1,128)S(1)} %copy-done.1), channel_id=1, source_target_pairs={{0,14},{1,15},{2,0},{3,1},{4,2},{5,3},{6,4},{7,5},{8,6},{9,7},{10,... | collective-permute-start | bytes 9224 | tf_op jit(solution)/shard_map/ppermute | solution.py:22
  209.6 3.6 %collective-permute-start.17 = (f32[1,768]{1,0:T(1,128)S(1)}, f32[1,768]{1,0:T(1,128)S(1)}, u32[]{:S(2)}, u32[]{:S(2)}) collective-permute-start(f32[1,768]{1,0:T(1,128)S(1)} %get-tuple-element.65), channel_id=1, source_target_pairs={{0,15},{1,0},{2,1},{3,2},{4,3},{5,4},{6,5},{7,6},{8,7},{9,8},{10,9... | collective-permute-start | bytes 9224 | tf_op jit(solution)/shard_map/ppermute | solution.py:22

commit v11 on v10

--- a/solution.py
+++ b/solution.py
@@ -13,7 +13,7 @@
 DEPTH = 1024
 TALL = 384
 BAND = 256
-PIECES = 4
+PIECES = 16
 NT = (((1,), (1,)), ((), ()))
 VMEM_LIMIT = 40 * 2**20
 
@@ -340,19 +340,19 @@
     back_z = [pair for pair in back_v if pair[0] % 2 == 0]
     partner1 = after(partner1, inside, sums, across_lanes)
     u, v = early_tiles(place, sketches, partner1, near1)
-    other1 = send(partner1, swap)
     behind1 = send(after(across_lanes, partner1), [(i, (i + 1) % size) for i in blocks])
+    behind2 = send(after(across_lanes, partner1), [(i, (i + 2) % size) for i in blocks])
     for bit in bits[:-4]:
         sums = sums + doubled(sums, bit, partner1)
     came = doubled(sums, bits[-4], u)
-    partner2, near2, u, v, behind1, came = lax.optimization_barrier(
-        (partner2, near2, u, v, behind1, came)
-    )
-    behind2 = send(after(across_lanes, partner2), [(i, (i + 2) % size) for i in blocks])
+    partner2, near2, u, v, behind1, behind2, came = lax.optimization_barrier(
+        (partner2, near2, u, v, behind1, behind2, came)
+    )
+    other1 = send(after(partner1, partner2), swap)
     u, v = late_tiles(place, side2, partner2, near2, u, v)
     vr = send(v, back_v)
     ur = send(u, across)
-    other2 = send(after(partner2, u, behind2), swap)
+    other2 = send(after(partner2, u), swap)
     sums = sums + came
     came = doubled(sums, bits[-3], u)
     x = cross_tile(place, sketches, near1, near2, after(other1, u), other2)

time: 214 us -> 213 us (level)
  no operation moved by 1% of the time
where the time goes in v11:
time: 213 us
  waiting for transfers between devices  116 us (54%)
  Pallas kernels  54.8 us (26%)
  starting transfers between devices  22.8 us (11%)
  other arithmetic  10.3 us (5%)
  matrix products  7.47 us (4%)
    ppermute x19, waiting for transfers between devices, send(): return lax.ppermute(value, 'blocks', pairs)  116 us
    ppermute x19, starting transfers between devices, send(): return lax.ppermute(value, 'blocks', pairs)  22.8 us
    pallas_call x2, Pallas kernels, halves(): pl.pallas_call(functools.partial(halves_kernel, start, sides), in_specs=[...  12.4 us
    pallas_call x1, Pallas kernels, early_tiles(): pl.pallas_call(early_kernel, grid_spec=pltpu.PrefetchScalarGridSpec(num_s...  11.4 us
    pallas_call x1, Pallas kernels, inside_tile(): pl.pallas_call(inside_kernel, grid_spec=pltpu.PrefetchScalarGridSpec(num_...  9.77 us
    pallas_call x1, Pallas kernels, cross_tile(): pl.pallas_call(cross_kernel, grid_spec=pltpu.PrefetchScalarGridSpec(num_s...  9.57 us
    reduce_sum x2, other arithmetic, inverse_norm(): return lax.rsqrt(jnp.mean(values * values, axis=1) + 1e-06)  7.7 us
    dot_general x1, matrix products, local(): lax.dot_general(members, similarity, (((0,), (0,)), ((), ())), preferred_...  7.47 us
  transfers between devices with their start and end apart: 19, of which 11 were waited for; matrix products, arithmetic and copies ran while one was open for 8% of the time, Pallas kernels for 20%

profile of v11, /device:TPU:0, one launch (start us, length us, event | category | flops | bytes accessed | tf_op | source)
XLA Modules:
  0.0 212.8 jit_solution(6502351306720883613)
XLA Ops:
  0.7 8.3 %shard_map.58 = (bf16[768,3072]{1,0:T(8,128)(2,1)}, bf16[768,3072]{1,0:T(8,128)(2,1)}) custom-call(s32[2]{0:T(128)S(1)} %pad_add_fusion.place, bf16[768,8192]{1,0:T(8,128)(2,1)} %own.6), custom_call_target="tpu_custom_call" | custom-call | bytes 18874368 | tf_op jit(solution)/shard_map/pallas_call | solution.py:83
  9.5 2.6 %collective-permute-start.3 = (bf16[768,3072]{1,0:T(8,128)(2,1)}, bf16[768,3072]{1,0:T(8,128)(2,1)}, u32[]{:S(2)}, u32[]{:S(2)}) collective-permute-start(bf16[768,3072]{1,0:T(8,128)(2,1)} %get-tuple-element.41), channel_id=1, source_target_pairs={{0,2},{1,3},{2,0},{3,1},{4,6},{5,7},{6,4},{7,5},{8,10},{9,11},{10,... | collective-permute-start | bytes 14155784 | tf_op jit(solution)/shard_map/ppermute | solution.py:22
  12.1 3.6 %collective-permute-start = (bf16[768,3072]{1,0:T(8,128)(2,1)}, bf16[768,3072]{1,0:T(8,128)(2,1)}, u32[]{:S(2)}, u32[]{:S(2)}) collective-permute-start(bf16[768,3072]{1,0:T(8,128)(2,1)} %get-tuple-element.37), channel_id=1, source_target_pairs={{0,12},{1,13},{2,6},{3,7},{4,0},{5,1},{6,10},{7,11},{8,4},{9,5},{1... | collective-permute-start | bytes 14155784 | tf_op jit(solution)/shard_map/ppermute | solution.py:22
  15.7 4.1 %shard_map.59 = (bf16[768,1024]{1,0:T(8,128)(2,1)}, bf16[768,1024]{1,0:T(8,128)(2,1)}) custom-call(s32[2]{0:T(128)S(1)} %pad_add_fusion.place, bf16[768,8192]{1,0:T(8,128)(2,1)} %own.6), custom_call_target="tpu_custom_call" | custom-call | bytes 6291456 | tf_op jit(solution)/shard_map/pallas_call | solution.py:83
  20.4 7.2 %multiply_reduce_fusion = f32[768]{0:T(1024)S(1)} fusion(bf16[768,8192]{1,0:T(8,128)(2,1)} %own.6), kind=kLoop, calls=%fused_computation | loop fusion | flops 18873600 | bytes 12585984 | tf_op jit(solution)/shard_map/reduce_sum | solution.py:31
  28.2 7.5 %fusion.3 = f32[64,128]{1,0:T(8,128)} fusion(bf16[768,8192]{1,0:T(8,128)(2,1)} %own.6, bf16[128,8192]{1,0:T(8,128)(2,1)S(1)} %copy-done.2, f32[128]{0:T(128)S(1)} %add_rsqrt_fusion.1, f32[768]{0:T(1024)S(1)} %add_rsqrt_fusion, s32[768]{0:T(1024)S(1)} %copy-done.4), kind=kOutput, calls=%fused_computation.6 | convolution fusion | flops 1623638016 | bytes 14719488 | tf_op jit(solution)/shard_map/dot_general | solution.py:328
  35.7 9.8 %shard_map.60.local = f32[768,768]{1,0:T(8,128)S(1)} custom-call(s32[2]{0:T(128)S(1)} %pad_add_fusion.place, bf16[768,8192]{1,0:T(8,128)(2,1)} %own.6, bf16[768,8192]{1,0:T(8,128)(2,1)} %collective-permute-done.4.other), custom_call_target="tpu_custom_call" | custom-call | flops 9663676416 | bytes 25165824 | tf_op jit(solution)/shard_map/pallas_call | solution.py:215
  45.4 69.7 %collective-permute-done.3.partner = bf16[768,3072]{1,0:T(8,128)(2,1)} collective-permute-done((bf16[768,3072]{1,0:T(8,128)(2,1)}, bf16[768,3072]{1,0:T(8,128)(2,1)}, u32[]{:S(2)}, u32[]{:S(2)}) %collective-permute-start.3) | collective-permute-done | bytes 4718624 | tf_op jit(solution)/shard_map/ppermute | solution.py:22
  115.1 3.1 %collective-permute-done.near.near1 = bf16[768,3072]{1,0:T(8,128)(2,1)} collective-permute-done((bf16[768,3072]{1,0:T(8,128)(2,1)}, bf16[768,3072]{1,0:T(8,128)(2,1)}, u32[]{:S(2)}, u32[]{:S(2)}) %collective-permute-start) | collective-permute-done | bytes 4718624 | tf_op jit(solution)/shard_map/ppermute | solution.py:22
  118.2 11.4 %shard_map.61 = (f32[768,768]{1,0:T(8,128)S(1)}, f32[768,768]{1,0:T(8,128)S(1)}) custom-call(s32[2]{0:T(128)S(1)} %pad_add_fusion.place, bf16[768,8192]{1,0:T(8,128)(2,1)} %own.6, bf16[768,3072]{1,0:T(8,128)(2,1)} %collective-permute-done.3.partner, bf16[768,3072]{1,0:T(8,128)(2,1)} %collective-permute-done.near.near1), custom_call_target="tpu_custom_call" | custom-call | flops 768 | bytes 768 | tf_op jit(solution)/shard_map/pallas_call | solution.py:118
  131.7 16.8 %collective-permute-done.1.partner = bf16[768,1024]{1,0:T(8,128)(2,1)} collective-permute-done((bf16[768,1024]{1,0:T(8,128)(2,1)}, bf16[768,1024]{1,0:T(8,128)(2,1)}, u32[]{:S(2)}, u32[]{:S(2)}) %collective-permute-start.1) | collective-permute-done | bytes 1572896 | tf_op jit(solution)/shard_map/ppermute | solution.py:22
  148.5 3.0 %collective-permute-done.2.near.near2 = bf16[768,1024]{1,0:T(8,128)(2,1)} collective-permute-done((bf16[768,1024]{1,0:T(8,128)(2,1)}, bf16[768,1024]{1,0:T(8,128)(2,1)}, u32[]{:S(2)}, u32[]{:S(2)}) %collective-permute-start.2) | collective-permute-done | bytes 1572896 | tf_op jit(solution)/shard_map/ppermute | solution.py:22
  152.6 5.1 %shard_map.62 = (bf16[768,768]{1,0:T(8,128)(2,1)S(1)}, bf16[768,768]{1,0:T(8,128)(2,1)S(1)}) custom-call(s32[2]{0:T(128)S(1)} %pad_add_fusion.place, bf16[768,1024]{1,0:T(8,128)(2,1)} %get-tuple-element.40.mine, bf16[768,1024]{1,0:T(8,128)(2,1)} %collective-permute-done.1.partner, bf16[768,1024]{1,0:T(8,128)(2,1)} %collective-permute-done.2.near.near2, ...), custom_call_target="tpu_custom_call" | custom-call | flops 35389440000 | bytes 94371840 | tf_op jit(solution)/shard_map/pallas_call | solution.py:150
  159.5 2.1 collective-permute-start.13
  161.5 1.9 collective-permute-start.11
  163.5 9.6 %shard_map.63.kept = bf16[768,768]{1,0:T(8,128)(2,1)S(1)} custom-call(s32[2]{0:T(128)S(1)} %pad_add_fusion.place, bf16[768,8192]{1,0:T(8,128)(2,1)} %own.6, bf16[768,3072]{1,0:T(8,128)(2,1)} %collective-permute-done.near.near1, bf16[768,1024]{1,0:T(8,128)(2,1)} %collective-permute-done.2.near.near2, bf16[768,3072]{1,0:T(8,128)(2,1)S(1)} %collective-permute-done.8.other1, ...), custom_call_target="tpu_custom_call" | custom-call | flops 3623878656 | bytes 14155776 | tf_op jit(solution)/shard_map/pallas_call | solution.py:189
  174.3 2.8 %collective-permute-start.16 = (bf16[768,768]{1,0:T(8,128)(2,1)S(1)}, bf16[768,768]{1,0:T(8,128)(2,1)}, u32[]{:S(2)}, u32[]{:S(2)}) collective-permute-start(bf16[768,768]{1,0:T(8,128)(2,1)S(1)} %shard_map.63.kept), channel_id=1, source_target_pairs={{0,4},{4,8},{8,12},{12,0},{16,20},{20,24},{24,28},{28,16}} | collective-permute-start | bytes 3538952 | tf_op jit(solution)/shard_map/ppermute | solution.py:22
  177.1 10.0 %collective-permute-done.12.u = bf16[768,768]{1,0:T(8,128)(2,1)S(1)} collective-permute-done((bf16[768,768]{1,0:T(8,128)(2,1)S(1)}, bf16[768,768]{1,0:T(8,128)(2,1)S(1)}, u32[]{:S(2)}, u32[]{:S(2)}) %collective-permute-start.12) | collective-permute-done | bytes 1179680 | tf_op jit(solution)/shard_map/ppermute | solution.py:22
  187.1 4.0 %collective-permute-done.13.v = bf16[768,768]{1,0:T(8,128)(2,1)S(1)} collective-permute-done((bf16[768,768]{1,0:T(8,128)(2,1)S(1)}, bf16[768,768]{1,0:T(8,128)(2,1)S(1)}, u32[]{:S(2)}, u32[]{:S(2)}) %collective-permute-start.13) | collective-permute-done | bytes 1179680 | tf_op jit(solution)/shard_map/ppermute | solution.py:22
  191.2 2.6 %shard_map.64 = (f32[2,768,768]{2,1,0:T(8,128)}, f32[1,768]{1,0:T(1,128)S(1)}, f32[1,768]{1,0:T(1,128)S(1)}) custom-call(s32[2]{0:T(128)S(1)} %pad_add_fusion.place, bf16[768,768]{1,0:T(8,128)(2,1)S(1)} %collective-permute-done.12.u, bf16[768,768]{1,0:T(8,128)(2,1)S(1)} %collective-permute-done.13.v, bf16[768,768]{1,0:T(8,128)(2,1)S(1)} %get-tuple-element.58.kept, ...), custom_call_target="tpu_custom_call" | custom-call | flops 35389440000 | bytes 94371840 | tf_op jit(solution)/shard_map/pallas_call | solution.py:273
  194.5 4.3 %collective-permute-done.14 = f32[64,128]{1,0:T(8,128)S(1)} collective-permute-done((f32[64,128]{1,0:T(8,128)S(1)}, f32[64,128]{1,0:T(8,128)S(1)}, u32[]{:S(2)}, u32[]{:S(2)}) %collective-permute-start.14) | collective-permute-done | bytes 32800 | tf_op jit(solution)/shard_map/ppermute | solution.py:22
  201.6 2.6 %collective-permute-done.16.z = bf16[768,768]{1,0:T(8,128)(2,1)} collective-permute-done((bf16[768,768]{1,0:T(8,128)(2,1)S(1)}, bf16[768,768]{1,0:T(8,128)(2,1)}, u32[]{:S(2)}, u32[]{:S(2)}) %collective-permute-start.16) | collective-permute-done | bytes 1179680 | tf_op jit(solution)/shard_map/ppermute | solution.py:22
  204.3 4.0 %shard_map.65 = (f32[2,768,768]{2,1,0:T(8,128)}, f32[1,768]{1,0:T(1,128)S(1)}, f32[1,768]{1,0:T(1,128)S(1)}) custom-call(s32[2]{0:T(128)S(1)} %pad_add_fusion.place, bf16[768,768]{1,0:T(8,128)(2,1)} %collective-permute-done.10.y, bf16[768,768]{1,0:T(8,128)(2,1)} %collective-permute-done.16.z, ...), custom_call_target="tpu_custom_call", output_to_operand_aliasing={{0}: (7, {})} | custom-call | flops 4718592 | bytes 7077888 | tf_op jit(solution)/shard_map/pallas_call | solution.py:273
  209.1 1.8 collective-permute-start.17
  (44 shorter events, 14.2 us)
Async XLA Ops:
  9.0 26.7 %collective-permute-start.4 = (bf16[768,8192]{1,0:T(8,128)(2,1)}, bf16[768,8192]{1,0:T(8,128)(2,1)}, u32[]{:S(2)}, u32[]{:S(2)}) collective-permute-start(bf16[768,8192]{1,0:T(8,128)(2,1)} %own.6), channel_id=1, source_target_pairs={{0,1},{1,0},{2,3},{3,2},{4,5},{5,4},{6,7},{7,6},{8,9},{9,8},{10,11... | collective-permute-start | bytes 37748744 | tf_op jit(solution)/shard_map/ppermute | solution.py:22
  9.5 105.6 %collective-permute-start.3 = (bf16[768,3072]{1,0:T(8,128)(2,1)}, bf16[768,3072]{1,0:T(8,128)(2,1)}, u32[]{:S(2)}, u32[]{:S(2)}) collective-permute-start(bf16[768,3072]{1,0:T(8,128)(2,1)} %get-tuple-element.41), channel_id=1, source_target_pairs={{0,2},{1,3},{2,0},{3,1},{4,6},{5,7},{6,4},{7,5},{8,10},{9,11},{10,... | collective-permute-start | bytes 14155784 | tf_op jit(solution)/shard_map/ppermute | solution.py:22
  12.1 106.1 %collective-permute-start = (bf16[768,3072]{1,0:T(8,128)(2,1)}, bf16[768,3072]{1,0:T(8,128)(2,1)}, u32[]{:S(2)}, u32[]{:S(2)}) collective-permute-start(bf16[768,3072]{1,0:T(8,128)(2,1)} %get-tuple-element.37), channel_id=1, source_target_pairs={{0,12},{1,13},{2,6},{3,7},{4,0},{5,1},{6,10},{7,11},{8,4},{9,5},{1... | collective-permute-start | bytes 14155784 | tf_op jit(solution)/shard_map/ppermute | solution.py:22
  19.8 128.7 %collective-permute-start.1 = (bf16[768,1024]{1,0:T(8,128)(2,1)}, bf16[768,1024]{1,0:T(8,128)(2,1)}, u32[]{:S(2)}, u32[]{:S(2)}) collective-permute-start(bf16[768,1024]{1,0:T(8,128)(2,1)} %get-tuple-element.39), channel_id=1, source_target_pairs={{0,2},{1,3},{2,0},{3,1},{4,6},{5,7},{6,4},{7,5},{8,10},{9,11},{10,... | collective-permute-start | bytes 4718600 | tf_op jit(solution)/shard_map/ppermute | solution.py:22
  19.9 7.8 %copy-start.2 = (bf16[128,8192]{1,0:T(8,128)(2,1)S(1)}, bf16[128,8192]{1,0:T(8,128)(2,1)}, u32[]{:S(2)}) copy-start(bf16[128,8192]{1,0:T(8,128)(2,1)} %param.4) | copy-start | bytes 6291460
  19.9 8.3 %copy-start.4 = (s32[768]{0:T(1024)S(1)}, s32[768]{0:T(1024)}, u32[]{:S(2)}) copy-start(s32[768]{0:T(1024)} %param.5) | copy-start | bytes 9220
  19.9 131.6 %collective-permute-start.2 = (bf16[768,1024]{1,0:T(8,128)(2,1)}, bf16[768,1024]{1,0:T(8,128)(2,1)}, u32[]{:S(2)}, u32[]{:S(2)}) collective-permute-start(bf16[768,1024]{1,0:T(8,128)(2,1)} %get-tuple-element.40.mine), channel_id=1, source_target_pairs={{0,12},{1,13},{2,6},{3,7},{4,0},{5,1},{6,10},{7,11},{8,4},{9,5},{1... | collective-permute-start | bytes 4718600 | tf_op jit(solution)/shard_map/ppermute | solution.py:22
  45.4 84.2 %copy-start.3 = (f32[64,128]{1,0:T(8,128)S(1)}, f32[64,128]{1,0:T(8,128)}, u32[]{:S(2)}) copy-start(f32[64,128]{1,0:T(8,128)} %fusion.3) | copy-start | bytes 98308
  129.6 23.0 %collective-permute-start.7 = (f32[64,128]{1,0:T(8,128)S(1)}, f32[64,128]{1,0:T(8,128)S(1)}, u32[]{:S(2)}, u32[]{:S(2)}) collective-permute-start(f32[64,128]{1,0:T(8,128)S(1)} %copy-done.3), channel_id=1, source_target_pairs={{0,8},{1,9},{2,10},{3,11},{4,12},{5,13},{6,14},{7,15},{8,0},{9,1},... | collective-permute-start | bytes 98312 | tf_op jit(solution)/shard_map/ppermute | solution.py:22
  131.2 20.9 %collective-permute-start.5 = (f32[1,768]{1,0:T(1,128)S(1)}, f32[1,768]{1,0:T(1,128)S(1)}, u32[]{:S(2)}, u32[]{:S(2)}) collective-permute-start(f32[1,768]{1,0:T(1,128)S(1)} %rsqrt.26.inverse), channel_id=1, source_target_pairs={{0,1},{1,2},{2,3},{3,4},{4,5},{5,6},{6,7},{7,8},{8,9},{9,10},{10,1... | collective-permute-start | bytes 9224 | tf_op jit(solution)/shard_map/ppermute | solution.py:22
  131.2 21.4 %collective-permute-start.6 = (f32[1,768]{1,0:T(1,128)S(1)}, f32[1,768]{1,0:T(1,128)S(1)}, u32[]{:S(2)}, u32[]{:S(2)}) collective-permute-start(f32[1,768]{1,0:T(1,128)S(1)} %rsqrt.26.inverse), channel_id=1, source_target_pairs={{0,2},{1,3},{2,4},{3,5},{4,6},{5,7},{6,8},{7,9},{8,10},{9,11},{10,... | collective-permute-start | bytes 9224 | tf_op jit(solution)/shard_map/ppermute | solution.py:22
  152.6 10.8 %collective-permute-start.8 = (bf16[768,3072]{1,0:T(8,128)(2,1)}, bf16[768,3072]{1,0:T(8,128)(2,1)S(1)}, u32[]{:S(2)}, u32[]{:S(2)}) collective-permute-start(bf16[768,3072]{1,0:T(8,128)(2,1)} %collective-permute-done.3.partner), channel_id=1, source_target_pairs={{0,1},{1,0},{2,3},{3,2},{4,5},{5,4},{6,7},{7,6},{8,9},{9,8},{10,11... | collective-permute-start | bytes 14155784 | tf_op jit(solution)/shard_map/ppermute | solution.py:22
  157.7 5.7 %collective-permute-start.9 = (bf16[768,1024]{1,0:T(8,128)(2,1)}, bf16[768,1024]{1,0:T(8,128)(2,1)S(1)}, u32[]{:S(2)}, u32[]{:S(2)}) collective-permute-start(bf16[768,1024]{1,0:T(8,128)(2,1)} %collective-permute-done.1.partner), channel_id=1, source_target_pairs={{0,1},{1,0},{2,3},{3,2},{4,5},{5,4},{6,7},{7,6},{8,9},{9,8},{10,11... | collective-permute-start | bytes 4718600 | tf_op jit(solution)/shard_map/ppermute | solution.py:22
  158.3 28.8 %collective-permute-start.12 = (bf16[768,768]{1,0:T(8,128)(2,1)S(1)}, bf16[768,768]{1,0:T(8,128)(2,1)S(1)}, u32[]{:S(2)}, u32[]{:S(2)}) collective-permute-start(bf16[768,768]{1,0:T(8,128)(2,1)S(1)} %get-tuple-element.53), channel_id=1, source_target_pairs={{0,2},{1,3},{2,0},{3,1},{4,6},{5,7},{6,4},{7,5},{8,10},{9,11},{10,... | collective-permute-start | bytes 3538952 | tf_op jit(solution)/shard_map/ppermute | solution.py:22
  159.5 31.7 %collective-permute-start.13 = (bf16[768,768]{1,0:T(8,128)(2,1)S(1)}, bf16[768,768]{1,0:T(8,128)(2,1)S(1)}, u32[]{:S(2)}, u32[]{:S(2)}) collective-permute-start(bf16[768,768]{1,0:T(8,128)(2,1)S(1)} %get-tuple-element.58.kept), channel_id=1, source_target_pairs={{0,4},{1,5},{4,8},{5,9},{8,12},{9,13},{12,0},{13,1},{16,20},{17,21... | collective-permute-start | bytes 3538952 | tf_op jit(solution)/shard_map/ppermute | solution.py:22
  161.5 32.9 %collective-permute-start.11 = (f32[64,128]{1,0:T(8,128)S(1)}, f32[64,128]{1,0:T(8,128)S(1)}, u32[]{:S(2)}, u32[]{:S(2)}) collective-permute-start(f32[64,128]{1,0:T(8,128)S(1)} %add.66), channel_id=1, source_target_pairs={{0,4},{1,5},{2,6},{3,7},{4,0},{5,1},{6,2},{7,3},{8,12},{9,13},{10,... | collective-permute-start | bytes 98312 | tf_op jit(solution)/shard_map/ppermute | solution.py:22
  173.0 28.6 %collective-permute-start.10 = (bf16[768,768]{1,0:T(8,128)(2,1)S(1)}, bf16[768,768]{1,0:T(8,128)(2,1)}, u32[]{:S(2)}, u32[]{:S(2)}) collective-permute-start(bf16[768,768]{1,0:T(8,128)(2,1)S(1)} %shard_map.63.kept), channel_id=1, source_target_pairs={{1,2},{3,0},{5,6},{7,4},{9,10},{11,8},{13,14},{15,12},{17,18},{19,... | collective-permute-start | bytes 3538952 | tf_op jit(solution)/shard_map/ppermute | solution.py:22
  174.3 29.9 %collective-permute-start.16 = (bf16[768,768]{1,0:T(8,128)(2,1)S(1)}, bf16[768,768]{1,0:T(8,128)(2,1)}, u32[]{:S(2)}, u32[]{:S(2)}) collective-permute-start(bf16[768,768]{1,0:T(8,128)(2,1)S(1)} %shard_map.63.kept), channel_id=1, source_target_pairs={{0,4},{4,8},{8,12},{12,0},{16,20},{20,24},{24,28},{28,16}} | collective-permute-start | bytes 3538952 | tf_op jit(solution)/shard_map/ppermute | solution.py:22
  193.8 0.6 copy-start
  194.4 4.4 %collective-permute-start.14 = (f32[64,128]{1,0:T(8,128)S(1)}, f32[64,128]{1,0:T(8,128)S(1)}, u32[]{:S(2)}, u32[]{:S(2)}) collective-permute-start(f32[64,128]{1,0:T(8,128)S(1)} %add.67), channel_id=1, source_target_pairs={{0,2},{1,3},{2,0},{3,1},{4,6},{5,7},{6,4},{7,5},{8,10},{9,11},{10,... | collective-permute-start | bytes 98312 | tf_op jit(solution)/shard_map/ppermute | solution.py:22
  199.4 2.2 %collective-permute-start.15 = (f32[64,128]{1,0:T(8,128)}, f32[64,128]{1,0:T(8,128)}, u32[]{:S(2)}, u32[]{:S(2)}) collective-permute-start(f32[64,128]{1,0:T(8,128)} %add.68), channel_id=1, source_target_pairs={{0,1},{1,0},{2,3},{3,2},{4,5},{5,4},{6,7},{7,6},{8,9},{9,8},{10,11... | collective-permute-start | bytes 98312 | tf_op jit(solution)/shard_map/ppermute | solution.py:22
  204.3 4.0 %copy-start.1 = (f32[1,768]{1,0:T(1,128)S(1)}, f32[1,768]{1,0:T(1,128)}, u32[]{:S(2)}) copy-start(f32[1,768]{1,0:T(1,128)} %copy-done) | copy-start | bytes 9220
  208.2 3.9 %collective-permute-start.18 = (f32[1,768]{1,0:T(1,128)S(1)}, f32[1,768]{1,0:T(1,128)S(1)}, u32[]{:S(2)}, u32[]{:S(2)}) collective-permute-start(f32[1,768]{1,0:T(1,128)S(1)} %copy-done.1), channel_id=1, source_target_pairs={{0,14},{1,15},{2,0},{3,1},{4,2},{5,3},{6,4},{7,5},{8,6},{9,7},{10,... | collective-permute-start | bytes 9224 | tf_op jit(solution)/shard_map/ppermute | solution.py:22
  209.1 3.1 %collective-permute-start.17 = (f32[1,768]{1,0:T(1,128)S(1)}, f32[1,768]{1,0:T(1,128)S(1)}, u32[]{:S(2)}, u32[]{:S(2)}) collective-permute-start(f32[1,768]{1,0:T(1,128)S(1)} %get-tuple-element.67), channel_id=1, source_target_pairs={{0,15},{1,0},{2,1},{3,2},{4,3},{5,4},{6,5},{7,6},{8,7},{9,8},{10,9... | collective-permute-start | bytes 9224 | tf_op jit(solution)/shard_map/ppermute | solution.py:22

commit v12 on v11

--- a/solution.py
+++ b/solution.py
@@ -13,7 +13,7 @@
 DEPTH = 1024
 TALL = 384
 BAND = 256
-PIECES = 16
+PIECES = 2
 NT = (((1,), (1,)), ((), ()))
 VMEM_LIMIT = 40 * 2**20
 
@@ -363,18 +363,19 @@
     )
     sums = sums + after(came, row_mass2)
     sums = sums + doubled(sums, bits[-2])
-    came = doubled(sums, bits[-1])
-    y, came = lax.optimization_barrier((y, came))
+    sums = sums + doubled(sums, bits[-1])
+    sums = lax.dynamic_slice_in_dim(sums, index * DOM_DEV, DOM_DEV)
+    domain_scores = sums * (1.0 / math.sqrt(rows / DOM_DEV))
+    y, z, domain_scores = lax.optimization_barrier((y, z, domain_scores))
+    from_second = send(after(column_mass2, sums), [(i, (i - 2) % size) for i in blocks])
     gram, row_mass1, column_mass1 = join(
         first_kernel, 0, scale, place, (y, z, x, inside), across_lanes, behind1, (gram,)
     )
-    sums = lax.dynamic_slice_in_dim(sums + came, index * DOM_DEV, DOM_DEV)
-    domain_scores = sums * (1.0 / math.sqrt(rows / DOM_DEV))
     mass = (
         row_mass1
         + row_mass2
         + send(column_mass1, [(i, (i - 1) % size) for i in blocks])
-        + send(after(column_mass2, row_mass1), [(i, (i - 2) % size) for i in blocks])
+        + from_second
     )
     redundancy = mass[0] / float(2 * ROUNDS * rows)
     return (gram, redundancy, domain_scores)

time: 213 us -> 215 us (level)
  starting transfers between devices: 22.8 us -> 25.2 us
    ppermute x19, starting transfers between devices: 22.8 us -> 25.2 us  [send(): return lax.ppermute(value, 'blocks', pairs)]
  transfers between devices with their start and end apart: 19 -> 19, of which waited for: 11 -> 11; matrix products, arithmetic and copies ran while one was open for 8% -> 8% of each run, Pallas kernels for 20% -> 21%
where the time goes in v12:
time: 215 us; the launch traced here: 214 us
  waiting for transfers between devices  116 us (54%)
  Pallas kernels  54.5 us (25%)
  starting transfers between devices  25.2 us (12%)
  other arithmetic  10.3 us (5%)
  matrix products  6.88 us (3%)
    ppermute x19, waiting for transfers between devices, send(): return lax.ppermute(value, 'blocks', pairs)  116 us
    ppermute x19, starting transfers between devices, send(): return lax.ppermute(value, 'blocks', pairs)  25.2 us
    pallas_call x2, Pallas kernels, halves(): pl.pallas_call(functools.partial(halves_kernel, start, sides), in_specs=[...  11.8 us
    pallas_call x1, Pallas kernels, early_tiles(): pl.pallas_call(early_kernel, grid_spec=pltpu.PrefetchScalarGridSpec(num_s...  11.4 us
    pallas_call x1, Pallas kernels, inside_tile(): pl.pallas_call(inside_kernel, grid_spec=pltpu.PrefetchScalarGridSpec(num_...  9.77 us
    pallas_call x1, Pallas kernels, cross_tile(): pl.pallas_call(cross_kernel, grid_spec=pltpu.PrefetchScalarGridSpec(num_s...  9.57 us
    reduce_sum x2, other arithmetic, inverse_norm(): return lax.rsqrt(jnp.mean(values * values, axis=1) + 1e-06)  7.7 us
    dot_general x1, matrix products, local(): lax.dot_general(members, similarity, (((0,), (0,)), ((), ())), preferred_...  6.88 us
  transfers between devices with their start and end apart: 19, of which 11 were waited for; matrix products, arithmetic and copies ran while one was open for 8% of the time, Pallas kernels for 21%

profile of v12, /device:TPU:0, one launch (start us, length us, event | category | flops | bytes accessed | tf_op | source)
XLA Modules:
  0.0 214.4 jit_solution(8080207518952040535)
XLA Ops:
  0.7 8.4 %shard_map.58 = (bf16[768,3072]{1,0:T(8,128)(2,1)}, bf16[768,3072]{1,0:T(8,128)(2,1)}) custom-call(s32[2]{0:T(128)S(1)} %pad_add_fusion.place, bf16[768,8192]{1,0:T(8,128)(2,1)} %own.6), custom_call_target="tpu_custom_call" | custom-call | bytes 18874368 | tf_op jit(solution)/shard_map/pallas_call | solution.py:83
  9.7 2.6 %collective-permute-start.3 = (bf16[768,3072]{1,0:T(8,128)(2,1)}, bf16[768,3072]{1,0:T(8,128)(2,1)}, u32[]{:S(2)}, u32[]{:S(2)}) collective-permute-start(bf16[768,3072]{1,0:T(8,128)(2,1)} %get-tuple-element.42), channel_id=1, source_target_pairs={{0,2},{1,3},{2,0},{3,1},{4,6},{5,7},{6,4},{7,5},{8,10},{9,11},{10,... | collective-permute-start | bytes 14155784 | tf_op jit(solution)/shard_map/ppermute | solution.py:22
  12.3 3.6 %collective-permute-start = (bf16[768,3072]{1,0:T(8,128)(2,1)}, bf16[768,3072]{1,0:T(8,128)(2,1)}, u32[]{:S(2)}, u32[]{:S(2)}) collective-permute-start(bf16[768,3072]{1,0:T(8,128)(2,1)} %get-tuple-element.38), channel_id=1, source_target_pairs={{0,12},{1,13},{2,6},{3,7},{4,0},{5,1},{6,10},{7,11},{8,4},{9,5},{1... | collective-permute-start | bytes 14155784 | tf_op jit(solution)/shard_map/ppermute | solution.py:22
  15.9 3.4 %shard_map.59 = (bf16[768,1024]{1,0:T(8,128)(2,1)}, bf16[768,1024]{1,0:T(8,128)(2,1)}) custom-call(s32[2]{0:T(128)S(1)} %pad_add_fusion.place, bf16[768,8192]{1,0:T(8,128)(2,1)} %own.6), custom_call_target="tpu_custom_call" | custom-call | bytes 6291456 | tf_op jit(solution)/shard_map/pallas_call | solution.py:83
  19.9 7.2 %multiply_reduce_fusion = f32[768]{0:T(1024)S(1)} fusion(bf16[768,8192]{1,0:T(8,128)(2,1)} %own.6), kind=kLoop, calls=%fused_computation | loop fusion | flops 18873600 | bytes 12585984 | tf_op jit(solution)/shard_map/reduce_sum | solution.py:31
  27.6 6.9 %fusion.3 = f32[64,128]{1,0:T(8,128)S(1)} fusion(bf16[768,8192]{1,0:T(8,128)(2,1)} %own.6, bf16[128,8192]{1,0:T(8,128)(2,1)S(1)} %copy-done.1, f32[128]{0:T(128)S(1)} %add_rsqrt_fusion.1, f32[768]{0:T(1024)S(1)} %add_rsqrt_fusion, s32[768]{0:T(1024)S(1)} %copy-done.2), kind=kOutput, calls=%fused_computation.6 | convolution fusion | flops 1623638016 | bytes 14719488 | tf_op jit(solution)/shard_map/dot_general | solution.py:328
  34.5 9.8 %shard_map.60.local = f32[768,768]{1,0:T(8,128)S(1)} custom-call(s32[2]{0:T(128)S(1)} %pad_add_fusion.place, bf16[768,8192]{1,0:T(8,128)(2,1)} %own.6, bf16[768,8192]{1,0:T(8,128)(2,1)} %collective-permute-done.4.other), custom_call_target="tpu_custom_call" | custom-call | flops 9663676416 | bytes 25165824 | tf_op jit(solution)/shard_map/pallas_call | solution.py:215
  44.3 71.0 %collective-permute-done.3.partner = bf16[768,3072]{1,0:T(8,128)(2,1)} collective-permute-done((bf16[768,3072]{1,0:T(8,128)(2,1)}, bf16[768,3072]{1,0:T(8,128)(2,1)}, u32[]{:S(2)}, u32[]{:S(2)}) %collective-permute-start.3) | collective-permute-done | bytes 4718624 | tf_op jit(solution)/shard_map/ppermute | solution.py:22
  115.3 3.1 %collective-permute-done.near.near1 = bf16[768,3072]{1,0:T(8,128)(2,1)} collective-permute-done((bf16[768,3072]{1,0:T(8,128)(2,1)}, bf16[768,3072]{1,0:T(8,128)(2,1)}, u32[]{:S(2)}, u32[]{:S(2)}) %collective-permute-start) | collective-permute-done | bytes 4718624 | tf_op jit(solution)/shard_map/ppermute | solution.py:22
  118.4 11.4 %shard_map.61 = (f32[768,768]{1,0:T(8,128)S(1)}, f32[768,768]{1,0:T(8,128)S(1)}) custom-call(s32[2]{0:T(128)S(1)} %pad_add_fusion.place, bf16[768,8192]{1,0:T(8,128)(2,1)} %own.6, bf16[768,3072]{1,0:T(8,128)(2,1)} %collective-permute-done.3.partner, bf16[768,3072]{1,0:T(8,128)(2,1)} %collective-permute-done.near.near1), custom_call_target="tpu_custom_call" | custom-call | flops 768 | bytes 768 | tf_op jit(solution)/shard_map/pallas_call | solution.py:118
  131.9 16.8 %collective-permute-done.1.partner = bf16[768,1024]{1,0:T(8,128)(2,1)} collective-permute-done((bf16[768,1024]{1,0:T(8,128)(2,1)}, bf16[768,1024]{1,0:T(8,128)(2,1)}, u32[]{:S(2)}, u32[]{:S(2)}) %collective-permute-start.1) | collective-permute-done | bytes 1572896 | tf_op jit(solution)/shard_map/ppermute | solution.py:22
  148.7 3.0 %collective-permute-done.2.near.near2 = bf16[768,1024]{1,0:T(8,128)(2,1)} collective-permute-done((bf16[768,1024]{1,0:T(8,128)(2,1)}, bf16[768,1024]{1,0:T(8,128)(2,1)}, u32[]{:S(2)}, u32[]{:S(2)}) %collective-permute-start.2) | collective-permute-done | bytes 1572896 | tf_op jit(solution)/shard_map/ppermute | solution.py:22
  152.8 5.3 %shard_map.62 = (bf16[768,768]{1,0:T(8,128)(2,1)S(1)}, bf16[768,768]{1,0:T(8,128)(2,1)S(1)}) custom-call(s32[2]{0:T(128)S(1)} %pad_add_fusion.place, bf16[768,1024]{1,0:T(8,128)(2,1)} %get-tuple-element.41.mine, bf16[768,1024]{1,0:T(8,128)(2,1)} %collective-permute-done.1.partner, bf16[768,1024]{1,0:T(8,128)(2,1)} %collective-permute-done.2.near.near2, ...), custom_call_target="tpu_custom_call" | custom-call | flops 35389440000 | bytes 94371840 | tf_op jit(solution)/shard_map/pallas_call | solution.py:150
  159.8 2.0 collective-permute-start.14
  161.9 1.9 collective-permute-start.12
  163.8 9.6 %shard_map.63.kept = bf16[768,768]{1,0:T(8,128)(2,1)S(1)} custom-call(s32[2]{0:T(128)S(1)} %pad_add_fusion.place, bf16[768,8192]{1,0:T(8,128)(2,1)} %own.6, bf16[768,3072]{1,0:T(8,128)(2,1)} %collective-permute-done.near.near1, bf16[768,1024]{1,0:T(8,128)(2,1)} %collective-permute-done.2.near.near2, bf16[768,3072]{1,0:T(8,128)(2,1)S(1)} %collective-permute-done.8.other1, ...), custom_call_target="tpu_custom_call" | custom-call | flops 3623878656 | bytes 14155776 | tf_op jit(solution)/shard_map/pallas_call | solution.py:189
  174.7 2.6 %collective-permute-start.11 = (bf16[768,768]{1,0:T(8,128)(2,1)S(1)}, bf16[768,768]{1,0:T(8,128)(2,1)}, u32[]{:S(2)}, u32[]{:S(2)}) collective-permute-start(bf16[768,768]{1,0:T(8,128)(2,1)S(1)} %shard_map.63.kept), channel_id=1, source_target_pairs={{0,4},{4,8},{8,12},{12,0},{16,20},{20,24},{24,28},{28,16}} | collective-permute-start | bytes 3538952 | tf_op jit(solution)/shard_map/ppermute | solution.py:22
  177.3 10.2 %collective-permute-done.13.u = bf16[768,768]{1,0:T(8,128)(2,1)S(1)} collective-permute-done((bf16[768,768]{1,0:T(8,128)(2,1)S(1)}, bf16[768,768]{1,0:T(8,128)(2,1)S(1)}, u32[]{:S(2)}, u32[]{:S(2)}) %collective-permute-start.13) | collective-permute-done | bytes 1179680 | tf_op jit(solution)/shard_map/ppermute | solution.py:22
  187.5 4.0 %collective-permute-done.14.v = bf16[768,768]{1,0:T(8,128)(2,1)S(1)} collective-permute-done((bf16[768,768]{1,0:T(8,128)(2,1)S(1)}, bf16[768,768]{1,0:T(8,128)(2,1)S(1)}, u32[]{:S(2)}, u32[]{:S(2)}) %collective-permute-start.14) | collective-permute-done | bytes 1179680 | tf_op jit(solution)/shard_map/ppermute | solution.py:22
  191.5 2.6 %shard_map.64 = (f32[2,768,768]{2,1,0:T(8,128)}, f32[1,768]{1,0:T(1,128)S(1)}, f32[1,768]{1,0:T(1,128)S(1)}) custom-call(s32[2]{0:T(128)S(1)} %pad_add_fusion.place, bf16[768,768]{1,0:T(8,128)(2,1)S(1)} %collective-permute-done.13.u, bf16[768,768]{1,0:T(8,128)(2,1)S(1)} %collective-permute-done.14.v, bf16[768,768]{1,0:T(8,128)(2,1)S(1)} %get-tuple-element.59.kept, ...), custom_call_target="tpu_custom_call" | custom-call | flops 35389440000 | bytes 94371840 | tf_op jit(solution)/shard_map/pallas_call | solution.py:273
  194.8 4.3 %collective-permute-done.15 = f32[64,128]{1,0:T(8,128)S(1)} collective-permute-done((f32[64,128]{1,0:T(8,128)S(1)}, f32[64,128]{1,0:T(8,128)S(1)}, u32[]{:S(2)}, u32[]{:S(2)}) %collective-permute-start.15) | collective-permute-done | bytes 32800 | tf_op jit(solution)/shard_map/ppermute | solution.py:22
  203.2 3.5 %collective-permute-start.18 = (f32[1,768]{1,0:T(1,128)}, f32[1,768]{1,0:T(1,128)S(1)}, u32[]{:S(2)}, u32[]{:S(2)}) collective-permute-start(f32[1,768]{1,0:T(1,128)} %copy-done), channel_id=1, source_target_pairs={{0,14},{1,15},{2,0},{3,1},{4,2},{5,3},{6,4},{7,5},{8,6},{9,7},{10,... | collective-permute-start | bytes 9224 | tf_op jit(solution)/shard_map/ppermute | solution.py:22
  206.7 4.0 %shard_map.65 = (f32[2,768,768]{2,1,0:T(8,128)}, f32[1,768]{1,0:T(1,128)S(1)}, f32[1,768]{1,0:T(1,128)S(1)}) custom-call(s32[2]{0:T(128)S(1)} %pad_add_fusion.place, bf16[768,768]{1,0:T(8,128)(2,1)} %collective-permute-done.10.y, bf16[768,768]{1,0:T(8,128)(2,1)} %collective-permute-done.11.z, ...), custom_call_target="tpu_custom_call", output_to_operand_aliasing={{0}: (7, {})} | custom-call | flops 4718592 | bytes 7077888 | tf_op jit(solution)/shard_map/pallas_call | solution.py:273
  210.7 1.8 collective-permute-start.17
  (40 shorter events, 14.6 us)
Async XLA Ops:
  9.2 25.4 %collective-permute-start.4 = (bf16[768,8192]{1,0:T(8,128)(2,1)}, bf16[768,8192]{1,0:T(8,128)(2,1)}, u32[]{:S(2)}, u32[]{:S(2)}) collective-permute-start(bf16[768,8192]{1,0:T(8,128)(2,1)} %own.6), channel_id=1, source_target_pairs={{0,1},{1,0},{2,3},{3,2},{4,5},{5,4},{6,7},{7,6},{8,9},{9,8},{10,11... | collective-permute-start | bytes 37748744 | tf_op jit(solution)/shard_map/ppermute | solution.py:22
  9.7 105.6 %collective-permute-start.3 = (bf16[768,3072]{1,0:T(8,128)(2,1)}, bf16[768,3072]{1,0:T(8,128)(2,1)}, u32[]{:S(2)}, u32[]{:S(2)}) collective-permute-start(bf16[768,3072]{1,0:T(8,128)(2,1)} %get-tuple-element.42), channel_id=1, source_target_pairs={{0,2},{1,3},{2,0},{3,1},{4,6},{5,7},{6,4},{7,5},{8,10},{9,11},{10,... | collective-permute-start | bytes 14155784 | tf_op jit(solution)/shard_map/ppermute | solution.py:22
  12.3 106.1 %collective-permute-start = (bf16[768,3072]{1,0:T(8,128)(2,1)}, bf16[768,3072]{1,0:T(8,128)(2,1)}, u32[]{:S(2)}, u32[]{:S(2)}) collective-permute-start(bf16[768,3072]{1,0:T(8,128)(2,1)} %get-tuple-element.38), channel_id=1, source_target_pairs={{0,12},{1,13},{2,6},{3,7},{4,0},{5,1},{6,10},{7,11},{8,4},{9,5},{1... | collective-permute-start | bytes 14155784 | tf_op jit(solution)/shard_map/ppermute | solution.py:22
  19.3 129.4 %collective-permute-start.1 = (bf16[768,1024]{1,0:T(8,128)(2,1)}, bf16[768,1024]{1,0:T(8,128)(2,1)}, u32[]{:S(2)}, u32[]{:S(2)}) collective-permute-start(bf16[768,1024]{1,0:T(8,128)(2,1)} %get-tuple-element.40), channel_id=1, source_target_pairs={{0,2},{1,3},{2,0},{3,1},{4,6},{5,7},{6,4},{7,5},{8,10},{9,11},{10,... | collective-permute-start | bytes 4718600 | tf_op jit(solution)/shard_map/ppermute | solution.py:22
  19.4 7.8 %copy-start.1 = (bf16[128,8192]{1,0:T(8,128)(2,1)S(1)}, bf16[128,8192]{1,0:T(8,128)(2,1)}, u32[]{:S(2)}) copy-start(bf16[128,8192]{1,0:T(8,128)(2,1)} %param.4) | copy-start | bytes 6291460
  19.4 8.3 %copy-start.2 = (s32[768]{0:T(1024)S(1)}, s32[768]{0:T(1024)}, u32[]{:S(2)}) copy-start(s32[768]{0:T(1024)} %param.5) | copy-start | bytes 9220
  19.4 132.3 %collective-permute-start.2 = (bf16[768,1024]{1,0:T(8,128)(2,1)}, bf16[768,1024]{1,0:T(8,128)(2,1)}, u32[]{:S(2)}, u32[]{:S(2)}) collective-permute-start(bf16[768,1024]{1,0:T(8,128)(2,1)} %get-tuple-element.41.mine), channel_id=1, source_target_pairs={{0,12},{1,13},{2,6},{3,7},{4,0},{5,1},{6,10},{7,11},{8,4},{9,5},{1... | collective-permute-start | bytes 4718600 | tf_op jit(solution)/shard_map/ppermute | solution.py:22
  129.8 23.0 %collective-permute-start.7 = (f32[64,128]{1,0:T(8,128)S(1)}, f32[64,128]{1,0:T(8,128)S(1)}, u32[]{:S(2)}, u32[]{:S(2)}) collective-permute-start(f32[64,128]{1,0:T(8,128)S(1)} %fusion.3), channel_id=1, source_target_pairs={{0,8},{1,9},{2,10},{3,11},{4,12},{5,13},{6,14},{7,15},{8,0},{9,1},... | collective-permute-start | bytes 98312 | tf_op jit(solution)/shard_map/ppermute | solution.py:22
  131.3 20.9 %collective-permute-start.5 = (f32[1,768]{1,0:T(1,128)S(1)}, f32[1,768]{1,0:T(1,128)S(1)}, u32[]{:S(2)}, u32[]{:S(2)}) collective-permute-start(f32[1,768]{1,0:T(1,128)S(1)} %rsqrt.26.inverse), channel_id=1, source_target_pairs={{0,1},{1,2},{2,3},{3,4},{4,5},{5,6},{6,7},{7,8},{8,9},{9,10},{10,1... | collective-permute-start | bytes 9224 | tf_op jit(solution)/shard_map/ppermute | solution.py:22
  131.3 21.4 %collective-permute-start.6 = (f32[1,768]{1,0:T(1,128)S(1)}, f32[1,768]{1,0:T(1,128)S(1)}, u32[]{:S(2)}, u32[]{:S(2)}) collective-permute-start(f32[1,768]{1,0:T(1,128)S(1)} %rsqrt.26.inverse), channel_id=1, source_target_pairs={{0,2},{1,3},{2,4},{3,5},{4,6},{5,7},{6,8},{7,9},{8,10},{9,11},{10,... | collective-permute-start | bytes 9224 | tf_op jit(solution)/shard_map/ppermute | solution.py:22
  152.8 11.0 %collective-permute-start.8 = (bf16[768,3072]{1,0:T(8,128)(2,1)}, bf16[768,3072]{1,0:T(8,128)(2,1)S(1)}, u32[]{:S(2)}, u32[]{:S(2)}) collective-permute-start(bf16[768,3072]{1,0:T(8,128)(2,1)} %collective-permute-done.3.partner), channel_id=1, source_target_pairs={{0,1},{1,0},{2,3},{3,2},{4,5},{5,4},{6,7},{7,6},{8,9},{9,8},{10,11... | collective-permute-start | bytes 14155784 | tf_op jit(solution)/shard_map/ppermute | solution.py:22
  158.1 5.7 %collective-permute-start.9 = (bf16[768,1024]{1,0:T(8,128)(2,1)}, bf16[768,1024]{1,0:T(8,128)(2,1)S(1)}, u32[]{:S(2)}, u32[]{:S(2)}) collective-permute-start(bf16[768,1024]{1,0:T(8,128)(2,1)} %collective-permute-done.1.partner), channel_id=1, source_target_pairs={{0,1},{1,0},{2,3},{3,2},{4,5},{5,4},{6,7},{7,6},{8,9},{9,8},{10,11... | collective-permute-start | bytes 4718600 | tf_op jit(solution)/shard_map/ppermute | solution.py:22
  158.6 28.8 %collective-permute-start.13 = (bf16[768,768]{1,0:T(8,128)(2,1)S(1)}, bf16[768,768]{1,0:T(8,128)(2,1)S(1)}, u32[]{:S(2)}, u32[]{:S(2)}) collective-permute-start(bf16[768,768]{1,0:T(8,128)(2,1)S(1)} %get-tuple-element.54), channel_id=1, source_target_pairs={{0,2},{1,3},{2,0},{3,1},{4,6},{5,7},{6,4},{7,5},{8,10},{9,11},{10,... | collective-permute-start | bytes 3538952 | tf_op jit(solution)/shard_map/ppermute | solution.py:22
  159.8 31.7 %collective-permute-start.14 = (bf16[768,768]{1,0:T(8,128)(2,1)S(1)}, bf16[768,768]{1,0:T(8,128)(2,1)S(1)}, u32[]{:S(2)}, u32[]{:S(2)}) collective-permute-start(bf16[768,768]{1,0:T(8,128)(2,1)S(1)} %get-tuple-element.59.kept), channel_id=1, source_target_pairs={{0,4},{1,5},{4,8},{5,9},{8,12},{9,13},{12,0},{13,1},{16,20},{17,21... | collective-permute-start | bytes 3538952 | tf_op jit(solution)/shard_map/ppermute | solution.py:22
  161.9 32.9 %collective-permute-start.12 = (f32[64,128]{1,0:T(8,128)S(1)}, f32[64,128]{1,0:T(8,128)S(1)}, u32[]{:S(2)}, u32[]{:S(2)}) collective-permute-start(f32[64,128]{1,0:T(8,128)S(1)} %add.66), channel_id=1, source_target_pairs={{0,4},{1,5},{2,6},{3,7},{4,0},{5,1},{6,2},{7,3},{8,12},{9,13},{10,... | collective-permute-start | bytes 98312 | tf_op jit(solution)/shard_map/ppermute | solution.py:22
  173.4 33.3 %collective-permute-start.10 = (bf16[768,768]{1,0:T(8,128)(2,1)S(1)}, bf16[768,768]{1,0:T(8,128)(2,1)}, u32[]{:S(2)}, u32[]{:S(2)}) collective-permute-start(bf16[768,768]{1,0:T(8,128)(2,1)S(1)} %shard_map.63.kept), channel_id=1, source_target_pairs={{1,2},{3,0},{5,6},{7,4},{9,10},{11,8},{13,14},{15,12},{17,18},{19,... | collective-permute-start | bytes 3538952 | tf_op jit(solution)/shard_map/ppermute | solution.py:22
  174.7 32.0 %collective-permute-start.11 = (bf16[768,768]{1,0:T(8,128)(2,1)S(1)}, bf16[768,768]{1,0:T(8,128)(2,1)}, u32[]{:S(2)}, u32[]{:S(2)}) collective-permute-start(bf16[768,768]{1,0:T(8,128)(2,1)S(1)} %shard_map.63.kept), channel_id=1, source_target_pairs={{0,4},{4,8},{8,12},{12,0},{16,20},{20,24},{24,28},{28,16}} | collective-permute-start | bytes 3538952 | tf_op jit(solution)/shard_map/ppermute | solution.py:22
  194.2 0.6 copy-start
  194.7 4.4 %collective-permute-start.15 = (f32[64,128]{1,0:T(8,128)S(1)}, f32[64,128]{1,0:T(8,128)S(1)}, u32[]{:S(2)}, u32[]{:S(2)}) collective-permute-start(f32[64,128]{1,0:T(8,128)S(1)} %add.67), channel_id=1, source_target_pairs={{0,2},{1,3},{2,0},{3,1},{4,6},{5,7},{6,4},{7,5},{8,10},{9,11},{10,... | collective-permute-start | bytes 98312 | tf_op jit(solution)/shard_map/ppermute | solution.py:22
  199.7 2.2 %collective-permute-start.16 = (f32[64,128]{1,0:T(8,128)}, f32[64,128]{1,0:T(8,128)}, u32[]{:S(2)}, u32[]{:S(2)}) collective-permute-start(f32[64,128]{1,0:T(8,128)} %add.68), channel_id=1, source_target_pairs={{0,1},{1,0},{2,3},{3,2},{4,5},{5,4},{6,7},{7,6},{8,9},{9,8},{10,11... | collective-permute-start | bytes 98312 | tf_op jit(solution)/shard_map/ppermute | solution.py:22
  203.2 9.2 %collective-permute-start.18 = (f32[1,768]{1,0:T(1,128)}, f32[1,768]{1,0:T(1,128)S(1)}, u32[]{:S(2)}, u32[]{:S(2)}) collective-permute-start(f32[1,768]{1,0:T(1,128)} %copy-done), channel_id=1, source_target_pairs={{0,14},{1,15},{2,0},{3,1},{4,2},{5,3},{6,4},{7,5},{8,6},{9,7},{10,... | collective-permute-start | bytes 9224 | tf_op jit(solution)/shard_map/ppermute | solution.py:22
  210.7 3.1 %collective-permute-start.17 = (f32[1,768]{1,0:T(1,128)S(1)}, f32[1,768]{1,0:T(1,128)S(1)}, u32[]{:S(2)}, u32[]{:S(2)}) collective-permute-start(f32[1,768]{1,0:T(1,128)S(1)} %get-tuple-element.69), channel_id=1, source_target_pairs={{0,15},{1,0},{2,1},{3,2},{4,3},{5,4},{6,5},{7,6},{8,7},{9,8},{10,9... | collective-permute-start | bytes 9224 | tf_op jit(solution)/shard_map/ppermute | solution.py:22

commit v13 on v12

--- a/solution.py
+++ b/solution.py
@@ -13,7 +13,7 @@
 DEPTH = 1024
 TALL = 384
 BAND = 256
-PIECES = 2
+PIECES = 4
 NT = (((1,), (1,)), ((), ()))
 VMEM_LIMIT = 40 * 2**20
 
@@ -367,7 +367,6 @@
     sums = lax.dynamic_slice_in_dim(sums, index * DOM_DEV, DOM_DEV)
     domain_scores = sums * (1.0 / math.sqrt(rows / DOM_DEV))
     y, z, domain_scores = lax.optimization_barrier((y, z, domain_scores))
-    from_second = send(after(column_mass2, sums), [(i, (i - 2) % size) for i in blocks])
     gram, row_mass1, column_mass1 = join(
         first_kernel, 0, scale, place, (y, z, x, inside), across_lanes, behind1, (gram,)
     )
@@ -375,7 +374,7 @@
         row_mass1
         + row_mass2
         + send(column_mass1, [(i, (i - 1) % size) for i in blocks])
-        + from_second
+        + send(after(column_mass2, row_mass1), [(i, (i - 2) % size) for i in blocks])
     )
     redundancy = mass[0] / float(2 * ROUNDS * rows)
     return (gram, redundancy, domain_scores)

time: 215 us -> 214 us (level)
  transfers between devices with their start and end apart: 19 -> 19, of which waited for: 11 -> 12; matrix products, arithmetic and copies ran while one was open for 8% -> 8% of each run, Pallas kernels for 21% -> 20%
where the time goes in v13:
time: 214 us
  waiting for transfers between devices  117 us (55%)
  Pallas kernels  53.9 us (25%)
  starting transfers between devices  23.9 us (11%)
  other arithmetic  10.3 us (5%)
  matrix products  7.47 us (3%)
    ppermute x19, waiting for transfers between devices, send(): return lax.ppermute(value, 'blocks', pairs)  117 us
    ppermute x19, starting transfers between devices, send(): return lax.ppermute(value, 'blocks', pairs)  23.9 us
    pallas_call x1, Pallas kernels, early_tiles(): pl.pallas_call(early_kernel, grid_spec=pltpu.PrefetchScalarGridSpec(num_s...  11.4 us
    pallas_call x2, Pallas kernels, halves(): pl.pallas_call(functools.partial(halves_kernel, start, sides), in_specs=[...  11.2 us
    pallas_call x1, Pallas kernels, inside_tile(): pl.pallas_call(inside_kernel, grid_spec=pltpu.PrefetchScalarGridSpec(num_...  9.77 us
    pallas_call x1, Pallas kernels, cross_tile(): pl.pallas_call(cross_kernel, grid_spec=pltpu.PrefetchScalarGridSpec(num_s...  9.57 us
    reduce_sum x2, other arithmetic, inverse_norm(): return lax.rsqrt(jnp.mean(values * values, axis=1) + 1e-06)  7.7 us
    dot_general x1, matrix products, local(): lax.dot_general(members, similarity, (((0,), (0,)), ((), ())), preferred_...  7.47 us
  transfers between devices with their start and end apart: 19, of which 12 were waited for; matrix products, arithmetic and copies ran while one was open for 8% of the time, Pallas kernels for 20%

profile of v13, /device:TPU:0, one launch (start us, length us, event | category | flops | bytes accessed | tf_op | source)
XLA Modules:
  0.0 213.9 jit_solution(16805783101345773570)
XLA Ops:
  0.7 7.9 %shard_map.58 = (bf16[768,3072]{1,0:T(8,128)(2,1)}, bf16[768,3072]{1,0:T(8,128)(2,1)}) custom-call(s32[2]{0:T(128)S(1)} %pad_add_fusion.place, bf16[768,8192]{1,0:T(8,128)(2,1)} %own.6), custom_call_target="tpu_custom_call" | custom-call | bytes 18874368 | tf_op jit(solution)/shard_map/pallas_call | solution.py:83
  9.2 2.6 %collective-permute-start.3 = (bf16[768,3072]{1,0:T(8,128)(2,1)}, bf16[768,3072]{1,0:T(8,128)(2,1)}, u32[]{:S(2)}, u32[]{:S(2)}) collective-permute-start(bf16[768,3072]{1,0:T(8,128)(2,1)} %get-tuple-element.42), channel_id=1, source_target_pairs={{0,2},{1,3},{2,0},{3,1},{4,6},{5,7},{6,4},{7,5},{8,10},{9,11},{10,... | collective-permute-start | bytes 14155784 | tf_op jit(solution)/shard_map/ppermute | solution.py:22
  11.8 3.6 %collective-permute-start = (bf16[768,3072]{1,0:T(8,128)(2,1)}, bf16[768,3072]{1,0:T(8,128)(2,1)}, u32[]{:S(2)}, u32[]{:S(2)}) collective-permute-start(bf16[768,3072]{1,0:T(8,128)(2,1)} %get-tuple-element.38), channel_id=1, source_target_pairs={{0,12},{1,13},{2,6},{3,7},{4,0},{5,1},{6,10},{7,11},{8,4},{9,5},{1... | collective-permute-start | bytes 14155784 | tf_op jit(solution)/shard_map/ppermute | solution.py:22
  15.4 3.3 %shard_map.59 = (bf16[768,1024]{1,0:T(8,128)(2,1)}, bf16[768,1024]{1,0:T(8,128)(2,1)}) custom-call(s32[2]{0:T(128)S(1)} %pad_add_fusion.place, bf16[768,8192]{1,0:T(8,128)(2,1)} %own.6), custom_call_target="tpu_custom_call" | custom-call | bytes 6291456 | tf_op jit(solution)/shard_map/pallas_call | solution.py:83
  19.3 7.2 %multiply_reduce_fusion = f32[768]{0:T(1024)S(1)} fusion(bf16[768,8192]{1,0:T(8,128)(2,1)} %own.6), kind=kLoop, calls=%fused_computation | loop fusion | flops 18873600 | bytes 12585984 | tf_op jit(solution)/shard_map/reduce_sum | solution.py:31
  27.0 7.5 %fusion.3 = f32[64,128]{1,0:T(8,128)} fusion(bf16[768,8192]{1,0:T(8,128)(2,1)} %own.6, bf16[128,8192]{1,0:T(8,128)(2,1)S(1)} %copy-done.2, f32[128]{0:T(128)S(1)} %add_rsqrt_fusion.1, f32[768]{0:T(1024)S(1)} %add_rsqrt_fusion, s32[768]{0:T(1024)S(1)} %copy-done.4), kind=kOutput, calls=%fused_computation.6 | convolution fusion | flops 1623638016 | bytes 14719488 | tf_op jit(solution)/shard_map/dot_general | solution.py:328
  34.5 9.8 %shard_map.60.local = f32[768,768]{1,0:T(8,128)S(1)} custom-call(s32[2]{0:T(128)S(1)} %pad_add_fusion.place, bf16[768,8192]{1,0:T(8,128)(2,1)} %own.6, bf16[768,8192]{1,0:T(8,128)(2,1)} %collective-permute-done.4.other), custom_call_target="tpu_custom_call" | custom-call | flops 9663676416 | bytes 25165824 | tf_op jit(solution)/shard_map/pallas_call | solution.py:215
  44.3 70.4 %collective-permute-done.3.partner = bf16[768,3072]{1,0:T(8,128)(2,1)} collective-permute-done((bf16[768,3072]{1,0:T(8,128)(2,1)}, bf16[768,3072]{1,0:T(8,128)(2,1)}, u32[]{:S(2)}, u32[]{:S(2)}) %collective-permute-start.3) | collective-permute-done | bytes 4718624 | tf_op jit(solution)/shard_map/ppermute | solution.py:22
  114.7 3.1 %collective-permute-done.near.near1 = bf16[768,3072]{1,0:T(8,128)(2,1)} collective-permute-done((bf16[768,3072]{1,0:T(8,128)(2,1)}, bf16[768,3072]{1,0:T(8,128)(2,1)}, u32[]{:S(2)}, u32[]{:S(2)}) %collective-permute-start) | collective-permute-done | bytes 4718624 | tf_op jit(solution)/shard_map/ppermute | solution.py:22
  117.9 11.4 %shard_map.61 = (f32[768,768]{1,0:T(8,128)S(1)}, f32[768,768]{1,0:T(8,128)S(1)}) custom-call(s32[2]{0:T(128)S(1)} %pad_add_fusion.place, bf16[768,8192]{1,0:T(8,128)(2,1)} %own.6, bf16[768,3072]{1,0:T(8,128)(2,1)} %collective-permute-done.3.partner, bf16[768,3072]{1,0:T(8,128)(2,1)} %collective-permute-done.near.near1), custom_call_target="tpu_custom_call" | custom-call | flops 768 | bytes 768 | tf_op jit(solution)/shard_map/pallas_call | solution.py:118
  131.4 16.8 %collective-permute-done.1.partner = bf16[768,1024]{1,0:T(8,128)(2,1)} collective-permute-done((bf16[768,1024]{1,0:T(8,128)(2,1)}, bf16[768,1024]{1,0:T(8,128)(2,1)}, u32[]{:S(2)}, u32[]{:S(2)}) %collective-permute-start.1) | collective-permute-done | bytes 1572896 | tf_op jit(solution)/shard_map/ppermute | solution.py:22
  148.2 3.0 %collective-permute-done.2.near.near2 = bf16[768,1024]{1,0:T(8,128)(2,1)} collective-permute-done((bf16[768,1024]{1,0:T(8,128)(2,1)}, bf16[768,1024]{1,0:T(8,128)(2,1)}, u32[]{:S(2)}, u32[]{:S(2)}) %collective-permute-start.2) | collective-permute-done | bytes 1572896 | tf_op jit(solution)/shard_map/ppermute | solution.py:22
  152.3 5.3 %shard_map.62 = (bf16[768,768]{1,0:T(8,128)(2,1)S(1)}, bf16[768,768]{1,0:T(8,128)(2,1)S(1)}) custom-call(s32[2]{0:T(128)S(1)} %pad_add_fusion.place, bf16[768,1024]{1,0:T(8,128)(2,1)} %get-tuple-element.41.mine, bf16[768,1024]{1,0:T(8,128)(2,1)} %collective-permute-done.1.partner, bf16[768,1024]{1,0:T(8,128)(2,1)} %collective-permute-done.2.near.near2, ...), custom_call_target="tpu_custom_call" | custom-call | flops 35389440000 | bytes 94371840 | tf_op jit(solution)/shard_map/pallas_call | solution.py:150
  159.3 2.1 collective-permute-start.14
  161.4 1.9 collective-permute-start.12
  163.3 9.6 %shard_map.63.kept = bf16[768,768]{1,0:T(8,128)(2,1)S(1)} custom-call(s32[2]{0:T(128)S(1)} %pad_add_fusion.place, bf16[768,8192]{1,0:T(8,128)(2,1)} %own.6, bf16[768,3072]{1,0:T(8,128)(2,1)} %collective-permute-done.near.near1, bf16[768,1024]{1,0:T(8,128)(2,1)} %collective-permute-done.2.near.near2, bf16[768,3072]{1,0:T(8,128)(2,1)S(1)} %collective-permute-done.8.other1, ...), custom_call_target="tpu_custom_call" | custom-call | flops 3623878656 | bytes 14155776 | tf_op jit(solution)/shard_map/pallas_call | solution.py:189
  174.2 2.6 %collective-permute-start.11 = (bf16[768,768]{1,0:T(8,128)(2,1)S(1)}, bf16[768,768]{1,0:T(8,128)(2,1)}, u32[]{:S(2)}, u32[]{:S(2)}) collective-permute-start(bf16[768,768]{1,0:T(8,128)(2,1)S(1)} %shard_map.63.kept), channel_id=1, source_target_pairs={{0,4},{4,8},{8,12},{12,0},{16,20},{20,24},{24,28},{28,16}} | collective-permute-start | bytes 3538952 | tf_op jit(solution)/shard_map/ppermute | solution.py:22
  176.7 10.2 %collective-permute-done.13.u = bf16[768,768]{1,0:T(8,128)(2,1)S(1)} collective-permute-done((bf16[768,768]{1,0:T(8,128)(2,1)S(1)}, bf16[768,768]{1,0:T(8,128)(2,1)S(1)}, u32[]{:S(2)}, u32[]{:S(2)}) %collective-permute-start.13) | collective-permute-done | bytes 1179680 | tf_op jit(solution)/shard_map/ppermute | solution.py:22
  187.0 4.0 %collective-permute-done.14.v = bf16[768,768]{1,0:T(8,128)(2,1)S(1)} collective-permute-done((bf16[768,768]{1,0:T(8,128)(2,1)S(1)}, bf16[768,768]{1,0:T(8,128)(2,1)S(1)}, u32[]{:S(2)}, u32[]{:S(2)}) %collective-permute-start.14) | collective-permute-done | bytes 1179680 | tf_op jit(solution)/shard_map/ppermute | solution.py:22
  191.0 2.6 %shard_map.64 = (f32[2,768,768]{2,1,0:T(8,128)}, f32[1,768]{1,0:T(1,128)S(1)}, f32[1,768]{1,0:T(1,128)S(1)}) custom-call(s32[2]{0:T(128)S(1)} %pad_add_fusion.place, bf16[768,768]{1,0:T(8,128)(2,1)S(1)} %collective-permute-done.13.u, bf16[768,768]{1,0:T(8,128)(2,1)S(1)} %collective-permute-done.14.v, bf16[768,768]{1,0:T(8,128)(2,1)S(1)} %get-tuple-element.59.kept, ...), custom_call_target="tpu_custom_call" | custom-call | flops 35389440000 | bytes 94371840 | tf_op jit(solution)/shard_map/pallas_call | solution.py:273
  194.3 4.3 %collective-permute-done.15 = f32[64,128]{1,0:T(8,128)S(1)} collective-permute-done((f32[64,128]{1,0:T(8,128)S(1)}, f32[64,128]{1,0:T(8,128)S(1)}, u32[]{:S(2)}, u32[]{:S(2)}) %collective-permute-start.15) | collective-permute-done | bytes 32800 | tf_op jit(solution)/shard_map/ppermute | solution.py:22
  204.1 4.0 %shard_map.65 = (f32[2,768,768]{2,1,0:T(8,128)}, f32[1,768]{1,0:T(1,128)S(1)}, f32[1,768]{1,0:T(1,128)S(1)}) custom-call(s32[2]{0:T(128)S(1)} %pad_add_fusion.place, bf16[768,768]{1,0:T(8,128)(2,1)} %collective-permute-done.10.y, bf16[768,768]{1,0:T(8,128)(2,1)} %collective-permute-done.11.z, ...), custom_call_target="tpu_custom_call", output_to_operand_aliasing={{0}: (7, {})} | custom-call | flops 4718592 | bytes 7077888 | tf_op jit(solution)/shard_map/pallas_call | solution.py:273
  208.1 2.1 collective-permute-start.18
  210.2 1.8 collective-permute-start.17
  (44 shorter events, 15.9 us)
Async XLA Ops:
  8.7 25.9 %collective-permute-start.4 = (bf16[768,8192]{1,0:T(8,128)(2,1)}, bf16[768,8192]{1,0:T(8,128)(2,1)}, u32[]{:S(2)}, u32[]{:S(2)}) collective-permute-start(bf16[768,8192]{1,0:T(8,128)(2,1)} %own.6), channel_id=1, source_target_pairs={{0,1},{1,0},{2,3},{3,2},{4,5},{5,4},{6,7},{7,6},{8,9},{9,8},{10,11... | collective-permute-start | bytes 37748744 | tf_op jit(solution)/shard_map/ppermute | solution.py:22
  9.2 105.6 %collective-permute-start.3 = (bf16[768,3072]{1,0:T(8,128)(2,1)}, bf16[768,3072]{1,0:T(8,128)(2,1)}, u32[]{:S(2)}, u32[]{:S(2)}) collective-permute-start(bf16[768,3072]{1,0:T(8,128)(2,1)} %get-tuple-element.42), channel_id=1, source_target_pairs={{0,2},{1,3},{2,0},{3,1},{4,6},{5,7},{6,4},{7,5},{8,10},{9,11},{10,... | collective-permute-start | bytes 14155784 | tf_op jit(solution)/shard_map/ppermute | solution.py:22
  11.8 106.1 %collective-permute-start = (bf16[768,3072]{1,0:T(8,128)(2,1)}, bf16[768,3072]{1,0:T(8,128)(2,1)}, u32[]{:S(2)}, u32[]{:S(2)}) collective-permute-start(bf16[768,3072]{1,0:T(8,128)(2,1)} %get-tuple-element.38), channel_id=1, source_target_pairs={{0,12},{1,13},{2,6},{3,7},{4,0},{5,1},{6,10},{7,11},{8,4},{9,5},{1... | collective-permute-start | bytes 14155784 | tf_op jit(solution)/shard_map/ppermute | solution.py:22
  18.7 129.5 %collective-permute-start.1 = (bf16[768,1024]{1,0:T(8,128)(2,1)}, bf16[768,1024]{1,0:T(8,128)(2,1)}, u32[]{:S(2)}, u32[]{:S(2)}) collective-permute-start(bf16[768,1024]{1,0:T(8,128)(2,1)} %get-tuple-element.40), channel_id=1, source_target_pairs={{0,2},{1,3},{2,0},{3,1},{4,6},{5,7},{6,4},{7,5},{8,10},{9,11},{10,... | collective-permute-start | bytes 4718600 | tf_op jit(solution)/shard_map/ppermute | solution.py:22
  18.8 7.8 %copy-start.2 = (bf16[128,8192]{1,0:T(8,128)(2,1)S(1)}, bf16[128,8192]{1,0:T(8,128)(2,1)}, u32[]{:S(2)}) copy-start(bf16[128,8192]{1,0:T(8,128)(2,1)} %param.4) | copy-start | bytes 6291460
  18.8 8.3 %copy-start.4 = (s32[768]{0:T(1024)S(1)}, s32[768]{0:T(1024)}, u32[]{:S(2)}) copy-start(s32[768]{0:T(1024)} %param.5) | copy-start | bytes 9220
  18.8 132.4 %collective-permute-start.2 = (bf16[768,1024]{1,0:T(8,128)(2,1)}, bf16[768,1024]{1,0:T(8,128)(2,1)}, u32[]{:S(2)}, u32[]{:S(2)}) collective-permute-start(bf16[768,1024]{1,0:T(8,128)(2,1)} %get-tuple-element.41.mine), channel_id=1, source_target_pairs={{0,12},{1,13},{2,6},{3,7},{4,0},{5,1},{6,10},{7,11},{8,4},{9,5},{1... | collective-permute-start | bytes 4718600 | tf_op jit(solution)/shard_map/ppermute | solution.py:22
  44.3 85.0 %copy-start.3 = (f32[64,128]{1,0:T(8,128)S(1)}, f32[64,128]{1,0:T(8,128)}, u32[]{:S(2)}) copy-start(f32[64,128]{1,0:T(8,128)} %fusion.3) | copy-start | bytes 98308
  129.3 23.0 %collective-permute-start.7 = (f32[64,128]{1,0:T(8,128)S(1)}, f32[64,128]{1,0:T(8,128)S(1)}, u32[]{:S(2)}, u32[]{:S(2)}) collective-permute-start(f32[64,128]{1,0:T(8,128)S(1)} %copy-done.3), channel_id=1, source_target_pairs={{0,8},{1,9},{2,10},{3,11},{4,12},{5,13},{6,14},{7,15},{8,0},{9,1},... | collective-permute-start | bytes 98312 | tf_op jit(solution)/shard_map/ppermute | solution.py:22
  130.8 20.9 %collective-permute-start.5 = (f32[1,768]{1,0:T(1,128)S(1)}, f32[1,768]{1,0:T(1,128)S(1)}, u32[]{:S(2)}, u32[]{:S(2)}) collective-permute-start(f32[1,768]{1,0:T(1,128)S(1)} %rsqrt.26.inverse), channel_id=1, source_target_pairs={{0,1},{1,2},{2,3},{3,4},{4,5},{5,6},{6,7},{7,8},{8,9},{9,10},{10,1... | collective-permute-start | bytes 9224 | tf_op jit(solution)/shard_map/ppermute | solution.py:22
  130.8 21.4 %collective-permute-start.6 = (f32[1,768]{1,0:T(1,128)S(1)}, f32[1,768]{1,0:T(1,128)S(1)}, u32[]{:S(2)}, u32[]{:S(2)}) collective-permute-start(f32[1,768]{1,0:T(1,128)S(1)} %rsqrt.26.inverse), channel_id=1, source_target_pairs={{0,2},{1,3},{2,4},{3,5},{4,6},{5,7},{6,8},{7,9},{8,10},{9,11},{10,... | collective-permute-start | bytes 9224 | tf_op jit(solution)/shard_map/ppermute | solution.py:22
  152.3 11.0 %collective-permute-start.8 = (bf16[768,3072]{1,0:T(8,128)(2,1)}, bf16[768,3072]{1,0:T(8,128)(2,1)S(1)}, u32[]{:S(2)}, u32[]{:S(2)}) collective-permute-start(bf16[768,3072]{1,0:T(8,128)(2,1)} %collective-permute-done.3.partner), channel_id=1, source_target_pairs={{0,1},{1,0},{2,3},{3,2},{4,5},{5,4},{6,7},{7,6},{8,9},{9,8},{10,11... | collective-permute-start | bytes 14155784 | tf_op jit(solution)/shard_map/ppermute | solution.py:22
  157.6 5.7 %collective-permute-start.9 = (bf16[768,1024]{1,0:T(8,128)(2,1)}, bf16[768,1024]{1,0:T(8,128)(2,1)S(1)}, u32[]{:S(2)}, u32[]{:S(2)}) collective-permute-start(bf16[768,1024]{1,0:T(8,128)(2,1)} %collective-permute-done.1.partner), channel_id=1, source_target_pairs={{0,1},{1,0},{2,3},{3,2},{4,5},{5,4},{6,7},{7,6},{8,9},{9,8},{10,11... | collective-permute-start | bytes 4718600 | tf_op jit(solution)/shard_map/ppermute | solution.py:22
  158.1 28.8 %collective-permute-start.13 = (bf16[768,768]{1,0:T(8,128)(2,1)S(1)}, bf16[768,768]{1,0:T(8,128)(2,1)S(1)}, u32[]{:S(2)}, u32[]{:S(2)}) collective-permute-start(bf16[768,768]{1,0:T(8,128)(2,1)S(1)} %get-tuple-element.54), channel_id=1, source_target_pairs={{0,2},{1,3},{2,0},{3,1},{4,6},{5,7},{6,4},{7,5},{8,10},{9,11},{10,... | collective-permute-start | bytes 3538952 | tf_op jit(solution)/shard_map/ppermute | solution.py:22
  159.3 31.7 %collective-permute-start.14 = (bf16[768,768]{1,0:T(8,128)(2,1)S(1)}, bf16[768,768]{1,0:T(8,128)(2,1)S(1)}, u32[]{:S(2)}, u32[]{:S(2)}) collective-permute-start(bf16[768,768]{1,0:T(8,128)(2,1)S(1)} %get-tuple-element.59.kept), channel_id=1, source_target_pairs={{0,4},{1,5},{4,8},{5,9},{8,12},{9,13},{12,0},{13,1},{16,20},{17,21... | collective-permute-start | bytes 3538952 | tf_op jit(solution)/shard_map/ppermute | solution.py:22
  161.4 32.9 %collective-permute-start.12 = (f32[64,128]{1,0:T(8,128)S(1)}, f32[64,128]{1,0:T(8,128)S(1)}, u32[]{:S(2)}, u32[]{:S(2)}) collective-permute-start(f32[64,128]{1,0:T(8,128)S(1)} %add.66), channel_id=1, source_target_pairs={{0,4},{1,5},{2,6},{3,7},{4,0},{5,1},{6,2},{7,3},{8,12},{9,13},{10,... | collective-permute-start | bytes 98312 | tf_op jit(solution)/shard_map/ppermute | solution.py:22
  172.9 29.9 %collective-permute-start.10 = (bf16[768,768]{1,0:T(8,128)(2,1)S(1)}, bf16[768,768]{1,0:T(8,128)(2,1)}, u32[]{:S(2)}, u32[]{:S(2)}) collective-permute-start(bf16[768,768]{1,0:T(8,128)(2,1)S(1)} %shard_map.63.kept), channel_id=1, source_target_pairs={{1,2},{3,0},{5,6},{7,4},{9,10},{11,8},{13,14},{15,12},{17,18},{19,... | collective-permute-start | bytes 3538952 | tf_op jit(solution)/shard_map/ppermute | solution.py:22
  174.2 29.9 %collective-permute-start.11 = (bf16[768,768]{1,0:T(8,128)(2,1)S(1)}, bf16[768,768]{1,0:T(8,128)(2,1)}, u32[]{:S(2)}, u32[]{:S(2)}) collective-permute-start(bf16[768,768]{1,0:T(8,128)(2,1)S(1)} %shard_map.63.kept), channel_id=1, source_target_pairs={{0,4},{4,8},{8,12},{12,0},{16,20},{20,24},{24,28},{28,16}} | collective-permute-start | bytes 3538952 | tf_op jit(solution)/shard_map/ppermute | solution.py:22
  193.6 0.6 copy-start
  194.2 4.4 %collective-permute-start.15 = (f32[64,128]{1,0:T(8,128)S(1)}, f32[64,128]{1,0:T(8,128)S(1)}, u32[]{:S(2)}, u32[]{:S(2)}) collective-permute-start(f32[64,128]{1,0:T(8,128)S(1)} %add.67), channel_id=1, source_target_pairs={{0,2},{1,3},{2,0},{3,1},{4,6},{5,7},{6,4},{7,5},{8,10},{9,11},{10,... | collective-permute-start | bytes 98312 | tf_op jit(solution)/shard_map/ppermute | solution.py:22
  199.2 2.2 %collective-permute-start.16 = (f32[64,128]{1,0:T(8,128)}, f32[64,128]{1,0:T(8,128)}, u32[]{:S(2)}, u32[]{:S(2)}) collective-permute-start(f32[64,128]{1,0:T(8,128)} %add.68), channel_id=1, source_target_pairs={{0,1},{1,0},{2,3},{3,2},{4,5},{5,4},{6,7},{7,6},{8,9},{9,8},{10,11... | collective-permute-start | bytes 98312 | tf_op jit(solution)/shard_map/ppermute | solution.py:22
  204.1 4.0 %copy-start.1 = (f32[1,768]{1,0:T(1,128)S(1)}, f32[1,768]{1,0:T(1,128)}, u32[]{:S(2)}) copy-start(f32[1,768]{1,0:T(1,128)} %copy-done) | copy-start | bytes 9220
  208.1 3.9 %collective-permute-start.18 = (f32[1,768]{1,0:T(1,128)S(1)}, f32[1,768]{1,0:T(1,128)S(1)}, u32[]{:S(2)}, u32[]{:S(2)}) collective-permute-start(f32[1,768]{1,0:T(1,128)S(1)} %copy-done.1), channel_id=1, source_target_pairs={{0,14},{1,15},{2,0},{3,1},{4,2},{5,3},{6,4},{7,5},{8,6},{9,7},{10,... | collective-permute-start | bytes 9224 | tf_op jit(solution)/shard_map/ppermute | solution.py:22
  210.2 3.1 %collective-permute-start.17 = (f32[1,768]{1,0:T(1,128)S(1)}, f32[1,768]{1,0:T(1,128)S(1)}, u32[]{:S(2)}, u32[]{:S(2)}) collective-permute-start(f32[1,768]{1,0:T(1,128)S(1)} %get-tuple-element.69), channel_id=1, source_target_pairs={{0,15},{1,0},{2,1},{3,2},{4,3},{5,4},{6,5},{7,6},{8,7},{9,8},{10,9... | collective-permute-start | bytes 9224 | tf_op jit(solution)/shard_map/ppermute | solution.py:22

commit v14 on v11

--- a/solution.py
+++ b/solution.py
@@ -13,7 +13,7 @@
 DEPTH = 1024
 TALL = 384
 BAND = 256
-PIECES = 16
+PIECES = 4
 NT = (((1,), (1,)), ((), ()))
 VMEM_LIMIT = 40 * 2**20
 

time: 213 us -> 213 us (level)
  no operation moved by 1% of the time
where the time goes in v14:
time: 213 us
  waiting for transfers between devices  117 us (55%)
  Pallas kernels  53.9 us (25%)
  starting transfers between devices  22.6 us (11%)
  other arithmetic  10.3 us (5%)
  matrix products  7.47 us (4%)
    ppermute x19, waiting for transfers between devices, send(): return lax.ppermute(value, 'blocks', pairs)  117 us
    ppermute x19, starting transfers between devices, send(): return lax.ppermute(value, 'blocks', pairs)  22.6 us
    pallas_call x1, Pallas kernels, early_tiles(): pl.pallas_call(early_kernel, grid_spec=pltpu.PrefetchScalarGridSpec(num_s...  11.4 us
    pallas_call x2, Pallas kernels, halves(): pl.pallas_call(functools.partial(halves_kernel, start, sides), in_specs=[...  11.2 us
    pallas_call x1, Pallas kernels, inside_tile(): pl.pallas_call(inside_kernel, grid_spec=pltpu.PrefetchScalarGridSpec(num_...  9.77 us
    pallas_call x1, Pallas kernels, cross_tile(): pl.pallas_call(cross_kernel, grid_spec=pltpu.PrefetchScalarGridSpec(num_s...  9.57 us
    reduce_sum x2, other arithmetic, inverse_norm(): return lax.rsqrt(jnp.mean(values * values, axis=1) + 1e-06)  7.7 us
    dot_general x1, matrix products, local(): lax.dot_general(members, similarity, (((0,), (0,)), ((), ())), preferred_...  7.47 us
  transfers between devices with their start and end apart: 19, of which 11 were waited for; matrix products, arithmetic and copies ran while one was open for 8% of the time, Pallas kernels for 20%

profile of v14, /device:TPU:0, one launch (start us, length us, event | category | flops | bytes accessed | tf_op | source)
XLA Modules:
  0.0 212.6 jit_solution(10390124028066372689)
XLA Ops:
  0.7 7.9 %shard_map.58 = (bf16[768,3072]{1,0:T(8,128)(2,1)}, bf16[768,3072]{1,0:T(8,128)(2,1)}) custom-call(s32[2]{0:T(128)S(1)} %pad_add_fusion.place, bf16[768,8192]{1,0:T(8,128)(2,1)} %own.6), custom_call_target="tpu_custom_call" | custom-call | bytes 18874368 | tf_op jit(solution)/shard_map/pallas_call | solution.py:83
  9.2 2.6 %collective-permute-start.3 = (bf16[768,3072]{1,0:T(8,128)(2,1)}, bf16[768,3072]{1,0:T(8,128)(2,1)}, u32[]{:S(2)}, u32[]{:S(2)}) collective-permute-start(bf16[768,3072]{1,0:T(8,128)(2,1)} %get-tuple-element.41), channel_id=1, source_target_pairs={{0,2},{1,3},{2,0},{3,1},{4,6},{5,7},{6,4},{7,5},{8,10},{9,11},{10,... | collective-permute-start | bytes 14155784 | tf_op jit(solution)/shard_map/ppermute | solution.py:22
  11.8 3.6 %collective-permute-start = (bf16[768,3072]{1,0:T(8,128)(2,1)}, bf16[768,3072]{1,0:T(8,128)(2,1)}, u32[]{:S(2)}, u32[]{:S(2)}) collective-permute-start(bf16[768,3072]{1,0:T(8,128)(2,1)} %get-tuple-element.37), channel_id=1, source_target_pairs={{0,12},{1,13},{2,6},{3,7},{4,0},{5,1},{6,10},{7,11},{8,4},{9,5},{1... | collective-permute-start | bytes 14155784 | tf_op jit(solution)/shard_map/ppermute | solution.py:22
  15.4 3.3 %shard_map.59 = (bf16[768,1024]{1,0:T(8,128)(2,1)}, bf16[768,1024]{1,0:T(8,128)(2,1)}) custom-call(s32[2]{0:T(128)S(1)} %pad_add_fusion.place, bf16[768,8192]{1,0:T(8,128)(2,1)} %own.6), custom_call_target="tpu_custom_call" | custom-call | bytes 6291456 | tf_op jit(solution)/shard_map/pallas_call | solution.py:83
  19.3 7.2 %multiply_reduce_fusion = f32[768]{0:T(1024)S(1)} fusion(bf16[768,8192]{1,0:T(8,128)(2,1)} %own.6), kind=kLoop, calls=%fused_computation | loop fusion | flops 18873600 | bytes 12585984 | tf_op jit(solution)/shard_map/reduce_sum | solution.py:31
  27.0 7.5 %fusion.3 = f32[64,128]{1,0:T(8,128)} fusion(bf16[768,8192]{1,0:T(8,128)(2,1)} %own.6, bf16[128,8192]{1,0:T(8,128)(2,1)S(1)} %copy-done.2, f32[128]{0:T(128)S(1)} %add_rsqrt_fusion.1, f32[768]{0:T(1024)S(1)} %add_rsqrt_fusion, s32[768]{0:T(1024)S(1)} %copy-done.4), kind=kOutput, calls=%fused_computation.6 | convolution fusion | flops 1623638016 | bytes 14719488 | tf_op jit(solution)/shard_map/dot_general | solution.py:328
  34.5 9.8 %shard_map.60.local = f32[768,768]{1,0:T(8,128)S(1)} custom-call(s32[2]{0:T(128)S(1)} %pad_add_fusion.place, bf16[768,8192]{1,0:T(8,128)(2,1)} %own.6, bf16[768,8192]{1,0:T(8,128)(2,1)} %collective-permute-done.4.other), custom_call_target="tpu_custom_call" | custom-call | flops 9663676416 | bytes 25165824 | tf_op jit(solution)/shard_map/pallas_call | solution.py:215
  44.3 70.4 %collective-permute-done.3.partner = bf16[768,3072]{1,0:T(8,128)(2,1)} collective-permute-done((bf16[768,3072]{1,0:T(8,128)(2,1)}, bf16[768,3072]{1,0:T(8,128)(2,1)}, u32[]{:S(2)}, u32[]{:S(2)}) %collective-permute-start.3) | collective-permute-done | bytes 4718624 | tf_op jit(solution)/shard_map/ppermute | solution.py:22
  114.7 3.1 %collective-permute-done.near.near1 = bf16[768,3072]{1,0:T(8,128)(2,1)} collective-permute-done((bf16[768,3072]{1,0:T(8,128)(2,1)}, bf16[768,3072]{1,0:T(8,128)(2,1)}, u32[]{:S(2)}, u32[]{:S(2)}) %collective-permute-start) | collective-permute-done | bytes 4718624 | tf_op jit(solution)/shard_map/ppermute | solution.py:22
  117.9 11.4 %shard_map.61 = (f32[768,768]{1,0:T(8,128)S(1)}, f32[768,768]{1,0:T(8,128)S(1)}) custom-call(s32[2]{0:T(128)S(1)} %pad_add_fusion.place, bf16[768,8192]{1,0:T(8,128)(2,1)} %own.6, bf16[768,3072]{1,0:T(8,128)(2,1)} %collective-permute-done.3.partner, bf16[768,3072]{1,0:T(8,128)(2,1)} %collective-permute-done.near.near1), custom_call_target="tpu_custom_call" | custom-call | flops 768 | bytes 768 | tf_op jit(solution)/shard_map/pallas_call | solution.py:118
  131.4 16.8 %collective-permute-done.1.partner = bf16[768,1024]{1,0:T(8,128)(2,1)} collective-permute-done((bf16[768,1024]{1,0:T(8,128)(2,1)}, bf16[768,1024]{1,0:T(8,128)(2,1)}, u32[]{:S(2)}, u32[]{:S(2)}) %collective-permute-start.1) | collective-permute-done | bytes 1572896 | tf_op jit(solution)/shard_map/ppermute | solution.py:22
  148.2 3.0 %collective-permute-done.2.near.near2 = bf16[768,1024]{1,0:T(8,128)(2,1)} collective-permute-done((bf16[768,1024]{1,0:T(8,128)(2,1)}, bf16[768,1024]{1,0:T(8,128)(2,1)}, u32[]{:S(2)}, u32[]{:S(2)}) %collective-permute-start.2) | collective-permute-done | bytes 1572896 | tf_op jit(solution)/shard_map/ppermute | solution.py:22
  152.3 5.3 %shard_map.62 = (bf16[768,768]{1,0:T(8,128)(2,1)S(1)}, bf16[768,768]{1,0:T(8,128)(2,1)S(1)}) custom-call(s32[2]{0:T(128)S(1)} %pad_add_fusion.place, bf16[768,1024]{1,0:T(8,128)(2,1)} %get-tuple-element.40.mine, bf16[768,1024]{1,0:T(8,128)(2,1)} %collective-permute-done.1.partner, bf16[768,1024]{1,0:T(8,128)(2,1)} %collective-permute-done.2.near.near2, ...), custom_call_target="tpu_custom_call" | custom-call | flops 35389440000 | bytes 94371840 | tf_op jit(solution)/shard_map/pallas_call | solution.py:150
  159.3 2.1 collective-permute-start.13
  161.4 1.9 collective-permute-start.11
  163.3 9.6 %shard_map.63.kept = bf16[768,768]{1,0:T(8,128)(2,1)S(1)} custom-call(s32[2]{0:T(128)S(1)} %pad_add_fusion.place, bf16[768,8192]{1,0:T(8,128)(2,1)} %own.6, bf16[768,3072]{1,0:T(8,128)(2,1)} %collective-permute-done.near.near1, bf16[768,1024]{1,0:T(8,128)(2,1)} %collective-permute-done.2.near.near2, bf16[768,3072]{1,0:T(8,128)(2,1)S(1)} %collective-permute-done.8.other1, ...), custom_call_target="tpu_custom_call" | custom-call | flops 3623878656 | bytes 14155776 | tf_op jit(solution)/shard_map/pallas_call | solution.py:189
  174.2 2.6 %collective-permute-start.16 = (bf16[768,768]{1,0:T(8,128)(2,1)S(1)}, bf16[768,768]{1,0:T(8,128)(2,1)}, u32[]{:S(2)}, u32[]{:S(2)}) collective-permute-start(bf16[768,768]{1,0:T(8,128)(2,1)S(1)} %shard_map.63.kept), channel_id=1, source_target_pairs={{0,4},{4,8},{8,12},{12,0},{16,20},{20,24},{24,28},{28,16}} | collective-permute-start | bytes 3538952 | tf_op jit(solution)/shard_map/ppermute | solution.py:22
  176.7 10.2 %collective-permute-done.12.u = bf16[768,768]{1,0:T(8,128)(2,1)S(1)} collective-permute-done((bf16[768,768]{1,0:T(8,128)(2,1)S(1)}, bf16[768,768]{1,0:T(8,128)(2,1)S(1)}, u32[]{:S(2)}, u32[]{:S(2)}) %collective-permute-start.12) | collective-permute-done | bytes 1179680 | tf_op jit(solution)/shard_map/ppermute | solution.py:22
  187.0 4.0 %collective-permute-done.13.v = bf16[768,768]{1,0:T(8,128)(2,1)S(1)} collective-permute-done((bf16[768,768]{1,0:T(8,128)(2,1)S(1)}, bf16[768,768]{1,0:T(8,128)(2,1)S(1)}, u32[]{:S(2)}, u32[]{:S(2)}) %collective-permute-start.13) | collective-permute-done | bytes 1179680 | tf_op jit(solution)/shard_map/ppermute | solution.py:22
  191.0 2.6 %shard_map.64 = (f32[2,768,768]{2,1,0:T(8,128)}, f32[1,768]{1,0:T(1,128)S(1)}, f32[1,768]{1,0:T(1,128)S(1)}) custom-call(s32[2]{0:T(128)S(1)} %pad_add_fusion.place, bf16[768,768]{1,0:T(8,128)(2,1)S(1)} %collective-permute-done.12.u, bf16[768,768]{1,0:T(8,128)(2,1)S(1)} %collective-permute-done.13.v, bf16[768,768]{1,0:T(8,128)(2,1)S(1)} %get-tuple-element.58.kept, ...), custom_call_target="tpu_custom_call" | custom-call | flops 35389440000 | bytes 94371840 | tf_op jit(solution)/shard_map/pallas_call | solution.py:273
  194.3 4.3 %collective-permute-done.14 = f32[64,128]{1,0:T(8,128)S(1)} collective-permute-done((f32[64,128]{1,0:T(8,128)S(1)}, f32[64,128]{1,0:T(8,128)S(1)}, u32[]{:S(2)}, u32[]{:S(2)}) %collective-permute-start.14) | collective-permute-done | bytes 32800 | tf_op jit(solution)/shard_map/ppermute | solution.py:22
  201.5 2.6 %collective-permute-done.16.z = bf16[768,768]{1,0:T(8,128)(2,1)} collective-permute-done((bf16[768,768]{1,0:T(8,128)(2,1)S(1)}, bf16[768,768]{1,0:T(8,128)(2,1)}, u32[]{:S(2)}, u32[]{:S(2)}) %collective-permute-start.16) | collective-permute-done | bytes 1179680 | tf_op jit(solution)/shard_map/ppermute | solution.py:22
  204.1 4.0 %shard_map.65 = (f32[2,768,768]{2,1,0:T(8,128)}, f32[1,768]{1,0:T(1,128)S(1)}, f32[1,768]{1,0:T(1,128)S(1)}) custom-call(s32[2]{0:T(128)S(1)} %pad_add_fusion.place, bf16[768,768]{1,0:T(8,128)(2,1)} %collective-permute-done.10.y, bf16[768,768]{1,0:T(8,128)(2,1)} %collective-permute-done.16.z, ...), custom_call_target="tpu_custom_call", output_to_operand_aliasing={{0}: (7, {})} | custom-call | flops 4718592 | bytes 7077888 | tf_op jit(solution)/shard_map/pallas_call | solution.py:273
  208.9 1.8 collective-permute-start.17
  (44 shorter events, 14.2 us)
Async XLA Ops:
  8.7 25.9 %collective-permute-start.4 = (bf16[768,8192]{1,0:T(8,128)(2,1)}, bf16[768,8192]{1,0:T(8,128)(2,1)}, u32[]{:S(2)}, u32[]{:S(2)}) collective-permute-start(bf16[768,8192]{1,0:T(8,128)(2,1)} %own.6), channel_id=1, source_target_pairs={{0,1},{1,0},{2,3},{3,2},{4,5},{5,4},{6,7},{7,6},{8,9},{9,8},{10,11... | collective-permute-start | bytes 37748744 | tf_op jit(solution)/shard_map/ppermute | solution.py:22
  9.2 105.6 %collective-permute-start.3 = (bf16[768,3072]{1,0:T(8,128)(2,1)}, bf16[768,3072]{1,0:T(8,128)(2,1)}, u32[]{:S(2)}, u32[]{:S(2)}) collective-permute-start(bf16[768,3072]{1,0:T(8,128)(2,1)} %get-tuple-element.41), channel_id=1, source_target_pairs={{0,2},{1,3},{2,0},{3,1},{4,6},{5,7},{6,4},{7,5},{8,10},{9,11},{10,... | collective-permute-start | bytes 14155784 | tf_op jit(solution)/shard_map/ppermute | solution.py:22
  11.8 106.1 %collective-permute-start = (bf16[768,3072]{1,0:T(8,128)(2,1)}, bf16[768,3072]{1,0:T(8,128)(2,1)}, u32[]{:S(2)}, u32[]{:S(2)}) collective-permute-start(bf16[768,3072]{1,0:T(8,128)(2,1)} %get-tuple-element.37), channel_id=1, source_target_pairs={{0,12},{1,13},{2,6},{3,7},{4,0},{5,1},{6,10},{7,11},{8,4},{9,5},{1... | collective-permute-start | bytes 14155784 | tf_op jit(solution)/shard_map/ppermute | solution.py:22
  18.7 129.5 %collective-permute-start.1 = (bf16[768,1024]{1,0:T(8,128)(2,1)}, bf16[768,1024]{1,0:T(8,128)(2,1)}, u32[]{:S(2)}, u32[]{:S(2)}) collective-permute-start(bf16[768,1024]{1,0:T(8,128)(2,1)} %get-tuple-element.39), channel_id=1, source_target_pairs={{0,2},{1,3},{2,0},{3,1},{4,6},{5,7},{6,4},{7,5},{8,10},{9,11},{10,... | collective-permute-start | bytes 4718600 | tf_op jit(solution)/shard_map/ppermute | solution.py:22
  18.8 7.8 %copy-start.2 = (bf16[128,8192]{1,0:T(8,128)(2,1)S(1)}, bf16[128,8192]{1,0:T(8,128)(2,1)}, u32[]{:S(2)}) copy-start(bf16[128,8192]{1,0:T(8,128)(2,1)} %param.4) | copy-start | bytes 6291460
  18.8 8.3 %copy-start.4 = (s32[768]{0:T(1024)S(1)}, s32[768]{0:T(1024)}, u32[]{:S(2)}) copy-start(s32[768]{0:T(1024)} %param.5) | copy-start | bytes 9220
  18.8 132.4 %collective-permute-start.2 = (bf16[768,1024]{1,0:T(8,128)(2,1)}, bf16[768,1024]{1,0:T(8,128)(2,1)}, u32[]{:S(2)}, u32[]{:S(2)}) collective-permute-start(bf16[768,1024]{1,0:T(8,128)(2,1)} %get-tuple-element.40.mine), channel_id=1, source_target_pairs={{0,12},{1,13},{2,6},{3,7},{4,0},{5,1},{6,10},{7,11},{8,4},{9,5},{1... | collective-permute-start | bytes 4718600 | tf_op jit(solution)/shard_map/ppermute | solution.py:22
  44.3 85.0 %copy-start.3 = (f32[64,128]{1,0:T(8,128)S(1)}, f32[64,128]{1,0:T(8,128)}, u32[]{:S(2)}) copy-start(f32[64,128]{1,0:T(8,128)} %fusion.3) | copy-start | bytes 98308
  129.3 23.0 %collective-permute-start.7 = (f32[64,128]{1,0:T(8,128)S(1)}, f32[64,128]{1,0:T(8,128)S(1)}, u32[]{:S(2)}, u32[]{:S(2)}) collective-permute-start(f32[64,128]{1,0:T(8,128)S(1)} %copy-done.3), channel_id=1, source_target_pairs={{0,8},{1,9},{2,10},{3,11},{4,12},{5,13},{6,14},{7,15},{8,0},{9,1},... | collective-permute-start | bytes 98312 | tf_op jit(solution)/shard_map/ppermute | solution.py:22
  130.8 20.9 %collective-permute-start.5 = (f32[1,768]{1,0:T(1,128)S(1)}, f32[1,768]{1,0:T(1,128)S(1)}, u32[]{:S(2)}, u32[]{:S(2)}) collective-permute-start(f32[1,768]{1,0:T(1,128)S(1)} %rsqrt.26.inverse), channel_id=1, source_target_pairs={{0,1},{1,2},{2,3},{3,4},{4,5},{5,6},{6,7},{7,8},{8,9},{9,10},{10,1... | collective-permute-start | bytes 9224 | tf_op jit(solution)/shard_map/ppermute | solution.py:22
  130.8 21.4 %collective-permute-start.6 = (f32[1,768]{1,0:T(1,128)S(1)}, f32[1,768]{1,0:T(1,128)S(1)}, u32[]{:S(2)}, u32[]{:S(2)}) collective-permute-start(f32[1,768]{1,0:T(1,128)S(1)} %rsqrt.26.inverse), channel_id=1, source_target_pairs={{0,2},{1,3},{2,4},{3,5},{4,6},{5,7},{6,8},{7,9},{8,10},{9,11},{10,... | collective-permute-start | bytes 9224 | tf_op jit(solution)/shard_map/ppermute | solution.py:22
  152.3 11.0 %collective-permute-start.8 = (bf16[768,3072]{1,0:T(8,128)(2,1)}, bf16[768,3072]{1,0:T(8,128)(2,1)S(1)}, u32[]{:S(2)}, u32[]{:S(2)}) collective-permute-start(bf16[768,3072]{1,0:T(8,128)(2,1)} %collective-permute-done.3.partner), channel_id=1, source_target_pairs={{0,1},{1,0},{2,3},{3,2},{4,5},{5,4},{6,7},{7,6},{8,9},{9,8},{10,11... | collective-permute-start | bytes 14155784 | tf_op jit(solution)/shard_map/ppermute | solution.py:22
  157.6 5.7 %collective-permute-start.9 = (bf16[768,1024]{1,0:T(8,128)(2,1)}, bf16[768,1024]{1,0:T(8,128)(2,1)S(1)}, u32[]{:S(2)}, u32[]{:S(2)}) collective-permute-start(bf16[768,1024]{1,0:T(8,128)(2,1)} %collective-permute-done.1.partner), channel_id=1, source_target_pairs={{0,1},{1,0},{2,3},{3,2},{4,5},{5,4},{6,7},{7,6},{8,9},{9,8},{10,11... | collective-permute-start | bytes 4718600 | tf_op jit(solution)/shard_map/ppermute | solution.py:22
  158.1 28.8 %collective-permute-start.12 = (bf16[768,768]{1,0:T(8,128)(2,1)S(1)}, bf16[768,768]{1,0:T(8,128)(2,1)S(1)}, u32[]{:S(2)}, u32[]{:S(2)}) collective-permute-start(bf16[768,768]{1,0:T(8,128)(2,1)S(1)} %get-tuple-element.53), channel_id=1, source_target_pairs={{0,2},{1,3},{2,0},{3,1},{4,6},{5,7},{6,4},{7,5},{8,10},{9,11},{10,... | collective-permute-start | bytes 3538952 | tf_op jit(solution)/shard_map/ppermute | solution.py:22
  159.3 31.7 %collective-permute-start.13 = (bf16[768,768]{1,0:T(8,128)(2,1)S(1)}, bf16[768,768]{1,0:T(8,128)(2,1)S(1)}, u32[]{:S(2)}, u32[]{:S(2)}) collective-permute-start(bf16[768,768]{1,0:T(8,128)(2,1)S(1)} %get-tuple-element.58.kept), channel_id=1, source_target_pairs={{0,4},{1,5},{4,8},{5,9},{8,12},{9,13},{12,0},{13,1},{16,20},{17,21... | collective-permute-start | bytes 3538952 | tf_op jit(solution)/shard_map/ppermute | solution.py:22
  161.4 32.9 %collective-permute-start.11 = (f32[64,128]{1,0:T(8,128)S(1)}, f32[64,128]{1,0:T(8,128)S(1)}, u32[]{:S(2)}, u32[]{:S(2)}) collective-permute-start(f32[64,128]{1,0:T(8,128)S(1)} %add.66), channel_id=1, source_target_pairs={{0,4},{1,5},{2,6},{3,7},{4,0},{5,1},{6,2},{7,3},{8,12},{9,13},{10,... | collective-permute-start | bytes 98312 | tf_op jit(solution)/shard_map/ppermute | solution.py:22
  172.9 28.6 %collective-permute-start.10 = (bf16[768,768]{1,0:T(8,128)(2,1)S(1)}, bf16[768,768]{1,0:T(8,128)(2,1)}, u32[]{:S(2)}, u32[]{:S(2)}) collective-permute-start(bf16[768,768]{1,0:T(8,128)(2,1)S(1)} %shard_map.63.kept), channel_id=1, source_target_pairs={{1,2},{3,0},{5,6},{7,4},{9,10},{11,8},{13,14},{15,12},{17,18},{19,... | collective-permute-start | bytes 3538952 | tf_op jit(solution)/shard_map/ppermute | solution.py:22
  174.2 29.9 %collective-permute-start.16 = (bf16[768,768]{1,0:T(8,128)(2,1)S(1)}, bf16[768,768]{1,0:T(8,128)(2,1)}, u32[]{:S(2)}, u32[]{:S(2)}) collective-permute-start(bf16[768,768]{1,0:T(8,128)(2,1)S(1)} %shard_map.63.kept), channel_id=1, source_target_pairs={{0,4},{4,8},{8,12},{12,0},{16,20},{20,24},{24,28},{28,16}} | collective-permute-start | bytes 3538952 | tf_op jit(solution)/shard_map/ppermute | solution.py:22
  193.6 0.6 copy-start
  194.2 4.4 %collective-permute-start.14 = (f32[64,128]{1,0:T(8,128)S(1)}, f32[64,128]{1,0:T(8,128)S(1)}, u32[]{:S(2)}, u32[]{:S(2)}) collective-permute-start(f32[64,128]{1,0:T(8,128)S(1)} %add.67), channel_id=1, source_target_pairs={{0,2},{1,3},{2,0},{3,1},{4,6},{5,7},{6,4},{7,5},{8,10},{9,11},{10,... | collective-permute-start | bytes 98312 | tf_op jit(solution)/shard_map/ppermute | solution.py:22
  199.2 2.2 %collective-permute-start.15 = (f32[64,128]{1,0:T(8,128)}, f32[64,128]{1,0:T(8,128)}, u32[]{:S(2)}, u32[]{:S(2)}) collective-permute-start(f32[64,128]{1,0:T(8,128)} %add.68), channel_id=1, source_target_pairs={{0,1},{1,0},{2,3},{3,2},{4,5},{5,4},{6,7},{7,6},{8,9},{9,8},{10,11... | collective-permute-start | bytes 98312 | tf_op jit(solution)/shard_map/ppermute | solution.py:22
  204.1 4.0 %copy-start.1 = (f32[1,768]{1,0:T(1,128)S(1)}, f32[1,768]{1,0:T(1,128)}, u32[]{:S(2)}) copy-start(f32[1,768]{1,0:T(1,128)} %copy-done) | copy-start | bytes 9220
  208.1 3.9 %collective-permute-start.18 = (f32[1,768]{1,0:T(1,128)S(1)}, f32[1,768]{1,0:T(1,128)S(1)}, u32[]{:S(2)}, u32[]{:S(2)}) collective-permute-start(f32[1,768]{1,0:T(1,128)S(1)} %copy-done.1), channel_id=1, source_target_pairs={{0,14},{1,15},{2,0},{3,1},{4,2},{5,3},{6,4},{7,5},{8,6},{9,7},{10,... | collective-permute-start | bytes 9224 | tf_op jit(solution)/shard_map/ppermute | solution.py:22
  208.9 3.1 %collective-permute-start.17 = (f32[1,768]{1,0:T(1,128)S(1)}, f32[1,768]{1,0:T(1,128)S(1)}, u32[]{:S(2)}, u32[]{:S(2)}) collective-permute-start(f32[1,768]{1,0:T(1,128)S(1)} %get-tuple-element.67), channel_id=1, source_target_pairs={{0,15},{1,0},{2,1},{3,2},{4,3},{5,4},{6,5},{7,6},{8,7},{9,8},{10,9... | collective-permute-start | bytes 9224 | tf_op jit(solution)/shard_map/ppermute | solution.py:22
